TPU v7x, 32 devices: a whole 2x2x4 slice. The times are simulated.
32 devices in a mesh: ka: 16 (over z, y, x), orb: 2 (over core).
Axes of the slice: x: 2, y: 2, z: 4, core: 2. Of those that a mesh axis runs over, the one named last changes fastest.
Arguments:
- coefficients: bfloat16 [16, 8192, 128], P('ka', 'orb'), may hold values from -0.59765625 to 0.59765625
- potential: bfloat16 [3, 64, 3, 128, 128], P(None, 'orb'), may hold values from -0.3125 to 0.3125
- block_cols: int32 [3, 64, 3], P(None, 'orb'), may hold values from 0 to 63
- block_counts: int32 [3, 64], P(None, 'orb'), may hold values from 1 to 3, as said below
- partners: int32 [3, 16], replicated, may hold values from 0 to 15, each once within a row
- gaps: float32 [3, 16, 128, 128], P(None, 'ka', 'orb'), may hold values from 0.5 to 4
Outputs:
- couplings: float32 [3, 16, 128, 128], P(None, 'ka', 'orb')
Inputs may be any that keep to these rules, and one draw needn't show every extreme that they name: `partners`: each row names every k-point once. `block_cols`: slots at or past a block row's count are unused and may hold any column. `block_counts`: some block row of every mode uses all 3 slots.
All inputs are finite; a program needn't handle non-finite values.
Results may differ from a plain program's by a relative error of at most 0.0029.
Values may be sent and summed in bfloat16 or wider, within the bound.
No kernel may reach another device: no remote copies, remote signals or barrier semaphores. Data moves between devices by JAX's collectives and lax.ppermute only.
A program may use at most 128 MiB of HBM per device.

v0:
```python
import jax
import jax.numpy as jnp
from jax import lax
from jax.sharding import PartitionSpec as P


def project(whole, potential, block_cols, block_counts, phonon):
    block_size = potential.shape[-1]
    slot_count = potential.shape[2]
    local_rows = potential.shape[1]
    points = whole.shape[0]
    bands = whole.shape[2]
    tiles = whole.reshape(points, whole.shape[1] // block_size, block_size, bands)
    total = jnp.zeros((points, local_rows, block_size, bands), jnp.float32)
    for slot in range(slot_count):
        chosen = jnp.take(tiles, block_cols[phonon, :, slot], axis=1)
        live = slot < block_counts[phonon]
        blocks = jnp.where(
            live[:, None, None], potential[phonon, :, slot], jnp.zeros((), potential.dtype)
        )
        total = total + jnp.einsum(
            "rab,krbn->kran", blocks, chosen, preferred_element_type=jnp.float32
        )
    return total.reshape(points, local_rows * block_size, bands).astype(jnp.bfloat16)


def per_device(coefficients, potential, block_cols, block_counts, partners, gaps):
    whole = lax.all_gather(coefficients, "orb", axis=1, tiled=True)
    projected = jnp.stack(
        [
            project(whole, potential, block_cols, block_counts, phonon)
            for phonon in range(potential.shape[0])
        ]
    )
    transposed = lax.all_to_all(coefficients, "ka", split_axis=1, concat_axis=0, tiled=True)
    permuted = [
        jnp.take(transposed, partners[phonon], axis=0) for phonon in range(partners.shape[0])
    ]
    returned = [
        lax.all_to_all(permuted_item, "ka", split_axis=0, concat_axis=1, tiled=True)
        for permuted_item in permuted
    ]
    matched = jnp.stack(returned)
    partial_value = jnp.einsum(
        "mkrp,mkrn->mkpn", matched, projected, preferred_element_type=jnp.float32
    )
    summed = lax.psum_scatter(partial_value, "orb", scatter_dimension=2, tiled=True)
    return summed / gaps


def solution(mesh):
    return jax.shard_map(
        per_device,
        mesh=mesh,
        in_specs=(
            P("ka", "orb", None),
            P(None, "orb", None, None, None),
            P(None, "orb", None),
            P(None, "orb"),
            P(),
            P(None, "ka", "orb", None),
        ),
        out_specs=P(None, "ka", "orb", None),
        check_vma=False,
    )
```

profile of v0, /device:TPU:0, one launch (start us, length us, event | category | flops | bytes accessed | tf_op | source)
XLA Modules:
  0.0 183.5 jit_solution(1731629767560282066)
XLA Ops:
  6.5 3.2 %copy.83 = bf16[1,4096,128]{2,0,1:T(2,128)(2,1)S(1)} copy(bf16[1,4096,128]{2,1,0:T(8,128)(2,1)} %param.10) | data formatting | bytes 2097152 | tf_op args[0]
  10.2 22.4 %reduce = bf16[4096,128]{1,0:T(8,128)(2,1)S(1)} reduce(bf16[4096,1,128]{2,1,0:T(2,128)(2,1)S(1)} %bitcast.240, bf16[]{:T(256)} %broadcast.182), dimensions={1}, to_apply=%bitcast.226.reduce_sub_computation | reduce | bytes 2097154
  33.8 8.3 %all-to-all-start = ((bf16[16,2,16384]{2,1,0:T(2,128)(2,1)}), bf16[16,2,16384]{2,1,0:T(2,128)(2,1)S(1)}, u32[]{:S(2)}, u32[]{:S(2)}) async-start(bf16[16,2,16384]{2,1,0:T(2,128)(2,1)} %reshape.378), calls=%async_computation | async-start | bytes 2097152 | tf_op jit(solution)/shard_map/all_to_all | solution.py:35
  42.1 24.4 %all-to-all-done = bf16[16,2,16384]{2,1,0:T(2,128)(2,1)S(1)} async-done(((bf16[16,2,16384]{2,1,0:T(2,128)(2,1)}), bf16[16,2,16384]{2,1,0:T(2,128)(2,1)S(1)}, u32[]{:S(2)}, u32[]{:S(2)}) %all-to-all-start) | async-done | bytes 1048608 | tf_op jit(solution)/shard_map/all_to_all | solution.py:35
  69.6 6.0 %all-to-all-start.3 = ((bf16[16,256,128]{2,1,0:T(8,128)(2,1)}), bf16[16,256,128]{2,1,0:T(8,128)(2,1)S(1)}, u32[]{:S(2)}, u32[]{:S(2)}) async-start(bf16[16,256,128]{2,1,0:T(8,128)(2,1)} %broadcast_select_fusion), calls=%async_computation.3 | async-start | bytes 2097152 | tf_op jit(solution)/shard_map/all_to_all | solution.py:40
  78.3 20.2 %all-to-all-done.3 = bf16[16,256,128]{2,1,0:T(8,128)(2,1)S(1)} async-done(((bf16[16,256,128]{2,1,0:T(8,128)(2,1)}), bf16[16,256,128]{2,1,0:T(8,128)(2,1)S(1)}, u32[]{:S(2)}, u32[]{:S(2)}) %all-to-all-start.3) | async-done | bytes 1048608 | tf_op jit(solution)/shard_map/all_to_all | solution.py:40
  98.5 6.1 %all-to-all-start.2 = ((bf16[16,256,128]{2,1,0:T(8,128)(2,1)}), bf16[16,256,128]{2,1,0:T(8,128)(2,1)}, u32[]{:S(2)}, u32[]{:S(2)}) async-start(bf16[16,256,128]{2,1,0:T(8,128)(2,1)} %broadcast_select_fusion.1), calls=%async_computation.2 | async-start | bytes 2097152 | tf_op jit(solution)/shard_map/all_to_all | solution.py:40
  106.6 3.4 %gather_fusion.9 = bf16[32,128,128]{2,1,0:T(8,128)(2,1)} fusion(bf16[64,128,128]{2,1,0:T(8,128)(2,1)} %bitcast.227, s32[1024]{0:T(1024)S(1)} %get-tuple-element.62), kind=kCustom, calls=%fused_computation.9.clone | custom fusion | bytes 2097280 | tf_op jit(solution)/shard_map/jit(_take)/gather | solution.py:16
  110.0 1.7 gather_fusion.10
  111.7 1.7 gather_fusion.6
  113.4 1.7 gather_fusion.7
  115.0 3.5 %fusion.17 = f32[32,128,128]{1,2,0:T(8,128)} fusion(bf16[32,128,128]{2,1,0:T(8,128)(2,1)} %gather_fusion.9, bf16[3,32,3,128,128]{4,3,2,1,0:T(8,128)(2,1)} %param.11, pred[32]{0:T(512)(128)(4,1)S(1)} %get-tuple-element.31, pred[32]{0:T(512)(128)(4,1)S(1)} %get-tuple-element.58), kind=kOutput, calls=%fused_computation.45 | convolution fusion | flops 135266304 | bytes 4194368 | tf_op jit(solution)/shard_map/rab,krbn->kran/dot_general | solution.py:21
  118.5 3.2 %fusion.10 = f32[32,128,128]{1,2,0:T(8,128)} fusion(bf16[32,128,128]{2,1,0:T(8,128)(2,1)S(1)} %copy-done.9, bf16[3,32,3,128,128]{4,3,2,1,0:T(8,128)(2,1)} %param.11, pred[32]{0:T(512)(128)(4,1)S(1)} %get-tuple-element.45, pred[32]{0:T(512)(128)(4,1)S(1)} %get-tuple-element.55), kind=kOutput, calls=%fused_computation.29 | convolution fusion | flops 135266304 | bytes 4194368 | tf_op jit(solution)/shard_map/rab,krbn->kran/dot_general | solution.py:21
  121.8 3.0 %fusion.12 = f32[32,128,128]{1,2,0:T(8,128)} fusion(bf16[32,128,128]{2,1,0:T(8,128)(2,1)S(1)} %copy-done.8, bf16[3,32,3,128,128]{4,3,2,1,0:T(8,128)(2,1)} %param.11, pred[32]{0:T(512)(128)(4,1)S(1)} %get-tuple-element.37, pred[32]{0:T(512)(128)(4,1)S(1)} %get-tuple-element.59), kind=kOutput, calls=%fused_computation.34 | convolution fusion | flops 135266304 | bytes 4194368 | tf_op jit(solution)/shard_map/rab,krbn->kran/dot_general | solution.py:21
  124.8 2.7 %all-to-all-done.2 = bf16[16,256,128]{2,1,0:T(8,128)(2,1)} async-done(((bf16[16,256,128]{2,1,0:T(8,128)(2,1)}), bf16[16,256,128]{2,1,0:T(8,128)(2,1)}, u32[]{:S(2)}, u32[]{:S(2)}) %all-to-all-start.2) | async-done | bytes 1048608 | tf_op jit(solution)/shard_map/all_to_all | solution.py:40
  127.5 6.1 %all-to-all-start.1 = ((bf16[16,256,128]{2,1,0:T(8,128)(2,1)}), bf16[16,256,128]{2,1,0:T(8,128)(2,1)}, u32[]{:S(2)}, u32[]{:S(2)}) async-start(bf16[16,256,128]{2,1,0:T(8,128)(2,1)} %broadcast_select_fusion.2), calls=%async_computation.1 | async-start | bytes 2097152 | tf_op jit(solution)/shard_map/all_to_all | solution.py:40
  133.8 3.4 %fusion.11 = f32[32,128,128]{1,2,0:T(8,128)} fusion(bf16[32,128,128]{2,1,0:T(8,128)(2,1)} %gather_fusion.7, bf16[3,32,3,128,128]{4,3,2,1,0:T(8,128)(2,1)} %param.11, pred[32]{0:T(512)(128)(4,1)S(1)} %get-tuple-element.35, pred[32]{0:T(512)(128)(4,1)S(1)} %get-tuple-element.53), kind=kOutput, calls=%fused_computation.32 | convolution fusion | flops 135266304 | bytes 4194368 | tf_op jit(solution)/shard_map/rab,krbn->kran/dot_general | solution.py:21
  137.2 1.7 gather_fusion.11
  138.9 1.7 gather_fusion.8
  140.6 1.7 gather_fusion.3
  142.3 1.7 gather_fusion.4
  143.9 1.7 gather_fusion.5
  145.6 2.2 %fusion.14 = f32[32,128,128]{1,2,0:T(8,128)S(1)} fusion(bf16[32,128,128]{2,1,0:T(8,128)(2,1)} %gather_fusion.3, bf16[3,32,3,128,128]{4,3,2,1,0:T(8,128)(2,1)} %param.11, pred[32]{0:T(512)(128)(4,1)S(1)} %get-tuple-element.41, pred[32]{0:T(512)(128)(4,1)S(1)} %get-tuple-element.57), kind=kOutput, calls=%fused_computation.39 | convolution fusion | flops 135266304 | bytes 4194368 | tf_op jit(solution)/shard_map/rab,krbn->kran/dot_general | solution.py:21
  147.9 1.9 %fusion.13 = f32[32,128,128]{1,2,0:T(8,128)S(1)} fusion(bf16[32,128,128]{2,1,0:T(8,128)(2,1)S(1)} %copy-done.10, bf16[3,32,3,128,128]{4,3,2,1,0:T(8,128)(2,1)} %param.11, pred[32]{0:T(512)(128)(4,1)S(1)} %get-tuple-element.39, pred[32]{0:T(512)(128)(4,1)S(1)} %get-tuple-element.52), kind=kOutput, calls=%fused_computation.37 | convolution fusion | flops 135266304 | bytes 4194368 | tf_op jit(solution)/shard_map/rab,krbn->kran/dot_general | solution.py:21
  150.2 3.0 %add_convert_fusion = bf16[32,128,128]{1,2,0:T(8,128)(2,1)} fusion(f32[32,128,128]{1,2,0:T(8,128)S(1)} %copy-done.4, f32[32,128,128]{1,2,0:T(8,128)S(1)} %copy-done.6, bf16[32,128,128]{2,1,0:T(8,128)(2,1)S(1)} %copy-done.3, bf16[3,32,3,128,128]{4,3,2,1,0:T(8,128)(2,1)} %param.11, pred[32]{0:T(512)(128)(4,1)S(1)} %get-tuple-element.43, ...), kind=kOutput, calls=%fused_computation.23 | convolution fusion | flops 136839168 | bytes 7340096 | tf_op jit(solution)/shard_map/rab,krbn->kran/dot_general | solution.py:21
  153.2 2.9 %add_convert_fusion.1 = bf16[32,128,128]{1,2,0:T(8,128)(2,1)} fusion(f32[32,128,128]{1,2,0:T(8,128)S(1)} %copy-done.5, f32[32,128,128]{1,2,0:T(8,128)S(1)} %copy-done.7, bf16[32,128,128]{2,1,0:T(8,128)(2,1)S(1)} %copy-done.1, bf16[3,32,3,128,128]{4,3,2,1,0:T(8,128)(2,1)} %param.11, pred[32]{0:T(512)(128)(4,1)S(1)} %get-tuple-element.33, ...), kind=kOutput, calls=%fused_computation.24 | convolution fusion | flops 136839168 | bytes 7340096 | tf_op jit(solution)/shard_map/rab,krbn->kran/dot_general | solution.py:21
  156.1 2.8 %add_convert_fusion.2 = bf16[32,128,128]{1,2,0:T(8,128)(2,1)} fusion(f32[32,128,128]{1,2,0:T(8,128)S(1)} %fusion.14, f32[32,128,128]{1,2,0:T(8,128)S(1)} %fusion.13, bf16[32,128,128]{2,1,0:T(8,128)(2,1)S(1)} %copy-done.2, bf16[3,32,3,128,128]{4,3,2,1,0:T(8,128)(2,1)} %param.11, pred[32]{0:T(512)(128)(4,1)S(1)} %get-tuple-element.13, ...), kind=kOutput, calls=%fused_computation.25 | convolution fusion | flops 136839168 | bytes 7340096 | tf_op jit(solution)/shard_map/rab,krbn->kran/dot_general | solution.py:21
  159.5 1.5 copy.71
  161.0 1.5 copy.70
  162.5 3.6 %fusion.9 = f32[3,1,128,128]{3,2,0,1:T(8,128)} fusion(bf16[1,1,4096,128]{3,2,0,1:T(8,128)(2,1)} %bitcast.242, bf16[1,1,4096,128]{3,2,0,1:T(8,128)(2,1)} %bitcast.243, bf16[1,1,4096,128]{3,2,0,1:T(8,128)(2,1)} %bitcast.244, bf16[1,1,4096,128]{2,3,0,1:T(8,128)(2,1)S(1)} %copy.72, bf16[1,1,4096,128]{2,3,0,1:T(8,128)(2,1)S(1)} %copy.71, ...), kind=kOutput, calls=%fused_computation.26 | convolution fusion | flops 408944640 | bytes 6488064 | tf_op jit(solution)/shard_map/mkrp,mkrn->mkpn/dot_general | solution.py:44
  166.1 9.0 %reduce-scatter.2.cloned.1.call-done = f32[3,1,64,128]{3,2,0,1:T(8,128)} async-done(((f32[3,1,128,128]{3,2,0,1:T(8,128)}), f32[3,1,64,128]{3,2,0,1:T(8,128)}) %reduce-scatter.2.cloned.1.call-update) | async-done | bytes 98320 | tf_op jit(solution)/shard_map/reduce_scatter | solution.py:47
  175.1 1.6 fusion.70
  (58 shorter events, 10.5 us)
Async XLA Ops:
  32.6 9.5 %copy-start.13 = (s32[3,16]{1,0:T(4,128)S(1)}, s32[3,16]{1,0:T(4,128)}, u32[]{:S(2)}) copy-start(s32[3,16]{1,0:T(4,128)} %param.14) | copy-start | bytes 580
  33.8 32.8 %all-to-all-start = ((bf16[16,2,16384]{2,1,0:T(2,128)(2,1)}), bf16[16,2,16384]{2,1,0:T(2,128)(2,1)S(1)}, u32[]{:S(2)}, u32[]{:S(2)}) async-start(bf16[16,2,16384]{2,1,0:T(2,128)(2,1)} %reshape.378), calls=%async_computation | async-start | bytes 2097152 | tf_op jit(solution)/shard_map/all_to_all | solution.py:35
  69.6 6.7 %copy-start.12 = (s32[3,32,3]{1,2,0:T(4,128)S(1)}, s32[3,32,3]{1,2,0:T(4,128)}, u32[]{:S(2)}) copy-start(s32[3,32,3]{1,2,0:T(4,128)} %param.12) | copy-start | bytes 3460
  69.6 28.9 %all-to-all-start.3 = ((bf16[16,256,128]{2,1,0:T(8,128)(2,1)}), bf16[16,256,128]{2,1,0:T(8,128)(2,1)S(1)}, u32[]{:S(2)}, u32[]{:S(2)}) async-start(bf16[16,256,128]{2,1,0:T(8,128)(2,1)} %broadcast_select_fusion), calls=%async_computation.3 | async-start | bytes 2097152 | tf_op jit(solution)/shard_map/all_to_all | solution.py:40
  75.6 31.0 %all-gather.2.cloned.1.call-start = ((), (), s32[]{:S(2)}) async-start(), calls=%async_computation.5 | async-start | bytes 3145728 | tf_op jit(solution)/shard_map/all_gather | solution.py:28
  77.1 27.5 %copy-start.14 = (s32[3,32]{1,0:T(4,128)S(1)}, s32[3,32]{1,0:T(4,128)}, u32[]{:S(2)}) copy-start(s32[3,32]{1,0:T(4,128)} %param.13) | copy-start | bytes 1156
  98.5 28.9 %all-to-all-start.2 = ((bf16[16,256,128]{2,1,0:T(8,128)(2,1)}), bf16[16,256,128]{2,1,0:T(8,128)(2,1)}, u32[]{:S(2)}, u32[]{:S(2)}) async-start(bf16[16,256,128]{2,1,0:T(8,128)(2,1)} %broadcast_select_fusion.1), calls=%async_computation.2 | async-start | bytes 2097152 | tf_op jit(solution)/shard_map/all_to_all | solution.py:40
  106.6 3.4 %copy-start = (bf16[1,8192,128]{2,1,0:T(8,128)(2,1)S(1)}, bf16[1,8192,128]{2,1,0:T(8,128)(2,1)}, u32[]{:S(2)}) copy-start(bf16[1,8192,128]{2,1,0:T(8,128)(2,1)} %all-gather.2.cloned.1.call-done) | copy-start | bytes 6291460
  115.0 3.5 %copy-start.9 = (bf16[32,128,128]{2,1,0:T(8,128)(2,1)S(1)}, bf16[32,128,128]{2,1,0:T(8,128)(2,1)}, u32[]{:S(2)}) copy-start(bf16[32,128,128]{2,1,0:T(8,128)(2,1)} %gather_fusion.10) | copy-start | bytes 3145732
  118.5 3.2 %copy-start.8 = (bf16[32,128,128]{2,1,0:T(8,128)(2,1)S(1)}, bf16[32,128,128]{2,1,0:T(8,128)(2,1)}, u32[]{:S(2)}) copy-start(bf16[32,128,128]{2,1,0:T(8,128)(2,1)} %gather_fusion.6) | copy-start | bytes 3145732
  127.5 33.5 %all-to-all-start.1 = ((bf16[16,256,128]{2,1,0:T(8,128)(2,1)}), bf16[16,256,128]{2,1,0:T(8,128)(2,1)}, u32[]{:S(2)}, u32[]{:S(2)}) async-start(bf16[16,256,128]{2,1,0:T(8,128)(2,1)} %broadcast_select_fusion.2), calls=%async_computation.1 | async-start | bytes 2097152 | tf_op jit(solution)/shard_map/all_to_all | solution.py:40
  133.6 41.5 %reduce-scatter.2.cloned.1.call-start = ((), (), s32[]{:S(2)}) async-start(), calls=%async_computation.6 | async-start | bytes 294912 | tf_op jit(solution)/shard_map/reduce_scatter | solution.py:47
  145.6 2.2 %copy-start.10 = (bf16[32,128,128]{2,1,0:T(8,128)(2,1)S(1)}, bf16[32,128,128]{2,1,0:T(8,128)(2,1)}, u32[]{:S(2)}) copy-start(bf16[32,128,128]{2,1,0:T(8,128)(2,1)} %gather_fusion.4) | copy-start | bytes 3145732
  145.6 4.1 %copy-start.6 = (f32[32,128,128]{1,2,0:T(8,128)S(1)}, f32[32,128,128]{1,2,0:T(8,128)}, u32[]{:S(2)}) copy-start(f32[32,128,128]{1,2,0:T(8,128)} %fusion.10) | copy-start | bytes 6291460
  147.8 1.9 %copy-start.3 = (bf16[32,128,128]{2,1,0:T(8,128)(2,1)S(1)}, bf16[32,128,128]{2,1,0:T(8,128)(2,1)}, u32[]{:S(2)}) copy-start(bf16[32,128,128]{2,1,0:T(8,128)(2,1)} %gather_fusion.11) | copy-start | bytes 3145732
  147.8 2.3 %copy-start.4 = (f32[32,128,128]{1,2,0:T(8,128)S(1)}, f32[32,128,128]{1,2,0:T(8,128)}, u32[]{:S(2)}) copy-start(f32[32,128,128]{1,2,0:T(8,128)} %fusion.17) | copy-start | bytes 6291460
  150.1 3.0 %copy-start.1 = (bf16[32,128,128]{2,1,0:T(8,128)(2,1)S(1)}, bf16[32,128,128]{2,1,0:T(8,128)(2,1)}, u32[]{:S(2)}) copy-start(bf16[32,128,128]{2,1,0:T(8,128)(2,1)} %gather_fusion.8) | copy-start | bytes 3145732
  150.1 3.0 %copy-start.5 = (f32[32,128,128]{1,2,0:T(8,128)S(1)}, f32[32,128,128]{1,2,0:T(8,128)}, u32[]{:S(2)}) copy-start(f32[32,128,128]{1,2,0:T(8,128)} %fusion.12) | copy-start | bytes 6291460
  150.2 3.0 %copy-start.7 = (f32[32,128,128]{1,2,0:T(8,128)S(1)}, f32[32,128,128]{1,2,0:T(8,128)}, u32[]{:S(2)}) copy-start(f32[32,128,128]{1,2,0:T(8,128)} %fusion.11) | copy-start | bytes 6291460
  153.2 2.9 %copy-start.2 = (bf16[32,128,128]{2,1,0:T(8,128)(2,1)S(1)}, bf16[32,128,128]{2,1,0:T(8,128)(2,1)}, u32[]{:S(2)}) copy-start(bf16[32,128,128]{2,1,0:T(8,128)(2,1)} %gather_fusion.5) | copy-start | bytes 3145732
  162.5 12.6 %copy-start.11 = (f32[3,1,64,128]{3,2,1,0:T(8,128)S(1)}, f32[3,1,64,128]{3,2,1,0:T(8,128)}, u32[]{:S(2)}) copy-start(f32[3,1,64,128]{3,2,1,0:T(8,128)} %param.15) | copy-start | bytes 294916
Sparse Core Ops, SparseCore 0:
  78.0 11.8 all-gather.1
  166.2 8.7 reduce-scatter.1
where the time goes:
time: 184 us; the launch traced here: 183 us
  waiting for transfers between devices  57 us (31%)
  matrix products  29.6 us (16%)
  local copies, waits for them, and re-layouts  29 us (16%)
  other arithmetic  27.5 us (15%)
  starting transfers between devices  26.6 us (14%)
  between operations  13.7 us (7%)
    dot_general x9, matrix products, project(): jnp.einsum('rab,krbn->kran', blocks, chosen, preferred_element_type=jnp.f...  26 us
    all_to_all x1, waiting for transfers between devices, per_device(): lax.all_to_all(coefficients, 'ka', split_axis=1, concat_axis=0, tiled=True)  24.4 us
    all_to_all x3, waiting for transfers between devices, per_device(): lax.all_to_all(permuted_item, 'ka', split_axis=0, concat_axis=1, tiled=True)  22.9 us
    unnamed x1, other arithmetic  22.4 us
    all_to_all x3, starting transfers between devices, per_device(): lax.all_to_all(permuted_item, 'ka', split_axis=0, concat_axis=1, tiled=True)  18.1 us
    gather x9, local copies, waits for them, and re-layouts, project(): chosen = jnp.take(tiles, block_cols[phonon, :, slot], axis=1)  16.8 us
    reduce_scatter x1, waiting for transfers between devices, per_device(): lax.psum_scatter(partial_value, 'orb', scatter_dimension=2, tiled=True)  8.96 us
    all_to_all x1, starting transfers between devices, per_device(): lax.all_to_all(coefficients, 'ka', split_axis=1, concat_axis=0, tiled=True)  8.31 us
  transfers between devices with their start and end apart: 6, of which 4 were waited for; matrix products, arithmetic and copies ran while one was open for 27% of the time, Pallas kernels for 0%

commit v1 on v0

v1 whole, which is shorter than its diff:
```python
import functools

import jax
import jax.numpy as jnp
from jax import lax
from jax.experimental import pallas as pl
from jax.experimental.pallas import tpu as pltpu
from jax.sharding import PartitionSpec as P

VMEM_LIMIT = 48 * 2**20
SMEM = pl.BlockSpec(memory_space=pltpu.SMEM)
VMEM = pl.BlockSpec(memory_space=pltpu.VMEM)
ANY = pl.BlockSpec(memory_space=pl.ANY)


def group_size(points, blocks):
    size = 1
    while (
        points % (2 * size) == 0 and 4 * size * size <= points and blocks % (2 * size) == 0
    ):
        size *= 2
    return size


def project_kernel(group, halves, pos, cols, counts, potential, *refs):
    sources = refs[: group * halves]
    out, whole, blocks, sems = refs[group * halves :]
    modes, rows, slots, size, _ = blocks.shape
    local_rows = potential.shape[1]
    chunk, half = pos[1], pos[2]
    copies = [
        pltpu.make_async_copy(
            potential.at[:, pl.ds(chunk * rows, rows)], blocks, sems.at[group * halves]
        )
    ]
    for shift in range(halves):
        for point in range(group):
            i = shift * group + point
            place = lax.rem(half + halves - shift, halves)
            copies.append(
                pltpu.make_async_copy(sources[i], whole.at[point, place], sems.at[i])
            )
    for copy in copies:
        copy.start()
    for copy in copies:
        copy.wait()
    for mode in range(modes):
        for row in range(rows):
            at = mode * local_rows + chunk * rows + row
            used = counts[at]
            left = []
            right = []
            for slot in range(slots):
                block = blocks[mode, row, slot]
                left.append(jnp.where(slot < used, block, jnp.zeros_like(block)))
                col = cols[at * slots + slot]
                place = lax.div(col, local_rows)
                start = pl.multiple_of(lax.rem(col, local_rows) * size, size)
                right.append(
                    jnp.concatenate(
                        [whole[point, place, pl.ds(start, size), :] for point in range(group)],
                        axis=1,
                    )
                )
            product = jnp.dot(
                jnp.concatenate(left, axis=1),
                jnp.concatenate(right, axis=0),
                preferred_element_type=jnp.float32,
            )
            turned = product.astype(jnp.bfloat16).T
            for point in range(group):
                out[point * modes + mode, :, row * size : (row + 1) * size] = turned[
                    point * size : (point + 1) * size
                ]


def project(pos, cols, counts, potential, sources, group, halves):
    modes, local_rows, slots, size, _ = potential.shape
    bands = sources[0].shape[1]
    rows = local_rows // group
    return pl.pallas_call(
        functools.partial(project_kernel, group, halves),
        out_shape=jax.ShapeDtypeStruct((group * modes, bands, rows * size), jnp.bfloat16),
        in_specs=[SMEM, SMEM, SMEM] + [ANY] * (1 + len(sources)),
        out_specs=VMEM,
        scratch_shapes=[
            pltpu.VMEM((group, halves, local_rows * size, bands), jnp.bfloat16),
            pltpu.VMEM((modes, rows, slots, size, size), jnp.bfloat16),
            pltpu.SemaphoreType.DMA((group * halves + 1,)),
        ],
        compiler_params=pltpu.CompilerParams(vmem_limit_bytes=VMEM_LIMIT),
        cost_estimate=pl.CostEstimate(
            flops=2 * modes * rows * slots * size * size * group * bands,
            bytes_accessed=30 * 2**20,
            transcendentals=0,
        ),
        name="project",
    )(pos, cols, counts, potential, *sources)


def couple_kernel(step, last, group, points, halves, pos, partners, *refs):
    sides = 1 if step == 0 else 2
    count = sides * group
    before = None
    if step > 0:
        before, refs = refs[0], refs[1:]
    projected, parts, refs = refs[0], refs[1 : 1 + count], refs[1 + count :]
    out, held, total, sems = refs
    pairs = projected.shape[0]
    modes = pairs // group
    outer, inner, half = pos[0], pos[1], pos[2]
    copies = [
        pltpu.make_async_copy(parts[i], held.at[i], sems.at[i]) for i in range(count)
    ]
    for copy in copies:
        copy.start()
    if step == 0:
        total[...] = jnp.zeros_like(total)
    else:
        total[...] = before[...]
    for copy in copies:
        copy.wait()

    def add(pair, carry):
        mine = outer * group + (inner ^ lax.div(pair, modes))
        other = partners[lax.rem(pair, modes) * points + mine]
        plane = lax.div(other, group)
        place = lax.rem(other, group) ^ inner
        if step == 0:
            hit = plane == outer
            at = place
        else:
            low = plane == outer - step
            hit = jnp.logical_or(low, plane == outer + step)
            at = place + jnp.where(low, 0, group)

        @pl.when(hit)
        def _():
            total[pair] += jnp.dot(
                projected[pair], held[at], preferred_element_type=jnp.float32
            )

        return carry

    lax.fori_loop(0, pairs, add, 0)
    if last:
        bands = total.shape[1]
        share = bands // halves
        for pair in range(pairs):
            turned = total[pair].T
            for part in range(halves):
                out[lax.rem(part + halves - half, halves), pair] = turned[
                    part * share : (part + 1) * share
                ]
    else:
        out[...] = total[...]


def couple(step, last, pos, partners, before, projected, parts, group, points, halves):
    pairs, bands, rows = projected.shape
    shape = (halves, pairs, bands // halves, bands) if last else (pairs, bands, bands)
    earlier = [] if before is None else [before]
    return pl.pallas_call(
        functools.partial(couple_kernel, step, last, group, points, halves),
        out_shape=jax.ShapeDtypeStruct(shape, jnp.float32),
        in_specs=[SMEM, SMEM] + [VMEM] * len(earlier) + [VMEM] + [ANY] * len(parts),
        out_specs=VMEM,
        scratch_shapes=[
            pltpu.VMEM((len(parts), rows, bands), jnp.bfloat16),
            pltpu.VMEM((pairs, bands, bands), jnp.float32),
            pltpu.SemaphoreType.DMA((len(parts),)),
        ],
        compiler_params=pltpu.CompilerParams(vmem_limit_bytes=VMEM_LIMIT),
        cost_estimate=pl.CostEstimate(
            flops=2 * pairs * bands * bands * rows,
            bytes_accessed=8 * 2**20,
            transcendentals=0,
        ),
        name=f"couple{step}",
    )(pos, partners, *earlier, projected, *parts)


def solution(mesh):
    points = mesh.shape["ka"]
    halves = mesh.shape["orb"]

    def per_device(coefficients, potential, block_cols, block_counts, partners, gaps):
        modes, local_rows, slots, size, _ = potential.shape
        group = group_size(points, local_rows)
        planes = points // group
        own = coefficients[0]
        rows = own.shape[0] // group
        place = lax.axis_index("ka")
        outer, inner = place // group, place % group
        half = lax.axis_index("orb")
        pos = jnp.stack([outer, inner, half]).astype(jnp.int32)
        cols = block_cols.reshape(-1)
        counts = block_counts.reshape(-1)
        pairing = partners.reshape(-1)

        def swap(value, bit):
            if bit == 0:
                return value
            return lax.ppermute(value, "ka", [(i, i ^ bit) for i in range(points)])

        def rotate(value, shift):
            if shift == 0:
                return value
            return lax.ppermute(
                value, "orb", [(i, (i + shift) % halves) for i in range(halves)]
            )

        def chunk_for(bit):
            return lax.dynamic_slice_in_dim(own, (inner ^ bit) * rows, rows, 0)

        chunks = [swap(chunk_for(bit), bit) for bit in range(group)]
        near = [swap(own, bit) for bit in range(group)]
        sources = list(near)
        for shift in range(1, halves):
            sources += [rotate(item, shift) for item in near]
        steps = [chunks]
        low, high = chunks, chunks
        for _ in range(1, planes):
            up = [(i, i + group) for i in range(points - group)]
            down = [(i + group, i) for i in range(points - group)]
            low = [lax.ppermute(item, "ka", up) for item in low]
            high = [lax.ppermute(item, "ka", down) for item in high]
            steps.append(low + high)
        projected = project(pos, cols, counts, potential, sources, group, halves)
        total = None
        for step, parts in enumerate(steps):
            total = couple(
                step,
                step == planes - 1,
                pos,
                pairing,
                total,
                projected,
                parts,
                group,
                points,
                halves,
            )
        summed = total[0]
        for shift in range(1, halves):
            summed = summed + rotate(total[shift], shift)
        summed = summed.reshape((group, modes) + summed.shape[1:])
        result = summed[0]
        for bit in range(1, group):
            result = result + swap(summed[bit], bit)
        return result[:, None] / gaps

    return jax.shard_map(
        per_device,
        mesh=mesh,
        in_specs=(
            P("ka", "orb", None),
            P(None, "orb", None, None, None),
            P(None, "orb", None),
            P(None, "orb"),
            P(),
            P(None, "ka", "orb", None),
        ),
        out_specs=P(None, "ka", "orb", None),
        check_vma=False,
    )
```

time: 184 us -> 164 us (0.89)
  the two profiles are of different devices: /device:TPU:0 before, /device:TPU:24 now
where the time goes in v1:
time: 164 us; the launch traced here: 162 us
  starting transfers between devices  75.1 us (46%)
  waiting for transfers between devices  47.8 us (29%)
  Pallas kernels  20.4 us (12%)
  local copies, waits for them, and re-layouts  17.5 us (11%)
    ppermute x12, starting transfers between devices, per_device(): high = [lax.ppermute(item, 'ka', down) for item in high]  47.6 us
    ppermute x12, waiting for transfers between devices, per_device(): low = [lax.ppermute(item, 'ka', up) for item in low]  25.3 us
    ppermute x12, starting transfers between devices, per_device(): low = [lax.ppermute(item, 'ka', up) for item in low]  15.4 us
    ppermute x9, waiting for transfers between devices, swap(): return lax.ppermute(value, 'ka', [(i, i ^ bit) for i in range(points)])  15 us
    unnamed x87, local copies, waits for them, and re-layouts  14.5 us
    pallas_call x4, Pallas kernels, couple(): pl.pallas_call(functools.partial(couple_kernel, step, last, group, points...  13.1 us
    ppermute x9, starting transfers between devices, swap(): return lax.ppermute(value, 'ka', [(i, i ^ bit) for i in range(points)])  11 us
    pallas_call x1, Pallas kernels, project(): pl.pallas_call(functools.partial(project_kernel, group, halves), out_shap...  7.29 us
  transfers between devices with their start and end apart: 38, of which 13 were waited for; matrix products, arithmetic and copies ran while one was open for 2% of the time, Pallas kernels for 10%

profile of v1, /device:TPU:24, one launch (start us, length us, event | category | flops | bytes accessed | tf_op | source)
XLA Modules:
  0.0 162.4 jit_solution(9721569858024090059)
XLA Ops:
  1.3 1.6 collective-permute-start.7
  6.1 4.6 %collective-permute-start.14 = (bf16[1024,128]{1,0:T(8,128)(2,1)S(1)}, bf16[1024,128]{1,0:T(8,128)(2,1)S(1)}, u32[]{:S(2)}, u32[]{:S(2)}) collective-permute-start(bf16[1024,128]{1,0:T(8,128)(2,1)S(1)} %get-tuple-element.7.refs_1_), channel_id=1, source_target_pairs={{8,0},{10,2},{12,4},{14,6},{16,8},{18,10},{20,12},{22,14},{24,16},... | collective-permute-start | bytes 786440 | tf_op jit(solution)/shard_map/ppermute | solution.py:227
  12.0 4.2 %collective-permute-done.8.refs_3_ = bf16[1024,128]{1,0:T(8,128)(2,1)S(1)} collective-permute-done((bf16[1024,128]{1,0:T(8,128)(2,1)S(1)}, bf16[1024,128]{1,0:T(8,128)(2,1)S(1)}, u32[]{:S(2)}, u32[]{:S(2)}) %collective-permute-start.8) | collective-permute-done | bytes 262176 | tf_op jit(solution)/shard_map/ppermute | solution.py:204
  18.8 5.2 %collective-permute-start.15 = (bf16[1024,128]{1,0:T(8,128)(2,1)S(1)}, bf16[1024,128]{1,0:T(8,128)(2,1)S(1)}, u32[]{:S(2)}, u32[]{:S(2)}) collective-permute-start(bf16[1024,128]{1,0:T(8,128)(2,1)S(1)} %collective-permute-done.7.refs_2_), channel_id=1, source_target_pairs={{8,0},{10,2},{12,4},{14,6},{16,8},{18,10},{20,12},{22,14},{24,16},... | collective-permute-start | bytes 786440 | tf_op jit(solution)/shard_map/ppermute | solution.py:227
  24.7 3.9 %collective-permute-start.16 = (bf16[1024,128]{1,0:T(8,128)(2,1)S(1)}, bf16[1024,128]{1,0:T(8,128)(2,1)S(1)}, u32[]{:S(2)}, u32[]{:S(2)}) collective-permute-start(bf16[1024,128]{1,0:T(8,128)(2,1)S(1)} %collective-permute-done.8.refs_3_), channel_id=1, source_target_pairs={{8,0},{10,2},{12,4},{14,6},{16,8},{18,10},{20,12},{22,14},{24,16},... | collective-permute-start | bytes 786440 | tf_op jit(solution)/shard_map/ppermute | solution.py:227
  29.3 2.4 %collective-permute-start.17 = (bf16[1024,128]{1,0:T(8,128)(2,1)S(1)}, bf16[1024,128]{1,0:T(8,128)(2,1)S(1)}, u32[]{:S(2)}, u32[]{:S(2)}) collective-permute-start(bf16[1024,128]{1,0:T(8,128)(2,1)S(1)} %collective-permute-done.9.refs_4_), channel_id=1, source_target_pairs={{8,0},{10,2},{12,4},{14,6},{16,8},{18,10},{20,12},{22,14},{24,16},... | collective-permute-start | bytes 786440 | tf_op jit(solution)/shard_map/ppermute | solution.py:227
  34.4 2.0 %collective-permute-start.1 = (bf16[4096,128]{1,0:T(8,128)(2,1)}, bf16[4096,128]{1,0:T(8,128)(2,1)S(1)}, u32[]{:S(2)}, u32[]{:S(2)}) collective-permute-start(bf16[4096,128]{1,0:T(8,128)(2,1)} %bitcast.29), channel_id=1, source_target_pairs={{0,4},{2,6},{4,0},{6,2},{8,12},{10,14},{12,8},{14,10},{16,20},{18,... | collective-permute-start | bytes 3145736 | tf_op jit(solution)/shard_map/ppermute | solution.py:204
  37.9 4.6 %collective-permute-start.22 = (bf16[1024,128]{1,0:T(8,128)(2,1)S(1)}, bf16[1024,128]{1,0:T(8,128)(2,1)S(1)}, u32[]{:S(2)}, u32[]{:S(2)}) collective-permute-start(bf16[1024,128]{1,0:T(8,128)(2,1)S(1)} %collective-permute-done.14.refs_6_), channel_id=1, source_target_pairs={{8,0},{10,2},{12,4},{14,6},{16,8},{18,10},{20,12},{22,14},{24,16},... | collective-permute-start | bytes 786440 | tf_op jit(solution)/shard_map/ppermute | solution.py:227
  48.3 4.9 %collective-permute-done.19.refs_3_ = bf16[1024,128]{1,0:T(8,128)(2,1)} collective-permute-done((bf16[1024,128]{1,0:T(8,128)(2,1)S(1)}, bf16[1024,128]{1,0:T(8,128)(2,1)}, u32[]{:S(2)}, u32[]{:S(2)}) %collective-permute-start.19) | collective-permute-done | bytes 262176 | tf_op jit(solution)/shard_map/ppermute | solution.py:226
  55.2 1.9 %collective-permute-done.20.refs_4_ = bf16[1024,128]{1,0:T(8,128)(2,1)S(1)} collective-permute-done((bf16[1024,128]{1,0:T(8,128)(2,1)S(1)}, bf16[1024,128]{1,0:T(8,128)(2,1)S(1)}, u32[]{:S(2)}, u32[]{:S(2)}) %collective-permute-start.20) | collective-permute-done | bytes 262176 | tf_op jit(solution)/shard_map/ppermute | solution.py:226
  57.1 3.5 %collective-permute-start.23 = (bf16[1024,128]{1,0:T(8,128)(2,1)S(1)}, bf16[1024,128]{1,0:T(8,128)(2,1)S(1)}, u32[]{:S(2)}, u32[]{:S(2)}) collective-permute-start(bf16[1024,128]{1,0:T(8,128)(2,1)S(1)} %collective-permute-done.15.refs_7_), channel_id=1, source_target_pairs={{8,0},{10,2},{12,4},{14,6},{16,8},{18,10},{20,12},{22,14},{24,16},... | collective-permute-start | bytes 786440 | tf_op jit(solution)/shard_map/ppermute | solution.py:227
  61.7 3.9 %collective-permute-start.24 = (bf16[1024,128]{1,0:T(8,128)(2,1)S(1)}, bf16[1024,128]{1,0:T(8,128)(2,1)S(1)}, u32[]{:S(2)}, u32[]{:S(2)}) collective-permute-start(bf16[1024,128]{1,0:T(8,128)(2,1)S(1)} %collective-permute-done.16.refs_8_), channel_id=1, source_target_pairs={{8,0},{10,2},{12,4},{14,6},{16,8},{18,10},{20,12},{22,14},{24,16},... | collective-permute-start | bytes 786440 | tf_op jit(solution)/shard_map/ppermute | solution.py:227
  66.9 4.4 %collective-permute-start.25 = (bf16[1024,128]{1,0:T(8,128)(2,1)S(1)}, bf16[1024,128]{1,0:T(8,128)(2,1)S(1)}, u32[]{:S(2)}, u32[]{:S(2)}) collective-permute-start(bf16[1024,128]{1,0:T(8,128)(2,1)S(1)} %collective-permute-done.17.refs_9_), channel_id=1, source_target_pairs={{8,0},{10,2},{12,4},{14,6},{16,8},{18,10},{20,12},{22,14},{24,16},... | collective-permute-start | bytes 786440 | tf_op jit(solution)/shard_map/ppermute | solution.py:227
  72.5 5.6 %collective-permute-done.1.refs_2_ = bf16[4096,128]{1,0:T(8,128)(2,1)S(1)} collective-permute-done((bf16[4096,128]{1,0:T(8,128)(2,1)}, bf16[4096,128]{1,0:T(8,128)(2,1)S(1)}, u32[]{:S(2)}, u32[]{:S(2)}) %collective-permute-start.1) | collective-permute-done | bytes 1048608 | tf_op jit(solution)/shard_map/ppermute | solution.py:204
  80.7 8.7 %collective-permute-done.26.refs_2_ = bf16[1024,128]{1,0:T(8,128)(2,1)S(1)} collective-permute-done((bf16[1024,128]{1,0:T(8,128)(2,1)S(1)}, bf16[1024,128]{1,0:T(8,128)(2,1)S(1)}, u32[]{:S(2)}, u32[]{:S(2)}) %collective-permute-start.26) | collective-permute-done | bytes 262176 | tf_op jit(solution)/shard_map/ppermute | solution.py:226
  90.1 3.6 %collective-permute-start.30 = (bf16[1024,128]{1,0:T(8,128)(2,1)S(1)}, bf16[1024,128]{1,0:T(8,128)(2,1)S(1)}, u32[]{:S(2)}, u32[]{:S(2)}) collective-permute-start(bf16[1024,128]{1,0:T(8,128)(2,1)S(1)} %collective-permute-done.22.refs_6_), channel_id=1, source_target_pairs={{8,0},{10,2},{12,4},{14,6},{16,8},{18,10},{20,12},{22,14},{24,16},... | collective-permute-start | bytes 786440 | tf_op jit(solution)/shard_map/ppermute | solution.py:227
  94.5 4.2 %collective-permute-done.30.refs_6_ = bf16[1024,128]{1,0:T(8,128)(2,1)S(1)} collective-permute-done((bf16[1024,128]{1,0:T(8,128)(2,1)S(1)}, bf16[1024,128]{1,0:T(8,128)(2,1)S(1)}, u32[]{:S(2)}, u32[]{:S(2)}) %collective-permute-start.30) | collective-permute-done | bytes 262176 | tf_op jit(solution)/shard_map/ppermute | solution.py:227
  102.0 9.3 %collective-permute-done.27.refs_3_ = bf16[1024,128]{1,0:T(8,128)(2,1)} collective-permute-done((bf16[1024,128]{1,0:T(8,128)(2,1)}, bf16[1024,128]{1,0:T(8,128)(2,1)}, u32[]{:S(2)}, u32[]{:S(2)}) %collective-permute-start.27) | collective-permute-done | bytes 262176 | tf_op jit(solution)/shard_map/ppermute | solution.py:226
  112.6 5.3 %collective-permute-start.31 = (bf16[1024,128]{1,0:T(8,128)(2,1)}, bf16[1024,128]{1,0:T(8,128)(2,1)}, u32[]{:S(2)}, u32[]{:S(2)}) collective-permute-start(bf16[1024,128]{1,0:T(8,128)(2,1)} %copy-done.26), channel_id=1, source_target_pairs={{8,0},{10,2},{12,4},{14,6},{16,8},{18,10},{20,12},{22,14},{24,16},... | collective-permute-start | bytes 786440 | tf_op jit(solution)/shard_map/ppermute | solution.py:227
  117.9 3.9 %collective-permute-start.32 = (bf16[1024,128]{1,0:T(8,128)(2,1)}, bf16[1024,128]{1,0:T(8,128)(2,1)}, u32[]{:S(2)}, u32[]{:S(2)}) collective-permute-start(bf16[1024,128]{1,0:T(8,128)(2,1)} %copy-done.28), channel_id=1, source_target_pairs={{8,0},{10,2},{12,4},{14,6},{16,8},{18,10},{20,12},{22,14},{24,16},... | collective-permute-start | bytes 786440 | tf_op jit(solution)/shard_map/ppermute | solution.py:227
  121.8 2.4 %collective-permute-start.33 = (bf16[1024,128]{1,0:T(8,128)(2,1)}, bf16[1024,128]{1,0:T(8,128)(2,1)}, u32[]{:S(2)}, u32[]{:S(2)}) collective-permute-start(bf16[1024,128]{1,0:T(8,128)(2,1)} %copy-done.30), channel_id=1, source_target_pairs={{8,0},{10,2},{12,4},{14,6},{16,8},{18,10},{20,12},{22,14},{24,16},... | collective-permute-start | bytes 786440 | tf_op jit(solution)/shard_map/ppermute | solution.py:227
  128.1 7.3 %project.1.refs_0_.refs_1_ = bf16[12,128,1024]{2,1,0:T(8,128)(2,1)} custom-call(s32[3]{0:T(128)S(1)} %pad_add_fusion.pos, s32[288]{0:T(512)S(1)} %reshape.23.cols, s32[96]{0:T(128)S(1)} %reshape.24.counts, bf16[3,32,3,128,128]{4,3,2,1,0:T(8,128)(2,1)} %potential.1, bf16[4096,128]{1,0:T(8,128)(2,1)S(1)} %bitcast.32, ...), custom_call_target="tpu_custom_call" | custom-call | flops 1207959552 | bytes 31457280 | tf_op jit(solution)/shard_map/project/pallas_call | solution.py:81
  135.4 1.9 %copy-done = bf16[12,128,1024]{2,1,0:T(8,128)(2,1)S(1)} copy-done((bf16[12,128,1024]{2,1,0:T(8,128)(2,1)S(1)}, bf16[12,128,1024]{2,1,0:T(8,128)(2,1)}, u32[]{:S(2)}) %copy-start) | copy-done | bytes 3145752
  137.4 1.9 %couple0.1.refs_0_ = f32[12,128,128]{2,1,0:T(8,128)S(1)} custom-call(s32[3]{0:T(128)S(1)} %pad_add_fusion.pos, s32[48]{0:T(128)S(1)} %reshape.22.partners, bf16[12,128,1024]{2,1,0:T(8,128)(2,1)S(1)} %copy-done, bf16[1024,128]{1,0:T(8,128)(2,1)S(1)} %get-tuple-element.7.refs_1_, bf16[1024,128]{1,0:T(8,128)(2,1)S(1)} %copy-done.37, ...), custom_call_target="tpu_custom_call" | custom-call | flops 402653184 | bytes 8388608 | tf_op jit(solution)/shard_map/couple0/pallas_call | solution.py:163
  139.4 3.0 %couple1.1.refs_0_ = f32[12,128,128]{2,1,0:T(8,128)S(1)} custom-call(s32[3]{0:T(128)S(1)} %pad_add_fusion.pos, s32[48]{0:T(128)S(1)} %reshape.22.partners, f32[12,128,128]{2,1,0:T(8,128)S(1)} %couple0.1.refs_0_, bf16[12,128,1024]{2,1,0:T(8,128)(2,1)} %project.1.refs_0_.refs_1_, bf16[1024,128]{1,0:T(8,128)(2,1)S(1)} %copy-done.3, ...), custom_call_target="tpu_custom_call" | custom-call | flops 402653184 | bytes 8388608 | tf_op jit(solution)/shard_map/couple1/pallas_call | solution.py:163
  142.4 3.3 %couple2.1.refs_0_ = f32[12,128,128]{2,1,0:T(8,128)S(1)} custom-call(s32[3]{0:T(128)S(1)} %pad_add_fusion.pos, s32[48]{0:T(128)S(1)} %reshape.22.partners, f32[12,128,128]{2,1,0:T(8,128)S(1)} %couple1.1.refs_0_, bf16[12,128,1024]{2,1,0:T(8,128)(2,1)} %project.1.refs_0_.refs_1_, bf16[1024,128]{1,0:T(8,128)(2,1)S(1)} %copy-done.19, ...), custom_call_target="tpu_custom_call" | custom-call | flops 402653184 | bytes 8388608 | tf_op jit(solution)/shard_map/couple2/pallas_call | solution.py:163
  145.8 4.9 %couple3.1 = f32[2,12,64,128]{3,2,1,0:T(8,128)S(1)} custom-call(s32[3]{0:T(128)S(1)} %pad_add_fusion.pos, s32[48]{0:T(128)S(1)} %reshape.22.partners, f32[12,128,128]{2,1,0:T(8,128)S(1)} %couple2.1.refs_0_, bf16[12,128,1024]{2,1,0:T(8,128)(2,1)} %project.1.refs_0_.refs_1_, bf16[1024,128]{1,0:T(8,128)(2,1)S(1)} %copy-done.33, ...), custom_call_target="tpu_custom_call" | custom-call | flops 402653184 | bytes 8388608 | tf_op jit(solution)/shard_map/couple3/pallas_call | solution.py:163
  150.8 1.7 %collective-permute-done.34 = f32[12,64,128]{2,1,0:T(8,128)S(1)} collective-permute-done((f32[12,64,128]{2,1,0:T(8,128)S(1)}, f32[12,64,128]{2,1,0:T(8,128)S(1)}, u32[]{:S(2)}, u32[]{:S(2)}) %collective-permute-start.34) | collective-permute-done | bytes 393248 | tf_op jit(solution)/shard_map/ppermute | solution.py:209
  152.6 2.4 %collective-permute-start.35 = (f32[3,64,128]{2,1,0:T(8,128)S(1)}, f32[3,64,128]{2,1,0:T(8,128)S(1)}, u32[]{:S(2)}, u32[]{:S(2)}) collective-permute-start(f32[3,64,128]{2,1,0:T(8,128)S(1)} %get-tuple-element.9), channel_id=1, source_target_pairs={{0,2},{2,0},{4,6},{6,4},{8,10},{10,8},{12,14},{14,12},{16,18},{18,... | collective-permute-start | bytes 294920 | tf_op jit(solution)/shard_map/ppermute | solution.py:204
  155.0 1.5 collective-permute-start.37
  156.6 1.6 collective-permute-done.35
  158.2 3.5 %collective-permute-done.36 = f32[3,64,128]{2,1,0:T(8,128)S(1)} collective-permute-done((f32[3,64,128]{2,1,0:T(8,128)S(1)}, f32[3,64,128]{2,1,0:T(8,128)S(1)}, u32[]{:S(2)}, u32[]{:S(2)}) %collective-permute-start.36) | collective-permute-done | bytes 98336 | tf_op jit(solution)/shard_map/ppermute | solution.py:204
  (145 shorter events, 38.5 us)
Async XLA Ops:
  1.3 9.4 %collective-permute-start.7 = (bf16[1024,128]{1,0:T(8,128)(2,1)S(1)}, bf16[1024,128]{1,0:T(8,128)(2,1)S(1)}, u32[]{:S(2)}, u32[]{:S(2)}) collective-permute-start(bf16[1024,128]{1,0:T(8,128)(2,1)S(1)} %get-tuple-element.6), channel_id=1, source_target_pairs={{0,2},{2,0},{4,6},{6,4},{8,10},{10,8},{12,14},{14,12},{16,18},{18,... | collective-permute-start | bytes 786440 | tf_op jit(solution)/shard_map/ppermute | solution.py:204
  2.8 13.4 %collective-permute-start.8 = (bf16[1024,128]{1,0:T(8,128)(2,1)S(1)}, bf16[1024,128]{1,0:T(8,128)(2,1)S(1)}, u32[]{:S(2)}, u32[]{:S(2)}) collective-permute-start(bf16[1024,128]{1,0:T(8,128)(2,1)S(1)} %get-tuple-element.8), channel_id=1, source_target_pairs={{0,4},{2,6},{4,0},{6,2},{8,12},{10,14},{12,8},{14,10},{16,20},{18,... | collective-permute-start | bytes 786440 | tf_op jit(solution)/shard_map/ppermute | solution.py:204
  4.3 13.2 %collective-permute-start.9 = (bf16[1024,128]{1,0:T(8,128)(2,1)S(1)}, bf16[1024,128]{1,0:T(8,128)(2,1)S(1)}, u32[]{:S(2)}, u32[]{:S(2)}) collective-permute-start(bf16[1024,128]{1,0:T(8,128)(2,1)S(1)} %get-tuple-element.5), channel_id=1, source_target_pairs={{0,6},{2,4},{4,2},{6,0},{8,14},{10,12},{12,10},{14,8},{16,22},{18,... | collective-permute-start | bytes 786440 | tf_op jit(solution)/shard_map/ppermute | solution.py:204
  4.8 14.0 %collective-permute-start.10 = (bf16[1024,128]{1,0:T(8,128)(2,1)S(1)}, bf16[1024,128]{1,0:T(8,128)(2,1)S(1)}, u32[]{:S(2)}, u32[]{:S(2)}) collective-permute-start(bf16[1024,128]{1,0:T(8,128)(2,1)S(1)} %get-tuple-element.7.refs_1_), channel_id=1, source_target_pairs={{0,8},{2,10},{4,12},{6,14},{8,16},{10,18},{12,20},{14,22},{16,24},... | collective-permute-start | bytes 786440 | tf_op jit(solution)/shard_map/ppermute | solution.py:226
  6.1 18.6 %collective-permute-start.14 = (bf16[1024,128]{1,0:T(8,128)(2,1)S(1)}, bf16[1024,128]{1,0:T(8,128)(2,1)S(1)}, u32[]{:S(2)}, u32[]{:S(2)}) collective-permute-start(bf16[1024,128]{1,0:T(8,128)(2,1)S(1)} %get-tuple-element.7.refs_1_), channel_id=1, source_target_pairs={{8,0},{10,2},{12,4},{14,6},{16,8},{18,10},{20,12},{22,14},{24,16},... | collective-permute-start | bytes 786440 | tf_op jit(solution)/shard_map/ppermute | solution.py:227
  10.7 18.7 %collective-permute-start.11 = (bf16[1024,128]{1,0:T(8,128)(2,1)S(1)}, bf16[1024,128]{1,0:T(8,128)(2,1)S(1)}, u32[]{:S(2)}, u32[]{:S(2)}) collective-permute-start(bf16[1024,128]{1,0:T(8,128)(2,1)S(1)} %collective-permute-done.7.refs_2_), channel_id=1, source_target_pairs={{0,8},{2,10},{4,12},{6,14},{8,16},{10,18},{12,20},{14,22},{16,24},... | collective-permute-start | bytes 786440 | tf_op jit(solution)/shard_map/ppermute | solution.py:226
  16.2 16.2 %collective-permute-start.12 = (bf16[1024,128]{1,0:T(8,128)(2,1)S(1)}, bf16[1024,128]{1,0:T(8,128)(2,1)S(1)}, u32[]{:S(2)}, u32[]{:S(2)}) collective-permute-start(bf16[1024,128]{1,0:T(8,128)(2,1)S(1)} %collective-permute-done.8.refs_3_), channel_id=1, source_target_pairs={{0,8},{2,10},{4,12},{6,14},{8,16},{10,18},{12,20},{14,22},{16,24},... | collective-permute-start | bytes 786440 | tf_op jit(solution)/shard_map/ppermute | solution.py:226
  17.5 16.9 %collective-permute-start.13 = (bf16[1024,128]{1,0:T(8,128)(2,1)S(1)}, bf16[1024,128]{1,0:T(8,128)(2,1)S(1)}, u32[]{:S(2)}, u32[]{:S(2)}) collective-permute-start(bf16[1024,128]{1,0:T(8,128)(2,1)S(1)} %collective-permute-done.9.refs_4_), channel_id=1, source_target_pairs={{0,8},{2,10},{4,12},{6,14},{8,16},{10,18},{12,20},{14,22},{16,24},... | collective-permute-start | bytes 786440 | tf_op jit(solution)/shard_map/ppermute | solution.py:226
  18.8 15.6 %collective-permute-start.15 = (bf16[1024,128]{1,0:T(8,128)(2,1)S(1)}, bf16[1024,128]{1,0:T(8,128)(2,1)S(1)}, u32[]{:S(2)}, u32[]{:S(2)}) collective-permute-start(bf16[1024,128]{1,0:T(8,128)(2,1)S(1)} %collective-permute-done.7.refs_2_), channel_id=1, source_target_pairs={{8,0},{10,2},{12,4},{14,6},{16,8},{18,10},{20,12},{22,14},{24,16},... | collective-permute-start | bytes 786440 | tf_op jit(solution)/shard_map/ppermute | solution.py:227
  24.7 11.8 %collective-permute-start.16 = (bf16[1024,128]{1,0:T(8,128)(2,1)S(1)}, bf16[1024,128]{1,0:T(8,128)(2,1)S(1)}, u32[]{:S(2)}, u32[]{:S(2)}) collective-permute-start(bf16[1024,128]{1,0:T(8,128)(2,1)S(1)} %collective-permute-done.8.refs_3_), channel_id=1, source_target_pairs={{8,0},{10,2},{12,4},{14,6},{16,8},{18,10},{20,12},{22,14},{24,16},... | collective-permute-start | bytes 786440 | tf_op jit(solution)/shard_map/ppermute | solution.py:227
  29.3 8.6 %collective-permute-start.17 = (bf16[1024,128]{1,0:T(8,128)(2,1)S(1)}, bf16[1024,128]{1,0:T(8,128)(2,1)S(1)}, u32[]{:S(2)}, u32[]{:S(2)}) collective-permute-start(bf16[1024,128]{1,0:T(8,128)(2,1)S(1)} %collective-permute-done.9.refs_4_), channel_id=1, source_target_pairs={{8,0},{10,2},{12,4},{14,6},{16,8},{18,10},{20,12},{22,14},{24,16},... | collective-permute-start | bytes 786440 | tf_op jit(solution)/shard_map/ppermute | solution.py:227
  32.4 10.8 %collective-permute-start.18 = (bf16[1024,128]{1,0:T(8,128)(2,1)S(1)}, bf16[1024,128]{1,0:T(8,128)(2,1)S(1)}, u32[]{:S(2)}, u32[]{:S(2)}) collective-permute-start(bf16[1024,128]{1,0:T(8,128)(2,1)S(1)} %collective-permute-done.10.refs_2_), channel_id=1, source_target_pairs={{0,8},{2,10},{4,12},{6,14},{8,16},{10,18},{12,20},{14,22},{16,24},... | collective-permute-start | bytes 786440 | tf_op jit(solution)/shard_map/ppermute | solution.py:226
  34.4 37.6 %collective-permute-start = (bf16[4096,128]{1,0:T(8,128)(2,1)}, bf16[4096,128]{1,0:T(8,128)(2,1)S(1)}, u32[]{:S(2)}, u32[]{:S(2)}) collective-permute-start(bf16[4096,128]{1,0:T(8,128)(2,1)} %bitcast.28), channel_id=1, source_target_pairs={{0,2},{2,0},{4,6},{6,4},{8,10},{10,8},{12,14},{14,12},{16,18},{18,... | collective-permute-start | bytes 3145736 | tf_op jit(solution)/shard_map/ppermute | solution.py:204
  34.4 43.7 %collective-permute-start.1 = (bf16[4096,128]{1,0:T(8,128)(2,1)}, bf16[4096,128]{1,0:T(8,128)(2,1)S(1)}, u32[]{:S(2)}, u32[]{:S(2)}) collective-permute-start(bf16[4096,128]{1,0:T(8,128)(2,1)} %bitcast.29), channel_id=1, source_target_pairs={{0,4},{2,6},{4,0},{6,2},{8,12},{10,14},{12,8},{14,10},{16,20},{18,... | collective-permute-start | bytes 3145736 | tf_op jit(solution)/shard_map/ppermute | solution.py:204
  36.5 41.7 %collective-permute-start.2 = (bf16[4096,128]{1,0:T(8,128)(2,1)}, bf16[4096,128]{1,0:T(8,128)(2,1)S(1)}, u32[]{:S(2)}, u32[]{:S(2)}) collective-permute-start(bf16[4096,128]{1,0:T(8,128)(2,1)} %bitcast.30), channel_id=1, source_target_pairs={{0,6},{2,4},{4,2},{6,0},{8,14},{10,12},{12,10},{14,8},{16,22},{18,... | collective-permute-start | bytes 3145736 | tf_op jit(solution)/shard_map/ppermute | solution.py:204
  43.2 10.0 %collective-permute-start.19 = (bf16[1024,128]{1,0:T(8,128)(2,1)S(1)}, bf16[1024,128]{1,0:T(8,128)(2,1)}, u32[]{:S(2)}, u32[]{:S(2)}) collective-permute-start(bf16[1024,128]{1,0:T(8,128)(2,1)S(1)} %collective-permute-done.11.refs_3_), channel_id=1, source_target_pairs={{0,8},{2,10},{4,12},{6,14},{8,16},{10,18},{12,20},{14,22},{16,24},... | collective-permute-start | bytes 786440 | tf_op jit(solution)/shard_map/ppermute | solution.py:226
  46.4 10.7 %collective-permute-start.20 = (bf16[1024,128]{1,0:T(8,128)(2,1)S(1)}, bf16[1024,128]{1,0:T(8,128)(2,1)S(1)}, u32[]{:S(2)}, u32[]{:S(2)}) collective-permute-start(bf16[1024,128]{1,0:T(8,128)(2,1)S(1)} %collective-permute-done.12.refs_4_), channel_id=1, source_target_pairs={{0,8},{2,10},{4,12},{6,14},{8,16},{10,18},{12,20},{14,22},{16,24},... | collective-permute-start | bytes 786440 | tf_op jit(solution)/shard_map/ppermute | solution.py:226
  57.1 9.8 %collective-permute-start.23 = (bf16[1024,128]{1,0:T(8,128)(2,1)S(1)}, bf16[1024,128]{1,0:T(8,128)(2,1)S(1)}, u32[]{:S(2)}, u32[]{:S(2)}) collective-permute-start(bf16[1024,128]{1,0:T(8,128)(2,1)S(1)} %collective-permute-done.15.refs_7_), channel_id=1, source_target_pairs={{8,0},{10,2},{12,4},{14,6},{16,8},{18,10},{20,12},{22,14},{24,16},... | collective-permute-start | bytes 786440 | tf_op jit(solution)/shard_map/ppermute | solution.py:227
  61.7 10.3 %collective-permute-start.24 = (bf16[1024,128]{1,0:T(8,128)(2,1)S(1)}, bf16[1024,128]{1,0:T(8,128)(2,1)S(1)}, u32[]{:S(2)}, u32[]{:S(2)}) collective-permute-start(bf16[1024,128]{1,0:T(8,128)(2,1)S(1)} %collective-permute-done.16.refs_8_), channel_id=1, source_target_pairs={{8,0},{10,2},{12,4},{14,6},{16,8},{18,10},{20,12},{22,14},{24,16},... | collective-permute-start | bytes 786440 | tf_op jit(solution)/shard_map/ppermute | solution.py:227
  66.9 11.8 %collective-permute-start.25 = (bf16[1024,128]{1,0:T(8,128)(2,1)S(1)}, bf16[1024,128]{1,0:T(8,128)(2,1)S(1)}, u32[]{:S(2)}, u32[]{:S(2)}) collective-permute-start(bf16[1024,128]{1,0:T(8,128)(2,1)S(1)} %collective-permute-done.17.refs_9_), channel_id=1, source_target_pairs={{8,0},{10,2},{12,4},{14,6},{16,8},{18,10},{20,12},{22,14},{24,16},... | collective-permute-start | bytes 786440 | tf_op jit(solution)/shard_map/ppermute | solution.py:227
  72.0 28.7 %collective-permute-start.3 = (bf16[4096,128]{1,0:T(8,128)(2,1)}, bf16[4096,128]{1,0:T(8,128)(2,1)}, u32[]{:S(2)}, u32[]{:S(2)}) collective-permute-start(bf16[4096,128]{1,0:T(8,128)(2,1)} %bitcast.31), channel_id=1, source_target_pairs={{0,1},{1,0},{2,3},{3,2},{4,5},{5,4},{6,7},{7,6},{8,9},{9,8},{10,11... | collective-permute-start | bytes 3145736 | tf_op jit(solution)/shard_map/ppermute | solution.py:209
  72.0 40.6 %collective-permute-start.4 = (bf16[4096,128]{1,0:T(8,128)(2,1)S(1)}, bf16[4096,128]{1,0:T(8,128)(2,1)}, u32[]{:S(2)}, u32[]{:S(2)}) collective-permute-start(bf16[4096,128]{1,0:T(8,128)(2,1)S(1)} %collective-permute-done.refs_1_), channel_id=1, source_target_pairs={{0,1},{1,0},{2,3},{3,2},{4,5},{5,4},{6,7},{7,6},{8,9},{9,8},{10,11... | collective-permute-start | bytes 3145736 | tf_op jit(solution)/shard_map/ppermute | solution.py:209
  78.2 39.7 %collective-permute-start.5 = (bf16[4096,128]{1,0:T(8,128)(2,1)S(1)}, bf16[4096,128]{1,0:T(8,128)(2,1)}, u32[]{:S(2)}, u32[]{:S(2)}) collective-permute-start(bf16[4096,128]{1,0:T(8,128)(2,1)S(1)} %collective-permute-done.1.refs_2_), channel_id=1, source_target_pairs={{0,1},{1,0},{2,3},{3,2},{4,5},{5,4},{6,7},{7,6},{8,9},{9,8},{10,11... | collective-permute-start | bytes 3145736 | tf_op jit(solution)/shard_map/ppermute | solution.py:209
  78.2 43.7 %collective-permute-start.6 = (bf16[4096,128]{1,0:T(8,128)(2,1)S(1)}, bf16[4096,128]{1,0:T(8,128)(2,1)}, u32[]{:S(2)}, u32[]{:S(2)}) collective-permute-start(bf16[4096,128]{1,0:T(8,128)(2,1)S(1)} %collective-permute-done.2.refs_3_), channel_id=1, source_target_pairs={{0,1},{1,0},{2,3},{3,2},{4,5},{5,4},{6,7},{7,6},{8,9},{9,8},{10,11... | collective-permute-start | bytes 3145736 | tf_op jit(solution)/shard_map/ppermute | solution.py:209
  78.7 10.7 %collective-permute-start.26 = (bf16[1024,128]{1,0:T(8,128)(2,1)S(1)}, bf16[1024,128]{1,0:T(8,128)(2,1)S(1)}, u32[]{:S(2)}, u32[]{:S(2)}) collective-permute-start(bf16[1024,128]{1,0:T(8,128)(2,1)S(1)} %collective-permute-done.18.refs_2_), channel_id=1, source_target_pairs={{0,8},{2,10},{4,12},{6,14},{8,16},{10,18},{12,20},{14,22},{16,24},... | collective-permute-start | bytes 786440 | tf_op jit(solution)/shard_map/ppermute | solution.py:226
  90.1 8.5 %collective-permute-start.30 = (bf16[1024,128]{1,0:T(8,128)(2,1)S(1)}, bf16[1024,128]{1,0:T(8,128)(2,1)S(1)}, u32[]{:S(2)}, u32[]{:S(2)}) collective-permute-start(bf16[1024,128]{1,0:T(8,128)(2,1)S(1)} %collective-permute-done.22.refs_6_), channel_id=1, source_target_pairs={{8,0},{10,2},{12,4},{14,6},{16,8},{18,10},{20,12},{22,14},{24,16},... | collective-permute-start | bytes 786440 | tf_op jit(solution)/shard_map/ppermute | solution.py:227
  99.4 11.9 %collective-permute-start.27 = (bf16[1024,128]{1,0:T(8,128)(2,1)}, bf16[1024,128]{1,0:T(8,128)(2,1)}, u32[]{:S(2)}, u32[]{:S(2)}) collective-permute-start(bf16[1024,128]{1,0:T(8,128)(2,1)} %collective-permute-done.19.refs_3_), channel_id=1, source_target_pairs={{0,8},{2,10},{4,12},{6,14},{8,16},{10,18},{12,20},{14,22},{16,24},... | collective-permute-start | bytes 786440 | tf_op jit(solution)/shard_map/ppermute | solution.py:226
  100.7 45.0 %collective-permute-start.28 = (bf16[1024,128]{1,0:T(8,128)(2,1)}, bf16[1024,128]{1,0:T(8,128)(2,1)}, u32[]{:S(2)}, u32[]{:S(2)}) collective-permute-start(bf16[1024,128]{1,0:T(8,128)(2,1)} %copy-done.22), channel_id=1, source_target_pairs={{0,8},{2,10},{4,12},{6,14},{8,16},{10,18},{12,20},{14,22},{16,24},... | collective-permute-start | bytes 786440 | tf_op jit(solution)/shard_map/ppermute | solution.py:226
  111.3 34.4 %collective-permute-start.29 = (bf16[1024,128]{1,0:T(8,128)(2,1)}, bf16[1024,128]{1,0:T(8,128)(2,1)}, u32[]{:S(2)}, u32[]{:S(2)}) collective-permute-start(bf16[1024,128]{1,0:T(8,128)(2,1)} %copy-done.24), channel_id=1, source_target_pairs={{0,8},{2,10},{4,12},{6,14},{8,16},{10,18},{12,20},{14,22},{16,24},... | collective-permute-start | bytes 786440 | tf_op jit(solution)/shard_map/ppermute | solution.py:226
  112.6 33.1 %collective-permute-start.31 = (bf16[1024,128]{1,0:T(8,128)(2,1)}, bf16[1024,128]{1,0:T(8,128)(2,1)}, u32[]{:S(2)}, u32[]{:S(2)}) collective-permute-start(bf16[1024,128]{1,0:T(8,128)(2,1)} %copy-done.26), channel_id=1, source_target_pairs={{8,0},{10,2},{12,4},{14,6},{16,8},{18,10},{20,12},{22,14},{24,16},... | collective-permute-start | bytes 786440 | tf_op jit(solution)/shard_map/ppermute | solution.py:227
  117.9 27.9 %collective-permute-start.32 = (bf16[1024,128]{1,0:T(8,128)(2,1)}, bf16[1024,128]{1,0:T(8,128)(2,1)}, u32[]{:S(2)}, u32[]{:S(2)}) collective-permute-start(bf16[1024,128]{1,0:T(8,128)(2,1)} %copy-done.28), channel_id=1, source_target_pairs={{8,0},{10,2},{12,4},{14,6},{16,8},{18,10},{20,12},{22,14},{24,16},... | collective-permute-start | bytes 786440 | tf_op jit(solution)/shard_map/ppermute | solution.py:227
  121.8 23.9 %collective-permute-start.33 = (bf16[1024,128]{1,0:T(8,128)(2,1)}, bf16[1024,128]{1,0:T(8,128)(2,1)}, u32[]{:S(2)}, u32[]{:S(2)}) collective-permute-start(bf16[1024,128]{1,0:T(8,128)(2,1)} %copy-done.30), channel_id=1, source_target_pairs={{8,0},{10,2},{12,4},{14,6},{16,8},{18,10},{20,12},{22,14},{24,16},... | collective-permute-start | bytes 786440 | tf_op jit(solution)/shard_map/ppermute | solution.py:227
  (49 other events, 392.1 us)

commit v2 on v1

v2 whole, which is shorter than its diff:
```python
import functools

import jax
import jax.numpy as jnp
from jax import lax
from jax.experimental import pallas as pl
from jax.experimental.pallas import tpu as pltpu
from jax.sharding import PartitionSpec as P

VMEM_LIMIT = 48 * 2**20
SMEM = pl.BlockSpec(memory_space=pltpu.SMEM)
VMEM = pl.BlockSpec(memory_space=pltpu.VMEM)
ANY = pl.BlockSpec(memory_space=pl.ANY)


def split_bits(points, blocks):
    bits = points.bit_length() - 1
    inside = [bit for bit in range(bits) if bit % 2 == 0][: bits // 2]
    while blocks % (1 << len(inside)):
        inside.pop()
    return inside, [bit for bit in range(bits) if bit not in inside]


def spread(value, bits):
    return sum(((value >> i) & 1) << bit for i, bit in enumerate(bits))


def gathered(value, bits):
    return sum((((value >> bit) & 1) << i for i, bit in enumerate(bits)), 0 * value)


def project_kernel(inside, halves, pos, cols, counts, potential, *refs):
    group = 1 << len(inside)
    sources = refs[: group * halves]
    out, blocks, sem = refs[group * halves :]
    modes, rows, slots, size, _ = blocks.shape
    local_rows = potential.shape[1]
    chunk, half = gathered(pos[0], inside), pos[1]
    copy = pltpu.make_async_copy(potential.at[:, pl.ds(chunk * rows, rows)], blocks, sem)
    copy.start()
    copy.wait()
    for mode in range(modes):
        for row in range(rows):
            at = mode * local_rows + chunk * rows + row
            used = counts[at]
            left = []
            right = []
            for slot in range(slots):
                block = blocks[mode, row, slot]
                left.append(jnp.where(slot < used, block, jnp.zeros_like(block)))
                col = cols[at * slots + slot]
                shift = lax.rem(half + halves - lax.div(col, local_rows), halves)
                start = pl.multiple_of(lax.rem(col, local_rows) * size, size)
                chosen = []
                for point in range(group):
                    value = sources[point][pl.ds(start, size), :]
                    for other in range(1, halves):
                        value = jnp.where(
                            shift == other,
                            sources[other * group + point][pl.ds(start, size), :],
                            value,
                        )
                    chosen.append(value)
                right.append(jnp.concatenate(chosen, axis=1))
            product = jnp.dot(
                jnp.concatenate(left, axis=1),
                jnp.concatenate(right, axis=0),
                preferred_element_type=jnp.float32,
            )
            turned = product.astype(jnp.bfloat16).T
            for point in range(group):
                out[point * modes + mode, :, row * size : (row + 1) * size] = turned[
                    point * size : (point + 1) * size
                ]


def project(pos, cols, counts, potential, sources, inside, halves):
    group = 1 << len(inside)
    modes, local_rows, slots, size, _ = potential.shape
    bands = sources[0].shape[1]
    rows = local_rows // group
    return pl.pallas_call(
        functools.partial(project_kernel, inside, halves),
        out_shape=jax.ShapeDtypeStruct((group * modes, bands, rows * size), jnp.bfloat16),
        in_specs=[SMEM, SMEM, SMEM, ANY] + [VMEM] * len(sources),
        out_specs=VMEM,
        scratch_shapes=[
            pltpu.VMEM((modes, rows, slots, size, size), jnp.bfloat16),
            pltpu.SemaphoreType.DMA,
        ],
        compiler_params=pltpu.CompilerParams(vmem_limit_bytes=VMEM_LIMIT),
        cost_estimate=pl.CostEstimate(
            flops=2 * modes * rows * slots * size * size * group * bands,
            bytes_accessed=16 * 2**20,
            transcendentals=0,
        ),
        name="project",
    )(pos, cols, counts, potential, *sources)


def couple_kernel(first, last, inside, outside, halves, pos, partners, *refs):
    group = 1 << len(inside)
    points = group << len(outside)
    before = None
    if first > 0:
        before, refs = refs[0], refs[1:]
    projected, parts, (out, total) = refs[0], refs[1:-2], refs[-2:]
    pairs, _, rows = projected.shape
    modes = pairs // group
    me, half = pos[0], pos[1]
    if first == 0:
        total[...] = jnp.zeros_like(total)
    else:
        total[...] = before[...]

    def add(pair, carry):
        point = lax.div(pair, modes)
        mine = me ^ spread(point, inside)
        away = partners[lax.rem(pair, modes) * points + mine] ^ me
        at = (gathered(away, outside) - first) * group + gathered(away, inside)
        base = 0
        for part in parts:
            count = part.shape[0] // rows
            start = at - base
            base += count

            @pl.when(jnp.logical_and(start >= 0, start < count))
            def _(part=part, start=start):
                chunk = part[pl.ds(pl.multiple_of(start * rows, rows), rows), :]
                total[pair] += jnp.dot(
                    projected[pair], chunk, preferred_element_type=jnp.float32
                )

        return carry

    lax.fori_loop(0, pairs, add, 0)
    if last:
        bands = total.shape[1]
        share = bands // halves
        for pair in range(pairs):
            turned = total[pair].T
            for part in range(halves):
                out[lax.rem(part + halves - half, halves), pair] = turned[
                    part * share : (part + 1) * share
                ]
    else:
        out[...] = total[...]


def couple(first, last, pos, partners, before, projected, parts, inside, outside, halves):
    pairs, bands, rows = projected.shape
    shape = (halves, pairs, bands // halves, bands) if last else (pairs, bands, bands)
    earlier = [] if before is None else [before]
    return pl.pallas_call(
        functools.partial(couple_kernel, first, last, inside, outside, halves),
        out_shape=jax.ShapeDtypeStruct(shape, jnp.float32),
        in_specs=[SMEM, SMEM] + [VMEM] * (len(earlier) + 1 + len(parts)),
        out_specs=VMEM,
        scratch_shapes=[pltpu.VMEM((pairs, bands, bands), jnp.float32)],
        compiler_params=pltpu.CompilerParams(vmem_limit_bytes=VMEM_LIMIT),
        cost_estimate=pl.CostEstimate(
            flops=2 * pairs * bands * bands * rows,
            bytes_accessed=8 * 2**20,
            transcendentals=0,
        ),
        name=f"couple{first}",
    )(pos, partners, *earlier, projected, *parts)


def solution(mesh):
    points = mesh.shape["ka"]
    halves = mesh.shape["orb"]

    def per_device(coefficients, potential, block_cols, block_counts, partners, gaps):
        modes, local_rows, _, _, _ = potential.shape
        inside, outside = split_bits(points, local_rows)
        group = 1 << len(inside)
        own = coefficients[0]
        rows = own.shape[0] // group
        me = lax.axis_index("ka").astype(jnp.int32)
        chunk = gathered(me, inside)
        pos = jnp.stack([me, lax.axis_index("orb").astype(jnp.int32)])
        cols = block_cols.reshape(-1)
        counts = block_counts.reshape(-1)
        pairing = partners.reshape(-1)

        def swap(value, mask):
            return lax.ppermute(value, "ka", [(i, i ^ mask) for i in range(points)])

        def rotate(value, shift):
            return lax.ppermute(
                value, "orb", [(i, (i + shift) % halves) for i in range(halves)]
            )

        def chunk_for(point):
            return lax.dynamic_slice_in_dim(own, (chunk ^ point) * rows, rows, 0)

        def after(value, *others):
            return lax.optimization_barrier((value,) + others)[0]

        parts = [chunk_for(0)]
        parts += [swap(chunk_for(p), spread(p, inside)) for p in range(1, group)]
        pieces = [parts[0], parts[1], jnp.concatenate(parts[2:], axis=0)]
        whole_set = jnp.concatenate(parts, axis=0)
        top = 1 << outside[-1]
        first_far = swap(pieces[0], top)
        held = {0: [whole_set]}
        for i in reversed(range(len(outside) - 1)):
            for key, items in list(held.items()):
                held[key | (1 << i)] = [swap(item, 1 << outside[i]) for item in items]
        second_far = swap(after(pieces[1], first_far), top)
        near = {0: after(own, first_far, *parts)}
        for i in reversed(range(len(inside))):
            ready = [near[1 << i]] if (1 << i) in near else []
            for key, item in list(near.items()):
                if key:
                    item = after(item, second_far, *ready, *held.get(1, []))
                near[key | (1 << i)] = swap(item, 1 << inside[i])
                ready = [near[key | (1 << i)]]
        third_far = swap(after(pieces[2], second_far), top)
        far = {1 << (len(outside) - 1): [first_far, second_far, third_far]}
        for i in reversed(range(len(outside) - 1)):
            for key, items in list(far.items()):
                far[key | (1 << i)] = [
                    swap(after(item, *held[1 << i]), 1 << outside[i]) for item in items
                ]
        sets = {**held, **far}
        late = far[max(far)]
        near[group - 1] = after(near[group - 1], third_far, late[0], late[1])
        sources = [near[key] for key in range(group)]
        for shift in range(1, halves):
            sources += [rotate(near[key], shift) for key in range(group)]
        projected = project(pos, cols, counts, potential, sources, inside, halves)
        count = 1 << len(outside)
        early = [part for key in range(count - 1) for part in sets[key]]
        total = couple(
            0, False, pos, pairing, None, projected, early, inside, outside, halves
        )
        total = couple(
            count - 1, True, pos, pairing, total, projected, late, inside, outside, halves
        )
        summed = total[0]
        for shift in range(1, halves):
            summed = summed + rotate(total[shift], shift)
        summed = summed.reshape((group, modes) + summed.shape[1:])
        result = summed[0]
        for point in range(1, group):
            result = result + swap(summed[point], spread(point, inside))
        return result[:, None] / gaps

    return jax.shard_map(
        per_device,
        mesh=mesh,
        in_specs=(
            P("ka", "orb", None),
            P(None, "orb", None, None, None),
            P(None, "orb", None),
            P(None, "orb"),
            P(),
            P(None, "ka", "orb", None),
        ),
        out_specs=P(None, "ka", "orb", None),
        check_vma=False,
    )
```

time: 164 us -> 114 us (0.70)
  the two profiles are of different devices: /device:TPU:24 before, /device:TPU:0 now
where the time goes in v2:
time: 114 us
  waiting for transfers between devices  64.4 us (56%)
  starting transfers between devices  26.3 us (23%)
  Pallas kernels  16.8 us (15%)
  local copies, waits for them, and re-layouts  4.95 us (4%)
    ppermute x16, waiting for transfers between devices, swap(): return lax.ppermute(value, 'ka', [(i, i ^ mask) for i in range(points)])  60 us
    ppermute x16, starting transfers between devices, swap(): return lax.ppermute(value, 'ka', [(i, i ^ mask) for i in range(points)])  25.5 us
    pallas_call x1, Pallas kernels, project(): pl.pallas_call(functools.partial(project_kernel, inside, halves), out_sha...  9.47 us
    pallas_call x2, Pallas kernels, couple(): pl.pallas_call(functools.partial(couple_kernel, first, last, inside, outs...  7.32 us
    ppermute x5, waiting for transfers between devices, rotate(): lax.ppermute(value, 'orb', [(i, (i + shift) % halves) for i in range(halv...  4.46 us
    unnamed x29, local copies, waits for them, and re-layouts  3.23 us
  transfers between devices with their start and end apart: 21, of which 13 were waited for; matrix products, arithmetic and copies ran while one was open for 1% of the time, Pallas kernels for 12%

profile of v2, /device:TPU:0, one launch (start us, length us, event | category | flops | bytes accessed | tf_op | source)
XLA Modules:
  0.0 113.5 jit_solution(17150513162823037756)
XLA Ops:
  0.0 1.3 %dynamic-slice_bitcast_fusion = (bf16[1024,128]{1,0:T(8,128)(2,1)S(1)}, bf16[1024,128]{1,0:T(8,128)(2,1)S(1)}, bf16[1024,128]{1,0:T(8,128)(2,1)S(1)}, bf16[1024,128]{1,0:T(8,128)(2,1)S(1)}) fusion(bf16[1,4096,128]{2,1,0:T(8,128)(2,1)} %param.6, s32[]{:T(128)S(6)} %select_n.15, s32[]{:T(128)S(6)} %select_n.13, s32[]{:T(128)S(6)} %select_n.12, s32[]{:T(128)S(6)} %select_n.14), kind=kLoop, calls=%fused_computation.5 | loop fusion | bytes 2097168 | tf_op jit(solution)/shard_map/dynamic_slice | solution.py:196
  1.4 3.0 %collective-permute-start.1 = (bf16[1024,128]{1,0:T(8,128)(2,1)S(1)}, bf16[1024,128]{1,0:T(8,128)(2,1)S(1)}, u32[]{:S(2)}, u32[]{:S(2)}) collective-permute-start(bf16[1024,128]{1,0:T(8,128)(2,1)S(1)} %get-tuple-element.22), channel_id=1, source_target_pairs={{0,2},{2,0},{4,6},{6,4},{8,10},{10,8},{12,14},{14,12},{16,18},{18,... | collective-permute-start | bytes 786440 | tf_op jit(solution)/shard_map/ppermute | solution.py:188
  4.4 1.6 %collective-permute-start.2 = (bf16[1024,128]{1,0:T(8,128)(2,1)S(1)}, bf16[1024,128]{1,0:T(8,128)(2,1)S(1)}, u32[]{:S(2)}, u32[]{:S(2)}) collective-permute-start(bf16[1024,128]{1,0:T(8,128)(2,1)S(1)} %get-tuple-element.24), channel_id=1, source_target_pairs={{0,8},{2,10},{4,12},{6,14},{8,0},{10,2},{12,4},{14,6},{16,24},{18,... | collective-permute-start | bytes 786440 | tf_op jit(solution)/shard_map/ppermute | solution.py:188
  6.0 3.0 %collective-permute-start = (bf16[1024,128]{1,0:T(8,128)(2,1)S(1)}, bf16[1024,128]{1,0:T(8,128)(2,1)S(1)}, u32[]{:S(2)}, u32[]{:S(2)}) collective-permute-start(bf16[1024,128]{1,0:T(8,128)(2,1)S(1)} %get-tuple-element.23), channel_id=1, source_target_pairs={{0,16},{2,18},{4,20},{6,22},{8,24},{10,26},{12,28},{14,30},{16,0},... | collective-permute-start | bytes 786440 | tf_op jit(solution)/shard_map/ppermute | solution.py:188
  9.0 1.7 %collective-permute-done.1 = bf16[1024,128]{1,0:T(8,128)(2,1)S(1)} collective-permute-done((bf16[1024,128]{1,0:T(8,128)(2,1)S(1)}, bf16[1024,128]{1,0:T(8,128)(2,1)S(1)}, u32[]{:S(2)}, u32[]{:S(2)}) %collective-permute-start.1) | collective-permute-done | bytes 262176 | tf_op jit(solution)/shard_map/ppermute | solution.py:188
  10.7 8.5 %collective-permute-done.2 = bf16[1024,128]{1,0:T(8,128)(2,1)S(1)} collective-permute-done((bf16[1024,128]{1,0:T(8,128)(2,1)S(1)}, bf16[1024,128]{1,0:T(8,128)(2,1)S(1)}, u32[]{:S(2)}, u32[]{:S(2)}) %collective-permute-start.2) | collective-permute-done | bytes 262176 | tf_op jit(solution)/shard_map/ppermute | solution.py:188
  19.2 4.0 %collective-permute-done.3 = bf16[1024,128]{1,0:T(8,128)(2,1)S(1)} collective-permute-done((bf16[1024,128]{1,0:T(8,128)(2,1)S(1)}, bf16[1024,128]{1,0:T(8,128)(2,1)S(1)}, u32[]{:S(2)}, u32[]{:S(2)}) %collective-permute-start.3) | collective-permute-done | bytes 262176 | tf_op jit(solution)/shard_map/ppermute | solution.py:188
  23.3 1.8 %collective-permute-start.7 = (bf16[4096,128]{1,0:T(8,128)(2,1)S(1)}, bf16[4096,128]{1,0:T(8,128)(2,1)S(1)}, u32[]{:S(2)}, u32[]{:S(2)}) collective-permute-start(bf16[4096,128]{1,0:T(8,128)(2,1)S(1)} %pad_maximum_fusion.refs_1_), channel_id=1, source_target_pairs={{0,4},{2,6},{4,0},{6,2},{8,12},{10,14},{12,8},{14,10},{16,20},{18,... | collective-permute-start | bytes 3145736 | tf_op jit(solution)/shard_map/ppermute | solution.py:188
  25.0 1.5 %collective-permute-start.4 = (bf16[4096,128]{1,0:T(8,128)(2,1)S(1)}, bf16[4096,128]{1,0:T(8,128)(2,1)S(1)}, u32[]{:S(2)}, u32[]{:S(2)}) collective-permute-start(bf16[4096,128]{1,0:T(8,128)(2,1)S(1)} %bitcast.27), channel_id=1, source_target_pairs={{0,2},{2,0},{4,6},{6,4},{8,10},{10,8},{12,14},{14,12},{16,18},{18,... | collective-permute-start | bytes 3145736 | tf_op jit(solution)/shard_map/ppermute | solution.py:188
  26.5 4.2 %collective-permute-start.6 = (bf16[1024,128]{1,0:T(8,128)(2,1)S(1)}, bf16[1024,128]{1,0:T(8,128)(2,1)S(1)}, u32[]{:S(2)}, u32[]{:S(2)}) collective-permute-start(bf16[1024,128]{1,0:T(8,128)(2,1)S(1)} %collective-permute-done.1), channel_id=1, source_target_pairs={{0,16},{2,18},{4,20},{6,22},{8,24},{10,26},{12,28},{14,30},{16,0},... | collective-permute-start | bytes 786440 | tf_op jit(solution)/shard_map/ppermute | solution.py:188
  30.7 22.4 %collective-permute-done.6.refs_4_ = bf16[1024,128]{1,0:T(8,128)(2,1)S(1)} collective-permute-done((bf16[1024,128]{1,0:T(8,128)(2,1)S(1)}, bf16[1024,128]{1,0:T(8,128)(2,1)S(1)}, u32[]{:S(2)}, u32[]{:S(2)}) %collective-permute-start.6) | collective-permute-done | bytes 262176 | tf_op jit(solution)/shard_map/ppermute | solution.py:188
  53.1 1.0 copy-done.2
  54.1 1.3 %collective-permute-done.5.refs_2_ = bf16[4096,128]{1,0:T(8,128)(2,1)} collective-permute-done((bf16[4096,128]{1,0:T(8,128)(2,1)S(1)}, bf16[4096,128]{1,0:T(8,128)(2,1)}, u32[]{:S(2)}, u32[]{:S(2)}) %collective-permute-start.5) | collective-permute-done | bytes 1048608 | tf_op jit(solution)/shard_map/ppermute | solution.py:188
  56.0 3.1 %collective-permute-start.9 = (bf16[2048,128]{1,0:T(8,128)(2,1)S(1)}, bf16[2048,128]{1,0:T(8,128)(2,1)}, u32[]{:S(2)}, u32[]{:S(2)}) collective-permute-start(bf16[2048,128]{1,0:T(8,128)(2,1)S(1)} %pad_maximum_fusion.1), channel_id=1, source_target_pairs={{0,16},{2,18},{4,20},{6,22},{8,24},{10,26},{12,28},{14,30},{16,0},... | collective-permute-start | bytes 1572872 | tf_op jit(solution)/shard_map/ppermute | solution.py:188
  59.0 1.5 %collective-permute-start.11 = (bf16[1024,128]{1,0:T(8,128)(2,1)S(1)}, bf16[1024,128]{1,0:T(8,128)(2,1)S(1)}, u32[]{:S(2)}, u32[]{:S(2)}) collective-permute-start(bf16[1024,128]{1,0:T(8,128)(2,1)S(1)} %collective-permute-done.6.refs_4_), channel_id=1, source_target_pairs={{0,4},{2,6},{4,0},{6,2},{8,12},{10,14},{12,8},{14,10},{16,20},{18,... | collective-permute-start | bytes 786440 | tf_op jit(solution)/shard_map/ppermute | solution.py:188
  60.6 0.7 copy-done.8
  61.8 0.7 copy-done.6
  62.5 17.3 %collective-permute-done.9.refs_5_ = bf16[2048,128]{1,0:T(8,128)(2,1)} collective-permute-done((bf16[2048,128]{1,0:T(8,128)(2,1)S(1)}, bf16[2048,128]{1,0:T(8,128)(2,1)}, u32[]{:S(2)}, u32[]{:S(2)}) %collective-permute-start.9) | collective-permute-done | bytes 524320 | tf_op jit(solution)/shard_map/ppermute | solution.py:188
  80.3 0.7 copy-done.4
  81.0 1.4 %collective-permute-start.16 = (bf16[2048,128]{1,0:T(8,128)(2,1)}, bf16[2048,128]{1,0:T(8,128)(2,1)}, u32[]{:S(2)}, u32[]{:S(2)}) collective-permute-start(bf16[2048,128]{1,0:T(8,128)(2,1)} %collective-permute-done.9.refs_5_), channel_id=1, source_target_pairs={{0,4},{2,6},{4,0},{6,2},{8,12},{10,14},{12,8},{14,10},{16,20},{18,... | collective-permute-start | bytes 1572872 | tf_op jit(solution)/shard_map/ppermute | solution.py:188
  82.9 1.1 collective-permute-done.13.refs_5_
  84.3 1.5 %collective-permute-done.15.refs_7_ = bf16[4096,128]{1,0:T(8,128)(2,1)} collective-permute-done((bf16[4096,128]{1,0:T(8,128)(2,1)}, bf16[4096,128]{1,0:T(8,128)(2,1)}, u32[]{:S(2)}, u32[]{:S(2)}) %collective-permute-start.15) | collective-permute-done | bytes 1048608 | tf_op jit(solution)/shard_map/ppermute | solution.py:191
  85.8 9.5 %project.1.refs_0_.refs_1_ = bf16[12,128,1024]{2,1,0:T(8,128)(2,1)} custom-call(s32[2]{0:T(128)S(1)} %pad_add_fusion.pos, s32[288]{0:T(512)S(1)} %reshape.23.cols, s32[96]{0:T(128)S(1)} %reshape.24.counts, bf16[3,32,3,128,128]{4,3,2,1,0:T(8,128)(2,1)} %potential.1, bf16[4096,128]{1,0:T(8,128)(2,1)S(1)} %bitcast.30, ...), custom_call_target="tpu_custom_call" | custom-call | flops 1207959552 | bytes 16777216 | tf_op jit(solution)/shard_map/project/pallas_call | solution.py:82
  95.3 4.6 %couple0.1.refs_0_ = f32[12,128,128]{2,1,0:T(8,128)S(1)} custom-call(s32[2]{0:T(128)S(1)} %pad_add_fusion.pos, s32[48]{0:T(128)S(1)} %reshape.22.partners, bf16[12,128,1024]{2,1,0:T(8,128)(2,1)} %project.1.refs_0_.refs_1_, bf16[4096,128]{1,0:T(8,128)(2,1)S(1)} %pad_maximum_fusion.refs_1_, bf16[4096,128]{1,0:T(8,128)(2,1)S(1)} %copy-done.3, ...), custom_call_target="tpu_custom_call" | custom-call | flops 402653184 | bytes 8388608 | tf_op jit(solution)/shard_map/couple0/pallas_call | solution.py:154
  100.0 2.7 %couple3.1 = f32[2,12,64,128]{3,2,1,0:T(8,128)S(1)} custom-call(s32[2]{0:T(128)S(1)} %pad_add_fusion.pos, s32[48]{0:T(128)S(1)} %reshape.22.partners, f32[12,128,128]{2,1,0:T(8,128)S(1)} %couple0.1.refs_0_, bf16[12,128,1024]{2,1,0:T(8,128)(2,1)S(1)} %copy-done, bf16[1024,128]{1,0:T(8,128)(2,1)S(1)} %copy-done.5, ...), custom_call_target="tpu_custom_call" | custom-call | flops 402653184 | bytes 8388608 | tf_op jit(solution)/shard_map/couple3/pallas_call | solution.py:154
  102.9 1.6 %collective-permute-done.17 = f32[12,64,128]{2,1,0:T(8,128)S(1)} collective-permute-done((f32[12,64,128]{2,1,0:T(8,128)S(1)}, f32[12,64,128]{2,1,0:T(8,128)S(1)}, u32[]{:S(2)}, u32[]{:S(2)}) %collective-permute-start.17) | collective-permute-done | bytes 393248 | tf_op jit(solution)/shard_map/ppermute | solution.py:191
  104.6 1.5 %collective-permute-start.18 = (f32[3,64,128]{2,1,0:T(8,128)S(1)}, f32[3,64,128]{2,1,0:T(8,128)S(1)}, u32[]{:S(2)}, u32[]{:S(2)}) collective-permute-start(f32[3,64,128]{2,1,0:T(8,128)S(1)} %get-tuple-element.25), channel_id=1, source_target_pairs={{0,2},{2,0},{4,6},{6,4},{8,10},{10,8},{12,14},{14,12},{16,18},{18,... | collective-permute-start | bytes 294920 | tf_op jit(solution)/shard_map/ppermute | solution.py:188
  106.8 1.4 %collective-permute-start.20 = (f32[3,64,128]{2,1,0:T(8,128)S(1)}, f32[3,64,128]{2,1,0:T(8,128)S(1)}, u32[]{:S(2)}, u32[]{:S(2)}) collective-permute-start(f32[3,64,128]{2,1,0:T(8,128)S(1)} %get-tuple-element.26), channel_id=1, source_target_pairs={{0,10},{2,8},{4,14},{6,12},{8,2},{10,0},{12,6},{14,4},{16,26},{18,... | collective-permute-start | bytes 294920 | tf_op jit(solution)/shard_map/ppermute | solution.py:188
  108.2 1.3 %collective-permute-done.18 = f32[3,64,128]{2,1,0:T(8,128)S(1)} collective-permute-done((f32[3,64,128]{2,1,0:T(8,128)S(1)}, f32[3,64,128]{2,1,0:T(8,128)S(1)}, u32[]{:S(2)}, u32[]{:S(2)}) %collective-permute-start.18) | collective-permute-done | bytes 98336 | tf_op jit(solution)/shard_map/ppermute | solution.py:188
  109.5 2.3 %collective-permute-done.19 = f32[3,64,128]{2,1,0:T(8,128)S(1)} collective-permute-done((f32[3,64,128]{2,1,0:T(8,128)S(1)}, f32[3,64,128]{2,1,0:T(8,128)S(1)}, u32[]{:S(2)}, u32[]{:S(2)}) %collective-permute-start.19) | collective-permute-done | bytes 98336 | tf_op jit(solution)/shard_map/ppermute | solution.py:188
  111.8 1.1 collective-permute-done.20
  112.9 0.7 fusion.5
  (53 shorter events, 3.5 us)
Async XLA Ops:
  0.0 25.0 %copy-start.1 = (bf16[1,4096,128]{2,1,0:T(8,128)(2,1)S(1)}, bf16[1,4096,128]{2,1,0:T(8,128)(2,1)}, u32[]{:S(2)}) copy-start(bf16[1,4096,128]{2,1,0:T(8,128)(2,1)} %param.6) | copy-start | bytes 3145732
  1.4 81.1 %copy-start.11 = (s32[3,32,3]{1,2,0:T(4,128)S(1)}, s32[3,32,3]{1,2,0:T(4,128)}, u32[]{:S(2)}) copy-start(s32[3,32,3]{1,2,0:T(4,128)} %param.8) | copy-start | bytes 3460
  1.4 81.3 %copy-start.12 = (s32[3,32]{1,0:T(4,128)S(1)}, s32[3,32]{1,0:T(4,128)}, u32[]{:S(2)}) copy-start(s32[3,32]{1,0:T(4,128)} %param.9) | copy-start | bytes 1156
  1.4 81.4 %copy-start.13 = (s32[3,16]{1,0:T(4,128)S(1)}, s32[3,16]{1,0:T(4,128)}, u32[]{:S(2)}) copy-start(s32[3,16]{1,0:T(4,128)} %param.10) | copy-start | bytes 580
  1.4 9.3 %collective-permute-start.1 = (bf16[1024,128]{1,0:T(8,128)(2,1)S(1)}, bf16[1024,128]{1,0:T(8,128)(2,1)S(1)}, u32[]{:S(2)}, u32[]{:S(2)}) collective-permute-start(bf16[1024,128]{1,0:T(8,128)(2,1)S(1)} %get-tuple-element.22), channel_id=1, source_target_pairs={{0,2},{2,0},{4,6},{6,4},{8,10},{10,8},{12,14},{14,12},{16,18},{18,... | collective-permute-start | bytes 786440 | tf_op jit(solution)/shard_map/ppermute | solution.py:188
  4.4 14.8 %collective-permute-start.2 = (bf16[1024,128]{1,0:T(8,128)(2,1)S(1)}, bf16[1024,128]{1,0:T(8,128)(2,1)S(1)}, u32[]{:S(2)}, u32[]{:S(2)}) collective-permute-start(bf16[1024,128]{1,0:T(8,128)(2,1)S(1)} %get-tuple-element.24), channel_id=1, source_target_pairs={{0,8},{2,10},{4,12},{6,14},{8,0},{10,2},{12,4},{14,6},{16,24},{18,... | collective-permute-start | bytes 786440 | tf_op jit(solution)/shard_map/ppermute | solution.py:188
  6.0 17.2 %collective-permute-start.3 = (bf16[1024,128]{1,0:T(8,128)(2,1)S(1)}, bf16[1024,128]{1,0:T(8,128)(2,1)S(1)}, u32[]{:S(2)}, u32[]{:S(2)}) collective-permute-start(bf16[1024,128]{1,0:T(8,128)(2,1)S(1)} %get-tuple-element.21), channel_id=1, source_target_pairs={{0,10},{2,8},{4,14},{6,12},{8,2},{10,0},{12,6},{14,4},{16,26},{18,... | collective-permute-start | bytes 786440 | tf_op jit(solution)/shard_map/ppermute | solution.py:188
  6.0 19.1 %collective-permute-start = (bf16[1024,128]{1,0:T(8,128)(2,1)S(1)}, bf16[1024,128]{1,0:T(8,128)(2,1)S(1)}, u32[]{:S(2)}, u32[]{:S(2)}) collective-permute-start(bf16[1024,128]{1,0:T(8,128)(2,1)S(1)} %get-tuple-element.23), channel_id=1, source_target_pairs={{0,16},{2,18},{4,20},{6,22},{8,24},{10,26},{12,28},{14,30},{16,0},... | collective-permute-start | bytes 786440 | tf_op jit(solution)/shard_map/ppermute | solution.py:188
  23.3 29.8 %collective-permute-start.7 = (bf16[4096,128]{1,0:T(8,128)(2,1)S(1)}, bf16[4096,128]{1,0:T(8,128)(2,1)S(1)}, u32[]{:S(2)}, u32[]{:S(2)}) collective-permute-start(bf16[4096,128]{1,0:T(8,128)(2,1)S(1)} %pad_maximum_fusion.refs_1_), channel_id=1, source_target_pairs={{0,4},{2,6},{4,0},{6,2},{8,12},{10,14},{12,8},{14,10},{16,20},{18,... | collective-permute-start | bytes 3145736 | tf_op jit(solution)/shard_map/ppermute | solution.py:188
  25.0 29.0 %collective-permute-start.4 = (bf16[4096,128]{1,0:T(8,128)(2,1)S(1)}, bf16[4096,128]{1,0:T(8,128)(2,1)S(1)}, u32[]{:S(2)}, u32[]{:S(2)}) collective-permute-start(bf16[4096,128]{1,0:T(8,128)(2,1)S(1)} %bitcast.27), channel_id=1, source_target_pairs={{0,2},{2,0},{4,6},{6,4},{8,10},{10,8},{12,14},{14,12},{16,18},{18,... | collective-permute-start | bytes 3145736 | tf_op jit(solution)/shard_map/ppermute | solution.py:188
  26.5 28.9 %collective-permute-start.5 = (bf16[4096,128]{1,0:T(8,128)(2,1)S(1)}, bf16[4096,128]{1,0:T(8,128)(2,1)}, u32[]{:S(2)}, u32[]{:S(2)}) collective-permute-start(bf16[4096,128]{1,0:T(8,128)(2,1)S(1)} %bitcast.28), channel_id=1, source_target_pairs={{0,8},{2,10},{4,12},{6,14},{8,0},{10,2},{12,4},{14,6},{16,24},{18,... | collective-permute-start | bytes 3145736 | tf_op jit(solution)/shard_map/ppermute | solution.py:188
  26.5 26.6 %collective-permute-start.6 = (bf16[1024,128]{1,0:T(8,128)(2,1)S(1)}, bf16[1024,128]{1,0:T(8,128)(2,1)S(1)}, u32[]{:S(2)}, u32[]{:S(2)}) collective-permute-start(bf16[1024,128]{1,0:T(8,128)(2,1)S(1)} %collective-permute-done.1), channel_id=1, source_target_pairs={{0,16},{2,18},{4,20},{6,22},{8,24},{10,26},{12,28},{14,30},{16,0},... | collective-permute-start | bytes 786440 | tf_op jit(solution)/shard_map/ppermute | solution.py:188
  53.1 1.0 copy-start.2
  55.4 25.6 %collective-permute-start.8 = (bf16[4096,128]{1,0:T(8,128)(2,1)}, bf16[4096,128]{1,0:T(8,128)(2,1)}, u32[]{:S(2)}, u32[]{:S(2)}) collective-permute-start(bf16[4096,128]{1,0:T(8,128)(2,1)} %collective-permute-done.5.refs_2_), channel_id=1, source_target_pairs={{0,2},{2,0},{4,6},{6,4},{8,10},{10,8},{12,14},{14,12},{16,18},{18,... | collective-permute-start | bytes 3145736 | tf_op jit(solution)/shard_map/ppermute | solution.py:188
  56.0 23.8 %collective-permute-start.9 = (bf16[2048,128]{1,0:T(8,128)(2,1)S(1)}, bf16[2048,128]{1,0:T(8,128)(2,1)}, u32[]{:S(2)}, u32[]{:S(2)}) collective-permute-start(bf16[2048,128]{1,0:T(8,128)(2,1)S(1)} %pad_maximum_fusion.1), channel_id=1, source_target_pairs={{0,16},{2,18},{4,20},{6,22},{8,24},{10,26},{12,28},{14,30},{16,0},... | collective-permute-start | bytes 1572872 | tf_op jit(solution)/shard_map/ppermute | solution.py:188
  59.0 20.8 %collective-permute-start.11 = (bf16[1024,128]{1,0:T(8,128)(2,1)S(1)}, bf16[1024,128]{1,0:T(8,128)(2,1)S(1)}, u32[]{:S(2)}, u32[]{:S(2)}) collective-permute-start(bf16[1024,128]{1,0:T(8,128)(2,1)S(1)} %collective-permute-done.6.refs_4_), channel_id=1, source_target_pairs={{0,4},{2,6},{4,0},{6,2},{8,12},{10,14},{12,8},{14,10},{16,20},{18,... | collective-permute-start | bytes 786440 | tf_op jit(solution)/shard_map/ppermute | solution.py:188
  61.3 19.1 %collective-permute-start.10 = (bf16[1024,128]{1,0:T(8,128)(2,1)S(1)}, bf16[1024,128]{1,0:T(8,128)(2,1)S(1)}, u32[]{:S(2)}, u32[]{:S(2)}) collective-permute-start(bf16[1024,128]{1,0:T(8,128)(2,1)S(1)} %collective-permute-done.refs_3_), channel_id=1, source_target_pairs={{0,4},{2,6},{4,0},{6,2},{8,12},{10,14},{12,8},{14,10},{16,20},{18,... | collective-permute-start | bytes 786440 | tf_op jit(solution)/shard_map/ppermute | solution.py:188
  62.5 20.5 %collective-permute-start.12 = (bf16[4096,128]{1,0:T(8,128)(2,1)S(1)}, bf16[4096,128]{1,0:T(8,128)(2,1)}, u32[]{:S(2)}, u32[]{:S(2)}) collective-permute-start(bf16[4096,128]{1,0:T(8,128)(2,1)S(1)} %bitcast.29), channel_id=1, source_target_pairs={{0,1},{1,0},{2,3},{3,2},{4,5},{5,4},{6,7},{7,6},{8,9},{9,8},{10,11... | collective-permute-start | bytes 3145736 | tf_op jit(solution)/shard_map/ppermute | solution.py:191
  79.8 4.2 %collective-permute-start.13 = (bf16[4096,128]{1,0:T(8,128)(2,1)S(1)}, bf16[4096,128]{1,0:T(8,128)(2,1)}, u32[]{:S(2)}, u32[]{:S(2)}) collective-permute-start(bf16[4096,128]{1,0:T(8,128)(2,1)S(1)} %collective-permute-done.4.refs_1_), channel_id=1, source_target_pairs={{0,1},{1,0},{2,3},{3,2},{4,5},{5,4},{6,7},{7,6},{8,9},{9,8},{10,11... | collective-permute-start | bytes 3145736 | tf_op jit(solution)/shard_map/ppermute | solution.py:191
  79.8 4.5 %collective-permute-start.14 = (bf16[4096,128]{1,0:T(8,128)(2,1)}, bf16[4096,128]{1,0:T(8,128)(2,1)}, u32[]{:S(2)}, u32[]{:S(2)}) collective-permute-start(bf16[4096,128]{1,0:T(8,128)(2,1)} %collective-permute-done.5.refs_2_), channel_id=1, source_target_pairs={{0,1},{1,0},{2,3},{3,2},{4,5},{5,4},{6,7},{7,6},{8,9},{9,8},{10,11... | collective-permute-start | bytes 3145736 | tf_op jit(solution)/shard_map/ppermute | solution.py:191
  81.0 4.8 %collective-permute-start.15 = (bf16[4096,128]{1,0:T(8,128)(2,1)}, bf16[4096,128]{1,0:T(8,128)(2,1)}, u32[]{:S(2)}, u32[]{:S(2)}) collective-permute-start(bf16[4096,128]{1,0:T(8,128)(2,1)} %collective-permute-done.8.refs_3_), channel_id=1, source_target_pairs={{0,1},{1,0},{2,3},{3,2},{4,5},{5,4},{6,7},{7,6},{8,9},{9,8},{10,11... | collective-permute-start | bytes 3145736 | tf_op jit(solution)/shard_map/ppermute | solution.py:191
  81.0 18.9 %collective-permute-start.16 = (bf16[2048,128]{1,0:T(8,128)(2,1)}, bf16[2048,128]{1,0:T(8,128)(2,1)}, u32[]{:S(2)}, u32[]{:S(2)}) collective-permute-start(bf16[2048,128]{1,0:T(8,128)(2,1)} %collective-permute-done.9.refs_5_), channel_id=1, source_target_pairs={{0,4},{2,6},{4,0},{6,2},{8,12},{10,14},{12,8},{14,10},{16,20},{18,... | collective-permute-start | bytes 1572872 | tf_op jit(solution)/shard_map/ppermute | solution.py:188
  82.9 12.4 %copy-start.3 = (bf16[4096,128]{1,0:T(8,128)(2,1)S(1)}, bf16[4096,128]{1,0:T(8,128)(2,1)}, u32[]{:S(2)}) copy-start(bf16[4096,128]{1,0:T(8,128)(2,1)} %copy-done.2) | copy-start | bytes 3145732
  82.9 12.4 %copy-start.7 = (bf16[1024,128]{1,0:T(8,128)(2,1)S(1)}, bf16[1024,128]{1,0:T(8,128)(2,1)}, u32[]{:S(2)}) copy-start(bf16[1024,128]{1,0:T(8,128)(2,1)} %copy-done.6) | copy-start | bytes 786436
  82.9 12.4 %copy-start.9 = (bf16[1024,128]{1,0:T(8,128)(2,1)S(1)}, bf16[1024,128]{1,0:T(8,128)(2,1)}, u32[]{:S(2)}) copy-start(bf16[1024,128]{1,0:T(8,128)(2,1)} %copy-done.8) | copy-start | bytes 786436
  95.3 4.6 %copy-start = (bf16[12,128,1024]{2,1,0:T(8,128)(2,1)S(1)}, bf16[12,128,1024]{2,1,0:T(8,128)(2,1)}, u32[]{:S(2)}) copy-start(bf16[12,128,1024]{2,1,0:T(8,128)(2,1)} %project.1.refs_0_.refs_1_) | copy-start | bytes 9437188
  95.3 4.6 %copy-start.5 = (bf16[1024,128]{1,0:T(8,128)(2,1)S(1)}, bf16[1024,128]{1,0:T(8,128)(2,1)}, u32[]{:S(2)}) copy-start(bf16[1024,128]{1,0:T(8,128)(2,1)} %copy-done.4) | copy-start | bytes 786436
  102.7 10.2 %copy-start.10 = (f32[3,1,64,128]{3,2,1,0:T(8,128)S(1)}, f32[3,1,64,128]{3,2,1,0:T(8,128)}, u32[]{:S(2)}) copy-start(f32[3,1,64,128]{3,2,1,0:T(8,128)} %param.11) | copy-start | bytes 294916
  102.7 1.8 %collective-permute-start.17 = (f32[12,64,128]{2,1,0:T(8,128)S(1)}, f32[12,64,128]{2,1,0:T(8,128)S(1)}, u32[]{:S(2)}, u32[]{:S(2)}) collective-permute-start(f32[12,64,128]{2,1,0:T(8,128)S(1)} %slice_bitcast_fusion), channel_id=1, source_target_pairs={{0,1},{1,0},{2,3},{3,2},{4,5},{5,4},{6,7},{7,6},{8,9},{9,8},{10,11... | collective-permute-start | bytes 1179656 | tf_op jit(solution)/shard_map/ppermute | solution.py:191
  104.6 4.9 %collective-permute-start.18 = (f32[3,64,128]{2,1,0:T(8,128)S(1)}, f32[3,64,128]{2,1,0:T(8,128)S(1)}, u32[]{:S(2)}, u32[]{:S(2)}) collective-permute-start(f32[3,64,128]{2,1,0:T(8,128)S(1)} %get-tuple-element.25), channel_id=1, source_target_pairs={{0,2},{2,0},{4,6},{6,4},{8,10},{10,8},{12,14},{14,12},{16,18},{18,... | collective-permute-start | bytes 294920 | tf_op jit(solution)/shard_map/ppermute | solution.py:188
  106.2 5.6 %collective-permute-start.19 = (f32[3,64,128]{2,1,0:T(8,128)S(1)}, f32[3,64,128]{2,1,0:T(8,128)S(1)}, u32[]{:S(2)}, u32[]{:S(2)}) collective-permute-start(f32[3,64,128]{2,1,0:T(8,128)S(1)} %get-tuple-element.27), channel_id=1, source_target_pairs={{0,8},{2,10},{4,12},{6,14},{8,0},{10,2},{12,4},{14,6},{16,24},{18,... | collective-permute-start | bytes 294920 | tf_op jit(solution)/shard_map/ppermute | solution.py:188
  106.8 6.1 %collective-permute-start.20 = (f32[3,64,128]{2,1,0:T(8,128)S(1)}, f32[3,64,128]{2,1,0:T(8,128)S(1)}, u32[]{:S(2)}, u32[]{:S(2)}) collective-permute-start(f32[3,64,128]{2,1,0:T(8,128)S(1)} %get-tuple-element.26), channel_id=1, source_target_pairs={{0,10},{2,8},{4,14},{6,12},{8,2},{10,0},{12,6},{14,4},{16,26},{18,... | collective-permute-start | bytes 294920 | tf_op jit(solution)/shard_map/ppermute | solution.py:188
  (3 other events, 2.1 us)

commit v3 on v2

v3 whole, which is shorter than its diff:
```python
import functools

import jax
import jax.numpy as jnp
from jax import lax
from jax.experimental import pallas as pl
from jax.experimental.pallas import tpu as pltpu
from jax.sharding import PartitionSpec as P

VMEM_LIMIT = 48 * 2**20
SMEM = pl.BlockSpec(memory_space=pltpu.SMEM)
VMEM = pl.BlockSpec(memory_space=pltpu.VMEM)
ANY = pl.BlockSpec(memory_space=pl.ANY)


def split_bits(points, blocks):
    bits = points.bit_length() - 1
    inside = [bit for bit in range(bits) if bit % 2 == 0][: bits // 2]
    while blocks % (1 << len(inside)):
        inside.pop()
    return inside, [bit for bit in range(bits) if bit not in inside]


def spread(value, bits):
    return sum(((value >> i) & 1) << bit for i, bit in enumerate(bits))


def gathered(value, bits):
    return sum((((value >> bit) & 1) << i for i, bit in enumerate(bits)), 0 * value)


def project_kernel(orders, inside, halves, pos, cols, counts, potential, *refs):
    sources, (out, whole, blocks, sem, sems) = refs[:-5], refs[-5:]
    modes, rows, slots, size, _ = blocks.shape
    points, _, chunks, length, _ = whole.shape
    local_rows = potential.shape[1]
    chunk, half = gathered(pos[0], inside), pos[1]
    first = pltpu.make_async_copy(potential.at[:, pl.ds(chunk * rows, rows)], blocks, sem)
    first.start()
    copies = []
    for i, source in enumerate(sources):
        shift, (point, order) = i // len(orders), orders[i % len(orders)]
        place = lax.rem(half + halves - shift, halves)
        for j, other in enumerate(order):
            copies.append(
                pltpu.make_async_copy(
                    source.at[pl.ds(j * length, length)],
                    whole.at[point, place, j if other is None else chunk ^ other],
                    sems.at[len(copies)],
                )
            )
    for copy in copies:
        copy.start()
    first.wait()
    for copy in copies:
        copy.wait()
    for mode in range(modes):
        for row in range(rows):
            at = mode * local_rows + chunk * rows + row
            used = counts[at]
            left = []
            right = []
            for slot in range(slots):
                block = blocks[mode, row, slot]
                left.append(jnp.where(slot < used, block, jnp.zeros_like(block)))
                col = cols[at * slots + slot]
                place = lax.div(col, local_rows)
                inner = lax.rem(col, local_rows)
                start = pl.multiple_of(lax.rem(inner, rows) * size, size)
                right.append(
                    jnp.concatenate(
                        [
                            whole[point, place, lax.div(inner, rows), pl.ds(start, size), :]
                            for point in range(points)
                        ],
                        axis=1,
                    )
                )
            product = jnp.dot(
                jnp.concatenate(left, axis=1),
                jnp.concatenate(right, axis=0),
                preferred_element_type=jnp.float32,
            )
            turned = product.astype(jnp.bfloat16).T
            for point in range(points):
                out[point * modes + mode, :, row * size : (row + 1) * size] = turned[
                    point * size : (point + 1) * size
                ]


def project(name, pos, cols, counts, potential, sources, orders, inside, halves):
    group = 1 << len(inside)
    modes, local_rows, slots, size, _ = potential.shape
    bands = sources[0].shape[1]
    rows = local_rows // group
    points = 1 + max(point for point, _ in orders)
    count = halves * sum(len(order) for _, order in orders)
    return pl.pallas_call(
        functools.partial(project_kernel, orders, inside, halves),
        out_shape=jax.ShapeDtypeStruct((points * modes, bands, rows * size), jnp.bfloat16),
        in_specs=[SMEM, SMEM, SMEM] + [ANY] * (1 + len(sources)),
        out_specs=VMEM,
        scratch_shapes=[
            pltpu.VMEM((points, halves, group, rows * size, bands), jnp.bfloat16),
            pltpu.VMEM((modes, rows, slots, size, size), jnp.bfloat16),
            pltpu.SemaphoreType.DMA,
            pltpu.SemaphoreType.DMA((count,)),
        ],
        compiler_params=pltpu.CompilerParams(vmem_limit_bytes=VMEM_LIMIT),
        cost_estimate=pl.CostEstimate(flops=0, bytes_accessed=0, transcendentals=0),
        name=name,
    )(pos, cols, counts, potential, *sources)


def couple_kernel(jobs, last, inside, outside, halves, pos, partners, *refs):
    group = 1 << len(inside)
    points = group << len(outside)
    refs, (out, total) = refs[:-2], refs[-2:]
    me, half = pos[0], pos[1]
    for start, pairs, first, count, resumed in jobs:
        projected, refs = refs[0], refs[1:]
        parts, refs = refs[:count], refs[count:]
        rows = projected.shape[2]
        modes = total.shape[0] // group
        if resumed:
            total[start : start + pairs] = refs[0][...]
            refs = refs[1:]
        else:
            total[start : start + pairs] = jnp.zeros((pairs,) + total.shape[1:], jnp.float32)

        def add(pair, carry, start=start, first=first, parts=parts, projected=projected):
            point = lax.div(pair + start, modes)
            mine = me ^ spread(point, inside)
            away = partners[lax.rem(pair, modes) * points + mine] ^ me
            at = (gathered(away, outside) - first) * group + gathered(away, inside)
            base = 0
            for part in parts:
                held = part.shape[0] // rows
                here = at - base
                base += held

                @pl.when(jnp.logical_and(here >= 0, here < held))
                def _(part=part, here=here):
                    chunk = part[pl.ds(pl.multiple_of(here * rows, rows), rows), :]
                    total[pair + start] += jnp.dot(
                        projected[pair], chunk, preferred_element_type=jnp.float32
                    )

            return carry

        lax.fori_loop(0, pairs, add, 0)
    if last:
        bands = total.shape[1]
        share = bands // halves
        for pair in range(total.shape[0]):
            turned = total[pair].T
            for part in range(halves):
                out[lax.rem(part + halves - half, halves), pair] = turned[
                    part * share : (part + 1) * share
                ]
    else:
        out[...] = total[: out.shape[0]]


def couple(name, last, pos, partners, work, group, inside, outside, halves):
    jobs = []
    values = []
    start = 0
    for projected, first, parts, before in work:
        pairs, bands, rows = projected.shape
        jobs.append((start, pairs, first, len(parts), before is not None))
        values += [projected] + parts + ([] if before is None else [before])
        start += pairs
    total = start if last else (start // (group - 1)) * group if group > 1 else start
    shape = (halves, start, bands // halves, bands) if last else (start, bands, bands)
    return pl.pallas_call(
        functools.partial(couple_kernel, jobs, last, inside, outside, halves),
        out_shape=jax.ShapeDtypeStruct(shape, jnp.float32),
        in_specs=[SMEM, SMEM] + [VMEM] * len(values),
        out_specs=VMEM,
        scratch_shapes=[pltpu.VMEM((total, bands, bands), jnp.float32)],
        compiler_params=pltpu.CompilerParams(vmem_limit_bytes=VMEM_LIMIT),
        cost_estimate=pl.CostEstimate(flops=0, bytes_accessed=0, transcendentals=0),
        name=name,
    )(pos, partners, *values)


def solution(mesh):
    points = mesh.shape["ka"]
    halves = mesh.shape["orb"]

    def per_device(coefficients, potential, block_cols, block_counts, partners, gaps):
        modes, local_rows, _, _, _ = potential.shape
        inside, outside = split_bits(points, local_rows)
        group = 1 << len(inside)
        own = coefficients[0]
        rows = own.shape[0] // group
        me = lax.axis_index("ka").astype(jnp.int32)
        chunk = gathered(me, inside)
        pos = jnp.stack([me, lax.axis_index("orb").astype(jnp.int32)])
        cols = block_cols.reshape(-1)
        counts = block_counts.reshape(-1)
        pairing = partners.reshape(-1)

        def swap(value, mask):
            return lax.ppermute(value, "ka", [(i, i ^ mask) for i in range(points)])

        def rotate(value, shift):
            return lax.ppermute(
                value, "orb", [(i, (i + shift) % halves) for i in range(halves)]
            )

        def chunk_for(point):
            return lax.dynamic_slice_in_dim(own, (chunk ^ point) * rows, rows, 0)

        def after(value, *others):
            return lax.optimization_barrier((value,) + others)[0]

        parts = [chunk_for(0)]
        parts += [swap(chunk_for(p), spread(p, inside)) for p in range(1, group)]
        top = 1 << outside[-1]
        first_far = swap(parts[0], top)
        second_far = swap(parts[1], top)
        held = {0: [jnp.concatenate(parts, axis=0)]}
        for i in reversed(range(len(outside) - 1)):
            for key, items in list(held.items()):
                held[key | (1 << i)] = [swap(item, 1 << outside[i]) for item in items]
        third_far = swap(after(jnp.concatenate(parts[2:], axis=0), first_far), top)
        far = {1 << (len(outside) - 1): [first_far, second_far, third_far]}
        for i in reversed(range(len(outside) - 1)):
            for key, items in list(far.items()):
                far[key | (1 << i)] = [
                    swap(after(item, *held[1 << i]), 1 << outside[i]) for item in items
                ]
        sets = {**held, **far}
        sets[0] = parts
        late = far[max(far)]
        own_away = [rotate(after(own, parts[1]), shift) for shift in range(1, halves)]
        chunks = {0: {p: chunk_for(p) for p in range(group)}}
        near = {}
        for i in reversed(range(len(inside))):
            bit = 1 << i
            for key in list(chunks):
                order = [p for p in range(group) if p != bit]
                rest = jnp.concatenate([chunks[key][p] for p in order], axis=0)
                if key:
                    rest = after(rest, second_far, *own_away, *near.get(bit, [])[:1])
                else:
                    rest = after(rest, parts[1], first_far)
                rest = swap(rest, spread(bit, inside))
                order = [p ^ bit for p in order]
                near[key | bit] = (rest, order)
                chunks[key | bit] = {
                    p: rest[j * rows : (j + 1) * rows] for j, p in enumerate(order)
                }
                chunks[key | bit][0] = parts[key | bit]

        def all_rows(keys):
            values = []
            orders = []
            for place, key in enumerate(keys):
                if key == 0:
                    values.append(own)
                    orders.append((place, [None] * group))
                else:
                    values += [parts[key], near[key][0]]
                    orders += [(place, [0]), (place, near[key][1])]
            return values, orders

        values, orders = all_rows(range(group - 1))
        for shift in range(1, halves):
            moved = [rotate(value, shift) for value in values[1 : len(orders)]]
            values = values + [own_away[shift - 1]] + moved
        projected = project(
            "project", pos, cols, counts, potential, values, orders, inside, halves
        )
        values, orders = all_rows([group - 1])
        for shift in range(1, halves):
            values = values + [
                rotate(after(value, projected, *late[:2]), shift) for value in values[: len(orders)]
            ]
        projected_last = project(
            "project_last", pos, cols, counts, potential, values, orders, inside, halves
        )
        count = 1 << len(outside)
        early = [part for key in range(count - 1) for part in sets[key]]
        total = couple(
            "couple",
            False,
            pos,
            pairing,
            [(projected, 0, early, None)],
            group,
            inside,
            outside,
            halves,
        )
        total = couple(
            "couple_last",
            True,
            pos,
            pairing,
            [(projected, count - 1, late, total), (projected_last, 0, early + late, None)],
            group,
            inside,
            outside,
            halves,
        )
        summed = total[0]
        for shift in range(1, halves):
            summed = summed + rotate(total[shift], shift)
        summed = summed.reshape((group, modes) + summed.shape[1:])
        result = summed[0]
        for point in range(1, group):
            result = result + swap(summed[point], spread(point, inside))
        return result[:, None] / gaps

    return jax.shard_map(
        per_device,
        mesh=mesh,
        in_specs=(
            P("ka", "orb", None),
            P(None, "orb", None, None, None),
            P(None, "orb", None),
            P(None, "orb"),
            P(),
            P(None, "ka", "orb", None),
        ),
        out_specs=P(None, "ka", "orb", None),
        check_vma=False,
    )
```

time: 114 us -> 111 us (0.974)
  waiting for transfers between devices: 64.4 us -> 58.8 us
  starting transfers between devices: 26.3 us -> 20.7 us
  local copies, waits for them, and re-layouts: 4.95 us -> 9.95 us
  other arithmetic: 0.9 us -> 2.8 us
    ppermute x16, starting transfers between devices: 25.5 us -> 19.6 us  [swap(): return lax.ppermute(value, 'ka', [(i, i ^ mask) for i in range(points)])]
    unnamed x29 -> x33, local copies, waits for them, and re-layouts: 3.23 us -> 8.27 us
    ppermute x16, waiting for transfers between devices: 60 us -> 56.7 us  [swap(): return lax.ppermute(value, 'ka', [(i, i ^ mask) for i in range(points)])]
    ppermute x5 -> x8, waiting for transfers between devices: 4.46 us -> 2.13 us  [rotate(): lax.ppermute(value, 'orb', [(i, (i + shift) % halves) for i in range(halv...]
    concatenate x2 -> x4, other arithmetic: 0.1 us -> 2 us  [the longest x2 1.05 us: per_device(): rest = jnp.concatenate([chunks[key][p] for p in order], axis=0)]
    pallas_call x3 -> x4, Pallas kernels: 16.8 us -> 17.9 us  [the longest x2 10.1 us: project(): pl.pallas_call(functools.partial(project_kernel, orders, inside, halves),...]
  transfers between devices with their start and end apart: 21 -> 24, of which waited for: 13 -> 13; matrix products, arithmetic and copies ran while one was open for 1% -> 2% of each run, Pallas kernels for 12% -> 12%
where the time goes in v3:
time: 111 us; the launch traced here: 110 us
  waiting for transfers between devices  58.8 us (53%)
  starting transfers between devices  20.7 us (19%)
  Pallas kernels  17.9 us (16%)
  local copies, waits for them, and re-layouts  9.95 us (9%)
  other arithmetic  2.8 us (3%)
    ppermute x16, waiting for transfers between devices, swap(): return lax.ppermute(value, 'ka', [(i, i ^ mask) for i in range(points)])  56.7 us
    ppermute x16, starting transfers between devices, swap(): return lax.ppermute(value, 'ka', [(i, i ^ mask) for i in range(points)])  19.6 us
    pallas_call x2, Pallas kernels, project(): pl.pallas_call(functools.partial(project_kernel, orders, inside, halves),...  10.1 us
    unnamed x33, local copies, waits for them, and re-layouts  8.27 us
    pallas_call x2, Pallas kernels, couple(): pl.pallas_call(functools.partial(couple_kernel, jobs, last, inside, outsi...  7.83 us
  transfers between devices with their start and end apart: 24, of which 13 were waited for; matrix products, arithmetic and copies ran while one was open for 2% of the time, Pallas kernels for 12%

profile of v3, /device:TPU:0, one launch (start us, length us, event | category | flops | bytes accessed | tf_op | source)
XLA Modules:
  0.0 110.4 jit_solution(15612930089639801743)
XLA Ops:
  0.0 1.3 %dynamic-slice_bitcast_fusion.1 = (bf16[1024,128]{1,0:T(8,128)(2,1)S(1)}, bf16[1024,128]{1,0:T(8,128)(2,1)S(1)}, bf16[1024,128]{1,0:T(8,128)(2,1)S(1)}, bf16[1024,128]{1,0:T(8,128)(2,1)S(1)}) fusion(bf16[1,4096,128]{2,1,0:T(8,128)(2,1)} %param.6, s32[]{:T(128)S(6)} %select_n.18, s32[]{:T(128)S(6)} %select_n.17, s32[]{:T(128)S(6)} %select_n.16, s32[]{:T(128)S(6)} %select_n.19), kind=kLoop, calls=%fused_computation.11 | loop fusion | bytes 2097168 | tf_op jit(solution)/shard_map/dynamic_slice | solution.py:214
  1.3 3.0 %collective-permute-start = (bf16[1024,128]{1,0:T(8,128)(2,1)S(1)}, bf16[1024,128]{1,0:T(8,128)(2,1)S(1)}, u32[]{:S(2)}, u32[]{:S(2)}) collective-permute-start(bf16[1024,128]{1,0:T(8,128)(2,1)S(1)} %get-tuple-element.27), channel_id=1, source_target_pairs={{0,2},{2,0},{4,6},{6,4},{8,10},{10,8},{12,14},{14,12},{16,18},{18,... | collective-permute-start | bytes 786440 | tf_op jit(solution)/shard_map/ppermute | solution.py:206
  4.3 2.6 %collective-permute-start.1 = (bf16[1024,128]{1,0:T(8,128)(2,1)S(1)}, bf16[1024,128]{1,0:T(8,128)(2,1)S(1)}, u32[]{:S(2)}, u32[]{:S(2)}) collective-permute-start(bf16[1024,128]{1,0:T(8,128)(2,1)S(1)} %get-tuple-element.26.refs_1_.refs_6_), channel_id=1, source_target_pairs={{0,16},{2,18},{4,20},{6,22},{8,24},{10,26},{12,28},{14,30},{16,0},... | collective-permute-start | bytes 786440 | tf_op jit(solution)/shard_map/ppermute | solution.py:206
  6.9 1.6 %collective-permute-start.3 = (bf16[1024,128]{1,0:T(8,128)(2,1)S(1)}, bf16[1024,128]{1,0:T(8,128)(2,1)S(1)}, u32[]{:S(2)}, u32[]{:S(2)}) collective-permute-start(bf16[1024,128]{1,0:T(8,128)(2,1)S(1)} %get-tuple-element.25), channel_id=1, source_target_pairs={{0,8},{2,10},{4,12},{6,14},{8,0},{10,2},{12,4},{14,6},{16,24},{18,... | collective-permute-start | bytes 786440 | tf_op jit(solution)/shard_map/ppermute | solution.py:206
  9.0 1.6 %collective-permute-done.refs_1_.refs_2_.refs_7_ = bf16[1024,128]{1,0:T(8,128)(2,1)S(1)} collective-permute-done((bf16[1024,128]{1,0:T(8,128)(2,1)S(1)}, bf16[1024,128]{1,0:T(8,128)(2,1)S(1)}, u32[]{:S(2)}, u32[]{:S(2)}) %collective-permute-start) | collective-permute-done | bytes 262176 | tf_op jit(solution)/shard_map/ppermute | solution.py:206
  10.6 8.1 %collective-permute-done.1.refs_6_.refs_11_ = bf16[1024,128]{1,0:T(8,128)(2,1)S(1)} collective-permute-done((bf16[1024,128]{1,0:T(8,128)(2,1)S(1)}, bf16[1024,128]{1,0:T(8,128)(2,1)S(1)}, u32[]{:S(2)}, u32[]{:S(2)}) %collective-permute-start.1) | collective-permute-done | bytes 262176 | tf_op jit(solution)/shard_map/ppermute | solution.py:206
  20.6 5.5 %collective-permute-done.10.refs_4_.refs_0_.refs_9_ = bf16[1024,128]{1,0:T(8,128)(2,1)S(1)} collective-permute-done((bf16[1024,128]{1,0:T(8,128)(2,1)S(1)}, bf16[1024,128]{1,0:T(8,128)(2,1)S(1)}, u32[]{:S(2)}, u32[]{:S(2)}) %collective-permute-start.10) | collective-permute-done | bytes 262176 | tf_op jit(solution)/shard_map/ppermute | solution.py:206
  26.2 1.6 %collective-permute-start.11 = (bf16[4096,128]{1,0:T(8,128)(2,1)S(1)}, bf16[4096,128]{1,0:T(8,128)(2,1)S(1)}, u32[]{:S(2)}, u32[]{:S(2)}) collective-permute-start(bf16[4096,128]{1,0:T(8,128)(2,1)S(1)} %pad_maximum_fusion), channel_id=1, source_target_pairs={{0,4},{2,6},{4,0},{6,2},{8,12},{10,14},{12,8},{14,10},{16,20},{18,... | collective-permute-start | bytes 3145736 | tf_op jit(solution)/shard_map/ppermute | solution.py:206
  27.9 1.0 collective-permute-start.13
  28.9 18.1 %collective-permute-done.4.refs_4_ = bf16[3072,128]{1,0:T(8,128)(2,1)S(1)} collective-permute-done((bf16[3072,128]{1,0:T(8,128)(2,1)S(1)}, bf16[3072,128]{1,0:T(8,128)(2,1)S(1)}, u32[]{:S(2)}, u32[]{:S(2)}) %collective-permute-start.4) | collective-permute-done | bytes 786464 | tf_op jit(solution)/shard_map/ppermute | solution.py:206
  47.6 0.9 pad_maximum_fusion.5
  51.6 1.5 %collective-permute-start.14 = (bf16[1024,128]{1,0:T(8,128)(2,1)}, bf16[1024,128]{1,0:T(8,128)(2,1)}, u32[]{:S(2)}, u32[]{:S(2)}) collective-permute-start(bf16[1024,128]{1,0:T(8,128)(2,1)} %collective-permute-done.13.refs_7_.refs_12_), channel_id=1, source_target_pairs={{0,4},{2,6},{4,0},{6,2},{8,12},{10,14},{12,8},{14,10},{16,20},{18,... | collective-permute-start | bytes 786440 | tf_op jit(solution)/shard_map/ppermute | solution.py:206
  54.4 0.9 copy-done.5
  56.3 1.1 %copy-done.4 = bf16[3072,128]{1,0:T(8,128)(2,1)S(1)} copy-done((bf16[3072,128]{1,0:T(8,128)(2,1)S(1)}, bf16[3072,128]{1,0:T(8,128)(2,1)}, u32[]{:S(2)}) %copy-start.4) | copy-done | bytes 786456
  57.4 1.1 %copy-done.6 = bf16[3072,128]{1,0:T(8,128)(2,1)S(1)} copy-done((bf16[3072,128]{1,0:T(8,128)(2,1)S(1)}, bf16[3072,128]{1,0:T(8,128)(2,1)}, u32[]{:S(2)}) %copy-start.6) | copy-done | bytes 786456
  58.6 0.9 copy-done.8
  59.5 0.9 copy-done.10
  60.5 6.4 %project.1.refs_0_ = bf16[9,128,1024]{2,1,0:T(8,128)(2,1)} custom-call(s32[2]{0:T(128)S(1)} %pad_add_fusion.pos, s32[288]{0:T(512)S(1)} %reshape.23.cols, s32[96]{0:T(128)S(1)} %reshape.24.counts, bf16[3,32,3,128,128]{4,3,2,1,0:T(8,128)(2,1)} %potential.3, bf16[4096,128]{1,0:T(8,128)(2,1)S(1)} %bitcast.28, ...), custom_call_target="tpu_custom_call" | custom-call | tf_op jit(solution)/shard_map/project/pallas_call | solution.py:98
  66.9 1.6 %collective-permute-done.17.refs_1_ = bf16[3072,128]{1,0:T(8,128)(2,1)} collective-permute-done((bf16[3072,128]{1,0:T(8,128)(2,1)}, bf16[3072,128]{1,0:T(8,128)(2,1)}, u32[]{:S(2)}, u32[]{:S(2)}) %collective-permute-start.17) | collective-permute-done | bytes 786464 | tf_op jit(solution)/shard_map/ppermute | solution.py:206
  68.5 12.4 %collective-permute-done.15.refs_8_.refs_13_ = bf16[2048,128]{1,0:T(8,128)(2,1)} collective-permute-done((bf16[2048,128]{1,0:T(8,128)(2,1)}, bf16[2048,128]{1,0:T(8,128)(2,1)}, u32[]{:S(2)}, u32[]{:S(2)}) %collective-permute-start.15) | collective-permute-done | bytes 524320 | tf_op jit(solution)/shard_map/ppermute | solution.py:206
  80.9 1.5 %collective-permute-start.16 = (bf16[2048,128]{1,0:T(8,128)(2,1)}, bf16[2048,128]{1,0:T(8,128)(2,1)S(1)}, u32[]{:S(2)}, u32[]{:S(2)}) collective-permute-start(bf16[2048,128]{1,0:T(8,128)(2,1)} %collective-permute-done.15.refs_8_.refs_13_), channel_id=1, source_target_pairs={{0,4},{2,6},{4,0},{6,2},{8,12},{10,14},{12,8},{14,10},{16,20},{18,... | collective-permute-start | bytes 1572872 | tf_op jit(solution)/shard_map/ppermute | solution.py:206
  82.5 1.7 %copy-done = bf16[9,128,1024]{2,1,0:T(8,128)(2,1)S(1)} copy-done((bf16[9,128,1024]{2,1,0:T(8,128)(2,1)S(1)}, bf16[9,128,1024]{2,1,0:T(8,128)(2,1)}, u32[]{:S(2)}) %copy-start) | copy-done | bytes 2359320
  84.2 3.1 %couple.1.refs_4_ = f32[9,128,128]{2,1,0:T(8,128)S(1)} custom-call(s32[2]{0:T(128)S(1)} %pad_add_fusion.pos, s32[48]{0:T(128)S(1)} %reshape.22.partners, bf16[9,128,1024]{2,1,0:T(8,128)(2,1)S(1)} %copy-done, bf16[1024,128]{1,0:T(8,128)(2,1)S(1)} %get-tuple-element.26.refs_1_.refs_6_, bf16[1024,128]{1,0:T(8,128)(2,1)S(1)} %collective-permute-done.refs_1_.refs_2_.refs_7_, ...), custom_call_target="tpu_custom_call" | custom-call | tf_op jit(solution)/shard_map/couple/pallas_call | solution.py:176
  87.3 3.7 %project_last.1.refs_5_ = bf16[3,128,1024]{2,1,0:T(8,128)(2,1)S(1)} custom-call(s32[2]{0:T(128)S(1)} %pad_add_fusion.pos, s32[288]{0:T(512)S(1)} %reshape.23.cols, s32[96]{0:T(128)S(1)} %reshape.24.counts, bf16[3,32,3,128,128]{4,3,2,1,0:T(8,128)(2,1)} %potential.3, bf16[1024,128]{1,0:T(8,128)(2,1)S(1)} %collective-permute-done.10.refs_4_.refs_0_.refs_9_, ...), custom_call_target="tpu_custom_call" | custom-call | tf_op jit(solution)/shard_map/project_last/pallas_call | solution.py:98
  91.0 3.9 %collective-permute-done.16.refs_3_.refs_16_ = bf16[2048,128]{1,0:T(8,128)(2,1)S(1)} collective-permute-done((bf16[2048,128]{1,0:T(8,128)(2,1)}, bf16[2048,128]{1,0:T(8,128)(2,1)S(1)}, u32[]{:S(2)}, u32[]{:S(2)}) %collective-permute-start.16) | collective-permute-done | bytes 524320 | tf_op jit(solution)/shard_map/ppermute | solution.py:206
  94.9 4.7 %couple_last.1 = f32[2,12,64,128]{3,2,1,0:T(8,128)S(1)} custom-call(s32[2]{0:T(128)S(1)} %pad_add_fusion.pos, s32[48]{0:T(128)S(1)} %reshape.22.partners, bf16[9,128,1024]{2,1,0:T(8,128)(2,1)} %project.1.refs_0_, bf16[1024,128]{1,0:T(8,128)(2,1)} %collective-permute-done.12.refs_1_.refs_14_, bf16[1024,128]{1,0:T(8,128)(2,1)} %collective-permute-done.14.refs_2_.refs_15_, ...), custom_call_target="tpu_custom_call" | custom-call | tf_op jit(solution)/shard_map/couple_last/pallas_call | solution.py:176
  99.8 1.7 %collective-permute-done.20 = f32[12,64,128]{2,1,0:T(8,128)S(1)} collective-permute-done((f32[12,64,128]{2,1,0:T(8,128)S(1)}, f32[12,64,128]{2,1,0:T(8,128)S(1)}, u32[]{:S(2)}, u32[]{:S(2)}) %collective-permute-start.20) | collective-permute-done | bytes 393248 | tf_op jit(solution)/shard_map/ppermute | solution.py:209
  101.6 1.4 %collective-permute-start.21 = (f32[3,64,128]{2,1,0:T(8,128)S(1)}, f32[3,64,128]{2,1,0:T(8,128)S(1)}, u32[]{:S(2)}, u32[]{:S(2)}) collective-permute-start(f32[3,64,128]{2,1,0:T(8,128)S(1)} %get-tuple-element.31), channel_id=1, source_target_pairs={{0,2},{2,0},{4,6},{6,4},{8,10},{10,8},{12,14},{14,12},{16,18},{18,... | collective-permute-start | bytes 294920 | tf_op jit(solution)/shard_map/ppermute | solution.py:206
  102.9 2.2 %collective-permute-start.23 = (f32[3,64,128]{2,1,0:T(8,128)S(1)}, f32[3,64,128]{2,1,0:T(8,128)S(1)}, u32[]{:S(2)}, u32[]{:S(2)}) collective-permute-start(f32[3,64,128]{2,1,0:T(8,128)S(1)} %get-tuple-element.32), channel_id=1, source_target_pairs={{0,10},{2,8},{4,14},{6,12},{8,2},{10,0},{12,6},{14,4},{16,26},{18,... | collective-permute-start | bytes 294920 | tf_op jit(solution)/shard_map/ppermute | solution.py:206
  105.1 1.3 %collective-permute-done.21 = f32[3,64,128]{2,1,0:T(8,128)S(1)} collective-permute-done((f32[3,64,128]{2,1,0:T(8,128)S(1)}, f32[3,64,128]{2,1,0:T(8,128)S(1)}, u32[]{:S(2)}, u32[]{:S(2)}) %collective-permute-start.21) | collective-permute-done | bytes 98336 | tf_op jit(solution)/shard_map/ppermute | solution.py:206
  106.5 2.1 %collective-permute-done.22 = f32[3,64,128]{2,1,0:T(8,128)S(1)} collective-permute-done((f32[3,64,128]{2,1,0:T(8,128)S(1)}, f32[3,64,128]{2,1,0:T(8,128)S(1)}, u32[]{:S(2)}, u32[]{:S(2)}) %collective-permute-start.22) | collective-permute-done | bytes 98336 | tf_op jit(solution)/shard_map/ppermute | solution.py:206
  108.5 1.2 %collective-permute-done.23 = f32[3,64,128]{2,1,0:T(8,128)S(1)} collective-permute-done((f32[3,64,128]{2,1,0:T(8,128)S(1)}, f32[3,64,128]{2,1,0:T(8,128)S(1)}, u32[]{:S(2)}, u32[]{:S(2)}) %collective-permute-start.23) | collective-permute-done | bytes 98336 | tf_op jit(solution)/shard_map/ppermute | solution.py:206
  (67 shorter events, 9.4 us)
Async XLA Ops:
  1.3 18.6 %copy-start.2 = (bf16[1,4096,128]{2,1,0:T(8,128)(2,1)S(1)}, bf16[1,4096,128]{2,1,0:T(8,128)(2,1)}, u32[]{:S(2)}) copy-start(bf16[1,4096,128]{2,1,0:T(8,128)(2,1)} %param.6) | copy-start | bytes 3145732
  1.3 9.3 %collective-permute-start = (bf16[1024,128]{1,0:T(8,128)(2,1)S(1)}, bf16[1024,128]{1,0:T(8,128)(2,1)S(1)}, u32[]{:S(2)}, u32[]{:S(2)}) collective-permute-start(bf16[1024,128]{1,0:T(8,128)(2,1)S(1)} %get-tuple-element.27), channel_id=1, source_target_pairs={{0,2},{2,0},{4,6},{6,4},{8,10},{10,8},{12,14},{14,12},{16,18},{18,... | collective-permute-start | bytes 786440 | tf_op jit(solution)/shard_map/ppermute | solution.py:206
  4.3 14.4 %collective-permute-start.1 = (bf16[1024,128]{1,0:T(8,128)(2,1)S(1)}, bf16[1024,128]{1,0:T(8,128)(2,1)S(1)}, u32[]{:S(2)}, u32[]{:S(2)}) collective-permute-start(bf16[1024,128]{1,0:T(8,128)(2,1)S(1)} %get-tuple-element.26.refs_1_.refs_6_), channel_id=1, source_target_pairs={{0,16},{2,18},{4,20},{6,22},{8,24},{10,26},{12,28},{14,30},{16,0},... | collective-permute-start | bytes 786440 | tf_op jit(solution)/shard_map/ppermute | solution.py:206
  6.9 13.8 %collective-permute-start.3 = (bf16[1024,128]{1,0:T(8,128)(2,1)S(1)}, bf16[1024,128]{1,0:T(8,128)(2,1)S(1)}, u32[]{:S(2)}, u32[]{:S(2)}) collective-permute-start(bf16[1024,128]{1,0:T(8,128)(2,1)S(1)} %get-tuple-element.25), channel_id=1, source_target_pairs={{0,8},{2,10},{4,12},{6,14},{8,0},{10,2},{12,4},{14,6},{16,24},{18,... | collective-permute-start | bytes 786440 | tf_op jit(solution)/shard_map/ppermute | solution.py:206
  8.5 17.7 %collective-permute-start.10 = (bf16[1024,128]{1,0:T(8,128)(2,1)S(1)}, bf16[1024,128]{1,0:T(8,128)(2,1)S(1)}, u32[]{:S(2)}, u32[]{:S(2)}) collective-permute-start(bf16[1024,128]{1,0:T(8,128)(2,1)S(1)} %get-tuple-element.28), channel_id=1, source_target_pairs={{0,10},{2,8},{4,14},{6,12},{8,2},{10,0},{12,6},{14,4},{16,26},{18,... | collective-permute-start | bytes 786440 | tf_op jit(solution)/shard_map/ppermute | solution.py:206
  18.7 28.3 %collective-permute-start.4 = (bf16[3072,128]{1,0:T(8,128)(2,1)S(1)}, bf16[3072,128]{1,0:T(8,128)(2,1)S(1)}, u32[]{:S(2)}, u32[]{:S(2)}) collective-permute-start(bf16[3072,128]{1,0:T(8,128)(2,1)S(1)} %get-tuple-element.16), channel_id=1, source_target_pairs={{0,8},{2,10},{4,12},{6,14},{8,0},{10,2},{12,4},{14,6},{16,24},{18,... | collective-permute-start | bytes 2359304 | tf_op jit(solution)/shard_map/ppermute | solution.py:206
  19.3 27.9 %collective-permute-start.2 = (bf16[3072,128]{1,0:T(8,128)(2,1)S(1)}, bf16[3072,128]{1,0:T(8,128)(2,1)}, u32[]{:S(2)}, u32[]{:S(2)}) collective-permute-start(bf16[3072,128]{1,0:T(8,128)(2,1)S(1)} %get-tuple-element.15), channel_id=1, source_target_pairs={{0,2},{2,0},{4,6},{6,4},{8,10},{10,8},{12,14},{14,12},{16,18},{18,... | collective-permute-start | bytes 2359304 | tf_op jit(solution)/shard_map/ppermute | solution.py:206
  19.8 28.8 %collective-permute-start.5 = (bf16[4096,128]{1,0:T(8,128)(2,1)S(1)}, bf16[4096,128]{1,0:T(8,128)(2,1)S(1)}, u32[]{:S(2)}, u32[]{:S(2)}) collective-permute-start(bf16[4096,128]{1,0:T(8,128)(2,1)S(1)} %bitcast.27), channel_id=1, source_target_pairs={{0,1},{1,0},{2,3},{3,2},{4,5},{5,4},{6,7},{7,6},{8,9},{9,8},{10,11... | collective-permute-start | bytes 3145736 | tf_op jit(solution)/shard_map/ppermute | solution.py:209
  26.2 22.9 %collective-permute-start.11 = (bf16[4096,128]{1,0:T(8,128)(2,1)S(1)}, bf16[4096,128]{1,0:T(8,128)(2,1)S(1)}, u32[]{:S(2)}, u32[]{:S(2)}) collective-permute-start(bf16[4096,128]{1,0:T(8,128)(2,1)S(1)} %pad_maximum_fusion), channel_id=1, source_target_pairs={{0,4},{2,6},{4,0},{6,2},{8,12},{10,14},{12,8},{14,10},{16,20},{18,... | collective-permute-start | bytes 3145736 | tf_op jit(solution)/shard_map/ppermute | solution.py:206
  27.9 20.7 %collective-permute-start.13 = (bf16[1024,128]{1,0:T(8,128)(2,1)S(1)}, bf16[1024,128]{1,0:T(8,128)(2,1)}, u32[]{:S(2)}, u32[]{:S(2)}) collective-permute-start(bf16[1024,128]{1,0:T(8,128)(2,1)S(1)} %collective-permute-done.refs_1_.refs_2_.refs_7_), channel_id=1, source_target_pairs={{0,16},{2,18},{4,20},{6,22},{8,24},{10,26},{12,28},{14,30},{16,0},... | collective-permute-start | bytes 786440 | tf_op jit(solution)/shard_map/ppermute | solution.py:206
  47.0 3.5 %copy-start.3 = (bf16[3072,128]{1,0:T(8,128)(2,1)}, bf16[3072,128]{1,0:T(8,128)(2,1)S(1)}, u32[]{:S(2)}) copy-start(bf16[3072,128]{1,0:T(8,128)(2,1)S(1)} %collective-permute-done.4.refs_4_) | copy-start | bytes 2359300
  47.0 8.8 %copy-start.13 = (s32[3,32,3]{1,2,0:T(4,128)S(1)}, s32[3,32,3]{1,2,0:T(4,128)}, u32[]{:S(2)}) copy-start(s32[3,32,3]{1,2,0:T(4,128)} %param.8) | copy-start | bytes 3460
  47.0 9.1 %copy-start.14 = (s32[3,32]{1,0:T(4,128)S(1)}, s32[3,32]{1,0:T(4,128)}, u32[]{:S(2)}) copy-start(s32[3,32]{1,0:T(4,128)} %param.9) | copy-start | bytes 1156
  47.1 7.3 %collective-permute-start.9 = (bf16[3072,128]{1,0:T(8,128)(2,1)S(1)}, bf16[3072,128]{1,0:T(8,128)(2,1)S(1)}, u32[]{:S(2)}, u32[]{:S(2)}) collective-permute-start(bf16[3072,128]{1,0:T(8,128)(2,1)S(1)} %collective-permute-done.4.refs_4_), channel_id=1, source_target_pairs={{0,1},{1,0},{2,3},{3,2},{4,5},{5,4},{6,7},{7,6},{8,9},{9,8},{10,11... | collective-permute-start | bytes 2359304 | tf_op jit(solution)/shard_map/ppermute | solution.py:209
  47.2 9.1 %collective-permute-start.7 = (bf16[3072,128]{1,0:T(8,128)(2,1)}, bf16[3072,128]{1,0:T(8,128)(2,1)}, u32[]{:S(2)}, u32[]{:S(2)}) collective-permute-start(bf16[3072,128]{1,0:T(8,128)(2,1)} %collective-permute-done.2.refs_2_), channel_id=1, source_target_pairs={{0,1},{1,0},{2,3},{3,2},{4,5},{5,4},{6,7},{7,6},{8,9},{9,8},{10,11... | collective-permute-start | bytes 2359304 | tf_op jit(solution)/shard_map/ppermute | solution.py:209
  48.6 5.8 %copy-start.11 = (bf16[4096,128]{1,0:T(8,128)(2,1)}, bf16[4096,128]{1,0:T(8,128)(2,1)S(1)}, u32[]{:S(2)}) copy-start(bf16[4096,128]{1,0:T(8,128)(2,1)S(1)} %collective-permute-done.5.refs_5_) | copy-start | bytes 3145732
  48.6 19.9 %collective-permute-start.17 = (bf16[3072,128]{1,0:T(8,128)(2,1)}, bf16[3072,128]{1,0:T(8,128)(2,1)}, u32[]{:S(2)}, u32[]{:S(2)}) collective-permute-start(bf16[3072,128]{1,0:T(8,128)(2,1)} %pad_maximum_fusion.5), channel_id=1, source_target_pairs={{0,2},{2,0},{4,6},{6,4},{8,10},{10,8},{12,14},{14,12},{16,18},{18,... | collective-permute-start | bytes 2359304 | tf_op jit(solution)/shard_map/ppermute | solution.py:206
  49.1 1.8 %collective-permute-start.6 = (bf16[1024,128]{1,0:T(8,128)(2,1)S(1)}, bf16[1024,128]{1,0:T(8,128)(2,1)S(1)}, u32[]{:S(2)}, u32[]{:S(2)}) collective-permute-start(bf16[1024,128]{1,0:T(8,128)(2,1)S(1)} %collective-permute-done.refs_1_.refs_2_.refs_7_), channel_id=1, source_target_pairs={{0,1},{1,0},{2,3},{3,2},{4,5},{5,4},{6,7},{7,6},{8,9},{9,8},{10,11... | collective-permute-start | bytes 786440 | tf_op jit(solution)/shard_map/ppermute | solution.py:209
  49.1 33.4 %copy-start.1 = (bf16[4096,128]{1,0:T(8,128)(2,1)}, bf16[4096,128]{1,0:T(8,128)(2,1)S(1)}, u32[]{:S(2)}) copy-start(bf16[4096,128]{1,0:T(8,128)(2,1)S(1)} %collective-permute-done.11.refs_5_.refs_10_) | copy-start | bytes 3145732
  49.1 4.0 %collective-permute-start.8 = (bf16[1024,128]{1,0:T(8,128)(2,1)S(1)}, bf16[1024,128]{1,0:T(8,128)(2,1)S(1)}, u32[]{:S(2)}, u32[]{:S(2)}) collective-permute-start(bf16[1024,128]{1,0:T(8,128)(2,1)S(1)} %collective-permute-done.3.refs_3_.refs_8_), channel_id=1, source_target_pairs={{0,1},{1,0},{2,3},{3,2},{4,5},{5,4},{6,7},{7,6},{8,9},{9,8},{10,11... | collective-permute-start | bytes 786440 | tf_op jit(solution)/shard_map/ppermute | solution.py:209
  51.6 15.3 %collective-permute-start.14 = (bf16[1024,128]{1,0:T(8,128)(2,1)}, bf16[1024,128]{1,0:T(8,128)(2,1)}, u32[]{:S(2)}, u32[]{:S(2)}) collective-permute-start(bf16[1024,128]{1,0:T(8,128)(2,1)} %collective-permute-done.13.refs_7_.refs_12_), channel_id=1, source_target_pairs={{0,4},{2,6},{4,0},{6,2},{8,12},{10,14},{12,8},{14,10},{16,20},{18,... | collective-permute-start | bytes 786440 | tf_op jit(solution)/shard_map/ppermute | solution.py:206
  53.8 13.1 %collective-permute-start.12 = (bf16[1024,128]{1,0:T(8,128)(2,1)S(1)}, bf16[1024,128]{1,0:T(8,128)(2,1)}, u32[]{:S(2)}, u32[]{:S(2)}) collective-permute-start(bf16[1024,128]{1,0:T(8,128)(2,1)S(1)} %collective-permute-done.1.refs_6_.refs_11_), channel_id=1, source_target_pairs={{0,4},{2,6},{4,0},{6,2},{8,12},{10,14},{12,8},{14,10},{16,20},{18,... | collective-permute-start | bytes 786440 | tf_op jit(solution)/shard_map/ppermute | solution.py:206
  55.2 25.6 %collective-permute-start.15 = (bf16[2048,128]{1,0:T(8,128)(2,1)}, bf16[2048,128]{1,0:T(8,128)(2,1)}, u32[]{:S(2)}, u32[]{:S(2)}) collective-permute-start(bf16[2048,128]{1,0:T(8,128)(2,1)} %pad_maximum_fusion.6), channel_id=1, source_target_pairs={{0,16},{2,18},{4,20},{6,22},{8,24},{10,26},{12,28},{14,30},{16,0},... | collective-permute-start | bytes 1572872 | tf_op jit(solution)/shard_map/ppermute | solution.py:206
  60.5 21.9 %copy-start.15 = (s32[3,16]{1,0:T(4,128)S(1)}, s32[3,16]{1,0:T(4,128)}, u32[]{:S(2)}) copy-start(s32[3,16]{1,0:T(4,128)} %param.10) | copy-start | bytes 580
  68.5 18.8 %collective-permute-start.19 = (bf16[3072,128]{1,0:T(8,128)(2,1)}, bf16[3072,128]{1,0:T(8,128)(2,1)}, u32[]{:S(2)}, u32[]{:S(2)}) collective-permute-start(bf16[3072,128]{1,0:T(8,128)(2,1)} %collective-permute-done.17.refs_1_), channel_id=1, source_target_pairs={{0,1},{1,0},{2,3},{3,2},{4,5},{5,4},{6,7},{7,6},{8,9},{9,8},{10,11... | collective-permute-start | bytes 2359304 | tf_op jit(solution)/shard_map/ppermute | solution.py:209
  80.9 14.1 %collective-permute-start.16 = (bf16[2048,128]{1,0:T(8,128)(2,1)}, bf16[2048,128]{1,0:T(8,128)(2,1)S(1)}, u32[]{:S(2)}, u32[]{:S(2)}) collective-permute-start(bf16[2048,128]{1,0:T(8,128)(2,1)} %collective-permute-done.15.refs_8_.refs_13_), channel_id=1, source_target_pairs={{0,4},{2,6},{4,0},{6,2},{8,12},{10,14},{12,8},{14,10},{16,20},{18,... | collective-permute-start | bytes 1572872 | tf_op jit(solution)/shard_map/ppermute | solution.py:206
  82.4 4.9 %collective-permute-start.18 = (bf16[1024,128]{1,0:T(8,128)(2,1)S(1)}, bf16[1024,128]{1,0:T(8,128)(2,1)S(1)}, u32[]{:S(2)}, u32[]{:S(2)}) collective-permute-start(bf16[1024,128]{1,0:T(8,128)(2,1)S(1)} %collective-permute-done.10.refs_4_.refs_0_.refs_9_), channel_id=1, source_target_pairs={{0,1},{1,0},{2,3},{3,2},{4,5},{5,4},{6,7},{7,6},{8,9},{9,8},{10,11... | collective-permute-start | bytes 786440 | tf_op jit(solution)/shard_map/ppermute | solution.py:209
  99.6 10.1 %copy-start.12 = (f32[3,1,64,128]{3,2,1,0:T(8,128)S(1)}, f32[3,1,64,128]{3,2,1,0:T(8,128)}, u32[]{:S(2)}) copy-start(f32[3,1,64,128]{3,2,1,0:T(8,128)} %param.11) | copy-start | bytes 294916
  99.7 1.8 %collective-permute-start.20 = (f32[12,64,128]{2,1,0:T(8,128)S(1)}, f32[12,64,128]{2,1,0:T(8,128)S(1)}, u32[]{:S(2)}, u32[]{:S(2)}) collective-permute-start(f32[12,64,128]{2,1,0:T(8,128)S(1)} %slice_bitcast_fusion), channel_id=1, source_target_pairs={{0,1},{1,0},{2,3},{3,2},{4,5},{5,4},{6,7},{7,6},{8,9},{9,8},{10,11... | collective-permute-start | bytes 1179656 | tf_op jit(solution)/shard_map/ppermute | solution.py:209
  101.6 4.9 %collective-permute-start.21 = (f32[3,64,128]{2,1,0:T(8,128)S(1)}, f32[3,64,128]{2,1,0:T(8,128)S(1)}, u32[]{:S(2)}, u32[]{:S(2)}) collective-permute-start(f32[3,64,128]{2,1,0:T(8,128)S(1)} %get-tuple-element.31), channel_id=1, source_target_pairs={{0,2},{2,0},{4,6},{6,4},{8,10},{10,8},{12,14},{14,12},{16,18},{18,... | collective-permute-start | bytes 294920 | tf_op jit(solution)/shard_map/ppermute | solution.py:206
  102.9 5.6 %collective-permute-start.22 = (f32[3,64,128]{2,1,0:T(8,128)S(1)}, f32[3,64,128]{2,1,0:T(8,128)S(1)}, u32[]{:S(2)}, u32[]{:S(2)}) collective-permute-start(f32[3,64,128]{2,1,0:T(8,128)S(1)} %get-tuple-element.33), channel_id=1, source_target_pairs={{0,8},{2,10},{4,12},{6,14},{8,0},{10,2},{12,4},{14,6},{16,24},{18,... | collective-permute-start | bytes 294920 | tf_op jit(solution)/shard_map/ppermute | solution.py:206
  102.9 6.8 %collective-permute-start.23 = (f32[3,64,128]{2,1,0:T(8,128)S(1)}, f32[3,64,128]{2,1,0:T(8,128)S(1)}, u32[]{:S(2)}, u32[]{:S(2)}) collective-permute-start(f32[3,64,128]{2,1,0:T(8,128)S(1)} %get-tuple-element.32), channel_id=1, source_target_pairs={{0,10},{2,8},{4,14},{6,12},{8,2},{10,0},{12,6},{14,4},{16,26},{18,... | collective-permute-start | bytes 294920 | tf_op jit(solution)/shard_map/ppermute | solution.py:206
  (8 other events, 8.1 us)

commit v4 on v3

--- a/solution.py
+++ b/solution.py
@@ -11,6 +11,30 @@
 SMEM = pl.BlockSpec(memory_space=pltpu.SMEM)
 VMEM = pl.BlockSpec(memory_space=pltpu.VMEM)
 ANY = pl.BlockSpec(memory_space=pl.ANY)
+
+
+WAITS = {
+    "carry 0": [],
+    "carry 1": [],
+    "piece 2.0": [],
+    "piece 1.0": [],
+    "rest 1": ["carry 0", "piece 1.0"],
+    "rest 2": ["carry 0", "piece 1.0", "carry 1"],
+    "part 3": ["carry 0", "piece 1.0", "carry 1"],
+    "piece 2.1": ["carry 0", "piece 1.0", "carry 1"],
+    "piece 1.1": ["carry 0", "piece 1.0", "carry 1"],
+    "turn 1 0": ["carry 0", "piece 1.0", "carry 1", "piece 2.0"],
+    "piece 2.2": ["carry 0", "piece 1.0", "carry 1", "piece 2.0", "piece 2.1", "part 3"],
+    "piece 3.0": ["carry 0", "piece 1.0", "carry 1", "piece 2.0", "piece 2.1", "part 3"],
+    "rest 3": ["carry 0", "piece 1.0", "carry 1", "piece 2.0", "piece 2.1", "part 3", "turn 1 0", "rest 1", "rest 2"],
+    "piece 1.2": ["carry 0", "piece 1.0", "carry 1", "piece 2.0", "piece 2.1", "part 3", "turn 1 0", "rest 1", "rest 2"],
+    "turn 1 1": ["carry 0", "piece 1.0", "carry 1", "piece 2.0", "piece 2.1", "part 3", "turn 1 0", "rest 1", "rest 2"],
+    "turn 1 2": ["carry 0", "piece 1.0", "carry 1", "piece 2.0", "piece 2.1", "part 3", "turn 1 0", "rest 1", "rest 2"],
+    "piece 3.1": ["carry 0", "piece 1.0", "carry 1", "piece 2.0", "piece 2.1", "part 3", "turn 1 0", "rest 1", "rest 2", "piece 3.0"],
+    "project": ["carry 0", "piece 1.0", "carry 1", "piece 2.0", "piece 2.1", "part 3", "turn 1 0", "rest 1", "rest 2", "piece 3.0"],
+    "piece 3.2": ["carry 0", "piece 1.0", "carry 1", "piece 2.0", "piece 2.1", "part 3", "turn 1 0", "rest 1", "rest 2", "piece 3.0", "piece 1.1", "piece 1.2", "piece 2.2"],
+    "turn 1 3": ["carry 0", "piece 1.0", "carry 1", "piece 2.0", "piece 2.1", "part 3", "turn 1 0", "rest 1", "rest 2", "piece 3.0", "piece 1.1", "piece 1.2", "piece 2.2", "piece 3.2", "project"],
+}
 
 
 def split_bits(points, blocks):
@@ -39,7 +63,7 @@
     first.start()
     copies = []
     for i, source in enumerate(sources):
-        shift, (point, order) = i // len(orders), orders[i % len(orders)]
+        point, shift, order = orders[i]
         place = lax.rem(half + halves - shift, halves)
         for j, other in enumerate(order):
             copies.append(
@@ -93,8 +117,8 @@
     modes, local_rows, slots, size, _ = potential.shape
     bands = sources[0].shape[1]
     rows = local_rows // group
-    points = 1 + max(point for point, _ in orders)
-    count = halves * sum(len(order) for _, order in orders)
+    points = 1 + max(point for point, _, _ in orders)
+    count = sum(len(order) for _, _, order in orders)
     return pl.pallas_call(
         functools.partial(project_kernel, orders, inside, halves),
         out_shape=jax.ShapeDtypeStruct((points * modes, bands, rows * size), jnp.bfloat16),
@@ -213,77 +237,129 @@
         def chunk_for(point):
             return lax.dynamic_slice_in_dim(own, (chunk ^ point) * rows, rows, 0)
 
-        def after(value, *others):
-            return lax.optimization_barrier((value,) + others)[0]
-
-        parts = [chunk_for(0)]
-        parts += [swap(chunk_for(p), spread(p, inside)) for p in range(1, group)]
-        top = 1 << outside[-1]
-        first_far = swap(parts[0], top)
-        second_far = swap(parts[1], top)
-        held = {0: [jnp.concatenate(parts, axis=0)]}
-        for i in reversed(range(len(outside) - 1)):
-            for key, items in list(held.items()):
-                held[key | (1 << i)] = [swap(item, 1 << outside[i]) for item in items]
-        third_far = swap(after(jnp.concatenate(parts[2:], axis=0), first_far), top)
-        far = {1 << (len(outside) - 1): [first_far, second_far, third_far]}
-        for i in reversed(range(len(outside) - 1)):
-            for key, items in list(far.items()):
-                far[key | (1 << i)] = [
-                    swap(after(item, *held[1 << i]), 1 << outside[i]) for item in items
-                ]
-        sets = {**held, **far}
-        sets[0] = parts
-        late = far[max(far)]
-        own_away = [rotate(after(own, parts[1]), shift) for shift in range(1, halves)]
-        chunks = {0: {p: chunk_for(p) for p in range(group)}}
-        near = {}
-        for i in reversed(range(len(inside))):
-            bit = 1 << i
-            for key in list(chunks):
-                order = [p for p in range(group) if p != bit]
-                rest = jnp.concatenate([chunks[key][p] for p in order], axis=0)
-                if key:
-                    rest = after(rest, second_far, *own_away, *near.get(bit, [])[:1])
+        plan = {}
+        done = {}
+
+        def get(name):
+            if name not in done:
+                inputs, combine, move = plan[name]
+                inputs = list(inputs())
+                waits = [done[other] for other in WAITS.get(name, ()) if other in done]
+                if waits:
+                    inputs = lax.optimization_barrier((*inputs, *waits))[: len(inputs)]
+                done[name] = move(combine(inputs))
+            return done[name]
+
+        far = 1 << (len(outside) - 1)
+        pieces = [[0], list(range(1, group - 1)), [group - 1]]
+        orders = {}
+
+        def joined(values):
+            return jnp.concatenate(values, axis=0) if values[1:] else values[0]
+
+        def section(value, at):
+            if value.shape[0] == rows:
+                return value
+            return value[at * rows : (at + 1) * rows]
+
+        def part(j):
+            if j == 0:
+                return chunk_for(0)
+            top = j.bit_length() - 1
+            return section(get(f"carry {top}"), 0) if j == 1 << top else get(f"part {j}")
+
+        def held(key, j):
+            if key == 0:
+                return chunk_for(j)
+            if j in orders[key]:
+                return section(get(f"rest {key}"), orders[key].index(j))
+            return section(get(f"carry {key.bit_length() - 1}"), j) if j else part(key)
+
+        for j in range(1, group):
+            top = j.bit_length() - 1
+            lower = j ^ (1 << top)
+            if lower == 0:
+                plan[f"carry {top}"] = (
+                    lambda j=j: [chunk_for(j + k) for k in range(j)],
+                    joined,
+                    functools.partial(swap, mask=spread(j, inside)),
+                )
+            else:
+                plan[f"part {j}"] = (
+                    lambda top=top, lower=lower: [section(get(f"carry {top}"), lower)],
+                    joined,
+                    functools.partial(swap, mask=spread(lower, inside)),
+                )
+        for key in range(1, 2 * far):
+            bit = key & -key
+            before = key ^ bit
+            for i, js in enumerate(pieces):
+                if before:
+                    source = lambda before=before, i=i: [get(f"piece {before}.{i}")]
                 else:
-                    rest = after(rest, parts[1], first_far)
-                rest = swap(rest, spread(bit, inside))
-                order = [p ^ bit for p in order]
-                near[key | bit] = (rest, order)
-                chunks[key | bit] = {
-                    p: rest[j * rows : (j + 1) * rows] for j, p in enumerate(order)
-                }
-                chunks[key | bit][0] = parts[key | bit]
-
-        def all_rows(keys):
+                    source = lambda js=js: [part(j) for j in js]
+                plan[f"piece {key}.{i}"] = (
+                    source,
+                    joined,
+                    functools.partial(swap, mask=1 << outside[bit.bit_length() - 1]),
+                )
+        for key in sorted(range(1, group), key=lambda k: (bin(k).count("1"), k)):
+            bit = key & -key
+            before = key ^ bit
+            known = 1 if before else bit
+            send = [j for j in range(group) if j ^ bit >= known]
+            orders[key] = [j ^ bit for j in send]
+            plan[f"rest {key}"] = (
+                lambda before=before, send=send: [held(before, j) for j in send],
+                joined,
+                functools.partial(swap, mask=spread(bit, inside)),
+            )
+        def rows_of(key):
+            if key == 0:
+                return [own], [[None] * group]
+            top = key.bit_length() - 1
+            if key == 1 << top:
+                first, order = f"carry {top}", list(range(key))
+            else:
+                first, order = f"part {key}", [0]
+            return [get(first), get(f"rest {key}")], [order, orders[key]]
+
+        for shift in range(1, halves):
+            for key in range(group):
+                plan[f"turn {shift} {key}"] = (
+                    lambda key=key: rows_of(key)[0],
+                    joined,
+                    functools.partial(rotate, shift=shift),
+                )
+
+        def projection(name, keys):
             values = []
-            orders = []
+            places = []
             for place, key in enumerate(keys):
-                if key == 0:
-                    values.append(own)
-                    orders.append((place, [None] * group))
-                else:
-                    values += [parts[key], near[key][0]]
-                    orders += [(place, [0]), (place, near[key][1])]
-            return values, orders
-
-        values, orders = all_rows(range(group - 1))
-        for shift in range(1, halves):
-            moved = [rotate(value, shift) for value in values[1 : len(orders)]]
-            values = values + [own_away[shift - 1]] + moved
-        projected = project(
-            "project", pos, cols, counts, potential, values, orders, inside, halves
+                sources, order = rows_of(key)
+                values += sources
+                places += [(place, 0, js) for js in order]
+                for shift in range(1, halves):
+                    values.append(get(f"turn {shift} {key}"))
+                    places.append((place, shift, sum(order, [])))
+            return project(
+                name, pos, cols, counts, potential, values, places, inside, halves
+            )
+
+        plan["project"] = (
+            lambda: [projection("project", range(group - 1))],
+            joined,
+            lambda value: value,
         )
-        values, orders = all_rows([group - 1])
-        for shift in range(1, halves):
-            values = values + [
-                rotate(after(value, projected, *late[:2]), shift) for value in values[: len(orders)]
-            ]
-        projected_last = project(
-            "project_last", pos, cols, counts, potential, values, orders, inside, halves
-        )
-        count = 1 << len(outside)
-        early = [part for key in range(count - 1) for part in sets[key]]
+        for name in WAITS:
+            if name in plan:
+                get(name)
+        projected = get("project")
+        projected_last = projection("project_last", [group - 1])
+        early = [part(j) for j in range(group)]
+        for key in range(1, 2 * far - 1):
+            early += [get(f"piece {key}.{i}") for i in range(len(pieces))]
+        late = [get(f"piece {2 * far - 1}.{i}") for i in range(len(pieces))]
         total = couple(
             "couple",
             False,
@@ -300,7 +376,7 @@
             True,
             pos,
             pairing,
-            [(projected, count - 1, late, total), (projected_last, 0, early + late, None)],
+            [(projected, 2 * far - 1, late, total), (projected_last, 0, early + late, None)],
             group,
             inside,
             outside,

time: 111 us -> 116 us (1.045)
  other arithmetic: 2.8 us -> 6.32 us
  starting transfers between devices: 20.7 us -> 24.2 us
  waiting for transfers between devices: 58.8 us -> 55.7 us
  local copies, waits for them, and re-layouts: 9.95 us -> 11.4 us
    ppermute x16 -> x18, starting transfers between devices: 19.6 us -> 23.6 us  [swap(): return lax.ppermute(value, 'ka', [(i, i ^ mask) for i in range(points)])]
    concatenate x4 -> x7, other arithmetic: 2 us -> 5.53 us  [joined(): return jnp.concatenate(values, axis=0) if values[1:] else values[0]]
    ppermute x16 -> x18, waiting for transfers between devices: 56.7 us -> 53.9 us  [swap(): return lax.ppermute(value, 'ka', [(i, i ^ mask) for i in range(points)])]
    unnamed x33 -> x50, local copies, waits for them, and re-layouts: 8.27 us -> 9.56 us
  transfers between devices with their start and end apart: 24 -> 23, of which waited for: 13 -> 12; matrix products, arithmetic and copies ran while one was open for 2% -> 3% of each run, Pallas kernels for 12% -> 12%
where the time goes in v4:
time: 116 us
  waiting for transfers between devices  55.7 us (48%)
  starting transfers between devices  24.2 us (21%)
  Pallas kernels  17.8 us (15%)
  local copies, waits for them, and re-layouts  11.4 us (10%)
  other arithmetic  6.32 us (5%)
    ppermute x18, waiting for transfers between devices, swap(): return lax.ppermute(value, 'ka', [(i, i ^ mask) for i in range(points)])  53.9 us
    ppermute x18, starting transfers between devices, swap(): return lax.ppermute(value, 'ka', [(i, i ^ mask) for i in range(points)])  23.6 us
    pallas_call x2, Pallas kernels, project(): pl.pallas_call(functools.partial(project_kernel, orders, inside, halves),...  10.1 us
    unnamed x50, local copies, waits for them, and re-layouts  9.56 us
    pallas_call x2, Pallas kernels, couple(): pl.pallas_call(functools.partial(couple_kernel, jobs, last, inside, outsi...  7.74 us
    concatenate x7, other arithmetic, joined(): return jnp.concatenate(values, axis=0) if values[1:] else values[0]  5.53 us
  transfers between devices with their start and end apart: 23, of which 12 were waited for; matrix products, arithmetic and copies ran while one was open for 3% of the time, Pallas kernels for 12%

profile of v4, /device:TPU:0, one launch (start us, length us, event | category | flops | bytes accessed | tf_op | source)
XLA Modules:
  0.0 115.6 jit_solution(3592020464469420741)
XLA Ops:
  0.0 1.3 %dynamic-slice_bitcast_fusion.1 = (bf16[1024,128]{1,0:T(8,128)(2,1)S(1)}, bf16[1024,128]{1,0:T(8,128)(2,1)S(1)}, bf16[1024,128]{1,0:T(8,128)(2,1)S(1)}, bf16[1024,128]{1,0:T(8,128)(2,1)S(1)}) fusion(bf16[1,4096,128]{2,1,0:T(8,128)(2,1)} %param.6, s32[]{:T(128)S(6)} %select_n.10, s32[]{:T(128)S(6)} %select_n.9, s32[]{:T(128)S(6)} %select_n.8, s32[]{:T(128)S(6)} %select_n.22), kind=kLoop, calls=%fused_computation.11 | loop fusion | bytes 2097168 | tf_op jit(solution)/shard_map/dynamic_slice | solution.py:238
  1.4 3.0 %collective-permute-start = (bf16[1024,128]{1,0:T(8,128)(2,1)S(1)}, bf16[1024,128]{1,0:T(8,128)(2,1)S(1)}, u32[]{:S(2)}, u32[]{:S(2)}) collective-permute-start(bf16[1024,128]{1,0:T(8,128)(2,1)S(1)} %get-tuple-element.37), channel_id=1, source_target_pairs={{0,2},{2,0},{4,6},{6,4},{8,10},{10,8},{12,14},{14,12},{16,18},{18,... | collective-permute-start | bytes 786440 | tf_op jit(solution)/shard_map/ppermute | solution.py:230
  4.4 1.5 %collective-permute-start.1 = (bf16[1024,128]{1,0:T(8,128)(2,1)S(1)}, bf16[1024,128]{1,0:T(8,128)(2,1)S(1)}, u32[]{:S(2)}, u32[]{:S(2)}) collective-permute-start(bf16[1024,128]{1,0:T(8,128)(2,1)S(1)} %get-tuple-element.36.refs_1_.refs_6_), channel_id=1, source_target_pairs={{0,4},{2,6},{4,0},{6,2},{8,12},{10,14},{12,8},{14,10},{16,20},{18,... | collective-permute-start | bytes 786440 | tf_op jit(solution)/shard_map/ppermute | solution.py:230
  5.9 1.6 %collective-permute-start.2 = (bf16[2048,128]{1,0:T(8,128)(2,1)S(1)}, bf16[2048,128]{1,0:T(8,128)(2,1)S(1)}, u32[]{:S(2)}, u32[]{:S(2)}) collective-permute-start(bf16[2048,128]{1,0:T(8,128)(2,1)S(1)} %pad_maximum_fusion.5), channel_id=1, source_target_pairs={{0,8},{2,10},{4,12},{6,14},{8,0},{10,2},{12,4},{14,6},{16,24},{18,... | collective-permute-start | bytes 1572872 | tf_op jit(solution)/shard_map/ppermute | solution.py:230
  7.6 2.6 %collective-permute-start.3 = (bf16[1024,128]{1,0:T(8,128)(2,1)S(1)}, bf16[1024,128]{1,0:T(8,128)(2,1)S(1)}, u32[]{:S(2)}, u32[]{:S(2)}) collective-permute-start(bf16[1024,128]{1,0:T(8,128)(2,1)S(1)} %get-tuple-element.36.refs_1_.refs_6_), channel_id=1, source_target_pairs={{0,16},{2,18},{4,20},{6,22},{8,24},{10,26},{12,28},{14,30},{16,0},... | collective-permute-start | bytes 786440 | tf_op jit(solution)/shard_map/ppermute | solution.py:230
  10.7 1.5 %collective-permute-done.1.refs_5_.refs_10_ = bf16[1024,128]{1,0:T(8,128)(2,1)S(1)} collective-permute-done((bf16[1024,128]{1,0:T(8,128)(2,1)S(1)}, bf16[1024,128]{1,0:T(8,128)(2,1)S(1)}, u32[]{:S(2)}, u32[]{:S(2)}) %collective-permute-start.1) | collective-permute-done | bytes 262176 | tf_op jit(solution)/shard_map/ppermute | solution.py:230
  12.6 11.2 %collective-permute-done.3.refs_8_.refs_13_ = bf16[1024,128]{1,0:T(8,128)(2,1)S(1)} collective-permute-done((bf16[1024,128]{1,0:T(8,128)(2,1)S(1)}, bf16[1024,128]{1,0:T(8,128)(2,1)S(1)}, u32[]{:S(2)}, u32[]{:S(2)}) %collective-permute-start.3) | collective-permute-done | bytes 262176 | tf_op jit(solution)/shard_map/ppermute | solution.py:230
  24.8 2.6 %collective-permute-start.6 = (bf16[2048,128]{1,0:T(8,128)(2,1)S(1)}, bf16[2048,128]{1,0:T(8,128)(2,1)S(1)}, u32[]{:S(2)}, u32[]{:S(2)}) collective-permute-start(bf16[2048,128]{1,0:T(8,128)(2,1)S(1)} %constant_dynamic-update-slice_fusion), channel_id=1, source_target_pairs={{0,16},{2,18},{4,20},{6,22},{8,24},{10,26},{12,28},{14,30},{16,0},... | collective-permute-start | bytes 1572872 | tf_op jit(solution)/shard_map/ppermute | solution.py:230
  27.5 1.7 %collective-permute-start.8 = (bf16[2048,128]{1,0:T(8,128)(2,1)S(1)}, bf16[2048,128]{1,0:T(8,128)(2,1)S(1)}, u32[]{:S(2)}, u32[]{:S(2)}) collective-permute-start(bf16[2048,128]{1,0:T(8,128)(2,1)S(1)} %pad_maximum_fusion.6), channel_id=1, source_target_pairs={{0,8},{2,10},{4,12},{6,14},{8,0},{10,2},{12,4},{14,6},{16,24},{18,... | collective-permute-start | bytes 1572872 | tf_op jit(solution)/shard_map/ppermute | solution.py:230
  29.7 7.6 %collective-permute-done.7.refs_4_.refs_0_.refs_9_ = bf16[1024,128]{1,0:T(8,128)(2,1)S(1)} collective-permute-done((bf16[1024,128]{1,0:T(8,128)(2,1)S(1)}, bf16[1024,128]{1,0:T(8,128)(2,1)S(1)}, u32[]{:S(2)}, u32[]{:S(2)}) %collective-permute-start.7) | collective-permute-done | bytes 262176 | tf_op jit(solution)/shard_map/ppermute | solution.py:230
  37.8 13.5 %collective-permute-done.6.refs_9_.refs_14_ = bf16[2048,128]{1,0:T(8,128)(2,1)S(1)} collective-permute-done((bf16[2048,128]{1,0:T(8,128)(2,1)S(1)}, bf16[2048,128]{1,0:T(8,128)(2,1)S(1)}, u32[]{:S(2)}, u32[]{:S(2)}) %collective-permute-start.6) | collective-permute-done | bytes 524320 | tf_op jit(solution)/shard_map/ppermute | solution.py:230
  52.2 1.0 copy-done.10
  53.2 1.1 pad_maximum_fusion
  54.3 1.1 pad_maximum_fusion.1
  55.9 1.0 pad_maximum_fusion.4
  58.2 2.0 %collective-permute-start.13 = (bf16[1024,128]{1,0:T(8,128)(2,1)S(1)}, bf16[1024,128]{1,0:T(8,128)(2,1)}, u32[]{:S(2)}, u32[]{:S(2)}) collective-permute-start(bf16[1024,128]{1,0:T(8,128)(2,1)S(1)} %collective-permute-done.7.refs_4_.refs_0_.refs_9_), channel_id=1, source_target_pairs={{0,16},{2,18},{4,20},{6,22},{8,24},{10,26},{12,28},{14,30},{16,0},... | collective-permute-start | bytes 786440 | tf_op jit(solution)/shard_map/ppermute | solution.py:230
  61.4 11.4 %collective-permute-done.13.refs_10_.refs_15_ = bf16[1024,128]{1,0:T(8,128)(2,1)} collective-permute-done((bf16[1024,128]{1,0:T(8,128)(2,1)S(1)}, bf16[1024,128]{1,0:T(8,128)(2,1)}, u32[]{:S(2)}, u32[]{:S(2)}) %collective-permute-start.13) | collective-permute-done | bytes 262176 | tf_op jit(solution)/shard_map/ppermute | solution.py:230
  73.5 1.3 %collective-permute-start.16 = (bf16[1024,128]{1,0:T(8,128)(2,1)}, bf16[1024,128]{1,0:T(8,128)(2,1)}, u32[]{:S(2)}, u32[]{:S(2)}) collective-permute-start(bf16[1024,128]{1,0:T(8,128)(2,1)} %collective-permute-done.13.refs_10_.refs_15_), channel_id=1, source_target_pairs={{0,4},{2,6},{4,0},{6,2},{8,12},{10,14},{12,8},{14,10},{16,20},{18,... | collective-permute-start | bytes 786440 | tf_op jit(solution)/shard_map/ppermute | solution.py:230
  75.2 1.1 copy-done.3
  76.4 1.2 %copy-done.11 = bf16[4096,128]{1,0:T(8,128)(2,1)S(1)} copy-done((bf16[4096,128]{1,0:T(8,128)(2,1)S(1)}, bf16[4096,128]{1,0:T(8,128)(2,1)}, u32[]{:S(2)}) %copy-start.11) | copy-done | bytes 1048600
  77.6 6.3 %project.1.refs_0_ = bf16[9,128,1024]{2,1,0:T(8,128)(2,1)} custom-call(s32[2]{0:T(128)S(1)} %pad_add_fusion.pos, s32[288]{0:T(512)S(1)} %reshape.23.cols, s32[96]{0:T(128)S(1)} %reshape.24.counts, bf16[3,32,3,128,128]{4,3,2,1,0:T(8,128)(2,1)} %potential.3, bf16[4096,128]{1,0:T(8,128)(2,1)S(1)} %bitcast.28, bf16[4096,128]{1,0:T(8,128)(2,1)S(1)} %copy-done.11, ...), custom_call_target="tpu_custom_call" | custom-call | tf_op jit(solution)/shard_map/project/pallas_call | solution.py:122
  84.0 2.3 %pad_maximum_fusion.2 = bf16[4096,128]{1,0:T(8,128)(2,1)} fusion(bf16[3072,128]{1,0:T(8,128)(2,1)} %collective-permute-done.17.refs_1_, bf16[1024,128]{1,0:T(8,128)(2,1)S(1)} %collective-permute-done.7.refs_4_.refs_0_.refs_9_), kind=kLoop, calls=%fused_computation.2 | loop fusion | flops 2097152 | bytes 2097152 | tf_op jit(solution)/shard_map/concatenate | solution.py:258
  87.1 1.7 %copy-done = bf16[9,128,1024]{2,1,0:T(8,128)(2,1)S(1)} copy-done((bf16[9,128,1024]{2,1,0:T(8,128)(2,1)S(1)}, bf16[9,128,1024]{2,1,0:T(8,128)(2,1)}, u32[]{:S(2)}) %copy-start) | copy-done | bytes 2359320
  88.7 0.9 copy-done.18
  89.7 3.3 %couple.1.refs_4_ = f32[9,128,128]{2,1,0:T(8,128)S(1)} custom-call(s32[2]{0:T(128)S(1)} %pad_add_fusion.pos, s32[48]{0:T(128)S(1)} %reshape.22.partners, bf16[9,128,1024]{2,1,0:T(8,128)(2,1)S(1)} %copy-done, bf16[1024,128]{1,0:T(8,128)(2,1)S(1)} %get-tuple-element.36.refs_1_.refs_6_, bf16[1024,128]{1,0:T(8,128)(2,1)S(1)} %collective-permute-done.refs_2_.refs_7_, ...), custom_call_target="tpu_custom_call" | custom-call | tf_op jit(solution)/shard_map/couple/pallas_call | solution.py:200
  93.1 3.8 %project_last.1.refs_5_ = bf16[3,128,1024]{2,1,0:T(8,128)(2,1)S(1)} custom-call(s32[2]{0:T(128)S(1)} %pad_add_fusion.pos, s32[288]{0:T(512)S(1)} %reshape.23.cols, s32[96]{0:T(128)S(1)} %reshape.24.counts, bf16[3,32,3,128,128]{4,3,2,1,0:T(8,128)(2,1)} %potential.3, bf16[1024,128]{1,0:T(8,128)(2,1)S(1)} %collective-permute-done.7.refs_4_.refs_0_.refs_9_, ...), custom_call_target="tpu_custom_call" | custom-call | tf_op jit(solution)/shard_map/project_last/pallas_call | solution.py:122
  97.7 3.0 %collective-permute-done.12.refs_2_.refs_17_ = bf16[2048,128]{1,0:T(8,128)(2,1)} collective-permute-done((bf16[2048,128]{1,0:T(8,128)(2,1)S(1)}, bf16[2048,128]{1,0:T(8,128)(2,1)}, u32[]{:S(2)}, u32[]{:S(2)}) %collective-permute-start.12) | collective-permute-done | bytes 524320 | tf_op jit(solution)/shard_map/ppermute | solution.py:230
  100.7 4.4 %couple_last.1 = f32[2,12,64,128]{3,2,1,0:T(8,128)S(1)} custom-call(s32[2]{0:T(128)S(1)} %pad_add_fusion.pos, s32[48]{0:T(128)S(1)} %reshape.22.partners, bf16[9,128,1024]{2,1,0:T(8,128)(2,1)} %project.1.refs_0_, bf16[1024,128]{1,0:T(8,128)(2,1)S(1)} %copy-done.16, bf16[2048,128]{1,0:T(8,128)(2,1)} %collective-permute-done.12.refs_2_.refs_17_, ...), custom_call_target="tpu_custom_call" | custom-call | tf_op jit(solution)/shard_map/couple_last/pallas_call | solution.py:200
  105.3 1.7 %collective-permute-done.19 = f32[12,64,128]{2,1,0:T(8,128)S(1)} collective-permute-done((f32[12,64,128]{2,1,0:T(8,128)S(1)}, f32[12,64,128]{2,1,0:T(8,128)S(1)}, u32[]{:S(2)}, u32[]{:S(2)}) %collective-permute-start.19) | collective-permute-done | bytes 393248 | tf_op jit(solution)/shard_map/ppermute | solution.py:233
  107.4 2.5 %collective-permute-start.21 = (f32[3,64,128]{2,1,0:T(8,128)S(1)}, f32[3,64,128]{2,1,0:T(8,128)S(1)}, u32[]{:S(2)}, u32[]{:S(2)}) collective-permute-start(f32[3,64,128]{2,1,0:T(8,128)S(1)} %get-tuple-element.63), channel_id=1, source_target_pairs={{0,8},{2,10},{4,12},{6,14},{8,0},{10,2},{12,4},{14,6},{16,24},{18,... | collective-permute-start | bytes 294920 | tf_op jit(solution)/shard_map/ppermute | solution.py:230
  110.6 3.0 %collective-permute-done.22 = f32[3,64,128]{2,1,0:T(8,128)S(1)} collective-permute-done((f32[3,64,128]{2,1,0:T(8,128)S(1)}, f32[3,64,128]{2,1,0:T(8,128)S(1)}, u32[]{:S(2)}, u32[]{:S(2)}) %collective-permute-start.22) | collective-permute-done | bytes 98336 | tf_op jit(solution)/shard_map/ppermute | solution.py:230
  113.7 1.1 collective-permute-done.21
  (87 shorter events, 12.0 us)
Async XLA Ops:
  0.0 24.7 %copy-start.1 = (bf16[1,4096,128]{2,1,0:T(8,128)(2,1)S(1)}, bf16[1,4096,128]{2,1,0:T(8,128)(2,1)}, u32[]{:S(2)}) copy-start(bf16[1,4096,128]{2,1,0:T(8,128)(2,1)} %param.6) | copy-start | bytes 3145732
  1.4 9.3 %collective-permute-start = (bf16[1024,128]{1,0:T(8,128)(2,1)S(1)}, bf16[1024,128]{1,0:T(8,128)(2,1)S(1)}, u32[]{:S(2)}, u32[]{:S(2)}) collective-permute-start(bf16[1024,128]{1,0:T(8,128)(2,1)S(1)} %get-tuple-element.37), channel_id=1, source_target_pairs={{0,2},{2,0},{4,6},{6,4},{8,10},{10,8},{12,14},{14,12},{16,18},{18,... | collective-permute-start | bytes 786440 | tf_op jit(solution)/shard_map/ppermute | solution.py:230
  4.4 7.8 %collective-permute-start.1 = (bf16[1024,128]{1,0:T(8,128)(2,1)S(1)}, bf16[1024,128]{1,0:T(8,128)(2,1)S(1)}, u32[]{:S(2)}, u32[]{:S(2)}) collective-permute-start(bf16[1024,128]{1,0:T(8,128)(2,1)S(1)} %get-tuple-element.36.refs_1_.refs_6_), channel_id=1, source_target_pairs={{0,4},{2,6},{4,0},{6,2},{8,12},{10,14},{12,8},{14,10},{16,20},{18,... | collective-permute-start | bytes 786440 | tf_op jit(solution)/shard_map/ppermute | solution.py:230
  5.9 18.8 %collective-permute-start.2 = (bf16[2048,128]{1,0:T(8,128)(2,1)S(1)}, bf16[2048,128]{1,0:T(8,128)(2,1)S(1)}, u32[]{:S(2)}, u32[]{:S(2)}) collective-permute-start(bf16[2048,128]{1,0:T(8,128)(2,1)S(1)} %pad_maximum_fusion.5), channel_id=1, source_target_pairs={{0,8},{2,10},{4,12},{6,14},{8,0},{10,2},{12,4},{14,6},{16,24},{18,... | collective-permute-start | bytes 1572872 | tf_op jit(solution)/shard_map/ppermute | solution.py:230
  7.6 16.2 %collective-permute-start.3 = (bf16[1024,128]{1,0:T(8,128)(2,1)S(1)}, bf16[1024,128]{1,0:T(8,128)(2,1)S(1)}, u32[]{:S(2)}, u32[]{:S(2)}) collective-permute-start(bf16[1024,128]{1,0:T(8,128)(2,1)S(1)} %get-tuple-element.36.refs_1_.refs_6_), channel_id=1, source_target_pairs={{0,16},{2,18},{4,20},{6,22},{8,24},{10,26},{12,28},{14,30},{16,0},... | collective-permute-start | bytes 786440 | tf_op jit(solution)/shard_map/ppermute | solution.py:230
  12.2 39.7 %collective-permute-start.5 = (bf16[3072,128]{1,0:T(8,128)(2,1)S(1)}, bf16[3072,128]{1,0:T(8,128)(2,1)S(1)}, u32[]{:S(2)}, u32[]{:S(2)}) collective-permute-start(bf16[3072,128]{1,0:T(8,128)(2,1)S(1)} %pad_maximum_fusion.3), channel_id=1, source_target_pairs={{0,2},{2,0},{4,6},{6,4},{8,10},{10,8},{12,14},{14,12},{16,18},{18,... | collective-permute-start | bytes 2359304 | tf_op jit(solution)/shard_map/ppermute | solution.py:230
  23.8 28.1 %copy-start.12 = (bf16[1024,128]{1,0:T(8,128)(2,1)}, bf16[1024,128]{1,0:T(8,128)(2,1)S(1)}, u32[]{:S(2)}) copy-start(bf16[1024,128]{1,0:T(8,128)(2,1)S(1)} %collective-permute-done.3.refs_8_.refs_13_) | copy-start | bytes 786436
  24.7 27.5 %collective-permute-start.4 = (bf16[4096,128]{1,0:T(8,128)(2,1)S(1)}, bf16[4096,128]{1,0:T(8,128)(2,1)S(1)}, u32[]{:S(2)}, u32[]{:S(2)}) collective-permute-start(bf16[4096,128]{1,0:T(8,128)(2,1)S(1)} %bitcast.27), channel_id=1, source_target_pairs={{0,1},{1,0},{2,3},{3,2},{4,5},{5,4},{6,7},{7,6},{8,9},{9,8},{10,11... | collective-permute-start | bytes 3145736 | tf_op jit(solution)/shard_map/ppermute | solution.py:233
  24.8 26.5 %collective-permute-start.6 = (bf16[2048,128]{1,0:T(8,128)(2,1)S(1)}, bf16[2048,128]{1,0:T(8,128)(2,1)S(1)}, u32[]{:S(2)}, u32[]{:S(2)}) collective-permute-start(bf16[2048,128]{1,0:T(8,128)(2,1)S(1)} %constant_dynamic-update-slice_fusion), channel_id=1, source_target_pairs={{0,16},{2,18},{4,20},{6,22},{8,24},{10,26},{12,28},{14,30},{16,0},... | collective-permute-start | bytes 1572872 | tf_op jit(solution)/shard_map/ppermute | solution.py:230
  27.5 24.4 %collective-permute-start.8 = (bf16[2048,128]{1,0:T(8,128)(2,1)S(1)}, bf16[2048,128]{1,0:T(8,128)(2,1)S(1)}, u32[]{:S(2)}, u32[]{:S(2)}) collective-permute-start(bf16[2048,128]{1,0:T(8,128)(2,1)S(1)} %pad_maximum_fusion.6), channel_id=1, source_target_pairs={{0,8},{2,10},{4,12},{6,14},{8,0},{10,2},{12,4},{14,6},{16,24},{18,... | collective-permute-start | bytes 1572872 | tf_op jit(solution)/shard_map/ppermute | solution.py:230
  29.2 8.2 %collective-permute-start.7 = (bf16[1024,128]{1,0:T(8,128)(2,1)S(1)}, bf16[1024,128]{1,0:T(8,128)(2,1)S(1)}, u32[]{:S(2)}, u32[]{:S(2)}) collective-permute-start(bf16[1024,128]{1,0:T(8,128)(2,1)S(1)} %get-tuple-element.35), channel_id=1, source_target_pairs={{0,2},{2,0},{4,6},{6,4},{8,10},{10,8},{12,14},{14,12},{16,18},{18,... | collective-permute-start | bytes 786440 | tf_op jit(solution)/shard_map/ppermute | solution.py:230
  37.3 20.1 %collective-permute-start.14 = (bf16[2048,128]{1,0:T(8,128)(2,1)S(1)}, bf16[2048,128]{1,0:T(8,128)(2,1)S(1)}, u32[]{:S(2)}, u32[]{:S(2)}) collective-permute-start(bf16[2048,128]{1,0:T(8,128)(2,1)S(1)} %constant_dynamic-update-slice_fusion), channel_id=1, source_target_pairs={{0,4},{2,6},{4,0},{6,2},{8,12},{10,14},{12,8},{14,10},{16,20},{18,... | collective-permute-start | bytes 1572872 | tf_op jit(solution)/shard_map/ppermute | solution.py:230
  51.4 8.8 %collective-permute-start.11 = (bf16[1024,128]{1,0:T(8,128)(2,1)S(1)}, bf16[1024,128]{1,0:T(8,128)(2,1)S(1)}, u32[]{:S(2)}, u32[]{:S(2)}) collective-permute-start(bf16[1024,128]{1,0:T(8,128)(2,1)S(1)} %collective-permute-done.3.refs_8_.refs_13_), channel_id=1, source_target_pairs={{0,4},{2,6},{4,0},{6,2},{8,12},{10,14},{12,8},{14,10},{16,20},{18,... | collective-permute-start | bytes 786440 | tf_op jit(solution)/shard_map/ppermute | solution.py:230
  54.3 20.5 %copy-start.21 = (s32[3,32,3]{1,2,0:T(4,128)S(1)}, s32[3,32,3]{1,2,0:T(4,128)}, u32[]{:S(2)}) copy-start(s32[3,32,3]{1,2,0:T(4,128)} %param.8) | copy-start | bytes 3460
  54.3 20.8 %copy-start.22 = (s32[3,32]{1,0:T(4,128)S(1)}, s32[3,32]{1,0:T(4,128)}, u32[]{:S(2)}) copy-start(s32[3,32]{1,0:T(4,128)} %param.9) | copy-start | bytes 1156
  54.3 20.9 %collective-permute-start.9 = (bf16[4096,128]{1,0:T(8,128)(2,1)}, bf16[4096,128]{1,0:T(8,128)(2,1)}, u32[]{:S(2)}, u32[]{:S(2)}) collective-permute-start(bf16[4096,128]{1,0:T(8,128)(2,1)} %pad_maximum_fusion), channel_id=1, source_target_pairs={{0,1},{1,0},{2,3},{3,2},{4,5},{5,4},{6,7},{7,6},{8,9},{9,8},{10,11... | collective-permute-start | bytes 3145736 | tf_op jit(solution)/shard_map/ppermute | solution.py:233
  55.4 19.9 %collective-permute-start.10 = (bf16[4096,128]{1,0:T(8,128)(2,1)}, bf16[4096,128]{1,0:T(8,128)(2,1)}, u32[]{:S(2)}, u32[]{:S(2)}) collective-permute-start(bf16[4096,128]{1,0:T(8,128)(2,1)} %pad_maximum_fusion.1), channel_id=1, source_target_pairs={{0,1},{1,0},{2,3},{3,2},{4,5},{5,4},{6,7},{7,6},{8,9},{9,8},{10,11... | collective-permute-start | bytes 3145736 | tf_op jit(solution)/shard_map/ppermute | solution.py:233
  56.9 27.1 %collective-permute-start.17 = (bf16[3072,128]{1,0:T(8,128)(2,1)}, bf16[3072,128]{1,0:T(8,128)(2,1)}, u32[]{:S(2)}, u32[]{:S(2)}) collective-permute-start(bf16[3072,128]{1,0:T(8,128)(2,1)} %pad_maximum_fusion.4), channel_id=1, source_target_pairs={{0,2},{2,0},{4,6},{6,4},{8,10},{10,8},{12,14},{14,12},{16,18},{18,... | collective-permute-start | bytes 2359304 | tf_op jit(solution)/shard_map/ppermute | solution.py:230
  58.2 14.6 %collective-permute-start.13 = (bf16[1024,128]{1,0:T(8,128)(2,1)S(1)}, bf16[1024,128]{1,0:T(8,128)(2,1)}, u32[]{:S(2)}, u32[]{:S(2)}) collective-permute-start(bf16[1024,128]{1,0:T(8,128)(2,1)S(1)} %collective-permute-done.7.refs_4_.refs_0_.refs_9_), channel_id=1, source_target_pairs={{0,16},{2,18},{4,20},{6,22},{8,24},{10,26},{12,28},{14,30},{16,0},... | collective-permute-start | bytes 786440 | tf_op jit(solution)/shard_map/ppermute | solution.py:230
  60.9 11.9 %collective-permute-start.15 = (bf16[1024,128]{1,0:T(8,128)(2,1)S(1)}, bf16[1024,128]{1,0:T(8,128)(2,1)S(1)}, u32[]{:S(2)}, u32[]{:S(2)}) collective-permute-start(bf16[1024,128]{1,0:T(8,128)(2,1)S(1)} %collective-permute-done.7.refs_4_.refs_0_.refs_9_), channel_id=1, source_target_pairs={{0,4},{2,6},{4,0},{6,2},{8,12},{10,14},{12,8},{14,10},{16,20},{18,... | collective-permute-start | bytes 786440 | tf_op jit(solution)/shard_map/ppermute | solution.py:230
  73.5 10.4 %collective-permute-start.16 = (bf16[1024,128]{1,0:T(8,128)(2,1)}, bf16[1024,128]{1,0:T(8,128)(2,1)}, u32[]{:S(2)}, u32[]{:S(2)}) collective-permute-start(bf16[1024,128]{1,0:T(8,128)(2,1)} %collective-permute-done.13.refs_10_.refs_15_), channel_id=1, source_target_pairs={{0,4},{2,6},{4,0},{6,2},{8,12},{10,14},{12,8},{14,10},{16,20},{18,... | collective-permute-start | bytes 786440 | tf_op jit(solution)/shard_map/ppermute | solution.py:230
  86.2 6.8 %collective-permute-start.18 = (bf16[4096,128]{1,0:T(8,128)(2,1)}, bf16[4096,128]{1,0:T(8,128)(2,1)}, u32[]{:S(2)}, u32[]{:S(2)}) collective-permute-start(bf16[4096,128]{1,0:T(8,128)(2,1)} %pad_maximum_fusion.2), channel_id=1, source_target_pairs={{0,1},{1,0},{2,3},{3,2},{4,5},{5,4},{6,7},{7,6},{8,9},{9,8},{10,11... | collective-permute-start | bytes 3145736 | tf_op jit(solution)/shard_map/ppermute | solution.py:233
  86.2 14.4 %collective-permute-start.12 = (bf16[2048,128]{1,0:T(8,128)(2,1)S(1)}, bf16[2048,128]{1,0:T(8,128)(2,1)}, u32[]{:S(2)}, u32[]{:S(2)}) collective-permute-start(bf16[2048,128]{1,0:T(8,128)(2,1)S(1)} %copy-done.6), channel_id=1, source_target_pairs={{0,4},{2,6},{4,0},{6,2},{8,12},{10,14},{12,8},{14,10},{16,20},{18,... | collective-permute-start | bytes 1572872 | tf_op jit(solution)/shard_map/ppermute | solution.py:230
  93.0 7.7 %copy-start.9 = (bf16[2048,128]{1,0:T(8,128)(2,1)S(1)}, bf16[2048,128]{1,0:T(8,128)(2,1)}, u32[]{:S(2)}) copy-start(bf16[2048,128]{1,0:T(8,128)(2,1)} %copy-done.7) | copy-start | bytes 1572868
  93.0 7.7 %copy-start.14 = (bf16[1024,128]{1,0:T(8,128)(2,1)S(1)}, bf16[1024,128]{1,0:T(8,128)(2,1)}, u32[]{:S(2)}) copy-start(bf16[1024,128]{1,0:T(8,128)(2,1)} %copy-done.12) | copy-start | bytes 786436
  93.0 7.7 %copy-start.16 = (bf16[1024,128]{1,0:T(8,128)(2,1)S(1)}, bf16[1024,128]{1,0:T(8,128)(2,1)}, u32[]{:S(2)}) copy-start(bf16[1024,128]{1,0:T(8,128)(2,1)} %copy-done.15) | copy-start | bytes 786436
  93.0 7.7 %copy-start.19 = (bf16[1024,128]{1,0:T(8,128)(2,1)S(1)}, bf16[1024,128]{1,0:T(8,128)(2,1)}, u32[]{:S(2)}) copy-start(bf16[1024,128]{1,0:T(8,128)(2,1)} %copy-done.17) | copy-start | bytes 786436
  105.1 9.8 %copy-start.20 = (f32[3,1,64,128]{3,2,1,0:T(8,128)S(1)}, f32[3,1,64,128]{3,2,1,0:T(8,128)}, u32[]{:S(2)}) copy-start(f32[3,1,64,128]{3,2,1,0:T(8,128)} %param.11) | copy-start | bytes 294916
  105.2 1.8 %collective-permute-start.19 = (f32[12,64,128]{2,1,0:T(8,128)S(1)}, f32[12,64,128]{2,1,0:T(8,128)S(1)}, u32[]{:S(2)}, u32[]{:S(2)}) collective-permute-start(f32[12,64,128]{2,1,0:T(8,128)S(1)} %slice_bitcast_fusion), channel_id=1, source_target_pairs={{0,1},{1,0},{2,3},{3,2},{4,5},{5,4},{6,7},{7,6},{8,9},{9,8},{10,11... | collective-permute-start | bytes 1179656 | tf_op jit(solution)/shard_map/ppermute | solution.py:233
  107.1 6.6 %collective-permute-start.22 = (f32[3,64,128]{2,1,0:T(8,128)S(1)}, f32[3,64,128]{2,1,0:T(8,128)S(1)}, u32[]{:S(2)}, u32[]{:S(2)}) collective-permute-start(f32[3,64,128]{2,1,0:T(8,128)S(1)} %get-tuple-element.62), channel_id=1, source_target_pairs={{0,10},{2,8},{4,14},{6,12},{8,2},{10,0},{12,6},{14,4},{16,26},{18,... | collective-permute-start | bytes 294920 | tf_op jit(solution)/shard_map/ppermute | solution.py:230
  107.4 7.4 %collective-permute-start.21 = (f32[3,64,128]{2,1,0:T(8,128)S(1)}, f32[3,64,128]{2,1,0:T(8,128)S(1)}, u32[]{:S(2)}, u32[]{:S(2)}) collective-permute-start(f32[3,64,128]{2,1,0:T(8,128)S(1)} %get-tuple-element.63), channel_id=1, source_target_pairs={{0,8},{2,10},{4,12},{6,14},{8,0},{10,2},{12,4},{14,6},{16,24},{18,... | collective-permute-start | bytes 294920 | tf_op jit(solution)/shard_map/ppermute | solution.py:230
  109.9 5.1 %collective-permute-start.20 = (f32[3,64,128]{2,1,0:T(8,128)S(1)}, f32[3,64,128]{2,1,0:T(8,128)S(1)}, u32[]{:S(2)}, u32[]{:S(2)}) collective-permute-start(f32[3,64,128]{2,1,0:T(8,128)S(1)} %get-tuple-element.61), channel_id=1, source_target_pairs={{0,2},{2,0},{4,6},{6,4},{8,10},{10,8},{12,14},{14,12},{16,18},{18,... | collective-permute-start | bytes 294920 | tf_op jit(solution)/shard_map/ppermute | solution.py:230
  (15 other events, 25.4 us)

commit v5 on v4

--- a/solution.py
+++ b/solution.py
@@ -7,33 +7,22 @@
 from jax.experimental.pallas import tpu as pltpu
 from jax.sharding import PartitionSpec as P
 
-VMEM_LIMIT = 48 * 2**20
+SPARE_VMEM = 6 * 2**20
 SMEM = pl.BlockSpec(memory_space=pltpu.SMEM)
 VMEM = pl.BlockSpec(memory_space=pltpu.VMEM)
 ANY = pl.BlockSpec(memory_space=pl.ANY)
 
 
+FIRST = ("c0", "c1", "s1.0")
+SECOND = ("p3", "r1", "r2", "s2.1", "s1.1", "s3.0")
 WAITS = {
-    "carry 0": [],
-    "carry 1": [],
-    "piece 2.0": [],
-    "piece 1.0": [],
-    "rest 1": ["carry 0", "piece 1.0"],
-    "rest 2": ["carry 0", "piece 1.0", "carry 1"],
-    "part 3": ["carry 0", "piece 1.0", "carry 1"],
-    "piece 2.1": ["carry 0", "piece 1.0", "carry 1"],
-    "piece 1.1": ["carry 0", "piece 1.0", "carry 1"],
-    "turn 1 0": ["carry 0", "piece 1.0", "carry 1", "piece 2.0"],
-    "piece 2.2": ["carry 0", "piece 1.0", "carry 1", "piece 2.0", "piece 2.1", "part 3"],
-    "piece 3.0": ["carry 0", "piece 1.0", "carry 1", "piece 2.0", "piece 2.1", "part 3"],
-    "rest 3": ["carry 0", "piece 1.0", "carry 1", "piece 2.0", "piece 2.1", "part 3", "turn 1 0", "rest 1", "rest 2"],
-    "piece 1.2": ["carry 0", "piece 1.0", "carry 1", "piece 2.0", "piece 2.1", "part 3", "turn 1 0", "rest 1", "rest 2"],
-    "turn 1 1": ["carry 0", "piece 1.0", "carry 1", "piece 2.0", "piece 2.1", "part 3", "turn 1 0", "rest 1", "rest 2"],
-    "turn 1 2": ["carry 0", "piece 1.0", "carry 1", "piece 2.0", "piece 2.1", "part 3", "turn 1 0", "rest 1", "rest 2"],
-    "piece 3.1": ["carry 0", "piece 1.0", "carry 1", "piece 2.0", "piece 2.1", "part 3", "turn 1 0", "rest 1", "rest 2", "piece 3.0"],
-    "project": ["carry 0", "piece 1.0", "carry 1", "piece 2.0", "piece 2.1", "part 3", "turn 1 0", "rest 1", "rest 2", "piece 3.0"],
-    "piece 3.2": ["carry 0", "piece 1.0", "carry 1", "piece 2.0", "piece 2.1", "part 3", "turn 1 0", "rest 1", "rest 2", "piece 3.0", "piece 1.1", "piece 1.2", "piece 2.2"],
-    "turn 1 3": ["carry 0", "piece 1.0", "carry 1", "piece 2.0", "piece 2.1", "part 3", "turn 1 0", "rest 1", "rest 2", "piece 3.0", "piece 1.1", "piece 1.2", "piece 2.2", "piece 3.2", "project"],
+    **dict.fromkeys(FIRST, ()),
+    "r1": ("c0", "s1.0"),
+    **dict.fromkeys(("p3", "r2", "s2.1", "s1.1"), FIRST),
+    "s3.0": ("p3",),
+    **dict.fromkeys(("r3", "s2.2", "s3.1", "s1.2", "t1c0", "t1c1", "t1r1", "t1r2", "t1p3"), SECOND),
+    "q": (),
+    "t1r3": ("q", "s2.2", "s3.1", "s1.2"),
 }
 
 
@@ -119,6 +108,8 @@
     rows = local_rows // group
     points = 1 + max(point for point, _, _ in orders)
     count = sum(len(order) for _, _, order in orders)
+    held = 2 * size * (points * halves * local_rows * bands + modes * rows * slots * size)
+    made = 2 * points * modes * bands * rows * size
     return pl.pallas_call(
         functools.partial(project_kernel, orders, inside, halves),
         out_shape=jax.ShapeDtypeStruct((points * modes, bands, rows * size), jnp.bfloat16),
@@ -130,7 +121,7 @@
             pltpu.SemaphoreType.DMA,
             pltpu.SemaphoreType.DMA((count,)),
         ],
-        compiler_params=pltpu.CompilerParams(vmem_limit_bytes=VMEM_LIMIT),
+        compiler_params=pltpu.CompilerParams(vmem_limit_bytes=held + made + SPARE_VMEM),
         cost_estimate=pl.CostEstimate(flops=0, bytes_accessed=0, transcendentals=0),
         name=name,
     )(pos, cols, counts, potential, *sources)
@@ -197,13 +188,15 @@
         start += pairs
     total = start if last else (start // (group - 1)) * group if group > 1 else start
     shape = (halves, start, bands // halves, bands) if last else (start, bands, bands)
+    held = sum(value.size * value.dtype.itemsize for value in values)
+    held += 4 * (total + start) * bands * bands
     return pl.pallas_call(
         functools.partial(couple_kernel, jobs, last, inside, outside, halves),
         out_shape=jax.ShapeDtypeStruct(shape, jnp.float32),
         in_specs=[SMEM, SMEM] + [VMEM] * len(values),
         out_specs=VMEM,
         scratch_shapes=[pltpu.VMEM((total, bands, bands), jnp.float32)],
-        compiler_params=pltpu.CompilerParams(vmem_limit_bytes=VMEM_LIMIT),
+        compiler_params=pltpu.CompilerParams(vmem_limit_bytes=held + SPARE_VMEM),
         cost_estimate=pl.CostEstimate(flops=0, bytes_accessed=0, transcendentals=0),
         name=name,
     )(pos, partners, *values)
@@ -251,7 +244,8 @@
             return done[name]
 
         far = 1 << (len(outside) - 1)
-        pieces = [[0], list(range(1, group - 1)), [group - 1]]
+        pieces = {0: [[0], list(range(1, group - 1)), [group - 1]], far: [[0], list(range(1, group - 1)), [group - 1]]}
+        sizes = {}
         orders = {}
 
         def joined(values):
@@ -266,39 +260,40 @@
             if j == 0:
                 return chunk_for(0)
             top = j.bit_length() - 1
-            return section(get(f"carry {top}"), 0) if j == 1 << top else get(f"part {j}")
+            return section(get(f"c{top}"), 0) if j == 1 << top else get(f"p{j}")
 
         def held(key, j):
             if key == 0:
                 return chunk_for(j)
             if j in orders[key]:
-                return section(get(f"rest {key}"), orders[key].index(j))
-            return section(get(f"carry {key.bit_length() - 1}"), j) if j else part(key)
+                return section(get(f"r{key}"), orders[key].index(j))
+            return section(get(f"c{key.bit_length() - 1}"), j) if j else part(key)
 
         for j in range(1, group):
             top = j.bit_length() - 1
             lower = j ^ (1 << top)
             if lower == 0:
-                plan[f"carry {top}"] = (
+                plan[f"c{top}"] = (
                     lambda j=j: [chunk_for(j + k) for k in range(j)],
                     joined,
                     functools.partial(swap, mask=spread(j, inside)),
                 )
             else:
-                plan[f"part {j}"] = (
-                    lambda top=top, lower=lower: [section(get(f"carry {top}"), lower)],
+                plan[f"p{j}"] = (
+                    lambda top=top, lower=lower: [section(get(f"c{top}"), lower)],
                     joined,
                     functools.partial(swap, mask=spread(lower, inside)),
                 )
         for key in range(1, 2 * far):
             bit = key & -key
             before = key ^ bit
-            for i, js in enumerate(pieces):
+            sizes[key] = pieces[far if key >= far else 0]
+            for i, js in enumerate(sizes[key]):
                 if before:
-                    source = lambda before=before, i=i: [get(f"piece {before}.{i}")]
+                    source = lambda before=before, i=i: [get(f"s{before}.{i}")]
                 else:
                     source = lambda js=js: [part(j) for j in js]
-                plan[f"piece {key}.{i}"] = (
+                plan[f"s{key}.{i}"] = (
                     source,
                     joined,
                     functools.partial(swap, mask=1 << outside[bit.bit_length() - 1]),
@@ -309,44 +304,42 @@
             known = 1 if before else bit
             send = [j for j in range(group) if j ^ bit >= known]
             orders[key] = [j ^ bit for j in send]
-            plan[f"rest {key}"] = (
+            plan[f"r{key}"] = (
                 lambda before=before, send=send: [held(before, j) for j in send],
                 joined,
                 functools.partial(swap, mask=spread(bit, inside)),
             )
         def rows_of(key):
-            if key == 0:
-                return [own], [[None] * group]
             top = key.bit_length() - 1
             if key == 1 << top:
-                first, order = f"carry {top}", list(range(key))
-            else:
-                first, order = f"part {key}", [0]
-            return [get(first), get(f"rest {key}")], [order, orders[key]]
+                return [(f"c{top}", list(range(key))), (f"r{key}", orders[key])]
+            return [(f"p{key}", [0]), (f"r{key}", orders[key])]
 
         for shift in range(1, halves):
-            for key in range(group):
-                plan[f"turn {shift} {key}"] = (
-                    lambda key=key: rows_of(key)[0],
-                    joined,
-                    functools.partial(rotate, shift=shift),
-                )
+            turn = functools.partial(rotate, shift=shift)
+            plan[f"t{shift}o"] = (lambda: [own], joined, turn)
+            for key in range(1, group):
+                for name, _ in rows_of(key):
+                    plan[f"t{shift}{name}"] = (lambda name=name: [get(name)], joined, turn)
 
         def projection(name, keys):
             values = []
             places = []
-            for place, key in enumerate(keys):
-                sources, order = rows_of(key)
-                values += sources
-                places += [(place, 0, js) for js in order]
-                for shift in range(1, halves):
-                    values.append(get(f"turn {shift} {key}"))
-                    places.append((place, shift, sum(order, [])))
+            for shift in range(halves):
+                away = f"t{shift}" if shift else ""
+                for place, key in enumerate(keys):
+                    if key == 0:
+                        values.append(get(away + "o") if shift else own)
+                        places.append((place, shift, [None] * group))
+                        continue
+                    for source, order in rows_of(key):
+                        values.append(get(away + source))
+                        places.append((place, shift, order))
             return project(
                 name, pos, cols, counts, potential, values, places, inside, halves
             )
 
-        plan["project"] = (
+        plan["q"] = (
             lambda: [projection("project", range(group - 1))],
             joined,
             lambda value: value,
@@ -354,12 +347,12 @@
         for name in WAITS:
             if name in plan:
                 get(name)
-        projected = get("project")
+        projected = get("q")
         projected_last = projection("project_last", [group - 1])
         early = [part(j) for j in range(group)]
         for key in range(1, 2 * far - 1):
-            early += [get(f"piece {key}.{i}") for i in range(len(pieces))]
-        late = [get(f"piece {2 * far - 1}.{i}") for i in range(len(pieces))]
+            early += [get(f"s{key}.{i}") for i in range(len(sizes[key]))]
+        late = [get(f"s{2 * far - 1}.{i}") for i in range(len(sizes[2 * far - 1]))]
         total = couple(
             "couple",
             False,

time: 116 us -> 112 us (0.966)
  local copies, waits for them, and re-layouts: 11.4 us -> 30.2 us
  waiting for transfers between devices: 55.7 us -> 38.5 us
  other arithmetic: 6.32 us -> 1.84 us
  Pallas kernels: 17.8 us -> 13.9 us
  starting transfers between devices: 24.2 us -> 26.3 us
    unnamed x50 -> x72, local copies, waits for them, and re-layouts: 9.56 us -> 28.5 us
    ppermute x18, waiting for transfers between devices: 53.9 us -> 36.8 us  [swap(): return lax.ppermute(value, 'ka', [(i, i ^ mask) for i in range(points)])]
    concatenate x7 -> x4, other arithmetic: 5.53 us -> 1.05 us  [joined(): return jnp.concatenate(values, axis=0) if values[1:] else values[0]]
    pallas_call x2, Pallas kernels: 10.1 us -> 6.5 us  [project(): pl.pallas_call(functools.partial(project_kernel, orders, inside, halves),...]
  transfers between devices with their start and end apart: 23 -> 26, of which waited for: 12 -> 9; matrix products, arithmetic and copies ran while one was open for 3% -> 2% of each run, Pallas kernels for 12% -> 9%
where the time goes in v5:
time: 112 us; the launch traced here: 111 us
  waiting for transfers between devices  38.5 us (34%)
  local copies, waits for them, and re-layouts  30.2 us (27%)
  starting transfers between devices  26.3 us (23%)
  Pallas kernels  13.9 us (12%)
  other arithmetic  1.84 us (2%)
    ppermute x18, waiting for transfers between devices, swap(): return lax.ppermute(value, 'ka', [(i, i ^ mask) for i in range(points)])  36.8 us
    unnamed x72, local copies, waits for them, and re-layouts  28.5 us
    ppermute x18, starting transfers between devices, swap(): return lax.ppermute(value, 'ka', [(i, i ^ mask) for i in range(points)])  24.7 us
    pallas_call x2, Pallas kernels, couple(): pl.pallas_call(functools.partial(couple_kernel, jobs, last, inside, outsi...  7.39 us
    pallas_call x2, Pallas kernels, project(): pl.pallas_call(functools.partial(project_kernel, orders, inside, halves),...  6.5 us
  transfers between devices with their start and end apart: 26, of which 9 were waited for; matrix products, arithmetic and copies ran while one was open for 2% of the time, Pallas kernels for 9%

profile of v5, /device:TPU:0, one launch (start us, length us, event | category | flops | bytes accessed | tf_op | source)
XLA Modules:
  0.0 111.1 jit_solution(3226502397601504165)
XLA Ops:
  0.0 1.3 %dynamic-slice_bitcast_fusion = (bf16[1024,128]{1,0:T(8,128)(2,1)S(1)}, bf16[1024,128]{1,0:T(8,128)(2,1)S(1)}, bf16[1024,128]{1,0:T(8,128)(2,1)S(1)}, bf16[1024,128]{1,0:T(8,128)(2,1)S(1)}) fusion(bf16[1,4096,128]{2,1,0:T(8,128)(2,1)} %param.6, s32[]{:T(128)S(6)} %select_n.22, s32[]{:T(128)S(6)} %select_n.9, s32[]{:T(128)S(6)} %select_n.8, s32[]{:T(128)S(6)} %select_n.10), kind=kLoop, calls=%fused_computation.7 | loop fusion | bytes 2097168 | tf_op jit(solution)/shard_map/dynamic_slice | solution.py:231
  1.3 3.0 %collective-permute-start = (bf16[1024,128]{1,0:T(8,128)(2,1)S(1)}, bf16[1024,128]{1,0:T(8,128)(2,1)S(1)}, u32[]{:S(2)}, u32[]{:S(2)}) collective-permute-start(bf16[1024,128]{1,0:T(8,128)(2,1)S(1)} %get-tuple-element.28), channel_id=1, source_target_pairs={{0,2},{2,0},{4,6},{6,4},{8,10},{10,8},{12,14},{14,12},{16,18},{18,... | collective-permute-start | bytes 786440 | tf_op jit(solution)/shard_map/ppermute | solution.py:223
  4.3 1.5 %collective-permute-start.1 = (bf16[1024,128]{1,0:T(8,128)(2,1)S(1)}, bf16[1024,128]{1,0:T(8,128)(2,1)S(1)}, u32[]{:S(2)}, u32[]{:S(2)}) collective-permute-start(bf16[1024,128]{1,0:T(8,128)(2,1)S(1)} %get-tuple-element.27.refs_1_.refs_6_), channel_id=1, source_target_pairs={{0,4},{2,6},{4,0},{6,2},{8,12},{10,14},{12,8},{14,10},{16,20},{18,... | collective-permute-start | bytes 786440 | tf_op jit(solution)/shard_map/ppermute | solution.py:223
  5.8 1.6 %collective-permute-start.3 = (bf16[2048,128]{1,0:T(8,128)(2,1)S(1)}, bf16[2048,128]{1,0:T(8,128)(2,1)S(1)}, u32[]{:S(2)}, u32[]{:S(2)}) collective-permute-start(bf16[2048,128]{1,0:T(8,128)(2,1)S(1)} %pad_maximum_fusion.2), channel_id=1, source_target_pairs={{0,8},{2,10},{4,12},{6,14},{8,0},{10,2},{12,4},{14,6},{16,24},{18,... | collective-permute-start | bytes 1572872 | tf_op jit(solution)/shard_map/ppermute | solution.py:223
  7.5 2.6 %collective-permute-start.9 = (bf16[1024,128]{1,0:T(8,128)(2,1)S(1)}, bf16[1024,128]{1,0:T(8,128)(2,1)S(1)}, u32[]{:S(2)}, u32[]{:S(2)}) collective-permute-start(bf16[1024,128]{1,0:T(8,128)(2,1)S(1)} %get-tuple-element.27.refs_1_.refs_6_), channel_id=1, source_target_pairs={{0,16},{2,18},{4,20},{6,22},{8,24},{10,26},{12,28},{14,30},{16,0},... | collective-permute-start | bytes 786440 | tf_op jit(solution)/shard_map/ppermute | solution.py:223
  10.6 1.5 %collective-permute-done.1.refs_5_.refs_10_ = bf16[1024,128]{1,0:T(8,128)(2,1)S(1)} collective-permute-done((bf16[1024,128]{1,0:T(8,128)(2,1)S(1)}, bf16[1024,128]{1,0:T(8,128)(2,1)S(1)}, u32[]{:S(2)}, u32[]{:S(2)}) %collective-permute-start.1) | collective-permute-done | bytes 262176 | tf_op jit(solution)/shard_map/ppermute | solution.py:223
  12.5 12.1 %collective-permute-done.3.refs_3_ = bf16[2048,128]{1,0:T(8,128)(2,1)S(1)} collective-permute-done((bf16[2048,128]{1,0:T(8,128)(2,1)S(1)}, bf16[2048,128]{1,0:T(8,128)(2,1)S(1)}, u32[]{:S(2)}, u32[]{:S(2)}) %collective-permute-start.3) | collective-permute-done | bytes 524320 | tf_op jit(solution)/shard_map/ppermute | solution.py:223
  25.5 4.2 %collective-permute-start.7 = (bf16[2048,128]{1,0:T(8,128)(2,1)S(1)}, bf16[2048,128]{1,0:T(8,128)(2,1)}, u32[]{:S(2)}, u32[]{:S(2)}) collective-permute-start(bf16[2048,128]{1,0:T(8,128)(2,1)S(1)} %constant_dynamic-update-slice_fusion), channel_id=1, source_target_pairs={{0,16},{2,18},{4,20},{6,22},{8,24},{10,26},{12,28},{14,30},{16,0},... | collective-permute-start | bytes 1572872 | tf_op jit(solution)/shard_map/ppermute | solution.py:223
  30.2 5.7 %collective-permute-done.6.refs_4_.refs_0_.refs_9_ = bf16[1024,128]{1,0:T(8,128)(2,1)S(1)} collective-permute-done((bf16[1024,128]{1,0:T(8,128)(2,1)S(1)}, bf16[1024,128]{1,0:T(8,128)(2,1)S(1)}, u32[]{:S(2)}, u32[]{:S(2)}) %collective-permute-start.6) | collective-permute-done | bytes 262176 | tf_op jit(solution)/shard_map/ppermute | solution.py:223
  35.9 1.6 %collective-permute-start.10 = (bf16[1024,128]{1,0:T(8,128)(2,1)S(1)}, bf16[1024,128]{1,0:T(8,128)(2,1)S(1)}, u32[]{:S(2)}, u32[]{:S(2)}) collective-permute-start(bf16[1024,128]{1,0:T(8,128)(2,1)S(1)} %collective-permute-done.9.refs_8_.refs_13_), channel_id=1, source_target_pairs={{0,4},{2,6},{4,0},{6,2},{8,12},{10,14},{12,8},{14,10},{16,20},{18,... | collective-permute-start | bytes 786440 | tf_op jit(solution)/shard_map/ppermute | solution.py:223
  38.2 9.2 %collective-permute-done.4.refs_4_ = bf16[2048,128]{1,0:T(8,128)(2,1)S(1)} collective-permute-done((bf16[2048,128]{1,0:T(8,128)(2,1)S(1)}, bf16[2048,128]{1,0:T(8,128)(2,1)S(1)}, u32[]{:S(2)}, u32[]{:S(2)}) %collective-permute-start.4) | collective-permute-done | bytes 524320 | tf_op jit(solution)/shard_map/ppermute | solution.py:223
  47.4 4.1 %collective-permute-done.7.refs_9_.refs_14_ = bf16[2048,128]{1,0:T(8,128)(2,1)} collective-permute-done((bf16[2048,128]{1,0:T(8,128)(2,1)S(1)}, bf16[2048,128]{1,0:T(8,128)(2,1)}, u32[]{:S(2)}, u32[]{:S(2)}) %collective-permute-start.7) | collective-permute-done | bytes 524320 | tf_op jit(solution)/shard_map/ppermute | solution.py:223
  57.7 1.5 %collective-permute-start.19 = (bf16[3072,128]{1,0:T(8,128)(2,1)}, bf16[3072,128]{1,0:T(8,128)(2,1)}, u32[]{:S(2)}, u32[]{:S(2)}) collective-permute-start(bf16[3072,128]{1,0:T(8,128)(2,1)} %pad_maximum_fusion.1), channel_id=1, source_target_pairs={{0,2},{2,0},{4,6},{6,4},{8,10},{10,8},{12,14},{14,12},{16,18},{18,... | collective-permute-start | bytes 2359304 | tf_op jit(solution)/shard_map/ppermute | solution.py:223
  62.1 1.5 %collective-permute-start.18 = (bf16[1024,128]{1,0:T(8,128)(2,1)S(1)}, bf16[1024,128]{1,0:T(8,128)(2,1)}, u32[]{:S(2)}, u32[]{:S(2)}) collective-permute-start(bf16[1024,128]{1,0:T(8,128)(2,1)S(1)} %collective-permute-done.6.refs_4_.refs_0_.refs_9_), channel_id=1, source_target_pairs={{0,4},{2,6},{4,0},{6,2},{8,12},{10,14},{12,8},{14,10},{16,20},{18,... | collective-permute-start | bytes 786440 | tf_op jit(solution)/shard_map/ppermute | solution.py:223
  65.0 3.7 %copy-done = bf16[3,32,3,128,128]{4,3,2,1,0:T(8,128)(2,1)S(1)} copy-done((bf16[3,32,3,128,128]{4,3,2,1,0:T(8,128)(2,1)S(1)}, bf16[3,32,3,128,128]{4,3,2,1,0:T(8,128)(2,1)}, u32[]{:S(2)}) %copy-start) | copy-done | bytes 9437208
  68.7 1.2 %copy-done.3 = bf16[1,4096,128]{2,1,0:T(8,128)(2,1)S(1)} copy-done((bf16[1,4096,128]{2,1,0:T(8,128)(2,1)S(1)}, bf16[1,4096,128]{2,1,0:T(8,128)(2,1)}, u32[]{:S(2)}) %copy-start.3) | copy-done | bytes 1048600
  69.9 1.0 copy-done.8
  72.0 1.2 %copy-done.12 = bf16[4096,128]{1,0:T(8,128)(2,1)S(1)} copy-done((bf16[4096,128]{1,0:T(8,128)(2,1)S(1)}, bf16[4096,128]{1,0:T(8,128)(2,1)}, u32[]{:S(2)}) %copy-start.12) | copy-done | bytes 1048600
  73.2 1.1 %copy-done.22 = bf16[3072,128]{1,0:T(8,128)(2,1)S(1)} copy-done((bf16[3072,128]{1,0:T(8,128)(2,1)S(1)}, bf16[3072,128]{1,0:T(8,128)(2,1)}, u32[]{:S(2)}) %copy-start.22) | copy-done | bytes 786456
  74.3 1.1 %copy-done.24 = bf16[3072,128]{1,0:T(8,128)(2,1)S(1)} copy-done((bf16[3072,128]{1,0:T(8,128)(2,1)S(1)}, bf16[3072,128]{1,0:T(8,128)(2,1)}, u32[]{:S(2)}) %copy-start.24) | copy-done | bytes 786456
  76.5 1.0 copy-done.28
  78.5 3.3 %project.1.refs_0_ = bf16[9,128,1024]{2,1,0:T(8,128)(2,1)S(1)} custom-call(s32[2]{0:T(128)S(1)} %pad_add_fusion.pos, s32[288]{0:T(512)S(1)} %reshape.23.cols, s32[96]{0:T(128)S(1)} %reshape.24.counts, bf16[3,32,3,128,128]{4,3,2,1,0:T(8,128)(2,1)S(1)} %copy-done, bf16[4096,128]{1,0:T(8,128)(2,1)S(1)} %bitcast.28, ...), custom_call_target="tpu_custom_call" | custom-call | tf_op jit(solution)/shard_map/project/pallas_call | solution.py:113
  83.0 1.0 copy-done.5
  85.9 3.4 %couple.1.refs_4_ = f32[9,128,128]{2,1,0:T(8,128)S(1)} custom-call(s32[2]{0:T(128)S(1)} %pad_add_fusion.pos, s32[48]{0:T(128)S(1)} %reshape.22.partners, bf16[9,128,1024]{2,1,0:T(8,128)(2,1)S(1)} %project.1.refs_0_, bf16[1024,128]{1,0:T(8,128)(2,1)S(1)} %get-tuple-element.27.refs_1_.refs_6_, ...), custom_call_target="tpu_custom_call" | custom-call | tf_op jit(solution)/shard_map/couple/pallas_call | solution.py:193
  89.4 3.7 %copy-done.1 = bf16[3,32,3,128,128]{4,3,2,1,0:T(8,128)(2,1)S(1)} copy-done((bf16[3,32,3,128,128]{4,3,2,1,0:T(8,128)(2,1)S(1)}, bf16[3,32,3,128,128]{4,3,2,1,0:T(8,128)(2,1)}, u32[]{:S(2)}) %copy-start.1) | copy-done | bytes 9437208
  93.1 3.2 %project_last.1.refs_5_ = bf16[3,128,1024]{2,1,0:T(8,128)(2,1)S(1)} custom-call(s32[2]{0:T(128)S(1)} %pad_add_fusion.pos, s32[288]{0:T(512)S(1)} %reshape.23.cols, s32[96]{0:T(128)S(1)} %reshape.24.counts, bf16[3,32,3,128,128]{4,3,2,1,0:T(8,128)(2,1)S(1)} %copy-done.1, bf16[1024,128]{1,0:T(8,128)(2,1)S(1)} %collective-permute-done.6.refs_4_.refs_0_.refs_9_, ...), custom_call_target="tpu_custom_call" | custom-call | tf_op jit(solution)/shard_map/project_last/pallas_call | solution.py:113
  96.3 4.0 %couple_last.1 = f32[2,12,64,128]{3,2,1,0:T(8,128)S(1)} custom-call(s32[2]{0:T(128)S(1)} %pad_add_fusion.pos, s32[48]{0:T(128)S(1)} %reshape.22.partners, bf16[9,128,1024]{2,1,0:T(8,128)(2,1)S(1)} %project.1.refs_0_, bf16[1024,128]{1,0:T(8,128)(2,1)S(1)} %copy-done.20, bf16[2048,128]{1,0:T(8,128)(2,1)} %collective-permute-done.15.refs_2_.refs_17_, ...), custom_call_target="tpu_custom_call" | custom-call | tf_op jit(solution)/shard_map/couple_last/pallas_call | solution.py:193
  100.5 1.7 %collective-permute-done.22 = f32[12,64,128]{2,1,0:T(8,128)S(1)} collective-permute-done((f32[12,64,128]{2,1,0:T(8,128)S(1)}, f32[12,64,128]{2,1,0:T(8,128)S(1)}, u32[]{:S(2)}, u32[]{:S(2)}) %collective-permute-start.22) | collective-permute-done | bytes 393248 | tf_op jit(solution)/shard_map/ppermute | solution.py:226
  102.3 3.0 %collective-permute-start.25 = (f32[3,64,128]{2,1,0:T(8,128)S(1)}, f32[3,64,128]{2,1,0:T(8,128)S(1)}, u32[]{:S(2)}, u32[]{:S(2)}) collective-permute-start(f32[3,64,128]{2,1,0:T(8,128)S(1)} %get-tuple-element.52), channel_id=1, source_target_pairs={{0,10},{2,8},{4,14},{6,12},{8,2},{10,0},{12,6},{14,4},{16,26},{18,... | collective-permute-start | bytes 294920 | tf_op jit(solution)/shard_map/ppermute | solution.py:223
  105.3 1.4 %collective-permute-start.23 = (f32[3,64,128]{2,1,0:T(8,128)S(1)}, f32[3,64,128]{2,1,0:T(8,128)S(1)}, u32[]{:S(2)}, u32[]{:S(2)}) collective-permute-start(f32[3,64,128]{2,1,0:T(8,128)S(1)} %get-tuple-element.51), channel_id=1, source_target_pairs={{0,2},{2,0},{4,6},{6,4},{8,10},{10,8},{12,14},{14,12},{16,18},{18,... | collective-permute-start | bytes 294920 | tf_op jit(solution)/shard_map/ppermute | solution.py:223
  106.7 1.7 %collective-permute-done.25 = f32[3,64,128]{2,1,0:T(8,128)S(1)} collective-permute-done((f32[3,64,128]{2,1,0:T(8,128)S(1)}, f32[3,64,128]{2,1,0:T(8,128)S(1)}, u32[]{:S(2)}, u32[]{:S(2)}) %collective-permute-start.25) | collective-permute-done | bytes 98336 | tf_op jit(solution)/shard_map/ppermute | solution.py:223
  108.4 2.1 %collective-permute-done.24 = f32[3,64,128]{2,1,0:T(8,128)S(1)} collective-permute-done((f32[3,64,128]{2,1,0:T(8,128)S(1)}, f32[3,64,128]{2,1,0:T(8,128)S(1)}, u32[]{:S(2)}, u32[]{:S(2)}) %collective-permute-start.24) | collective-permute-done | bytes 98336 | tf_op jit(solution)/shard_map/ppermute | solution.py:223
  (112 shorter events, 20.6 us)
Async XLA Ops:
  1.3 9.3 %collective-permute-start = (bf16[1024,128]{1,0:T(8,128)(2,1)S(1)}, bf16[1024,128]{1,0:T(8,128)(2,1)S(1)}, u32[]{:S(2)}, u32[]{:S(2)}) collective-permute-start(bf16[1024,128]{1,0:T(8,128)(2,1)S(1)} %get-tuple-element.28), channel_id=1, source_target_pairs={{0,2},{2,0},{4,6},{6,4},{8,10},{10,8},{12,14},{14,12},{16,18},{18,... | collective-permute-start | bytes 786440 | tf_op jit(solution)/shard_map/ppermute | solution.py:223
  4.3 7.8 %collective-permute-start.1 = (bf16[1024,128]{1,0:T(8,128)(2,1)S(1)}, bf16[1024,128]{1,0:T(8,128)(2,1)S(1)}, u32[]{:S(2)}, u32[]{:S(2)}) collective-permute-start(bf16[1024,128]{1,0:T(8,128)(2,1)S(1)} %get-tuple-element.27.refs_1_.refs_6_), channel_id=1, source_target_pairs={{0,4},{2,6},{4,0},{6,2},{8,12},{10,14},{12,8},{14,10},{16,20},{18,... | collective-permute-start | bytes 786440 | tf_op jit(solution)/shard_map/ppermute | solution.py:223
  5.8 18.8 %collective-permute-start.3 = (bf16[2048,128]{1,0:T(8,128)(2,1)S(1)}, bf16[2048,128]{1,0:T(8,128)(2,1)S(1)}, u32[]{:S(2)}, u32[]{:S(2)}) collective-permute-start(bf16[2048,128]{1,0:T(8,128)(2,1)S(1)} %pad_maximum_fusion.2), channel_id=1, source_target_pairs={{0,8},{2,10},{4,12},{6,14},{8,0},{10,2},{12,4},{14,6},{16,24},{18,... | collective-permute-start | bytes 1572872 | tf_op jit(solution)/shard_map/ppermute | solution.py:223
  7.5 22.2 %collective-permute-start.9 = (bf16[1024,128]{1,0:T(8,128)(2,1)S(1)}, bf16[1024,128]{1,0:T(8,128)(2,1)S(1)}, u32[]{:S(2)}, u32[]{:S(2)}) collective-permute-start(bf16[1024,128]{1,0:T(8,128)(2,1)S(1)} %get-tuple-element.27.refs_1_.refs_6_), channel_id=1, source_target_pairs={{0,16},{2,18},{4,20},{6,22},{8,24},{10,26},{12,28},{14,30},{16,0},... | collective-permute-start | bytes 786440 | tf_op jit(solution)/shard_map/ppermute | solution.py:223
  12.0 12.6 %copy-start.13 = (bf16[1024,128]{1,0:T(8,128)(2,1)}, bf16[1024,128]{1,0:T(8,128)(2,1)S(1)}, u32[]{:S(2)}) copy-start(bf16[1024,128]{1,0:T(8,128)(2,1)S(1)} %collective-permute-done.1.refs_5_.refs_10_) | copy-start | bytes 786436
  12.1 23.8 %copy-start.2 = (bf16[1,4096,128]{2,1,0:T(8,128)(2,1)S(1)}, bf16[1,4096,128]{2,1,0:T(8,128)(2,1)}, u32[]{:S(2)}) copy-start(bf16[1,4096,128]{2,1,0:T(8,128)(2,1)} %param.6) | copy-start | bytes 3145732
  12.1 23.8 %collective-permute-start.2 = (bf16[3072,128]{1,0:T(8,128)(2,1)S(1)}, bf16[3072,128]{1,0:T(8,128)(2,1)S(1)}, u32[]{:S(2)}, u32[]{:S(2)}) collective-permute-start(bf16[3072,128]{1,0:T(8,128)(2,1)S(1)} %pad_maximum_fusion), channel_id=1, source_target_pairs={{0,2},{2,0},{4,6},{6,4},{8,10},{10,8},{12,14},{14,12},{16,18},{18,... | collective-permute-start | bytes 2359304 | tf_op jit(solution)/shard_map/ppermute | solution.py:223
  24.6 28.9 %copy-start.7 = (bf16[2048,128]{1,0:T(8,128)(2,1)}, bf16[2048,128]{1,0:T(8,128)(2,1)S(1)}, u32[]{:S(2)}) copy-start(bf16[2048,128]{1,0:T(8,128)(2,1)S(1)} %collective-permute-done.3.refs_3_) | copy-start | bytes 1572868
  24.7 22.7 %collective-permute-start.4 = (bf16[2048,128]{1,0:T(8,128)(2,1)S(1)}, bf16[2048,128]{1,0:T(8,128)(2,1)S(1)}, u32[]{:S(2)}, u32[]{:S(2)}) collective-permute-start(bf16[2048,128]{1,0:T(8,128)(2,1)S(1)} %pad_maximum_fusion.3), channel_id=1, source_target_pairs={{0,8},{2,10},{4,12},{6,14},{8,0},{10,2},{12,4},{14,6},{16,24},{18,... | collective-permute-start | bytes 1572872 | tf_op jit(solution)/shard_map/ppermute | solution.py:223
  24.8 11.1 %collective-permute-start.6 = (bf16[1024,128]{1,0:T(8,128)(2,1)S(1)}, bf16[1024,128]{1,0:T(8,128)(2,1)S(1)}, u32[]{:S(2)}, u32[]{:S(2)}) collective-permute-start(bf16[1024,128]{1,0:T(8,128)(2,1)S(1)} %get-tuple-element.29), channel_id=1, source_target_pairs={{0,2},{2,0},{4,6},{6,4},{8,10},{10,8},{12,14},{14,12},{16,18},{18,... | collective-permute-start | bytes 786440 | tf_op jit(solution)/shard_map/ppermute | solution.py:223
  25.4 38.2 %copy-start.32 = (s32[3,32,3]{1,2,0:T(4,128)S(1)}, s32[3,32,3]{1,2,0:T(4,128)}, u32[]{:S(2)}) copy-start(s32[3,32,3]{1,2,0:T(4,128)} %param.8) | copy-start | bytes 3460
  25.4 38.5 %copy-start.33 = (s32[3,32]{1,0:T(4,128)S(1)}, s32[3,32]{1,0:T(4,128)}, u32[]{:S(2)}) copy-start(s32[3,32]{1,0:T(4,128)} %param.9) | copy-start | bytes 1156
  25.5 26.0 %collective-permute-start.7 = (bf16[2048,128]{1,0:T(8,128)(2,1)S(1)}, bf16[2048,128]{1,0:T(8,128)(2,1)}, u32[]{:S(2)}, u32[]{:S(2)}) collective-permute-start(bf16[2048,128]{1,0:T(8,128)(2,1)S(1)} %constant_dynamic-update-slice_fusion), channel_id=1, source_target_pairs={{0,16},{2,18},{4,20},{6,22},{8,24},{10,26},{12,28},{14,30},{16,0},... | collective-permute-start | bytes 1572872 | tf_op jit(solution)/shard_map/ppermute | solution.py:223
  29.7 21.8 %collective-permute-start.8 = (bf16[2048,128]{1,0:T(8,128)(2,1)S(1)}, bf16[2048,128]{1,0:T(8,128)(2,1)S(1)}, u32[]{:S(2)}, u32[]{:S(2)}) collective-permute-start(bf16[2048,128]{1,0:T(8,128)(2,1)S(1)} %constant_dynamic-update-slice_fusion), channel_id=1, source_target_pairs={{0,4},{2,6},{4,0},{6,2},{8,12},{10,14},{12,8},{14,10},{16,20},{18,... | collective-permute-start | bytes 1572872 | tf_op jit(solution)/shard_map/ppermute | solution.py:223
  35.9 20.8 %collective-permute-start.5 = (bf16[4096,128]{1,0:T(8,128)(2,1)S(1)}, bf16[4096,128]{1,0:T(8,128)(2,1)S(1)}, u32[]{:S(2)}, u32[]{:S(2)}) collective-permute-start(bf16[4096,128]{1,0:T(8,128)(2,1)S(1)} %bitcast.27), channel_id=1, source_target_pairs={{0,1},{1,0},{2,3},{3,2},{4,5},{5,4},{6,7},{7,6},{8,9},{9,8},{10,11... | collective-permute-start | bytes 3145736 | tf_op jit(solution)/shard_map/ppermute | solution.py:226
  35.9 16.4 %collective-permute-start.10 = (bf16[1024,128]{1,0:T(8,128)(2,1)S(1)}, bf16[1024,128]{1,0:T(8,128)(2,1)S(1)}, u32[]{:S(2)}, u32[]{:S(2)}) collective-permute-start(bf16[1024,128]{1,0:T(8,128)(2,1)S(1)} %collective-permute-done.9.refs_8_.refs_13_), channel_id=1, source_target_pairs={{0,4},{2,6},{4,0},{6,2},{8,12},{10,14},{12,8},{14,10},{16,20},{18,... | collective-permute-start | bytes 786440 | tf_op jit(solution)/shard_map/ppermute | solution.py:223
  53.0 6.2 %collective-permute-start.11 = (bf16[1024,128]{1,0:T(8,128)(2,1)S(1)}, bf16[1024,128]{1,0:T(8,128)(2,1)S(1)}, u32[]{:S(2)}, u32[]{:S(2)}) collective-permute-start(bf16[1024,128]{1,0:T(8,128)(2,1)S(1)} %collective-permute-done.refs_1_.refs_2_.refs_7_), channel_id=1, source_target_pairs={{0,1},{1,0},{2,3},{3,2},{4,5},{5,4},{6,7},{7,6},{8,9},{9,8},{10,11... | collective-permute-start | bytes 786440 | tf_op jit(solution)/shard_map/ppermute | solution.py:226
  53.0 11.1 %collective-permute-start.12 = (bf16[3072,128]{1,0:T(8,128)(2,1)S(1)}, bf16[3072,128]{1,0:T(8,128)(2,1)S(1)}, u32[]{:S(2)}, u32[]{:S(2)}) collective-permute-start(bf16[3072,128]{1,0:T(8,128)(2,1)S(1)} %collective-permute-done.2.refs_2_), channel_id=1, source_target_pairs={{0,1},{1,0},{2,3},{3,2},{4,5},{5,4},{6,7},{7,6},{8,9},{9,8},{10,11... | collective-permute-start | bytes 2359304 | tf_op jit(solution)/shard_map/ppermute | solution.py:226
  54.4 6.0 %collective-permute-start.13 = (bf16[2048,128]{1,0:T(8,128)(2,1)S(1)}, bf16[2048,128]{1,0:T(8,128)(2,1)S(1)}, u32[]{:S(2)}, u32[]{:S(2)}) collective-permute-start(bf16[2048,128]{1,0:T(8,128)(2,1)S(1)} %collective-permute-done.3.refs_3_), channel_id=1, source_target_pairs={{0,1},{1,0},{2,3},{3,2},{4,5},{5,4},{6,7},{7,6},{8,9},{9,8},{10,11... | collective-permute-start | bytes 1572872 | tf_op jit(solution)/shard_map/ppermute | solution.py:226
  54.4 6.8 %collective-permute-start.14 = (bf16[2048,128]{1,0:T(8,128)(2,1)S(1)}, bf16[2048,128]{1,0:T(8,128)(2,1)S(1)}, u32[]{:S(2)}, u32[]{:S(2)}) collective-permute-start(bf16[2048,128]{1,0:T(8,128)(2,1)S(1)} %collective-permute-done.4.refs_4_), channel_id=1, source_target_pairs={{0,1},{1,0},{2,3},{3,2},{4,5},{5,4},{6,7},{7,6},{8,9},{9,8},{10,11... | collective-permute-start | bytes 1572872 | tf_op jit(solution)/shard_map/ppermute | solution.py:226
  57.7 24.1 %collective-permute-start.19 = (bf16[3072,128]{1,0:T(8,128)(2,1)}, bf16[3072,128]{1,0:T(8,128)(2,1)}, u32[]{:S(2)}, u32[]{:S(2)}) collective-permute-start(bf16[3072,128]{1,0:T(8,128)(2,1)} %pad_maximum_fusion.1), channel_id=1, source_target_pairs={{0,2},{2,0},{4,6},{6,4},{8,10},{10,8},{12,14},{14,12},{16,18},{18,... | collective-permute-start | bytes 2359304 | tf_op jit(solution)/shard_map/ppermute | solution.py:223
  59.9 21.9 %collective-permute-start.15 = (bf16[2048,128]{1,0:T(8,128)(2,1)}, bf16[2048,128]{1,0:T(8,128)(2,1)}, u32[]{:S(2)}, u32[]{:S(2)}) collective-permute-start(bf16[2048,128]{1,0:T(8,128)(2,1)} %collective-permute-done.7.refs_9_.refs_14_), channel_id=1, source_target_pairs={{0,4},{2,6},{4,0},{6,2},{8,12},{10,14},{12,8},{14,10},{16,20},{18,... | collective-permute-start | bytes 1572872 | tf_op jit(solution)/shard_map/ppermute | solution.py:223
  61.3 20.5 %collective-permute-start.16 = (bf16[1024,128]{1,0:T(8,128)(2,1)S(1)}, bf16[1024,128]{1,0:T(8,128)(2,1)}, u32[]{:S(2)}, u32[]{:S(2)}) collective-permute-start(bf16[1024,128]{1,0:T(8,128)(2,1)S(1)} %collective-permute-done.6.refs_4_.refs_0_.refs_9_), channel_id=1, source_target_pairs={{0,16},{2,18},{4,20},{6,22},{8,24},{10,26},{12,28},{14,30},{16,0},... | collective-permute-start | bytes 786440 | tf_op jit(solution)/shard_map/ppermute | solution.py:223
  62.1 19.7 %collective-permute-start.18 = (bf16[1024,128]{1,0:T(8,128)(2,1)S(1)}, bf16[1024,128]{1,0:T(8,128)(2,1)}, u32[]{:S(2)}, u32[]{:S(2)}) collective-permute-start(bf16[1024,128]{1,0:T(8,128)(2,1)S(1)} %collective-permute-done.6.refs_4_.refs_0_.refs_9_), channel_id=1, source_target_pairs={{0,4},{2,6},{4,0},{6,2},{8,12},{10,14},{12,8},{14,10},{16,20},{18,... | collective-permute-start | bytes 786440 | tf_op jit(solution)/shard_map/ppermute | solution.py:223
  81.8 7.5 %collective-permute-start.21 = (bf16[3072,128]{1,0:T(8,128)(2,1)}, bf16[3072,128]{1,0:T(8,128)(2,1)}, u32[]{:S(2)}, u32[]{:S(2)}) collective-permute-start(bf16[3072,128]{1,0:T(8,128)(2,1)} %collective-permute-done.19.refs_1_), channel_id=1, source_target_pairs={{0,1},{1,0},{2,3},{3,2},{4,5},{5,4},{6,7},{7,6},{8,9},{9,8},{10,11... | collective-permute-start | bytes 2359304 | tf_op jit(solution)/shard_map/ppermute | solution.py:226
  81.9 7.5 %collective-permute-start.20 = (bf16[1024,128]{1,0:T(8,128)(2,1)S(1)}, bf16[1024,128]{1,0:T(8,128)(2,1)}, u32[]{:S(2)}, u32[]{:S(2)}) collective-permute-start(bf16[1024,128]{1,0:T(8,128)(2,1)S(1)} %collective-permute-done.6.refs_4_.refs_0_.refs_9_), channel_id=1, source_target_pairs={{0,1},{1,0},{2,3},{3,2},{4,5},{5,4},{6,7},{7,6},{8,9},{9,8},{10,11... | collective-permute-start | bytes 786440 | tf_op jit(solution)/shard_map/ppermute | solution.py:226
  82.4 13.9 %collective-permute-start.17 = (bf16[1024,128]{1,0:T(8,128)(2,1)}, bf16[1024,128]{1,0:T(8,128)(2,1)}, u32[]{:S(2)}, u32[]{:S(2)}) collective-permute-start(bf16[1024,128]{1,0:T(8,128)(2,1)} %collective-permute-done.16.refs_10_.refs_15_), channel_id=1, source_target_pairs={{0,4},{2,6},{4,0},{6,2},{8,12},{10,14},{12,8},{14,10},{16,20},{18,... | collective-permute-start | bytes 786440 | tf_op jit(solution)/shard_map/ppermute | solution.py:223
  85.9 10.4 %copy-start.20 = (bf16[1024,128]{1,0:T(8,128)(2,1)S(1)}, bf16[1024,128]{1,0:T(8,128)(2,1)}, u32[]{:S(2)}) copy-start(bf16[1024,128]{1,0:T(8,128)(2,1)} %copy-done.19) | copy-start | bytes 786436
  100.4 1.8 %collective-permute-start.22 = (f32[12,64,128]{2,1,0:T(8,128)S(1)}, f32[12,64,128]{2,1,0:T(8,128)S(1)}, u32[]{:S(2)}, u32[]{:S(2)}) collective-permute-start(f32[12,64,128]{2,1,0:T(8,128)S(1)} %slice_bitcast_fusion), channel_id=1, source_target_pairs={{0,1},{1,0},{2,3},{3,2},{4,5},{5,4},{6,7},{7,6},{8,9},{9,8},{10,11... | collective-permute-start | bytes 1179656 | tf_op jit(solution)/shard_map/ppermute | solution.py:226
  102.3 6.1 %collective-permute-start.25 = (f32[3,64,128]{2,1,0:T(8,128)S(1)}, f32[3,64,128]{2,1,0:T(8,128)S(1)}, u32[]{:S(2)}, u32[]{:S(2)}) collective-permute-start(f32[3,64,128]{2,1,0:T(8,128)S(1)} %get-tuple-element.52), channel_id=1, source_target_pairs={{0,10},{2,8},{4,14},{6,12},{8,2},{10,0},{12,6},{14,4},{16,26},{18,... | collective-permute-start | bytes 294920 | tf_op jit(solution)/shard_map/ppermute | solution.py:223
  105.2 5.2 %collective-permute-start.24 = (f32[3,64,128]{2,1,0:T(8,128)S(1)}, f32[3,64,128]{2,1,0:T(8,128)S(1)}, u32[]{:S(2)}, u32[]{:S(2)}) collective-permute-start(f32[3,64,128]{2,1,0:T(8,128)S(1)} %get-tuple-element.53), channel_id=1, source_target_pairs={{0,8},{2,10},{4,12},{6,14},{8,0},{10,2},{12,4},{14,6},{16,24},{18,... | collective-permute-start | bytes 294920 | tf_op jit(solution)/shard_map/ppermute | solution.py:223
  105.3 5.1 %collective-permute-start.23 = (f32[3,64,128]{2,1,0:T(8,128)S(1)}, f32[3,64,128]{2,1,0:T(8,128)S(1)}, u32[]{:S(2)}, u32[]{:S(2)}) collective-permute-start(f32[3,64,128]{2,1,0:T(8,128)S(1)} %get-tuple-element.51), channel_id=1, source_target_pairs={{0,2},{2,0},{4,6},{6,4},{8,10},{10,8},{12,14},{14,12},{16,18},{18,... | collective-permute-start | bytes 294920 | tf_op jit(solution)/shard_map/ppermute | solution.py:223
  (29 other events, 74.0 us)

commit v6 on v5

--- a/solution.py
+++ b/solution.py
@@ -24,6 +24,14 @@
     "q": (),
     "t1r3": ("q", "s2.2", "s3.1", "s1.2"),
 }
+
+
+def in_hbm(value):
+    return pltpu.with_memory_space_constraint(value, pltpu.HBM)
+
+
+def in_vmem(value):
+    return pltpu.with_memory_space_constraint(value, pltpu.VMEM)
 
 
 def split_bits(points, blocks):
@@ -124,7 +132,7 @@
         compiler_params=pltpu.CompilerParams(vmem_limit_bytes=held + made + SPARE_VMEM),
         cost_estimate=pl.CostEstimate(flops=0, bytes_accessed=0, transcendentals=0),
         name=name,
-    )(pos, cols, counts, potential, *sources)
+    )(pos, cols, counts, in_hbm(potential), *[in_vmem(x) for x in sources])
 
 
 def couple_kernel(jobs, last, inside, outside, halves, pos, partners, *refs):
@@ -199,7 +207,7 @@
         compiler_params=pltpu.CompilerParams(vmem_limit_bytes=held + SPARE_VMEM),
         cost_estimate=pl.CostEstimate(flops=0, bytes_accessed=0, transcendentals=0),
         name=name,
-    )(pos, partners, *values)
+    )(pos, partners, *[in_vmem(x) for x in values])
 
 
 def solution(mesh):
@@ -380,8 +388,9 @@
             summed = summed + rotate(total[shift], shift)
         summed = summed.reshape((group, modes) + summed.shape[1:])
         result = summed[0]
+        sent = summed.astype(jnp.bfloat16)
         for point in range(1, group):
-            result = result + swap(summed[point], spread(point, inside))
+            result = result + swap(sent[point], spread(point, inside)).astype(jnp.float32)
         return result[:, None] / gaps
 
     return jax.shard_map(

time: 112 us -> 105 us (0.938)
  local copies, waits for them, and re-layouts: 30.2 us -> 22.9 us
  Pallas kernels: 13.9 us -> 15.4 us
    unnamed x72 -> x66, local copies, waits for them, and re-layouts: 28.5 us -> 21.2 us
    pallas_call x2, Pallas kernels: 6.5 us -> 8.08 us  [project(): pl.pallas_call(functools.partial(project_kernel, orders, inside, halves),...]
  transfers between devices with their start and end apart: 26 -> 26, of which waited for: 9 -> 11; matrix products, arithmetic and copies ran while one was open for 2% -> 2% of each run, Pallas kernels for 9% -> 11%
where the time goes in v6:
time: 105 us; the launch traced here: 104 us
  waiting for transfers between devices  37.7 us (36%)
  starting transfers between devices  26.1 us (25%)
  local copies, waits for them, and re-layouts  22.9 us (22%)
  Pallas kernels  15.4 us (15%)
  other arithmetic  1.86 us (2%)
    ppermute x18, waiting for transfers between devices, swap(): return lax.ppermute(value, 'ka', [(i, i ^ mask) for i in range(points)])  36 us
    ppermute x18, starting transfers between devices, swap(): return lax.ppermute(value, 'ka', [(i, i ^ mask) for i in range(points)])  24.5 us
    unnamed x66, local copies, waits for them, and re-layouts  21.2 us
    pallas_call x2, Pallas kernels, project(): pl.pallas_call(functools.partial(project_kernel, orders, inside, halves),...  8.08 us
    pallas_call x2, Pallas kernels, couple(): pl.pallas_call(functools.partial(couple_kernel, jobs, last, inside, outsi...  7.35 us
  transfers between devices with their start and end apart: 26, of which 11 were waited for; matrix products, arithmetic and copies ran while one was open for 2% of the time, Pallas kernels for 11%

profile of v6, /device:TPU:0, one launch (start us, length us, event | category | flops | bytes accessed | tf_op | source)
XLA Modules:
  0.0 104.3 jit_solution(5695606938705084351)
XLA Ops:
  0.0 1.3 %dynamic-slice_bitcast_fusion = (bf16[1024,128]{1,0:T(8,128)(2,1)S(1)}, bf16[1024,128]{1,0:T(8,128)(2,1)S(1)}, bf16[1024,128]{1,0:T(8,128)(2,1)S(1)}, bf16[1024,128]{1,0:T(8,128)(2,1)S(1)}) fusion(bf16[1,4096,128]{2,1,0:T(8,128)(2,1)} %param.6, s32[]{:T(128)S(6)} %select_n.22, s32[]{:T(128)S(6)} %select_n.9, s32[]{:T(128)S(6)} %select_n.8, s32[]{:T(128)S(6)} %select_n.10), kind=kLoop, calls=%fused_computation.7 | loop fusion | bytes 2097168 | tf_op jit(solution)/shard_map/dynamic_slice | solution.py:239
  1.3 3.0 %collective-permute-start = (bf16[1024,128]{1,0:T(8,128)(2,1)S(1)}, bf16[1024,128]{1,0:T(8,128)(2,1)S(1)}, u32[]{:S(2)}, u32[]{:S(2)}) collective-permute-start(bf16[1024,128]{1,0:T(8,128)(2,1)S(1)} %get-tuple-element.28), channel_id=1, source_target_pairs={{0,2},{2,0},{4,6},{6,4},{8,10},{10,8},{12,14},{14,12},{16,18},{18,... | collective-permute-start | bytes 786440 | tf_op jit(solution)/shard_map/ppermute | solution.py:231
  4.3 1.5 %collective-permute-start.1 = (bf16[1024,128]{1,0:T(8,128)(2,1)S(1)}, bf16[1024,128]{1,0:T(8,128)(2,1)S(1)}, u32[]{:S(2)}, u32[]{:S(2)}) collective-permute-start(bf16[1024,128]{1,0:T(8,128)(2,1)S(1)} %get-tuple-element.27.refs_1_.refs_6_), channel_id=1, source_target_pairs={{0,4},{2,6},{4,0},{6,2},{8,12},{10,14},{12,8},{14,10},{16,20},{18,... | collective-permute-start | bytes 786440 | tf_op jit(solution)/shard_map/ppermute | solution.py:231
  5.8 1.6 %collective-permute-start.3 = (bf16[2048,128]{1,0:T(8,128)(2,1)S(1)}, bf16[2048,128]{1,0:T(8,128)(2,1)S(1)}, u32[]{:S(2)}, u32[]{:S(2)}) collective-permute-start(bf16[2048,128]{1,0:T(8,128)(2,1)S(1)} %pad_maximum_fusion.2), channel_id=1, source_target_pairs={{0,8},{2,10},{4,12},{6,14},{8,0},{10,2},{12,4},{14,6},{16,24},{18,... | collective-permute-start | bytes 1572872 | tf_op jit(solution)/shard_map/ppermute | solution.py:231
  7.5 2.6 %collective-permute-start.9 = (bf16[1024,128]{1,0:T(8,128)(2,1)S(1)}, bf16[1024,128]{1,0:T(8,128)(2,1)S(1)}, u32[]{:S(2)}, u32[]{:S(2)}) collective-permute-start(bf16[1024,128]{1,0:T(8,128)(2,1)S(1)} %get-tuple-element.27.refs_1_.refs_6_), channel_id=1, source_target_pairs={{0,16},{2,18},{4,20},{6,22},{8,24},{10,26},{12,28},{14,30},{16,0},... | collective-permute-start | bytes 786440 | tf_op jit(solution)/shard_map/ppermute | solution.py:231
  10.6 1.5 %collective-permute-done.1.refs_5_.refs_10_ = bf16[1024,128]{1,0:T(8,128)(2,1)S(1)} collective-permute-done((bf16[1024,128]{1,0:T(8,128)(2,1)S(1)}, bf16[1024,128]{1,0:T(8,128)(2,1)S(1)}, u32[]{:S(2)}, u32[]{:S(2)}) %collective-permute-start.1) | collective-permute-done | bytes 262176 | tf_op jit(solution)/shard_map/ppermute | solution.py:231
  12.5 12.1 %collective-permute-done.3.refs_3_ = bf16[2048,128]{1,0:T(8,128)(2,1)S(1)} collective-permute-done((bf16[2048,128]{1,0:T(8,128)(2,1)S(1)}, bf16[2048,128]{1,0:T(8,128)(2,1)S(1)}, u32[]{:S(2)}, u32[]{:S(2)}) %collective-permute-start.3) | collective-permute-done | bytes 524320 | tf_op jit(solution)/shard_map/ppermute | solution.py:231
  25.5 4.2 %collective-permute-start.7 = (bf16[2048,128]{1,0:T(8,128)(2,1)S(1)}, bf16[2048,128]{1,0:T(8,128)(2,1)}, u32[]{:S(2)}, u32[]{:S(2)}) collective-permute-start(bf16[2048,128]{1,0:T(8,128)(2,1)S(1)} %constant_dynamic-update-slice_fusion), channel_id=1, source_target_pairs={{0,16},{2,18},{4,20},{6,22},{8,24},{10,26},{12,28},{14,30},{16,0},... | collective-permute-start | bytes 1572872 | tf_op jit(solution)/shard_map/ppermute | solution.py:231
  30.2 5.7 %collective-permute-done.6.refs_4_.refs_0_.refs_9_ = bf16[1024,128]{1,0:T(8,128)(2,1)S(1)} collective-permute-done((bf16[1024,128]{1,0:T(8,128)(2,1)S(1)}, bf16[1024,128]{1,0:T(8,128)(2,1)S(1)}, u32[]{:S(2)}, u32[]{:S(2)}) %collective-permute-start.6) | collective-permute-done | bytes 262176 | tf_op jit(solution)/shard_map/ppermute | solution.py:231
  35.9 1.6 %collective-permute-start.10 = (bf16[1024,128]{1,0:T(8,128)(2,1)S(1)}, bf16[1024,128]{1,0:T(8,128)(2,1)S(1)}, u32[]{:S(2)}, u32[]{:S(2)}) collective-permute-start(bf16[1024,128]{1,0:T(8,128)(2,1)S(1)} %collective-permute-done.9.refs_8_.refs_13_), channel_id=1, source_target_pairs={{0,4},{2,6},{4,0},{6,2},{8,12},{10,14},{12,8},{14,10},{16,20},{18,... | collective-permute-start | bytes 786440 | tf_op jit(solution)/shard_map/ppermute | solution.py:231
  38.2 9.2 %collective-permute-done.4.refs_4_ = bf16[2048,128]{1,0:T(8,128)(2,1)S(1)} collective-permute-done((bf16[2048,128]{1,0:T(8,128)(2,1)S(1)}, bf16[2048,128]{1,0:T(8,128)(2,1)S(1)}, u32[]{:S(2)}, u32[]{:S(2)}) %collective-permute-start.4) | collective-permute-done | bytes 524320 | tf_op jit(solution)/shard_map/ppermute | solution.py:231
  47.4 4.1 %collective-permute-done.7.refs_9_.refs_14_ = bf16[2048,128]{1,0:T(8,128)(2,1)} collective-permute-done((bf16[2048,128]{1,0:T(8,128)(2,1)S(1)}, bf16[2048,128]{1,0:T(8,128)(2,1)}, u32[]{:S(2)}, u32[]{:S(2)}) %collective-permute-start.7) | collective-permute-done | bytes 524320 | tf_op jit(solution)/shard_map/ppermute | solution.py:231
  56.7 1.0 copy-done.9
  57.7 1.5 %collective-permute-start.19 = (bf16[3072,128]{1,0:T(8,128)(2,1)}, bf16[3072,128]{1,0:T(8,128)(2,1)}, u32[]{:S(2)}, u32[]{:S(2)}) collective-permute-start(bf16[3072,128]{1,0:T(8,128)(2,1)} %pad_maximum_fusion.1), channel_id=1, source_target_pairs={{0,2},{2,0},{4,6},{6,4},{8,10},{10,8},{12,14},{14,12},{16,18},{18,... | collective-permute-start | bytes 2359304 | tf_op jit(solution)/shard_map/ppermute | solution.py:231
  62.2 1.5 %collective-permute-start.18 = (bf16[1024,128]{1,0:T(8,128)(2,1)S(1)}, bf16[1024,128]{1,0:T(8,128)(2,1)}, u32[]{:S(2)}, u32[]{:S(2)}) collective-permute-start(bf16[1024,128]{1,0:T(8,128)(2,1)S(1)} %collective-permute-done.6.refs_4_.refs_0_.refs_9_), channel_id=1, source_target_pairs={{0,4},{2,6},{4,0},{6,2},{8,12},{10,14},{12,8},{14,10},{16,20},{18,... | collective-permute-start | bytes 786440 | tf_op jit(solution)/shard_map/ppermute | solution.py:231
  65.0 1.2 %copy-done.1 = bf16[1,4096,128]{2,1,0:T(8,128)(2,1)S(1)} copy-done((bf16[1,4096,128]{2,1,0:T(8,128)(2,1)S(1)}, bf16[1,4096,128]{2,1,0:T(8,128)(2,1)}, u32[]{:S(2)}) %copy-start.1) | copy-done | bytes 1048600
  66.2 1.0 copy-done.6
  67.3 1.0 copy-done.8
  68.3 1.2 %copy-done.10 = bf16[4096,128]{1,0:T(8,128)(2,1)S(1)} copy-done((bf16[4096,128]{1,0:T(8,128)(2,1)S(1)}, bf16[4096,128]{1,0:T(8,128)(2,1)}, u32[]{:S(2)}) %copy-start.10) | copy-done | bytes 1048600
  69.6 1.1 %copy-done.19 = bf16[3072,128]{1,0:T(8,128)(2,1)S(1)} copy-done((bf16[3072,128]{1,0:T(8,128)(2,1)S(1)}, bf16[3072,128]{1,0:T(8,128)(2,1)}, u32[]{:S(2)}) %copy-start.19) | copy-done | bytes 786456
  70.7 1.1 %copy-done.21 = bf16[3072,128]{1,0:T(8,128)(2,1)S(1)} copy-done((bf16[3072,128]{1,0:T(8,128)(2,1)S(1)}, bf16[3072,128]{1,0:T(8,128)(2,1)}, u32[]{:S(2)}) %copy-start.21) | copy-done | bytes 786456
  71.8 1.0 copy-done.23
  72.9 1.0 copy-done.25
  74.9 4.3 %project.1.refs_0_ = bf16[9,128,1024]{2,1,0:T(8,128)(2,1)S(1)} custom-call(s32[2]{0:T(128)S(1)} %pad_add_fusion.pos, s32[288]{0:T(512)S(1)} %reshape.24.cols, s32[96]{0:T(128)S(1)} %reshape.25.counts, bf16[3,32,3,128,128]{4,3,2,1,0:T(8,128)(2,1)} %potential.3, bf16[4096,128]{1,0:T(8,128)(2,1)S(1)} %bitcast.29, ...), custom_call_target="tpu_custom_call" | custom-call | tf_op jit(solution)/shard_map/project/pallas_call | solution.py:121
  80.6 1.0 copy-done.3
  83.5 3.7 %couple.1.refs_4_ = f32[9,128,128]{2,1,0:T(8,128)S(1)} custom-call(s32[2]{0:T(128)S(1)} %pad_add_fusion.pos, s32[48]{0:T(128)S(1)} %reshape.23.partners, bf16[9,128,1024]{2,1,0:T(8,128)(2,1)S(1)} %project.1.refs_0_, bf16[1024,128]{1,0:T(8,128)(2,1)S(1)} %get-tuple-element.27.refs_1_.refs_6_, ...), custom_call_target="tpu_custom_call" | custom-call | tf_op jit(solution)/shard_map/couple/pallas_call | solution.py:201
  87.3 3.8 %project_last.1.refs_5_ = bf16[3,128,1024]{2,1,0:T(8,128)(2,1)S(1)} custom-call(s32[2]{0:T(128)S(1)} %pad_add_fusion.pos, s32[288]{0:T(512)S(1)} %reshape.24.cols, s32[96]{0:T(128)S(1)} %reshape.25.counts, bf16[3,32,3,128,128]{4,3,2,1,0:T(8,128)(2,1)} %potential.3, bf16[1024,128]{1,0:T(8,128)(2,1)S(1)} %collective-permute-done.6.refs_4_.refs_0_.refs_9_, ...), custom_call_target="tpu_custom_call" | custom-call | tf_op jit(solution)/shard_map/project_last/pallas_call | solution.py:121
  91.1 3.6 %couple_last.1 = f32[2,12,64,128]{3,2,1,0:T(8,128)S(1)} custom-call(s32[2]{0:T(128)S(1)} %pad_add_fusion.pos, s32[48]{0:T(128)S(1)} %reshape.23.partners, bf16[9,128,1024]{2,1,0:T(8,128)(2,1)S(1)} %project.1.refs_0_, bf16[1024,128]{1,0:T(8,128)(2,1)S(1)} %copy-done.17, bf16[2048,128]{1,0:T(8,128)(2,1)} %collective-permute-done.15.refs_2_.refs_17_, ...), custom_call_target="tpu_custom_call" | custom-call | tf_op jit(solution)/shard_map/couple_last/pallas_call | solution.py:201
  94.9 1.7 %collective-permute-done.22 = f32[12,64,128]{2,1,0:T(8,128)S(1)} collective-permute-done((f32[12,64,128]{2,1,0:T(8,128)S(1)}, f32[12,64,128]{2,1,0:T(8,128)S(1)}, u32[]{:S(2)}, u32[]{:S(2)}) %collective-permute-start.22) | collective-permute-done | bytes 393248 | tf_op jit(solution)/shard_map/ppermute | solution.py:234
  96.6 2.8 %collective-permute-start.25 = (bf16[3,64,128]{2,1,0:T(8,128)(2,1)S(1)}, bf16[3,64,128]{2,1,0:T(8,128)(2,1)S(1)}, u32[]{:S(2)}, u32[]{:S(2)}) collective-permute-start(bf16[3,64,128]{2,1,0:T(8,128)(2,1)S(1)} %get-tuple-element.54), channel_id=1, source_target_pairs={{0,10},{2,8},{4,14},{6,12},{8,2},{10,0},{12,6},{14,4},{16,26},{18,... | collective-permute-start | bytes 147464 | tf_op jit(solution)/shard_map/ppermute | solution.py:231
  99.6 1.4 %collective-permute-start.23 = (bf16[3,64,128]{2,1,0:T(8,128)(2,1)S(1)}, bf16[3,64,128]{2,1,0:T(8,128)(2,1)S(1)}, u32[]{:S(2)}, u32[]{:S(2)}) collective-permute-start(bf16[3,64,128]{2,1,0:T(8,128)(2,1)S(1)} %get-tuple-element.53), channel_id=1, source_target_pairs={{0,2},{2,0},{4,6},{6,4},{8,10},{10,8},{12,14},{14,12},{16,18},{18,... | collective-permute-start | bytes 147464 | tf_op jit(solution)/shard_map/ppermute | solution.py:231
  101.7 1.8 %collective-permute-done.24 = bf16[3,64,128]{2,1,0:T(8,128)(2,1)S(1)} collective-permute-done((bf16[3,64,128]{2,1,0:T(8,128)(2,1)S(1)}, bf16[3,64,128]{2,1,0:T(8,128)(2,1)S(1)}, u32[]{:S(2)}, u32[]{:S(2)}) %collective-permute-start.24) | collective-permute-done | bytes 49184 | tf_op jit(solution)/shard_map/ppermute | solution.py:231
  (106 shorter events, 18.6 us)
Async XLA Ops:
  1.3 9.3 %collective-permute-start = (bf16[1024,128]{1,0:T(8,128)(2,1)S(1)}, bf16[1024,128]{1,0:T(8,128)(2,1)S(1)}, u32[]{:S(2)}, u32[]{:S(2)}) collective-permute-start(bf16[1024,128]{1,0:T(8,128)(2,1)S(1)} %get-tuple-element.28), channel_id=1, source_target_pairs={{0,2},{2,0},{4,6},{6,4},{8,10},{10,8},{12,14},{14,12},{16,18},{18,... | collective-permute-start | bytes 786440 | tf_op jit(solution)/shard_map/ppermute | solution.py:231
  4.3 7.8 %collective-permute-start.1 = (bf16[1024,128]{1,0:T(8,128)(2,1)S(1)}, bf16[1024,128]{1,0:T(8,128)(2,1)S(1)}, u32[]{:S(2)}, u32[]{:S(2)}) collective-permute-start(bf16[1024,128]{1,0:T(8,128)(2,1)S(1)} %get-tuple-element.27.refs_1_.refs_6_), channel_id=1, source_target_pairs={{0,4},{2,6},{4,0},{6,2},{8,12},{10,14},{12,8},{14,10},{16,20},{18,... | collective-permute-start | bytes 786440 | tf_op jit(solution)/shard_map/ppermute | solution.py:231
  5.8 18.8 %collective-permute-start.3 = (bf16[2048,128]{1,0:T(8,128)(2,1)S(1)}, bf16[2048,128]{1,0:T(8,128)(2,1)S(1)}, u32[]{:S(2)}, u32[]{:S(2)}) collective-permute-start(bf16[2048,128]{1,0:T(8,128)(2,1)S(1)} %pad_maximum_fusion.2), channel_id=1, source_target_pairs={{0,8},{2,10},{4,12},{6,14},{8,0},{10,2},{12,4},{14,6},{16,24},{18,... | collective-permute-start | bytes 1572872 | tf_op jit(solution)/shard_map/ppermute | solution.py:231
  7.5 22.2 %collective-permute-start.9 = (bf16[1024,128]{1,0:T(8,128)(2,1)S(1)}, bf16[1024,128]{1,0:T(8,128)(2,1)S(1)}, u32[]{:S(2)}, u32[]{:S(2)}) collective-permute-start(bf16[1024,128]{1,0:T(8,128)(2,1)S(1)} %get-tuple-element.27.refs_1_.refs_6_), channel_id=1, source_target_pairs={{0,16},{2,18},{4,20},{6,22},{8,24},{10,26},{12,28},{14,30},{16,0},... | collective-permute-start | bytes 786440 | tf_op jit(solution)/shard_map/ppermute | solution.py:231
  12.0 12.6 %copy-start.11 = (bf16[1024,128]{1,0:T(8,128)(2,1)}, bf16[1024,128]{1,0:T(8,128)(2,1)S(1)}, u32[]{:S(2)}) copy-start(bf16[1024,128]{1,0:T(8,128)(2,1)S(1)} %collective-permute-done.1.refs_5_.refs_10_) | copy-start | bytes 786436
  12.1 23.8 %copy-start = (bf16[1,4096,128]{2,1,0:T(8,128)(2,1)S(1)}, bf16[1,4096,128]{2,1,0:T(8,128)(2,1)}, u32[]{:S(2)}) copy-start(bf16[1,4096,128]{2,1,0:T(8,128)(2,1)} %param.6) | copy-start | bytes 3145732
  12.1 23.8 %collective-permute-start.2 = (bf16[3072,128]{1,0:T(8,128)(2,1)S(1)}, bf16[3072,128]{1,0:T(8,128)(2,1)S(1)}, u32[]{:S(2)}, u32[]{:S(2)}) collective-permute-start(bf16[3072,128]{1,0:T(8,128)(2,1)S(1)} %pad_maximum_fusion), channel_id=1, source_target_pairs={{0,2},{2,0},{4,6},{6,4},{8,10},{10,8},{12,14},{14,12},{16,18},{18,... | collective-permute-start | bytes 2359304 | tf_op jit(solution)/shard_map/ppermute | solution.py:231
  24.6 28.9 %copy-start.5 = (bf16[2048,128]{1,0:T(8,128)(2,1)}, bf16[2048,128]{1,0:T(8,128)(2,1)S(1)}, u32[]{:S(2)}) copy-start(bf16[2048,128]{1,0:T(8,128)(2,1)S(1)} %collective-permute-done.3.refs_3_) | copy-start | bytes 1572868
  24.7 22.7 %collective-permute-start.4 = (bf16[2048,128]{1,0:T(8,128)(2,1)S(1)}, bf16[2048,128]{1,0:T(8,128)(2,1)S(1)}, u32[]{:S(2)}, u32[]{:S(2)}) collective-permute-start(bf16[2048,128]{1,0:T(8,128)(2,1)S(1)} %pad_maximum_fusion.3), channel_id=1, source_target_pairs={{0,8},{2,10},{4,12},{6,14},{8,0},{10,2},{12,4},{14,6},{16,24},{18,... | collective-permute-start | bytes 1572872 | tf_op jit(solution)/shard_map/ppermute | solution.py:231
  24.8 11.1 %collective-permute-start.6 = (bf16[1024,128]{1,0:T(8,128)(2,1)S(1)}, bf16[1024,128]{1,0:T(8,128)(2,1)S(1)}, u32[]{:S(2)}, u32[]{:S(2)}) collective-permute-start(bf16[1024,128]{1,0:T(8,128)(2,1)S(1)} %get-tuple-element.29), channel_id=1, source_target_pairs={{0,2},{2,0},{4,6},{6,4},{8,10},{10,8},{12,14},{14,12},{16,18},{18,... | collective-permute-start | bytes 786440 | tf_op jit(solution)/shard_map/ppermute | solution.py:231
  25.4 38.3 %copy-start.29 = (s32[3,32,3]{1,2,0:T(4,128)S(1)}, s32[3,32,3]{1,2,0:T(4,128)}, u32[]{:S(2)}) copy-start(s32[3,32,3]{1,2,0:T(4,128)} %param.8) | copy-start | bytes 3460
  25.4 38.5 %copy-start.30 = (s32[3,32]{1,0:T(4,128)S(1)}, s32[3,32]{1,0:T(4,128)}, u32[]{:S(2)}) copy-start(s32[3,32]{1,0:T(4,128)} %param.9) | copy-start | bytes 1156
  25.5 26.0 %collective-permute-start.7 = (bf16[2048,128]{1,0:T(8,128)(2,1)S(1)}, bf16[2048,128]{1,0:T(8,128)(2,1)}, u32[]{:S(2)}, u32[]{:S(2)}) collective-permute-start(bf16[2048,128]{1,0:T(8,128)(2,1)S(1)} %constant_dynamic-update-slice_fusion), channel_id=1, source_target_pairs={{0,16},{2,18},{4,20},{6,22},{8,24},{10,26},{12,28},{14,30},{16,0},... | collective-permute-start | bytes 1572872 | tf_op jit(solution)/shard_map/ppermute | solution.py:231
  29.7 21.8 %collective-permute-start.8 = (bf16[2048,128]{1,0:T(8,128)(2,1)S(1)}, bf16[2048,128]{1,0:T(8,128)(2,1)S(1)}, u32[]{:S(2)}, u32[]{:S(2)}) collective-permute-start(bf16[2048,128]{1,0:T(8,128)(2,1)S(1)} %constant_dynamic-update-slice_fusion), channel_id=1, source_target_pairs={{0,4},{2,6},{4,0},{6,2},{8,12},{10,14},{12,8},{14,10},{16,20},{18,... | collective-permute-start | bytes 1572872 | tf_op jit(solution)/shard_map/ppermute | solution.py:231
  35.9 20.8 %collective-permute-start.5 = (bf16[4096,128]{1,0:T(8,128)(2,1)S(1)}, bf16[4096,128]{1,0:T(8,128)(2,1)S(1)}, u32[]{:S(2)}, u32[]{:S(2)}) collective-permute-start(bf16[4096,128]{1,0:T(8,128)(2,1)S(1)} %bitcast.28), channel_id=1, source_target_pairs={{0,1},{1,0},{2,3},{3,2},{4,5},{5,4},{6,7},{7,6},{8,9},{9,8},{10,11... | collective-permute-start | bytes 3145736 | tf_op jit(solution)/shard_map/ppermute | solution.py:234
  35.9 16.4 %collective-permute-start.10 = (bf16[1024,128]{1,0:T(8,128)(2,1)S(1)}, bf16[1024,128]{1,0:T(8,128)(2,1)S(1)}, u32[]{:S(2)}, u32[]{:S(2)}) collective-permute-start(bf16[1024,128]{1,0:T(8,128)(2,1)S(1)} %collective-permute-done.9.refs_8_.refs_13_), channel_id=1, source_target_pairs={{0,4},{2,6},{4,0},{6,2},{8,12},{10,14},{12,8},{14,10},{16,20},{18,... | collective-permute-start | bytes 786440 | tf_op jit(solution)/shard_map/ppermute | solution.py:231
  53.0 6.2 %collective-permute-start.11 = (bf16[1024,128]{1,0:T(8,128)(2,1)S(1)}, bf16[1024,128]{1,0:T(8,128)(2,1)S(1)}, u32[]{:S(2)}, u32[]{:S(2)}) collective-permute-start(bf16[1024,128]{1,0:T(8,128)(2,1)S(1)} %collective-permute-done.refs_1_.refs_2_.refs_7_), channel_id=1, source_target_pairs={{0,1},{1,0},{2,3},{3,2},{4,5},{5,4},{6,7},{7,6},{8,9},{9,8},{10,11... | collective-permute-start | bytes 786440 | tf_op jit(solution)/shard_map/ppermute | solution.py:234
  53.0 11.1 %collective-permute-start.12 = (bf16[3072,128]{1,0:T(8,128)(2,1)S(1)}, bf16[3072,128]{1,0:T(8,128)(2,1)S(1)}, u32[]{:S(2)}, u32[]{:S(2)}) collective-permute-start(bf16[3072,128]{1,0:T(8,128)(2,1)S(1)} %collective-permute-done.2.refs_2_), channel_id=1, source_target_pairs={{0,1},{1,0},{2,3},{3,2},{4,5},{5,4},{6,7},{7,6},{8,9},{9,8},{10,11... | collective-permute-start | bytes 2359304 | tf_op jit(solution)/shard_map/ppermute | solution.py:234
  54.4 6.0 %collective-permute-start.13 = (bf16[2048,128]{1,0:T(8,128)(2,1)S(1)}, bf16[2048,128]{1,0:T(8,128)(2,1)S(1)}, u32[]{:S(2)}, u32[]{:S(2)}) collective-permute-start(bf16[2048,128]{1,0:T(8,128)(2,1)S(1)} %collective-permute-done.3.refs_3_), channel_id=1, source_target_pairs={{0,1},{1,0},{2,3},{3,2},{4,5},{5,4},{6,7},{7,6},{8,9},{9,8},{10,11... | collective-permute-start | bytes 1572872 | tf_op jit(solution)/shard_map/ppermute | solution.py:234
  54.4 6.9 %collective-permute-start.14 = (bf16[2048,128]{1,0:T(8,128)(2,1)S(1)}, bf16[2048,128]{1,0:T(8,128)(2,1)S(1)}, u32[]{:S(2)}, u32[]{:S(2)}) collective-permute-start(bf16[2048,128]{1,0:T(8,128)(2,1)S(1)} %collective-permute-done.4.refs_4_), channel_id=1, source_target_pairs={{0,1},{1,0},{2,3},{3,2},{4,5},{5,4},{6,7},{7,6},{8,9},{9,8},{10,11... | collective-permute-start | bytes 1572872 | tf_op jit(solution)/shard_map/ppermute | solution.py:234
  57.7 21.7 %collective-permute-start.19 = (bf16[3072,128]{1,0:T(8,128)(2,1)}, bf16[3072,128]{1,0:T(8,128)(2,1)}, u32[]{:S(2)}, u32[]{:S(2)}) collective-permute-start(bf16[3072,128]{1,0:T(8,128)(2,1)} %pad_maximum_fusion.1), channel_id=1, source_target_pairs={{0,2},{2,0},{4,6},{6,4},{8,10},{10,8},{12,14},{14,12},{16,18},{18,... | collective-permute-start | bytes 2359304 | tf_op jit(solution)/shard_map/ppermute | solution.py:231
  60.0 19.5 %collective-permute-start.15 = (bf16[2048,128]{1,0:T(8,128)(2,1)}, bf16[2048,128]{1,0:T(8,128)(2,1)}, u32[]{:S(2)}, u32[]{:S(2)}) collective-permute-start(bf16[2048,128]{1,0:T(8,128)(2,1)} %collective-permute-done.7.refs_9_.refs_14_), channel_id=1, source_target_pairs={{0,4},{2,6},{4,0},{6,2},{8,12},{10,14},{12,8},{14,10},{16,20},{18,... | collective-permute-start | bytes 1572872 | tf_op jit(solution)/shard_map/ppermute | solution.py:231
  61.3 17.9 %collective-permute-start.16 = (bf16[1024,128]{1,0:T(8,128)(2,1)S(1)}, bf16[1024,128]{1,0:T(8,128)(2,1)}, u32[]{:S(2)}, u32[]{:S(2)}) collective-permute-start(bf16[1024,128]{1,0:T(8,128)(2,1)S(1)} %collective-permute-done.6.refs_4_.refs_0_.refs_9_), channel_id=1, source_target_pairs={{0,16},{2,18},{4,20},{6,22},{8,24},{10,26},{12,28},{14,30},{16,0},... | collective-permute-start | bytes 786440 | tf_op jit(solution)/shard_map/ppermute | solution.py:231
  62.2 17.3 %collective-permute-start.18 = (bf16[1024,128]{1,0:T(8,128)(2,1)S(1)}, bf16[1024,128]{1,0:T(8,128)(2,1)}, u32[]{:S(2)}, u32[]{:S(2)}) collective-permute-start(bf16[1024,128]{1,0:T(8,128)(2,1)S(1)} %collective-permute-done.6.refs_4_.refs_0_.refs_9_), channel_id=1, source_target_pairs={{0,4},{2,6},{4,0},{6,2},{8,12},{10,14},{12,8},{14,10},{16,20},{18,... | collective-permute-start | bytes 786440 | tf_op jit(solution)/shard_map/ppermute | solution.py:231
  79.5 7.8 %collective-permute-start.21 = (bf16[3072,128]{1,0:T(8,128)(2,1)}, bf16[3072,128]{1,0:T(8,128)(2,1)}, u32[]{:S(2)}, u32[]{:S(2)}) collective-permute-start(bf16[3072,128]{1,0:T(8,128)(2,1)} %collective-permute-done.19.refs_1_), channel_id=1, source_target_pairs={{0,1},{1,0},{2,3},{3,2},{4,5},{5,4},{6,7},{7,6},{8,9},{9,8},{10,11... | collective-permute-start | bytes 2359304 | tf_op jit(solution)/shard_map/ppermute | solution.py:234
  79.5 7.8 %collective-permute-start.20 = (bf16[1024,128]{1,0:T(8,128)(2,1)S(1)}, bf16[1024,128]{1,0:T(8,128)(2,1)}, u32[]{:S(2)}, u32[]{:S(2)}) collective-permute-start(bf16[1024,128]{1,0:T(8,128)(2,1)S(1)} %collective-permute-done.6.refs_4_.refs_0_.refs_9_), channel_id=1, source_target_pairs={{0,1},{1,0},{2,3},{3,2},{4,5},{5,4},{6,7},{7,6},{8,9},{9,8},{10,11... | collective-permute-start | bytes 786440 | tf_op jit(solution)/shard_map/ppermute | solution.py:234
  80.0 11.1 %collective-permute-start.17 = (bf16[1024,128]{1,0:T(8,128)(2,1)}, bf16[1024,128]{1,0:T(8,128)(2,1)}, u32[]{:S(2)}, u32[]{:S(2)}) collective-permute-start(bf16[1024,128]{1,0:T(8,128)(2,1)} %collective-permute-done.16.refs_10_.refs_15_), channel_id=1, source_target_pairs={{0,4},{2,6},{4,0},{6,2},{8,12},{10,14},{12,8},{14,10},{16,20},{18,... | collective-permute-start | bytes 786440 | tf_op jit(solution)/shard_map/ppermute | solution.py:231
  94.7 8.9 %copy-start.28 = (f32[3,1,64,128]{3,2,1,0:T(8,128)S(1)}, f32[3,1,64,128]{3,2,1,0:T(8,128)}, u32[]{:S(2)}) copy-start(f32[3,1,64,128]{3,2,1,0:T(8,128)} %param.11) | copy-start | bytes 294916
  94.8 1.8 %collective-permute-start.22 = (f32[12,64,128]{2,1,0:T(8,128)S(1)}, f32[12,64,128]{2,1,0:T(8,128)S(1)}, u32[]{:S(2)}, u32[]{:S(2)}) collective-permute-start(f32[12,64,128]{2,1,0:T(8,128)S(1)} %slice_bitcast_fusion), channel_id=1, source_target_pairs={{0,1},{1,0},{2,3},{3,2},{4,5},{5,4},{6,7},{7,6},{8,9},{9,8},{10,11... | collective-permute-start | bytes 1179656 | tf_op jit(solution)/shard_map/ppermute | solution.py:234
  96.6 5.1 %collective-permute-start.25 = (bf16[3,64,128]{2,1,0:T(8,128)(2,1)S(1)}, bf16[3,64,128]{2,1,0:T(8,128)(2,1)S(1)}, u32[]{:S(2)}, u32[]{:S(2)}) collective-permute-start(bf16[3,64,128]{2,1,0:T(8,128)(2,1)S(1)} %get-tuple-element.54), channel_id=1, source_target_pairs={{0,10},{2,8},{4,14},{6,12},{8,2},{10,0},{12,6},{14,4},{16,26},{18,... | collective-permute-start | bytes 147464 | tf_op jit(solution)/shard_map/ppermute | solution.py:231
  99.5 4.1 %collective-permute-start.24 = (bf16[3,64,128]{2,1,0:T(8,128)(2,1)S(1)}, bf16[3,64,128]{2,1,0:T(8,128)(2,1)S(1)}, u32[]{:S(2)}, u32[]{:S(2)}) collective-permute-start(bf16[3,64,128]{2,1,0:T(8,128)(2,1)S(1)} %get-tuple-element.55), channel_id=1, source_target_pairs={{0,8},{2,10},{4,12},{6,14},{8,0},{10,2},{12,4},{14,6},{16,24},{18,... | collective-permute-start | bytes 147464 | tf_op jit(solution)/shard_map/ppermute | solution.py:231
  99.6 4.1 %collective-permute-start.23 = (bf16[3,64,128]{2,1,0:T(8,128)(2,1)S(1)}, bf16[3,64,128]{2,1,0:T(8,128)(2,1)S(1)}, u32[]{:S(2)}, u32[]{:S(2)}) collective-permute-start(bf16[3,64,128]{2,1,0:T(8,128)(2,1)S(1)} %get-tuple-element.53), channel_id=1, source_target_pairs={{0,2},{2,0},{4,6},{6,4},{8,10},{10,8},{12,14},{14,12},{16,18},{18,... | collective-permute-start | bytes 147464 | tf_op jit(solution)/shard_map/ppermute | solution.py:231
  (26 other events, 38.1 us)

commit v7 on v6

--- a/solution.py
+++ b/solution.py
@@ -17,6 +17,8 @@
 SECOND = ("p3", "r1", "r2", "s2.1", "s1.1", "s3.0")
 WAITS = {
     **dict.fromkeys(FIRST, ()),
+    "s2.0": (),
+    "t1o": ("s2.0",),
     "r1": ("c0", "s1.0"),
     **dict.fromkeys(("p3", "r2", "s2.1", "s1.1"), FIRST),
     "s3.0": ("p3",),
@@ -48,6 +50,40 @@
 
 def gathered(value, bits):
     return sum((((value >> bit) & 1) << i for i, bit in enumerate(bits)), 0 * value)
+
+
+def stitch_kernel(inside, places, pos, *refs):
+    sources, (out, sems) = refs[: len(places)], refs[len(places) :]
+    rows = out.shape[0] // len(places)
+    chunk = gathered(pos[0], inside)
+    copies = []
+    for i, (source, (at, moving)) in enumerate(zip(sources, places)):
+        start = ((chunk ^ at) if moving else at) * rows
+        copies.append(
+            pltpu.make_async_copy(
+                source.at[pl.ds(pl.multiple_of(start, rows), rows)],
+                out.at[pl.ds(i * rows, rows)],
+                sems.at[i],
+            )
+        )
+    for copy in copies:
+        copy.start()
+    for copy in copies:
+        copy.wait()
+
+
+def stitch(pos, rows, sources, places, inside):
+    bands = sources[0].shape[1]
+    return pl.pallas_call(
+        functools.partial(stitch_kernel, inside, places),
+        out_shape=jax.ShapeDtypeStruct((len(places) * rows, bands), sources[0].dtype),
+        in_specs=[SMEM] + [ANY] * len(sources),
+        out_specs=ANY,
+        scratch_shapes=[pltpu.SemaphoreType.DMA((len(places),))],
+        compiler_params=pltpu.CompilerParams(vmem_limit_bytes=2**20),
+        cost_estimate=pl.CostEstimate(flops=0, bytes_accessed=0, transcendentals=0),
+        name="stitch",
+    )(pos, *[in_hbm(x) if p[1] else in_vmem(x) for x, p in zip(sources, places)])
 
 
 def project_kernel(orders, inside, halves, pos, cols, counts, potential, *refs):
@@ -132,7 +168,7 @@
         compiler_params=pltpu.CompilerParams(vmem_limit_bytes=held + made + SPARE_VMEM),
         cost_estimate=pl.CostEstimate(flops=0, bytes_accessed=0, transcendentals=0),
         name=name,
-    )(pos, cols, counts, in_hbm(potential), *[in_vmem(x) for x in sources])
+    )(pos, cols, counts, in_hbm(potential), *sources)
 
 
 def couple_kernel(jobs, last, inside, outside, halves, pos, partners, *refs):
@@ -140,9 +176,9 @@
     points = group << len(outside)
     refs, (out, total) = refs[:-2], refs[-2:]
     me, half = pos[0], pos[1]
-    for start, pairs, first, count, resumed in jobs:
+    for start, pairs, first, counts, resumed in jobs:
         projected, refs = refs[0], refs[1:]
-        parts, refs = refs[:count], refs[count:]
+        parts, refs = refs[: len(counts)], refs[len(counts) :]
         rows = projected.shape[2]
         modes = total.shape[0] // group
         if resumed:
@@ -151,14 +187,20 @@
         else:
             total[start : start + pairs] = jnp.zeros((pairs,) + total.shape[1:], jnp.float32)
 
-        def add(pair, carry, start=start, first=first, parts=parts, projected=projected):
+        def add(
+            pair,
+            carry,
+            start=start,
+            first=first,
+            parts=tuple(zip(parts, counts)),
+            projected=projected,
+        ):
             point = lax.div(pair + start, modes)
             mine = me ^ spread(point, inside)
             away = partners[lax.rem(pair, modes) * points + mine] ^ me
             at = (gathered(away, outside) - first) * group + gathered(away, inside)
             base = 0
-            for part in parts:
-                held = part.shape[0] // rows
+            for part, held in parts:
                 here = at - base
                 base += held
 
@@ -191,8 +233,9 @@
     start = 0
     for projected, first, parts, before in work:
         pairs, bands, rows = projected.shape
-        jobs.append((start, pairs, first, len(parts), before is not None))
-        values += [projected] + parts + ([] if before is None else [before])
+        jobs.append((start, pairs, first, [count for _, count in parts], before is not None))
+        values += [projected] + [value for value, _ in parts]
+        values += [] if before is None else [before]
         start += pairs
     total = start if last else (start // (group - 1)) * group if group > 1 else start
     shape = (halves, start, bands // halves, bands) if last else (start, bands, bands)
@@ -223,9 +266,9 @@
         me = lax.axis_index("ka").astype(jnp.int32)
         chunk = gathered(me, inside)
         pos = jnp.stack([me, lax.axis_index("orb").astype(jnp.int32)])
-        cols = block_cols.reshape(-1)
-        counts = block_counts.reshape(-1)
-        pairing = partners.reshape(-1)
+        pos, cols, counts, pairing, own = lax.optimization_barrier(
+            (pos, block_cols.reshape(-1), block_counts.reshape(-1), partners.reshape(-1), own)
+        )
 
         def swap(value, mask):
             return lax.ppermute(value, "ka", [(i, i ^ mask) for i in range(points)])
@@ -235,20 +278,20 @@
                 value, "orb", [(i, (i + shift) % halves) for i in range(halves)]
             )
 
-        def chunk_for(point):
-            return lax.dynamic_slice_in_dim(own, (chunk ^ point) * rows, rows, 0)
-
         plan = {}
         done = {}
 
         def get(name):
             if name not in done:
-                inputs, combine, move = plan[name]
-                inputs = list(inputs())
+                inputs, move = plan[name]
+                inputs = [item if isinstance(item, tuple) else (item, None) for item in inputs()]
+                places = [item[1:] for item in inputs]
+                inputs = [item[0] for item in inputs]
                 waits = [done[other] for other in WAITS.get(name, ()) if other in done]
                 if waits:
                     inputs = lax.optimization_barrier((*inputs, *waits))[: len(inputs)]
-                done[name] = move(combine(inputs))
+                whole = places[0] == (None,)
+                done[name] = move(inputs[0] if whole else joined(places, inputs))
             return done[name]
 
         far = 1 << (len(outside) - 1)
@@ -256,40 +299,37 @@
         sizes = {}
         orders = {}
 
-        def joined(values):
-            return jnp.concatenate(values, axis=0) if values[1:] else values[0]
-
-        def section(value, at):
-            if value.shape[0] == rows:
-                return value
-            return value[at * rows : (at + 1) * rows]
+        mine = lax.dynamic_slice_in_dim(own, chunk * rows, rows, 0)
 
         def part(j):
             if j == 0:
-                return chunk_for(0)
+                return mine, 0, False
             top = j.bit_length() - 1
-            return section(get(f"c{top}"), 0) if j == 1 << top else get(f"p{j}")
+            return (get(f"c{top}") if j == 1 << top else get(f"p{j}")), 0, False
 
         def held(key, j):
             if key == 0:
-                return chunk_for(j)
+                return own, j, True
             if j in orders[key]:
-                return section(get(f"r{key}"), orders[key].index(j))
-            return section(get(f"c{key.bit_length() - 1}"), j) if j else part(key)
+                return get(f"r{key}"), orders[key].index(j), False
+            return (get(f"c{key.bit_length() - 1}"), j, False) if j else part(key)
+
+        def joined(places, values):
+            if len(values) == 1 and values[0].shape[0] == rows:
+                return values[0]
+            return stitch(pos, rows, values, places, inside)
 
         for j in range(1, group):
             top = j.bit_length() - 1
             lower = j ^ (1 << top)
             if lower == 0:
                 plan[f"c{top}"] = (
-                    lambda j=j: [chunk_for(j + k) for k in range(j)],
-                    joined,
+                    lambda j=j: [held(0, j + k) for k in range(j)],
                     functools.partial(swap, mask=spread(j, inside)),
                 )
             else:
                 plan[f"p{j}"] = (
-                    lambda top=top, lower=lower: [section(get(f"c{top}"), lower)],
-                    joined,
+                    lambda top=top, lower=lower: [(get(f"c{top}"), lower, False)],
                     functools.partial(swap, mask=spread(lower, inside)),
                 )
         for key in range(1, 2 * far):
@@ -303,7 +343,6 @@
                     source = lambda js=js: [part(j) for j in js]
                 plan[f"s{key}.{i}"] = (
                     source,
-                    joined,
                     functools.partial(swap, mask=1 << outside[bit.bit_length() - 1]),
                 )
         for key in sorted(range(1, group), key=lambda k: (bin(k).count("1"), k)):
@@ -314,7 +353,6 @@
             orders[key] = [j ^ bit for j in send]
             plan[f"r{key}"] = (
                 lambda before=before, send=send: [held(before, j) for j in send],
-                joined,
                 functools.partial(swap, mask=spread(bit, inside)),
             )
         def rows_of(key):
@@ -325,10 +363,10 @@
 
         for shift in range(1, halves):
             turn = functools.partial(rotate, shift=shift)
-            plan[f"t{shift}o"] = (lambda: [own], joined, turn)
+            plan[f"t{shift}o"] = (lambda: [own], turn)
             for key in range(1, group):
                 for name, _ in rows_of(key):
-                    plan[f"t{shift}{name}"] = (lambda name=name: [get(name)], joined, turn)
+                    plan[f"t{shift}{name}"] = (lambda name=name: [get(name)], turn)
 
         def projection(name, keys):
             values = []
@@ -337,11 +375,11 @@
                 away = f"t{shift}" if shift else ""
                 for place, key in enumerate(keys):
                     if key == 0:
-                        values.append(get(away + "o") if shift else own)
+                        values.append(in_vmem(get(away + "o")) if shift else in_hbm(own))
                         places.append((place, shift, [None] * group))
                         continue
                     for source, order in rows_of(key):
-                        values.append(get(away + source))
+                        values.append(in_vmem(get(away + source)))
                         places.append((place, shift, order))
             return project(
                 name, pos, cols, counts, potential, values, places, inside, halves
@@ -349,7 +387,6 @@
 
         plan["q"] = (
             lambda: [projection("project", range(group - 1))],
-            joined,
             lambda value: value,
         )
         for name in WAITS:
@@ -357,10 +394,11 @@
                 get(name)
         projected = get("q")
         projected_last = projection("project_last", [group - 1])
-        early = [part(j) for j in range(group)]
+        early = [(part(j)[0], 1) for j in range(group)]
         for key in range(1, 2 * far - 1):
-            early += [get(f"s{key}.{i}") for i in range(len(sizes[key]))]
-        late = [get(f"s{2 * far - 1}.{i}") for i in range(len(sizes[2 * far - 1]))]
+            early += [(get(f"s{key}.{i}"), len(js)) for i, js in enumerate(sizes[key])]
+        key = 2 * far - 1
+        late = [(get(f"s{key}.{i}"), len(js)) for i, js in enumerate(sizes[key])]
         total = couple(
             "couple",
             False,

time: 105 us -> 105 us (level)
  local copies, waits for them, and re-layouts: 22.9 us -> 3.49 us
  waiting for transfers between devices: 37.7 us -> 53.9 us
  Pallas kernels: 15.4 us -> 21.5 us
  starting transfers between devices: 26.1 us -> 25 us
  other arithmetic: 1.86 us -> 0.81 us
    unnamed x66 -> x3, local copies, waits for them, and re-layouts: 21.2 us -> 0.79 us
    ppermute x18, waiting for transfers between devices: 36 us -> 51.7 us  [swap(): return lax.ppermute(value, 'ka', [(i, i ^ mask) for i in range(points)])]
    pallas_call x0 -> x7, Pallas kernels: none -> 8.16 us  [stitch(): pl.pallas_call(functools.partial(stitch_kernel, inside, places), out_shap...]
    pallas_call x2, Pallas kernels: 7.35 us -> 5.48 us  [couple(): pl.pallas_call(functools.partial(couple_kernel, jobs, last, inside, outsi...]
    reshape x3, local copies, waits for them, and re-layouts: 0.33 us -> 1.7 us  [the longest x1 0.77 us: per_device(): block_counts.reshape(-1)]
    ppermute x18, starting transfers between devices: 24.5 us -> 23.4 us  [swap(): return lax.ppermute(value, 'ka', [(i, i ^ mask) for i in range(points)])]
    concatenate x4 -> x0, other arithmetic: 1.05 us -> none  [joined(): return jnp.concatenate(values, axis=0) if values[1:] else values[0]]
  transfers between devices with their start and end apart: 26 -> 26, of which waited for: 11 -> 13; matrix products, arithmetic and copies ran while one was open for 2% -> 1% of each run, Pallas kernels for 11% -> 17%
where the time goes in v7:
time: 105 us
  waiting for transfers between devices  53.9 us (51%)
  starting transfers between devices  25 us (24%)
  Pallas kernels  21.5 us (20%)
  local copies, waits for them, and re-layouts  3.49 us (3%)
    ppermute x18, waiting for transfers between devices, swap(): return lax.ppermute(value, 'ka', [(i, i ^ mask) for i in range(points)])  51.7 us
    ppermute x18, starting transfers between devices, swap(): return lax.ppermute(value, 'ka', [(i, i ^ mask) for i in range(points)])  23.4 us
    pallas_call x7, Pallas kernels, stitch(): pl.pallas_call(functools.partial(stitch_kernel, inside, places), out_shap...  8.16 us
    pallas_call x2, Pallas kernels, project(): pl.pallas_call(functools.partial(project_kernel, orders, inside, halves),...  7.9 us
    pallas_call x2, Pallas kernels, couple(): pl.pallas_call(functools.partial(couple_kernel, jobs, last, inside, outsi...  5.48 us
    ppermute x8, waiting for transfers between devices, rotate(): lax.ppermute(value, 'orb', [(i, (i + shift) % halves) for i in range(halv...  2.14 us
  transfers between devices with their start and end apart: 26, of which 13 were waited for; matrix products, arithmetic and copies ran while one was open for 1% of the time, Pallas kernels for 17%

profile of v7, /device:TPU:0, one launch (start us, length us, event | category | flops | bytes accessed | tf_op | source)
XLA Modules:
  0.0 104.9 jit_solution(7836165361098586271)
XLA Ops:
  0.0 0.8 copy.9
  2.6 1.5 %stitch.7 = bf16[1024,128]{1,0:T(8,128)(2,1)S(1)} custom-call(s32[2]{0:T(128)S(1)} %pad_add_fusion.pos, bf16[4096,128]{1,0:T(8,128)(2,1)} %bitcast.20), custom_call_target="tpu_custom_call" | custom-call | tf_op jit(solution)/shard_map/stitch/pallas_call | solution.py:77
  4.1 3.0 %collective-permute-start = (bf16[1024,128]{1,0:T(8,128)(2,1)S(1)}, bf16[1024,128]{1,0:T(8,128)(2,1)S(1)}, u32[]{:S(2)}, u32[]{:S(2)}) collective-permute-start(bf16[1024,128]{1,0:T(8,128)(2,1)S(1)} %stitch.7), channel_id=1, source_target_pairs={{0,2},{2,0},{4,6},{6,4},{8,10},{10,8},{12,14},{14,12},{16,18},{18,... | collective-permute-start | bytes 786440 | tf_op jit(solution)/shard_map/ppermute | solution.py:274
  7.1 1.0 constant_dynamic-slice_fusion.refs_1_.refs_6_
  8.0 1.6 %collective-permute-start.1 = (bf16[1024,128]{1,0:T(8,128)(2,1)S(1)}, bf16[1024,128]{1,0:T(8,128)(2,1)S(1)}, u32[]{:S(2)}, u32[]{:S(2)}) collective-permute-start(bf16[1024,128]{1,0:T(8,128)(2,1)S(1)} %constant_dynamic-slice_fusion.refs_1_.refs_6_), channel_id=1, source_target_pairs={{0,4},{2,6},{4,0},{6,2},{8,12},{10,14},{12,8},{14,10},{16,20},{18,... | collective-permute-start | bytes 786440 | tf_op jit(solution)/shard_map/ppermute | solution.py:274
  9.6 1.6 %stitch.9 = bf16[2048,128]{1,0:T(8,128)(2,1)S(1)} custom-call(s32[2]{0:T(128)S(1)} %pad_add_fusion.pos, bf16[4096,128]{1,0:T(8,128)(2,1)} %bitcast.22, bf16[4096,128]{1,0:T(8,128)(2,1)} %bitcast.23), custom_call_target="tpu_custom_call" | custom-call | tf_op jit(solution)/shard_map/stitch/pallas_call | solution.py:77
  11.2 1.6 %collective-permute-start.3 = (bf16[2048,128]{1,0:T(8,128)(2,1)S(1)}, bf16[2048,128]{1,0:T(8,128)(2,1)S(1)}, u32[]{:S(2)}, u32[]{:S(2)}) collective-permute-start(bf16[2048,128]{1,0:T(8,128)(2,1)S(1)} %stitch.9), channel_id=1, source_target_pairs={{0,8},{2,10},{4,12},{6,14},{8,0},{10,2},{12,4},{14,6},{16,24},{18,... | collective-permute-start | bytes 1572872 | tf_op jit(solution)/shard_map/ppermute | solution.py:274
  12.9 2.6 %collective-permute-start.5 = (bf16[1024,128]{1,0:T(8,128)(2,1)S(1)}, bf16[1024,128]{1,0:T(8,128)(2,1)S(1)}, u32[]{:S(2)}, u32[]{:S(2)}) collective-permute-start(bf16[1024,128]{1,0:T(8,128)(2,1)S(1)} %constant_dynamic-slice_fusion.refs_1_.refs_6_), channel_id=1, source_target_pairs={{0,16},{2,18},{4,20},{6,22},{8,24},{10,26},{12,28},{14,30},{16,0},... | collective-permute-start | bytes 786440 | tf_op jit(solution)/shard_map/ppermute | solution.py:274
  15.9 1.7 %stitch.8 = bf16[3072,128]{1,0:T(8,128)(2,1)S(1)} custom-call(s32[2]{0:T(128)S(1)} %pad_add_fusion.pos, bf16[4096,128]{1,0:T(8,128)(2,1)} %bitcast.24, bf16[4096,128]{1,0:T(8,128)(2,1)} %bitcast.25, bf16[4096,128]{1,0:T(8,128)(2,1)} %bitcast.26), custom_call_target="tpu_custom_call" | custom-call | tf_op jit(solution)/shard_map/stitch/pallas_call | solution.py:77
  17.9 11.2 %collective-permute-done.5.refs_8_.refs_13_ = bf16[1024,128]{1,0:T(8,128)(2,1)S(1)} collective-permute-done((bf16[1024,128]{1,0:T(8,128)(2,1)S(1)}, bf16[1024,128]{1,0:T(8,128)(2,1)S(1)}, u32[]{:S(2)}, u32[]{:S(2)}) %collective-permute-start.5) | collective-permute-done | bytes 262176 | tf_op jit(solution)/shard_map/ppermute | solution.py:274
  29.1 0.9 collective-permute-done.3.refs_0_.refs_1_.refs_3_.refs_8_
  31.2 1.6 %stitch.10 = bf16[2048,128]{1,0:T(8,128)(2,1)S(1)} custom-call(s32[2]{0:T(128)S(1)} %pad_add_fusion.pos, bf16[4096,128]{1,0:T(8,128)(2,1)} %bitcast.28, bf16[4096,128]{1,0:T(8,128)(2,1)} %bitcast.29), custom_call_target="tpu_custom_call" | custom-call | tf_op jit(solution)/shard_map/stitch/pallas_call | solution.py:77
  32.8 2.7 %collective-permute-start.4 = (bf16[2048,128]{1,0:T(8,128)(2,1)S(1)}, bf16[2048,128]{1,0:T(8,128)(2,1)S(1)}, u32[]{:S(2)}, u32[]{:S(2)}) collective-permute-start(bf16[2048,128]{1,0:T(8,128)(2,1)S(1)} %stitch.10), channel_id=1, source_target_pairs={{0,8},{2,10},{4,12},{6,14},{8,0},{10,2},{12,4},{14,6},{16,24},{18,... | collective-permute-start | bytes 1572872 | tf_op jit(solution)/shard_map/ppermute | solution.py:274
  36.1 1.6 %collective-permute-start.8 = (bf16[2048,128]{1,0:T(8,128)(2,1)S(1)}, bf16[2048,128]{1,0:T(8,128)(2,1)S(1)}, u32[]{:S(2)}, u32[]{:S(2)}) collective-permute-start(bf16[2048,128]{1,0:T(8,128)(2,1)S(1)} %stitch.12), channel_id=1, source_target_pairs={{0,16},{2,18},{4,20},{6,22},{8,24},{10,26},{12,28},{14,30},{16,0},... | collective-permute-start | bytes 1572872 | tf_op jit(solution)/shard_map/ppermute | solution.py:274
  37.7 3.6 %collective-permute-done.7.refs_4_.refs_0_.refs_9_ = bf16[1024,128]{1,0:T(8,128)(2,1)S(1)} collective-permute-done((bf16[1024,128]{1,0:T(8,128)(2,1)S(1)}, bf16[1024,128]{1,0:T(8,128)(2,1)S(1)}, u32[]{:S(2)}, u32[]{:S(2)}) %collective-permute-start.7) | collective-permute-done | bytes 262176 | tf_op jit(solution)/shard_map/ppermute | solution.py:274
  41.3 1.5 %collective-permute-start.9 = (bf16[2048,128]{1,0:T(8,128)(2,1)S(1)}, bf16[2048,128]{1,0:T(8,128)(2,1)S(1)}, u32[]{:S(2)}, u32[]{:S(2)}) collective-permute-start(bf16[2048,128]{1,0:T(8,128)(2,1)S(1)} %stitch.12), channel_id=1, source_target_pairs={{0,4},{2,6},{4,0},{6,2},{8,12},{10,14},{12,8},{14,10},{16,20},{18,... | collective-permute-start | bytes 1572872 | tf_op jit(solution)/shard_map/ppermute | solution.py:274
  43.4 13.7 %collective-permute-done.4.refs_4_.refs_1_.refs_2_ = bf16[2048,128]{1,0:T(8,128)(2,1)S(1)} collective-permute-done((bf16[2048,128]{1,0:T(8,128)(2,1)S(1)}, bf16[2048,128]{1,0:T(8,128)(2,1)S(1)}, u32[]{:S(2)}, u32[]{:S(2)}) %collective-permute-start.4) | collective-permute-done | bytes 524320 | tf_op jit(solution)/shard_map/ppermute | solution.py:274
  57.1 5.0 %collective-permute-done.8.refs_9_.refs_14_ = bf16[2048,128]{1,0:T(8,128)(2,1)S(1)} collective-permute-done((bf16[2048,128]{1,0:T(8,128)(2,1)S(1)}, bf16[2048,128]{1,0:T(8,128)(2,1)S(1)}, u32[]{:S(2)}, u32[]{:S(2)}) %collective-permute-start.8) | collective-permute-done | bytes 524320 | tf_op jit(solution)/shard_map/ppermute | solution.py:274
  63.8 1.6 %collective-permute-start.19 = (bf16[3072,128]{1,0:T(8,128)(2,1)S(1)}, bf16[3072,128]{1,0:T(8,128)(2,1)S(1)}, u32[]{:S(2)}, u32[]{:S(2)}) collective-permute-start(bf16[3072,128]{1,0:T(8,128)(2,1)S(1)} %stitch.13), channel_id=1, source_target_pairs={{0,2},{2,0},{4,6},{6,4},{8,10},{10,8},{12,14},{14,12},{16,18},{18,... | collective-permute-start | bytes 2359304 | tf_op jit(solution)/shard_map/ppermute | solution.py:274
  66.3 1.2 %collective-permute-start.18 = (bf16[1024,128]{1,0:T(8,128)(2,1)S(1)}, bf16[1024,128]{1,0:T(8,128)(2,1)S(1)}, u32[]{:S(2)}, u32[]{:S(2)}) collective-permute-start(bf16[1024,128]{1,0:T(8,128)(2,1)S(1)} %collective-permute-done.7.refs_4_.refs_0_.refs_9_), channel_id=1, source_target_pairs={{0,4},{2,6},{4,0},{6,2},{8,12},{10,14},{12,8},{14,10},{16,20},{18,... | collective-permute-start | bytes 786440 | tf_op jit(solution)/shard_map/ppermute | solution.py:274
  67.4 4.6 %project.1.refs_0_ = bf16[9,128,1024]{2,1,0:T(8,128)(2,1)S(1)} custom-call(s32[2]{0:T(128)S(1)} %pad_add_fusion.pos, s32[288]{0:T(512)S(1)} %reshape.19.cols, s32[96]{0:T(128)S(1)} %reshape.20.counts, bf16[3,32,3,128,128]{4,3,2,1,0:T(8,128)(2,1)} %potential.3, bf16[4096,128]{1,0:T(8,128)(2,1)} %bitcast.30, ...), custom_call_target="tpu_custom_call" | custom-call | tf_op jit(solution)/shard_map/project/pallas_call | solution.py:157
  72.0 7.3 %collective-permute-done.16.refs_10_.refs_15_ = bf16[1024,128]{1,0:T(8,128)(2,1)S(1)} collective-permute-done((bf16[1024,128]{1,0:T(8,128)(2,1)S(1)}, bf16[1024,128]{1,0:T(8,128)(2,1)S(1)}, u32[]{:S(2)}, u32[]{:S(2)}) %collective-permute-start.16) | collective-permute-done | bytes 262176 | tf_op jit(solution)/shard_map/ppermute | solution.py:274
  79.3 5.2 %collective-permute-done.18.refs_7_.refs_12_ = bf16[1024,128]{1,0:T(8,128)(2,1)S(1)} collective-permute-done((bf16[1024,128]{1,0:T(8,128)(2,1)S(1)}, bf16[1024,128]{1,0:T(8,128)(2,1)S(1)}, u32[]{:S(2)}, u32[]{:S(2)}) %collective-permute-start.18) | collective-permute-done | bytes 262176 | tf_op jit(solution)/shard_map/ppermute | solution.py:274
  85.6 2.9 %couple.1.refs_4_ = f32[9,128,128]{2,1,0:T(8,128)S(1)} custom-call(s32[2]{0:T(128)S(1)} %pad_add_fusion.pos, s32[48]{0:T(128)S(1)} %reshape.21.partners, bf16[9,128,1024]{2,1,0:T(8,128)(2,1)S(1)} %project.1.refs_0_, bf16[1024,128]{1,0:T(8,128)(2,1)S(1)} %constant_dynamic-slice_fusion.refs_1_.refs_6_, ...), custom_call_target="tpu_custom_call" | custom-call | tf_op jit(solution)/shard_map/couple/pallas_call | solution.py:244
  88.5 3.3 %project_last.1.refs_5_ = bf16[3,128,1024]{2,1,0:T(8,128)(2,1)S(1)} custom-call(s32[2]{0:T(128)S(1)} %pad_add_fusion.pos, s32[288]{0:T(512)S(1)} %reshape.19.cols, s32[96]{0:T(128)S(1)} %reshape.20.counts, bf16[3,32,3,128,128]{4,3,2,1,0:T(8,128)(2,1)} %potential.3, bf16[1024,128]{1,0:T(8,128)(2,1)S(1)} %collective-permute-done.7.refs_4_.refs_0_.refs_9_, ...), custom_call_target="tpu_custom_call" | custom-call | tf_op jit(solution)/shard_map/project_last/pallas_call | solution.py:157
  91.8 1.5 %collective-permute-done.17.refs_3_.refs_18_ = bf16[1024,128]{1,0:T(8,128)(2,1)S(1)} collective-permute-done((bf16[1024,128]{1,0:T(8,128)(2,1)S(1)}, bf16[1024,128]{1,0:T(8,128)(2,1)S(1)}, u32[]{:S(2)}, u32[]{:S(2)}) %collective-permute-start.17) | collective-permute-done | bytes 262176 | tf_op jit(solution)/shard_map/ppermute | solution.py:274
  93.4 2.6 %couple_last.1 = f32[2,12,64,128]{3,2,1,0:T(8,128)S(1)} custom-call(s32[2]{0:T(128)S(1)} %pad_add_fusion.pos, s32[48]{0:T(128)S(1)} %reshape.21.partners, bf16[9,128,1024]{2,1,0:T(8,128)(2,1)S(1)} %project.1.refs_0_, bf16[1024,128]{1,0:T(8,128)(2,1)S(1)} %collective-permute-done.10.refs_1_.refs_16_, ...), custom_call_target="tpu_custom_call" | custom-call | tf_op jit(solution)/shard_map/couple_last/pallas_call | solution.py:244
  96.1 1.7 %collective-permute-done.22 = f32[12,64,128]{2,1,0:T(8,128)S(1)} collective-permute-done((f32[12,64,128]{2,1,0:T(8,128)S(1)}, f32[12,64,128]{2,1,0:T(8,128)S(1)}, u32[]{:S(2)}, u32[]{:S(2)}) %collective-permute-start.22) | collective-permute-done | bytes 393248 | tf_op jit(solution)/shard_map/ppermute | solution.py:277
  98.0 2.2 %collective-permute-start.24 = (bf16[3,64,128]{2,1,0:T(8,128)(2,1)S(1)}, bf16[3,64,128]{2,1,0:T(8,128)(2,1)S(1)}, u32[]{:S(2)}, u32[]{:S(2)}) collective-permute-start(bf16[3,64,128]{2,1,0:T(8,128)(2,1)S(1)} %get-tuple-element.59), channel_id=1, source_target_pairs={{0,8},{2,10},{4,12},{6,14},{8,0},{10,2},{12,4},{14,6},{16,24},{18,... | collective-permute-start | bytes 147464 | tf_op jit(solution)/shard_map/ppermute | solution.py:274
  100.2 1.3 %collective-permute-start.23 = (bf16[3,64,128]{2,1,0:T(8,128)(2,1)S(1)}, bf16[3,64,128]{2,1,0:T(8,128)(2,1)S(1)}, u32[]{:S(2)}, u32[]{:S(2)}) collective-permute-start(bf16[3,64,128]{2,1,0:T(8,128)(2,1)S(1)} %get-tuple-element.57), channel_id=1, source_target_pairs={{0,2},{2,0},{4,6},{6,4},{8,10},{10,8},{12,14},{14,12},{16,18},{18,... | collective-permute-start | bytes 147464 | tf_op jit(solution)/shard_map/ppermute | solution.py:274
  101.4 1.7 %collective-permute-done.25 = bf16[3,64,128]{2,1,0:T(8,128)(2,1)S(1)} collective-permute-done((bf16[3,64,128]{2,1,0:T(8,128)(2,1)S(1)}, bf16[3,64,128]{2,1,0:T(8,128)(2,1)S(1)}, u32[]{:S(2)}, u32[]{:S(2)}) %collective-permute-start.25) | collective-permute-done | bytes 49184 | tf_op jit(solution)/shard_map/ppermute | solution.py:274
  103.2 1.1 %collective-permute-done.23 = bf16[3,64,128]{2,1,0:T(8,128)(2,1)S(1)} collective-permute-done((bf16[3,64,128]{2,1,0:T(8,128)(2,1)S(1)}, bf16[3,64,128]{2,1,0:T(8,128)(2,1)S(1)}, u32[]{:S(2)}, u32[]{:S(2)}) %collective-permute-start.23) | collective-permute-done | bytes 49184 | tf_op jit(solution)/shard_map/ppermute | solution.py:274
  (43 shorter events, 9.4 us)
Async XLA Ops:
  4.1 11.4 %collective-permute-start = (bf16[1024,128]{1,0:T(8,128)(2,1)S(1)}, bf16[1024,128]{1,0:T(8,128)(2,1)S(1)}, u32[]{:S(2)}, u32[]{:S(2)}) collective-permute-start(bf16[1024,128]{1,0:T(8,128)(2,1)S(1)} %stitch.7), channel_id=1, source_target_pairs={{0,2},{2,0},{4,6},{6,4},{8,10},{10,8},{12,14},{14,12},{16,18},{18,... | collective-permute-start | bytes 786440 | tf_op jit(solution)/shard_map/ppermute | solution.py:274
  8.0 7.8 %collective-permute-start.1 = (bf16[1024,128]{1,0:T(8,128)(2,1)S(1)}, bf16[1024,128]{1,0:T(8,128)(2,1)S(1)}, u32[]{:S(2)}, u32[]{:S(2)}) collective-permute-start(bf16[1024,128]{1,0:T(8,128)(2,1)S(1)} %constant_dynamic-slice_fusion.refs_1_.refs_6_), channel_id=1, source_target_pairs={{0,4},{2,6},{4,0},{6,2},{8,12},{10,14},{12,8},{14,10},{16,20},{18,... | collective-permute-start | bytes 786440 | tf_op jit(solution)/shard_map/ppermute | solution.py:274
  11.2 18.8 %collective-permute-start.3 = (bf16[2048,128]{1,0:T(8,128)(2,1)S(1)}, bf16[2048,128]{1,0:T(8,128)(2,1)S(1)}, u32[]{:S(2)}, u32[]{:S(2)}) collective-permute-start(bf16[2048,128]{1,0:T(8,128)(2,1)S(1)} %stitch.9), channel_id=1, source_target_pairs={{0,8},{2,10},{4,12},{6,14},{8,0},{10,2},{12,4},{14,6},{16,24},{18,... | collective-permute-start | bytes 1572872 | tf_op jit(solution)/shard_map/ppermute | solution.py:274
  12.9 16.2 %collective-permute-start.5 = (bf16[1024,128]{1,0:T(8,128)(2,1)S(1)}, bf16[1024,128]{1,0:T(8,128)(2,1)S(1)}, u32[]{:S(2)}, u32[]{:S(2)}) collective-permute-start(bf16[1024,128]{1,0:T(8,128)(2,1)S(1)} %constant_dynamic-slice_fusion.refs_1_.refs_6_), channel_id=1, source_target_pairs={{0,16},{2,18},{4,20},{6,22},{8,24},{10,26},{12,28},{14,30},{16,0},... | collective-permute-start | bytes 786440 | tf_op jit(solution)/shard_map/ppermute | solution.py:274
  17.6 25.3 %collective-permute-start.2 = (bf16[3072,128]{1,0:T(8,128)(2,1)S(1)}, bf16[3072,128]{1,0:T(8,128)(2,1)S(1)}, u32[]{:S(2)}, u32[]{:S(2)}) collective-permute-start(bf16[3072,128]{1,0:T(8,128)(2,1)S(1)} %stitch.8), channel_id=1, source_target_pairs={{0,2},{2,0},{4,6},{6,4},{8,10},{10,8},{12,14},{14,12},{16,18},{18,... | collective-permute-start | bytes 2359304 | tf_op jit(solution)/shard_map/ppermute | solution.py:274
  29.1 34.6 %collective-permute-start.6 = (bf16[4096,128]{1,0:T(8,128)(2,1)}, bf16[4096,128]{1,0:T(8,128)(2,1)S(1)}, u32[]{:S(2)}, u32[]{:S(2)}) collective-permute-start(bf16[4096,128]{1,0:T(8,128)(2,1)} %bitcast.27), channel_id=1, source_target_pairs={{0,1},{1,0},{2,3},{3,2},{4,5},{5,4},{6,7},{7,6},{8,9},{9,8},{10,11... | collective-permute-start | bytes 3145736 | tf_op jit(solution)/shard_map/ppermute | solution.py:277
  30.6 10.7 %collective-permute-start.7 = (bf16[1024,128]{1,0:T(8,128)(2,1)S(1)}, bf16[1024,128]{1,0:T(8,128)(2,1)S(1)}, u32[]{:S(2)}, u32[]{:S(2)}) collective-permute-start(bf16[1024,128]{1,0:T(8,128)(2,1)S(1)} %stitch.11), channel_id=1, source_target_pairs={{0,2},{2,0},{4,6},{6,4},{8,10},{10,8},{12,14},{14,12},{16,18},{18,... | collective-permute-start | bytes 786440 | tf_op jit(solution)/shard_map/ppermute | solution.py:274
  32.8 24.3 %collective-permute-start.4 = (bf16[2048,128]{1,0:T(8,128)(2,1)S(1)}, bf16[2048,128]{1,0:T(8,128)(2,1)S(1)}, u32[]{:S(2)}, u32[]{:S(2)}) collective-permute-start(bf16[2048,128]{1,0:T(8,128)(2,1)S(1)} %stitch.10), channel_id=1, source_target_pairs={{0,8},{2,10},{4,12},{6,14},{8,0},{10,2},{12,4},{14,6},{16,24},{18,... | collective-permute-start | bytes 1572872 | tf_op jit(solution)/shard_map/ppermute | solution.py:274
  36.1 26.0 %collective-permute-start.8 = (bf16[2048,128]{1,0:T(8,128)(2,1)S(1)}, bf16[2048,128]{1,0:T(8,128)(2,1)S(1)}, u32[]{:S(2)}, u32[]{:S(2)}) collective-permute-start(bf16[2048,128]{1,0:T(8,128)(2,1)S(1)} %stitch.12), channel_id=1, source_target_pairs={{0,16},{2,18},{4,20},{6,22},{8,24},{10,26},{12,28},{14,30},{16,0},... | collective-permute-start | bytes 1572872 | tf_op jit(solution)/shard_map/ppermute | solution.py:274
  41.3 20.7 %collective-permute-start.9 = (bf16[2048,128]{1,0:T(8,128)(2,1)S(1)}, bf16[2048,128]{1,0:T(8,128)(2,1)S(1)}, u32[]{:S(2)}, u32[]{:S(2)}) collective-permute-start(bf16[2048,128]{1,0:T(8,128)(2,1)S(1)} %stitch.12), channel_id=1, source_target_pairs={{0,4},{2,6},{4,0},{6,2},{8,12},{10,14},{12,8},{14,10},{16,20},{18,... | collective-permute-start | bytes 1572872 | tf_op jit(solution)/shard_map/ppermute | solution.py:274
  42.9 19.2 %collective-permute-start.10 = (bf16[1024,128]{1,0:T(8,128)(2,1)S(1)}, bf16[1024,128]{1,0:T(8,128)(2,1)S(1)}, u32[]{:S(2)}, u32[]{:S(2)}) collective-permute-start(bf16[1024,128]{1,0:T(8,128)(2,1)S(1)} %collective-permute-done.5.refs_8_.refs_13_), channel_id=1, source_target_pairs={{0,4},{2,6},{4,0},{6,2},{8,12},{10,14},{12,8},{14,10},{16,20},{18,... | collective-permute-start | bytes 786440 | tf_op jit(solution)/shard_map/ppermute | solution.py:274
  62.1 3.2 %collective-permute-start.11 = (bf16[1024,128]{1,0:T(8,128)(2,1)S(1)}, bf16[1024,128]{1,0:T(8,128)(2,1)S(1)}, u32[]{:S(2)}, u32[]{:S(2)}) collective-permute-start(bf16[1024,128]{1,0:T(8,128)(2,1)S(1)} %collective-permute-done.refs_0_.refs_1_.refs_2_.refs_7_), channel_id=1, source_target_pairs={{0,1},{1,0},{2,3},{3,2},{4,5},{5,4},{6,7},{7,6},{8,9},{9,8},{10,11... | collective-permute-start | bytes 786440 | tf_op jit(solution)/shard_map/ppermute | solution.py:277
  62.1 5.3 %collective-permute-start.12 = (bf16[3072,128]{1,0:T(8,128)(2,1)S(1)}, bf16[3072,128]{1,0:T(8,128)(2,1)S(1)}, u32[]{:S(2)}, u32[]{:S(2)}) collective-permute-start(bf16[3072,128]{1,0:T(8,128)(2,1)S(1)} %collective-permute-done.2.refs_2_), channel_id=1, source_target_pairs={{0,1},{1,0},{2,3},{3,2},{4,5},{5,4},{6,7},{7,6},{8,9},{9,8},{10,11... | collective-permute-start | bytes 2359304 | tf_op jit(solution)/shard_map/ppermute | solution.py:277
  62.6 3.2 %collective-permute-start.13 = (bf16[2048,128]{1,0:T(8,128)(2,1)S(1)}, bf16[2048,128]{1,0:T(8,128)(2,1)S(1)}, u32[]{:S(2)}, u32[]{:S(2)}) collective-permute-start(bf16[2048,128]{1,0:T(8,128)(2,1)S(1)} %collective-permute-done.3.refs_0_.refs_1_.refs_3_.refs_8_), channel_id=1, source_target_pairs={{0,1},{1,0},{2,3},{3,2},{4,5},{5,4},{6,7},{7,6},{8,9},{9,8},{10,11... | collective-permute-start | bytes 1572872 | tf_op jit(solution)/shard_map/ppermute | solution.py:277
  62.7 3.6 %collective-permute-start.14 = (bf16[2048,128]{1,0:T(8,128)(2,1)S(1)}, bf16[2048,128]{1,0:T(8,128)(2,1)S(1)}, u32[]{:S(2)}, u32[]{:S(2)}) collective-permute-start(bf16[2048,128]{1,0:T(8,128)(2,1)S(1)} %collective-permute-done.4.refs_4_.refs_1_.refs_2_), channel_id=1, source_target_pairs={{0,1},{1,0},{2,3},{3,2},{4,5},{5,4},{6,7},{7,6},{8,9},{9,8},{10,11... | collective-permute-start | bytes 1572872 | tf_op jit(solution)/shard_map/ppermute | solution.py:277
  63.8 20.8 %collective-permute-start.19 = (bf16[3072,128]{1,0:T(8,128)(2,1)S(1)}, bf16[3072,128]{1,0:T(8,128)(2,1)S(1)}, u32[]{:S(2)}, u32[]{:S(2)}) collective-permute-start(bf16[3072,128]{1,0:T(8,128)(2,1)S(1)} %stitch.13), channel_id=1, source_target_pairs={{0,2},{2,0},{4,6},{6,4},{8,10},{10,8},{12,14},{14,12},{16,18},{18,... | collective-permute-start | bytes 2359304 | tf_op jit(solution)/shard_map/ppermute | solution.py:274
  65.3 19.2 %collective-permute-start.15 = (bf16[2048,128]{1,0:T(8,128)(2,1)S(1)}, bf16[2048,128]{1,0:T(8,128)(2,1)S(1)}, u32[]{:S(2)}, u32[]{:S(2)}) collective-permute-start(bf16[2048,128]{1,0:T(8,128)(2,1)S(1)} %collective-permute-done.8.refs_9_.refs_14_), channel_id=1, source_target_pairs={{0,4},{2,6},{4,0},{6,2},{8,12},{10,14},{12,8},{14,10},{16,20},{18,... | collective-permute-start | bytes 1572872 | tf_op jit(solution)/shard_map/ppermute | solution.py:274
  65.8 13.5 %collective-permute-start.16 = (bf16[1024,128]{1,0:T(8,128)(2,1)S(1)}, bf16[1024,128]{1,0:T(8,128)(2,1)S(1)}, u32[]{:S(2)}, u32[]{:S(2)}) collective-permute-start(bf16[1024,128]{1,0:T(8,128)(2,1)S(1)} %collective-permute-done.7.refs_4_.refs_0_.refs_9_), channel_id=1, source_target_pairs={{0,16},{2,18},{4,20},{6,22},{8,24},{10,26},{12,28},{14,30},{16,0},... | collective-permute-start | bytes 786440 | tf_op jit(solution)/shard_map/ppermute | solution.py:274
  66.3 18.3 %collective-permute-start.18 = (bf16[1024,128]{1,0:T(8,128)(2,1)S(1)}, bf16[1024,128]{1,0:T(8,128)(2,1)S(1)}, u32[]{:S(2)}, u32[]{:S(2)}) collective-permute-start(bf16[1024,128]{1,0:T(8,128)(2,1)S(1)} %collective-permute-done.7.refs_4_.refs_0_.refs_9_), channel_id=1, source_target_pairs={{0,4},{2,6},{4,0},{6,2},{8,12},{10,14},{12,8},{14,10},{16,20},{18,... | collective-permute-start | bytes 786440 | tf_op jit(solution)/shard_map/ppermute | solution.py:274
  84.6 3.9 %collective-permute-start.21 = (bf16[3072,128]{1,0:T(8,128)(2,1)S(1)}, bf16[3072,128]{1,0:T(8,128)(2,1)S(1)}, u32[]{:S(2)}, u32[]{:S(2)}) collective-permute-start(bf16[3072,128]{1,0:T(8,128)(2,1)S(1)} %collective-permute-done.19.refs_1_), channel_id=1, source_target_pairs={{0,1},{1,0},{2,3},{3,2},{4,5},{5,4},{6,7},{7,6},{8,9},{9,8},{10,11... | collective-permute-start | bytes 2359304 | tf_op jit(solution)/shard_map/ppermute | solution.py:277
  84.6 3.9 %collective-permute-start.20 = (bf16[1024,128]{1,0:T(8,128)(2,1)S(1)}, bf16[1024,128]{1,0:T(8,128)(2,1)S(1)}, u32[]{:S(2)}, u32[]{:S(2)}) collective-permute-start(bf16[1024,128]{1,0:T(8,128)(2,1)S(1)} %collective-permute-done.7.refs_4_.refs_0_.refs_9_), channel_id=1, source_target_pairs={{0,1},{1,0},{2,3},{3,2},{4,5},{5,4},{6,7},{7,6},{8,9},{9,8},{10,11... | collective-permute-start | bytes 786440 | tf_op jit(solution)/shard_map/ppermute | solution.py:277
  85.1 8.3 %collective-permute-start.17 = (bf16[1024,128]{1,0:T(8,128)(2,1)S(1)}, bf16[1024,128]{1,0:T(8,128)(2,1)S(1)}, u32[]{:S(2)}, u32[]{:S(2)}) collective-permute-start(bf16[1024,128]{1,0:T(8,128)(2,1)S(1)} %collective-permute-done.16.refs_10_.refs_15_), channel_id=1, source_target_pairs={{0,4},{2,6},{4,0},{6,2},{8,12},{10,14},{12,8},{14,10},{16,20},{18,... | collective-permute-start | bytes 786440 | tf_op jit(solution)/shard_map/ppermute | solution.py:274
  88.5 15.8 %copy-start = (f32[3,1,64,128]{3,2,1,0:T(8,128)S(1)}, f32[3,1,64,128]{3,2,1,0:T(8,128)}, u32[]{:S(2)}) copy-start(f32[3,1,64,128]{3,2,1,0:T(8,128)} %param.11) | copy-start | bytes 294916
  96.0 1.8 %collective-permute-start.22 = (f32[12,64,128]{2,1,0:T(8,128)S(1)}, f32[12,64,128]{2,1,0:T(8,128)S(1)}, u32[]{:S(2)}, u32[]{:S(2)}) collective-permute-start(f32[12,64,128]{2,1,0:T(8,128)S(1)} %slice_bitcast_fusion), channel_id=1, source_target_pairs={{0,1},{1,0},{2,3},{3,2},{4,5},{5,4},{6,7},{7,6},{8,9},{9,8},{10,11... | collective-permute-start | bytes 1179656 | tf_op jit(solution)/shard_map/ppermute | solution.py:277
  97.9 5.3 %collective-permute-start.25 = (bf16[3,64,128]{2,1,0:T(8,128)(2,1)S(1)}, bf16[3,64,128]{2,1,0:T(8,128)(2,1)S(1)}, u32[]{:S(2)}, u32[]{:S(2)}) collective-permute-start(bf16[3,64,128]{2,1,0:T(8,128)(2,1)S(1)} %get-tuple-element.58), channel_id=1, source_target_pairs={{0,10},{2,8},{4,14},{6,12},{8,2},{10,0},{12,6},{14,4},{16,26},{18,... | collective-permute-start | bytes 147464 | tf_op jit(solution)/shard_map/ppermute | solution.py:274
  98.0 5.2 %collective-permute-start.24 = (bf16[3,64,128]{2,1,0:T(8,128)(2,1)S(1)}, bf16[3,64,128]{2,1,0:T(8,128)(2,1)S(1)}, u32[]{:S(2)}, u32[]{:S(2)}) collective-permute-start(bf16[3,64,128]{2,1,0:T(8,128)(2,1)S(1)} %get-tuple-element.59), channel_id=1, source_target_pairs={{0,8},{2,10},{4,12},{6,14},{8,0},{10,2},{12,4},{14,6},{16,24},{18,... | collective-permute-start | bytes 147464 | tf_op jit(solution)/shard_map/ppermute | solution.py:274
  100.2 4.1 %collective-permute-start.23 = (bf16[3,64,128]{2,1,0:T(8,128)(2,1)S(1)}, bf16[3,64,128]{2,1,0:T(8,128)(2,1)S(1)}, u32[]{:S(2)}, u32[]{:S(2)}) collective-permute-start(bf16[3,64,128]{2,1,0:T(8,128)(2,1)S(1)} %get-tuple-element.57), channel_id=1, source_target_pairs={{0,2},{2,0},{4,6},{6,4},{8,10},{10,8},{12,14},{14,12},{16,18},{18,... | collective-permute-start | bytes 147464 | tf_op jit(solution)/shard_map/ppermute | solution.py:274

commit v8 on v7

--- a/solution.py
+++ b/solution.py
@@ -14,17 +14,22 @@
 
 
 FIRST = ("c0", "c1", "s1.0")
-SECOND = ("p3", "r1", "r2", "s2.1", "s1.1", "s3.0")
+GATHER = ("p3", "r1", "r2")
+SECOND = GATHER + ("s2.1", "s1.1","s3.0")
 WAITS = {
     **dict.fromkeys(FIRST, ()),
     "s2.0": (),
     "t1o": ("s2.0",),
-    "r1": ("c0", "s1.0"),
-    **dict.fromkeys(("p3", "r2", "s2.1", "s1.1"), FIRST),
-    "s3.0": ("p3",),
-    **dict.fromkeys(("r3", "s2.2", "s3.1", "s1.2", "t1c0", "t1c1", "t1r1", "t1r2", "t1p3"), SECOND),
+    "r1": ("c0","s1.0"),
+    **dict.fromkeys(("p3", "r2", "s2.1", "s1.1"), FIRST+("i","s2.0")),
+    **dict.fromkeys(("s3.0",), ("p3",)),
+
+    "r3": GATHER+("s1.1","s3.0"),
+    **dict.fromkeys(("s2.2","s3.1","s1.2"), SECOND),
+    **dict.fromkeys(("t1c0","t1c1","t1r1","t1r2","t1p3"), SECOND),
     "q": (),
-    "t1r3": ("q", "s2.2", "s3.1", "s1.2"),
+
+    "t1r3": ("q","s2.2","s3.1","s1.2"),
 }
 
 
@@ -52,16 +57,14 @@
     return sum((((value >> bit) & 1) << i for i, bit in enumerate(bits)), 0 * value)
 
 
-def stitch_kernel(inside, places, pos, *refs):
+def stitch_kernel(places, *refs):
     sources, (out, sems) = refs[: len(places)], refs[len(places) :]
     rows = out.shape[0] // len(places)
-    chunk = gathered(pos[0], inside)
     copies = []
-    for i, (source, (at, moving)) in enumerate(zip(sources, places)):
-        start = ((chunk ^ at) if moving else at) * rows
+    for i, (source, at) in enumerate(zip(sources, places)):
         copies.append(
             pltpu.make_async_copy(
-                source.at[pl.ds(pl.multiple_of(start, rows), rows)],
+                source.at[pl.ds(at * rows, rows)],
                 out.at[pl.ds(i * rows, rows)],
                 sems.at[i],
             )
@@ -72,18 +75,18 @@
         copy.wait()
 
 
-def stitch(pos, rows, sources, places, inside):
+def stitch(rows, sources, places):
     bands = sources[0].shape[1]
     return pl.pallas_call(
-        functools.partial(stitch_kernel, inside, places),
+        functools.partial(stitch_kernel, places),
         out_shape=jax.ShapeDtypeStruct((len(places) * rows, bands), sources[0].dtype),
-        in_specs=[SMEM] + [ANY] * len(sources),
+        in_specs=[ANY] * len(sources),
         out_specs=ANY,
         scratch_shapes=[pltpu.SemaphoreType.DMA((len(places),))],
         compiler_params=pltpu.CompilerParams(vmem_limit_bytes=2**20),
         cost_estimate=pl.CostEstimate(flops=0, bytes_accessed=0, transcendentals=0),
         name="stitch",
-    )(pos, *[in_hbm(x) if p[1] else in_vmem(x) for x, p in zip(sources, places)])
+    )(*[in_vmem(source) for source in sources])
 
 
 def project_kernel(orders, inside, halves, pos, cols, counts, potential, *refs):
@@ -266,9 +269,7 @@
         me = lax.axis_index("ka").astype(jnp.int32)
         chunk = gathered(me, inside)
         pos = jnp.stack([me, lax.axis_index("orb").astype(jnp.int32)])
-        pos, cols, counts, pairing, own = lax.optimization_barrier(
-            (pos, block_cols.reshape(-1), block_counts.reshape(-1), partners.reshape(-1), own)
-        )
+        pos, own = lax.optimization_barrier((pos, own))
 
         def swap(value, mask):
             return lax.ppermute(value, "ka", [(i, i ^ mask) for i in range(points)])
@@ -289,7 +290,7 @@
                 inputs = [item[0] for item in inputs]
                 waits = [done[other] for other in WAITS.get(name, ()) if other in done]
                 if waits:
-                    inputs = lax.optimization_barrier((*inputs, *waits))[: len(inputs)]
+                    inputs, _ = lax.optimization_barrier((inputs, waits))
                 whole = places[0] == (None,)
                 done[name] = move(inputs[0] if whole else joined(places, inputs))
             return done[name]
@@ -299,17 +300,19 @@
         sizes = {}
         orders = {}
 
-        mine = lax.dynamic_slice_in_dim(own, chunk * rows, rows, 0)
+        slices = [
+            lax.dynamic_slice_in_dim(own, (chunk ^ j) * rows, rows, 0) for j in range(group)
+        ]
 
         def part(j):
             if j == 0:
-                return mine, 0, False
+                return slices[0], 0, False
             top = j.bit_length() - 1
             return (get(f"c{top}") if j == 1 << top else get(f"p{j}")), 0, False
 
         def held(key, j):
             if key == 0:
-                return own, j, True
+                return slices[j], 0, True
             if j in orders[key]:
                 return get(f"r{key}"), orders[key].index(j), False
             return (get(f"c{key.bit_length() - 1}"), j, False) if j else part(key)
@@ -317,7 +320,9 @@
         def joined(places, values):
             if len(values) == 1 and values[0].shape[0] == rows:
                 return values[0]
-            return stitch(pos, rows, values, places, inside)
+            if all(value.shape[0] == rows for value in values) and places[0] == (0, True):
+                return jnp.concatenate(values, axis=0)
+            return stitch(rows, values, [at for at, _ in places])
 
         for j in range(1, group):
             top = j.bit_length() - 1
@@ -389,6 +394,9 @@
             lambda: [projection("project", range(group - 1))],
             lambda value: value,
         )
+        tables = (block_cols.reshape(-1), block_counts.reshape(-1), partners.reshape(-1))
+        tables = lax.optimization_barrier((get("c0"), *tables))[1:]
+        cols, counts, pairing = done["i"] = tables
         for name in WAITS:
             if name in plan:
                 get(name)

time: 105 us -> 96.8 us (0.922)
  Pallas kernels: 21.5 us -> 13.6 us
  waiting for transfers between devices: 53.9 us -> 49.8 us
  other arithmetic: 0.81 us -> 3.6 us
  starting transfers between devices: 25 us -> 27.6 us
  local copies, waits for them, and re-layouts: 3.49 us -> 1.76 us
    pallas_call x7 -> x3, Pallas kernels: 8.16 us -> 0.17 us  [stitch(): pl.pallas_call(functools.partial(stitch_kernel, places), out_shape=jax.Sh...]
    ppermute x18, waiting for transfers between devices: 51.7 us -> 48.1 us  [swap(): return lax.ppermute(value, 'ka', [(i, i ^ mask) for i in range(points)])]
    concatenate x0 -> x3, other arithmetic: none -> 2.79 us  [joined(): return jnp.concatenate(values, axis=0)]
    ppermute x18, starting transfers between devices: 23.4 us -> 26 us  [swap(): return lax.ppermute(value, 'ka', [(i, i ^ mask) for i in range(points)])]
  transfers between devices with their start and end apart: 26 -> 26, of which waited for: 13 -> 14; matrix products, arithmetic and copies ran while one was open for 1% -> 3% of each run, Pallas kernels for 17% -> 11%
where the time goes in v8:
time: 96.8 us; the launch traced here: 96.6 us
  waiting for transfers between devices  49.8 us (51%)
  starting transfers between devices  27.6 us (29%)
  Pallas kernels  13.6 us (14%)
  other arithmetic  3.6 us (4%)
  local copies, waits for them, and re-layouts  1.76 us (2%)
    ppermute x18, waiting for transfers between devices, swap(): return lax.ppermute(value, 'ka', [(i, i ^ mask) for i in range(points)])  48.1 us
    ppermute x18, starting transfers between devices, swap(): return lax.ppermute(value, 'ka', [(i, i ^ mask) for i in range(points)])  26 us
    pallas_call x2, Pallas kernels, project(): pl.pallas_call(functools.partial(project_kernel, orders, inside, halves),...  7.99 us
    pallas_call x2, Pallas kernels, couple(): pl.pallas_call(functools.partial(couple_kernel, jobs, last, inside, outsi...  5.46 us
    concatenate x3, other arithmetic, joined(): return jnp.concatenate(values, axis=0)  2.79 us
  transfers between devices with their start and end apart: 26, of which 14 were waited for; matrix products, arithmetic and copies ran while one was open for 3% of the time, Pallas kernels for 11%

profile of v8, /device:TPU:0, one launch (start us, length us, event | category | flops | bytes accessed | tf_op | source)
XLA Modules:
  0.0 96.6 jit_solution(4190963189767518702)
XLA Ops:
  0.1 1.3 %constant_dynamic-slice_fusion = (bf16[1024,128]{1,0:T(8,128)(2,1)S(1)}, bf16[1024,128]{1,0:T(8,128)(2,1)S(1)}, bf16[1024,128]{1,0:T(8,128)(2,1)S(1)}, bf16[1024,128]{1,0:T(8,128)(2,1)S(1)}) fusion(bf16[4096,128]{1,0:T(8,128)(2,1)} %bitcast.2.refs_0_, s32[]{:T(128)S(6)} %select_n.15, s32[]{:T(128)S(6)} %select_n.14, s32[]{:T(128)S(6)} %select_n.13, ...), kind=kLoop, calls=%fused_computation.12 | loop fusion | bytes 2097168 | tf_op jit(solution)/shard_map/dynamic_slice | solution.py:304
  1.4 3.0 %collective-permute-start = (bf16[1024,128]{1,0:T(8,128)(2,1)S(1)}, bf16[1024,128]{1,0:T(8,128)(2,1)S(1)}, u32[]{:S(2)}, u32[]{:S(2)}) collective-permute-start(bf16[1024,128]{1,0:T(8,128)(2,1)S(1)} %get-tuple-element.39), channel_id=1, source_target_pairs={{0,2},{2,0},{4,6},{6,4},{8,10},{10,8},{12,14},{14,12},{16,18},{18,... | collective-permute-start | bytes 786440 | tf_op jit(solution)/shard_map/ppermute | solution.py:275
  4.4 1.5 %collective-permute-start.1 = (bf16[1024,128]{1,0:T(8,128)(2,1)S(1)}, bf16[1024,128]{1,0:T(8,128)(2,1)S(1)}, u32[]{:S(2)}, u32[]{:S(2)}) collective-permute-start(bf16[1024,128]{1,0:T(8,128)(2,1)S(1)} %get-tuple-element.38.refs_1_.refs_6_), channel_id=1, source_target_pairs={{0,4},{2,6},{4,0},{6,2},{8,12},{10,14},{12,8},{14,10},{16,20},{18,... | collective-permute-start | bytes 786440 | tf_op jit(solution)/shard_map/ppermute | solution.py:275
  5.9 2.6 %collective-permute-start.4 = (bf16[1024,128]{1,0:T(8,128)(2,1)S(1)}, bf16[1024,128]{1,0:T(8,128)(2,1)S(1)}, u32[]{:S(2)}, u32[]{:S(2)}) collective-permute-start(bf16[1024,128]{1,0:T(8,128)(2,1)S(1)} %get-tuple-element.38.refs_1_.refs_6_), channel_id=1, source_target_pairs={{0,16},{2,18},{4,20},{6,22},{8,24},{10,26},{12,28},{14,30},{16,0},... | collective-permute-start | bytes 786440 | tf_op jit(solution)/shard_map/ppermute | solution.py:275
  9.4 1.6 %collective-permute-start.3 = (bf16[2048,128]{1,0:T(8,128)(2,1)}, bf16[2048,128]{1,0:T(8,128)(2,1)S(1)}, u32[]{:S(2)}, u32[]{:S(2)}) collective-permute-start(bf16[2048,128]{1,0:T(8,128)(2,1)} %pad_maximum_fusion.1), channel_id=1, source_target_pairs={{0,8},{2,10},{4,12},{6,14},{8,0},{10,2},{12,4},{14,6},{16,24},{18,... | collective-permute-start | bytes 1572872 | tf_op jit(solution)/shard_map/ppermute | solution.py:275
  10.9 1.2 %collective-permute-done.1.refs_5_.refs_10_ = bf16[1024,128]{1,0:T(8,128)(2,1)S(1)} collective-permute-done((bf16[1024,128]{1,0:T(8,128)(2,1)S(1)}, bf16[1024,128]{1,0:T(8,128)(2,1)S(1)}, u32[]{:S(2)}, u32[]{:S(2)}) %collective-permute-start.1) | collective-permute-done | bytes 262176 | tf_op jit(solution)/shard_map/ppermute | solution.py:275
  12.2 1.0 pad_maximum_fusion
  13.5 6.5 %collective-permute-done.4.refs_8_.refs_13_ = bf16[1024,128]{1,0:T(8,128)(2,1)S(1)} collective-permute-done((bf16[1024,128]{1,0:T(8,128)(2,1)S(1)}, bf16[1024,128]{1,0:T(8,128)(2,1)S(1)}, u32[]{:S(2)}, u32[]{:S(2)}) %collective-permute-start.4) | collective-permute-done | bytes 262176 | tf_op jit(solution)/shard_map/ppermute | solution.py:275
  20.5 6.4 %collective-permute-done.3.refs_0_.refs_1_.refs_3_.refs_8_ = bf16[2048,128]{1,0:T(8,128)(2,1)S(1)} collective-permute-done((bf16[2048,128]{1,0:T(8,128)(2,1)}, bf16[2048,128]{1,0:T(8,128)(2,1)S(1)}, u32[]{:S(2)}, u32[]{:S(2)}) %collective-permute-start.3) | collective-permute-done | bytes 524320 | tf_op jit(solution)/shard_map/ppermute | solution.py:275
  27.5 1.0 %pad_maximum_fusion.2 = bf16[2048,128]{1,0:T(8,128)(2,1)S(1)} fusion(bf16[1024,128]{1,0:T(8,128)(2,1)} %copy-done, bf16[1024,128]{1,0:T(8,128)(2,1)S(1)} %get-tuple-element.38.refs_1_.refs_6_), kind=kLoop, calls=%fused_computation.2 | loop fusion | flops 1048576 | bytes 1048576 | tf_op jit(solution)/shard_map/concatenate | solution.py:324
  29.0 2.7 %collective-permute-start.8 = (bf16[2048,128]{1,0:T(8,128)(2,1)S(1)}, bf16[2048,128]{1,0:T(8,128)(2,1)S(1)}, u32[]{:S(2)}, u32[]{:S(2)}) collective-permute-start(bf16[2048,128]{1,0:T(8,128)(2,1)S(1)} %stitch.4), channel_id=1, source_target_pairs={{0,16},{2,18},{4,20},{6,22},{8,24},{10,26},{12,28},{14,30},{16,0},... | collective-permute-start | bytes 1572872 | tf_op jit(solution)/shard_map/ppermute | solution.py:275
  31.7 5.3 %collective-permute-done.7.refs_4_.refs_0_.refs_9_ = bf16[1024,128]{1,0:T(8,128)(2,1)S(1)} collective-permute-done((bf16[1024,128]{1,0:T(8,128)(2,1)S(1)}, bf16[1024,128]{1,0:T(8,128)(2,1)S(1)}, u32[]{:S(2)}, u32[]{:S(2)}) %collective-permute-start.7) | collective-permute-done | bytes 262176 | tf_op jit(solution)/shard_map/ppermute | solution.py:275
  37.0 1.5 %collective-permute-start.9 = (bf16[2048,128]{1,0:T(8,128)(2,1)S(1)}, bf16[2048,128]{1,0:T(8,128)(2,1)S(1)}, u32[]{:S(2)}, u32[]{:S(2)}) collective-permute-start(bf16[2048,128]{1,0:T(8,128)(2,1)S(1)} %stitch.4), channel_id=1, source_target_pairs={{0,4},{2,6},{4,0},{6,2},{8,12},{10,14},{12,8},{14,10},{16,20},{18,... | collective-permute-start | bytes 1572872 | tf_op jit(solution)/shard_map/ppermute | solution.py:275
  39.1 11.8 %collective-permute-done.5.refs_4_.refs_1_.refs_2_ = bf16[2048,128]{1,0:T(8,128)(2,1)S(1)} collective-permute-done((bf16[2048,128]{1,0:T(8,128)(2,1)S(1)}, bf16[2048,128]{1,0:T(8,128)(2,1)S(1)}, u32[]{:S(2)}, u32[]{:S(2)}) %collective-permute-start.5) | collective-permute-done | bytes 524320 | tf_op jit(solution)/shard_map/ppermute | solution.py:275
  50.9 2.0 %collective-permute-done.8.refs_9_.refs_14_ = bf16[2048,128]{1,0:T(8,128)(2,1)S(1)} collective-permute-done((bf16[2048,128]{1,0:T(8,128)(2,1)S(1)}, bf16[2048,128]{1,0:T(8,128)(2,1)S(1)}, u32[]{:S(2)}, u32[]{:S(2)}) %collective-permute-start.8) | collective-permute-done | bytes 524320 | tf_op jit(solution)/shard_map/ppermute | solution.py:275
  52.9 1.3 %collective-permute-done.10.refs_1_.refs_16_ = bf16[1024,128]{1,0:T(8,128)(2,1)S(1)} collective-permute-done((bf16[1024,128]{1,0:T(8,128)(2,1)S(1)}, bf16[1024,128]{1,0:T(8,128)(2,1)S(1)}, u32[]{:S(2)}, u32[]{:S(2)}) %collective-permute-start.10) | collective-permute-done | bytes 262176 | tf_op jit(solution)/shard_map/ppermute | solution.py:275
  55.3 1.1 %collective-permute-start.19 = (bf16[3072,128]{1,0:T(8,128)(2,1)S(1)}, bf16[3072,128]{1,0:T(8,128)(2,1)S(1)}, u32[]{:S(2)}, u32[]{:S(2)}) collective-permute-start(bf16[3072,128]{1,0:T(8,128)(2,1)S(1)} %stitch.5), channel_id=1, source_target_pairs={{0,2},{2,0},{4,6},{6,4},{8,10},{10,8},{12,14},{14,12},{16,18},{18,... | collective-permute-start | bytes 2359304 | tf_op jit(solution)/shard_map/ppermute | solution.py:275
  56.4 1.2 %collective-permute-start.15 = (bf16[2048,128]{1,0:T(8,128)(2,1)S(1)}, bf16[2048,128]{1,0:T(8,128)(2,1)S(1)}, u32[]{:S(2)}, u32[]{:S(2)}) collective-permute-start(bf16[2048,128]{1,0:T(8,128)(2,1)S(1)} %collective-permute-done.8.refs_9_.refs_14_), channel_id=1, source_target_pairs={{0,4},{2,6},{4,0},{6,2},{8,12},{10,14},{12,8},{14,10},{16,20},{18,... | collective-permute-start | bytes 1572872 | tf_op jit(solution)/shard_map/ppermute | solution.py:275
  57.6 2.6 %collective-permute-start.16 = (bf16[1024,128]{1,0:T(8,128)(2,1)S(1)}, bf16[1024,128]{1,0:T(8,128)(2,1)S(1)}, u32[]{:S(2)}, u32[]{:S(2)}) collective-permute-start(bf16[1024,128]{1,0:T(8,128)(2,1)S(1)} %collective-permute-done.7.refs_4_.refs_0_.refs_9_), channel_id=1, source_target_pairs={{0,16},{2,18},{4,20},{6,22},{8,24},{10,26},{12,28},{14,30},{16,0},... | collective-permute-start | bytes 786440 | tf_op jit(solution)/shard_map/ppermute | solution.py:275
  60.2 1.5 %collective-permute-start.18 = (bf16[1024,128]{1,0:T(8,128)(2,1)S(1)}, bf16[1024,128]{1,0:T(8,128)(2,1)S(1)}, u32[]{:S(2)}, u32[]{:S(2)}) collective-permute-start(bf16[1024,128]{1,0:T(8,128)(2,1)S(1)} %collective-permute-done.7.refs_4_.refs_0_.refs_9_), channel_id=1, source_target_pairs={{0,4},{2,6},{4,0},{6,2},{8,12},{10,14},{12,8},{14,10},{16,20},{18,... | collective-permute-start | bytes 786440 | tf_op jit(solution)/shard_map/ppermute | solution.py:275
  61.7 4.6 %project.1.refs_0_ = bf16[9,128,1024]{2,1,0:T(8,128)(2,1)S(1)} custom-call(s32[2]{0:T(128)S(1)} %pad_add_fusion.pos, s32[288]{0:T(512)S(1)} %reshape.19.cols, s32[96]{0:T(128)S(1)} %reshape.20.counts, bf16[3,32,3,128,128]{4,3,2,1,0:T(8,128)(2,1)} %potential.3, bf16[4096,128]{1,0:T(8,128)(2,1)} %bitcast.2.refs_0_, ...), custom_call_target="tpu_custom_call" | custom-call | tf_op jit(solution)/shard_map/project/pallas_call | solution.py:160
  66.4 6.1 %collective-permute-done.16.refs_10_.refs_15_ = bf16[1024,128]{1,0:T(8,128)(2,1)S(1)} collective-permute-done((bf16[1024,128]{1,0:T(8,128)(2,1)S(1)}, bf16[1024,128]{1,0:T(8,128)(2,1)S(1)}, u32[]{:S(2)}, u32[]{:S(2)}) %collective-permute-start.16) | collective-permute-done | bytes 262176 | tf_op jit(solution)/shard_map/ppermute | solution.py:275
  72.5 3.1 %collective-permute-done.18.refs_7_.refs_12_ = bf16[1024,128]{1,0:T(8,128)(2,1)S(1)} collective-permute-done((bf16[1024,128]{1,0:T(8,128)(2,1)S(1)}, bf16[1024,128]{1,0:T(8,128)(2,1)S(1)}, u32[]{:S(2)}, u32[]{:S(2)}) %collective-permute-start.18) | collective-permute-done | bytes 262176 | tf_op jit(solution)/shard_map/ppermute | solution.py:275
  76.1 1.3 %collective-permute-start.17 = (bf16[1024,128]{1,0:T(8,128)(2,1)S(1)}, bf16[1024,128]{1,0:T(8,128)(2,1)S(1)}, u32[]{:S(2)}, u32[]{:S(2)}) collective-permute-start(bf16[1024,128]{1,0:T(8,128)(2,1)S(1)} %collective-permute-done.16.refs_10_.refs_15_), channel_id=1, source_target_pairs={{0,4},{2,6},{4,0},{6,2},{8,12},{10,14},{12,8},{14,10},{16,20},{18,... | collective-permute-start | bytes 786440 | tf_op jit(solution)/shard_map/ppermute | solution.py:275
  77.4 2.7 %couple.1.refs_4_ = f32[9,128,128]{2,1,0:T(8,128)S(1)} custom-call(s32[2]{0:T(128)S(1)} %pad_add_fusion.pos, s32[48]{0:T(128)S(1)} %reshape.21.partners, bf16[9,128,1024]{2,1,0:T(8,128)(2,1)S(1)} %project.1.refs_0_, bf16[1024,128]{1,0:T(8,128)(2,1)S(1)} %get-tuple-element.38.refs_1_.refs_6_, ...), custom_call_target="tpu_custom_call" | custom-call | tf_op jit(solution)/shard_map/couple/pallas_call | solution.py:247
  80.1 3.4 %project_last.1.refs_5_ = bf16[3,128,1024]{2,1,0:T(8,128)(2,1)S(1)} custom-call(s32[2]{0:T(128)S(1)} %pad_add_fusion.pos, s32[288]{0:T(512)S(1)} %reshape.19.cols, s32[96]{0:T(128)S(1)} %reshape.20.counts, bf16[3,32,3,128,128]{4,3,2,1,0:T(8,128)(2,1)} %potential.3, bf16[1024,128]{1,0:T(8,128)(2,1)S(1)} %collective-permute-done.7.refs_4_.refs_0_.refs_9_, ...), custom_call_target="tpu_custom_call" | custom-call | tf_op jit(solution)/shard_map/project_last/pallas_call | solution.py:160
  83.4 1.0 collective-permute-done.17.refs_3_.refs_18_
  84.4 2.8 %couple_last.1 = f32[2,12,64,128]{3,2,1,0:T(8,128)S(1)} custom-call(s32[2]{0:T(128)S(1)} %pad_add_fusion.pos, s32[48]{0:T(128)S(1)} %reshape.21.partners, bf16[9,128,1024]{2,1,0:T(8,128)(2,1)S(1)} %project.1.refs_0_, bf16[1024,128]{1,0:T(8,128)(2,1)S(1)} %collective-permute-done.10.refs_1_.refs_16_, ...), custom_call_target="tpu_custom_call" | custom-call | tf_op jit(solution)/shard_map/couple_last/pallas_call | solution.py:247
  87.3 1.7 %collective-permute-done.22 = f32[12,64,128]{2,1,0:T(8,128)S(1)} collective-permute-done((f32[12,64,128]{2,1,0:T(8,128)S(1)}, f32[12,64,128]{2,1,0:T(8,128)S(1)}, u32[]{:S(2)}, u32[]{:S(2)}) %collective-permute-start.22) | collective-permute-done | bytes 393248 | tf_op jit(solution)/shard_map/ppermute | solution.py:278
  89.1 2.3 %collective-permute-start.25 = (bf16[3,64,128]{2,1,0:T(8,128)(2,1)S(1)}, bf16[3,64,128]{2,1,0:T(8,128)(2,1)S(1)}, u32[]{:S(2)}, u32[]{:S(2)}) collective-permute-start(bf16[3,64,128]{2,1,0:T(8,128)(2,1)S(1)} %get-tuple-element.62), channel_id=1, source_target_pairs={{0,10},{2,8},{4,14},{6,12},{8,2},{10,0},{12,6},{14,4},{16,26},{18,... | collective-permute-start | bytes 147464 | tf_op jit(solution)/shard_map/ppermute | solution.py:275
  92.7 1.7 %collective-permute-done.25 = bf16[3,64,128]{2,1,0:T(8,128)(2,1)S(1)} collective-permute-done((bf16[3,64,128]{2,1,0:T(8,128)(2,1)S(1)}, bf16[3,64,128]{2,1,0:T(8,128)(2,1)S(1)}, u32[]{:S(2)}, u32[]{:S(2)}) %collective-permute-start.25) | collective-permute-done | bytes 49184 | tf_op jit(solution)/shard_map/ppermute | solution.py:275
  94.3 1.2 %collective-permute-done.24 = bf16[3,64,128]{2,1,0:T(8,128)(2,1)S(1)} collective-permute-done((bf16[3,64,128]{2,1,0:T(8,128)(2,1)S(1)}, bf16[3,64,128]{2,1,0:T(8,128)(2,1)S(1)}, u32[]{:S(2)}, u32[]{:S(2)}) %collective-permute-start.24) | collective-permute-done | bytes 49184 | tf_op jit(solution)/shard_map/ppermute | solution.py:275
  (50 shorter events, 7.6 us)
Async XLA Ops:
  1.3 9.6 %copy-start = (bf16[1024,128]{1,0:T(8,128)(2,1)}, bf16[1024,128]{1,0:T(8,128)(2,1)S(1)}, u32[]{:S(2)}) copy-start(bf16[1024,128]{1,0:T(8,128)(2,1)S(1)} %get-tuple-element.39) | copy-start | bytes 786436
  1.4 18.7 %copy-start.2 = (s32[3,32,3]{1,2,0:T(4,128)S(1)}, s32[3,32,3]{1,2,0:T(4,128)}, u32[]{:S(2)}) copy-start(s32[3,32,3]{1,2,0:T(4,128)} %param.8) | copy-start | bytes 3460
  1.4 18.9 %copy-start.3 = (s32[3,32]{1,0:T(4,128)S(1)}, s32[3,32]{1,0:T(4,128)}, u32[]{:S(2)}) copy-start(s32[3,32]{1,0:T(4,128)} %param.9) | copy-start | bytes 1156
  1.4 19.0 %copy-start.4 = (s32[3,16]{1,0:T(4,128)S(1)}, s32[3,16]{1,0:T(4,128)}, u32[]{:S(2)}) copy-start(s32[3,16]{1,0:T(4,128)} %param.10) | copy-start | bytes 580
  1.4 9.5 %collective-permute-start = (bf16[1024,128]{1,0:T(8,128)(2,1)S(1)}, bf16[1024,128]{1,0:T(8,128)(2,1)S(1)}, u32[]{:S(2)}, u32[]{:S(2)}) collective-permute-start(bf16[1024,128]{1,0:T(8,128)(2,1)S(1)} %get-tuple-element.39), channel_id=1, source_target_pairs={{0,2},{2,0},{4,6},{6,4},{8,10},{10,8},{12,14},{14,12},{16,18},{18,... | collective-permute-start | bytes 786440 | tf_op jit(solution)/shard_map/ppermute | solution.py:275
  4.4 7.8 %collective-permute-start.1 = (bf16[1024,128]{1,0:T(8,128)(2,1)S(1)}, bf16[1024,128]{1,0:T(8,128)(2,1)S(1)}, u32[]{:S(2)}, u32[]{:S(2)}) collective-permute-start(bf16[1024,128]{1,0:T(8,128)(2,1)S(1)} %get-tuple-element.38.refs_1_.refs_6_), channel_id=1, source_target_pairs={{0,4},{2,6},{4,0},{6,2},{8,12},{10,14},{12,8},{14,10},{16,20},{18,... | collective-permute-start | bytes 786440 | tf_op jit(solution)/shard_map/ppermute | solution.py:275
  5.9 14.1 %collective-permute-start.4 = (bf16[1024,128]{1,0:T(8,128)(2,1)S(1)}, bf16[1024,128]{1,0:T(8,128)(2,1)S(1)}, u32[]{:S(2)}, u32[]{:S(2)}) collective-permute-start(bf16[1024,128]{1,0:T(8,128)(2,1)S(1)} %get-tuple-element.38.refs_1_.refs_6_), channel_id=1, source_target_pairs={{0,16},{2,18},{4,20},{6,22},{8,24},{10,26},{12,28},{14,30},{16,0},... | collective-permute-start | bytes 786440 | tf_op jit(solution)/shard_map/ppermute | solution.py:275
  9.4 17.5 %collective-permute-start.3 = (bf16[2048,128]{1,0:T(8,128)(2,1)}, bf16[2048,128]{1,0:T(8,128)(2,1)S(1)}, u32[]{:S(2)}, u32[]{:S(2)}) collective-permute-start(bf16[2048,128]{1,0:T(8,128)(2,1)} %pad_maximum_fusion.1), channel_id=1, source_target_pairs={{0,8},{2,10},{4,12},{6,14},{8,0},{10,2},{12,4},{14,6},{16,24},{18,... | collective-permute-start | bytes 1572872 | tf_op jit(solution)/shard_map/ppermute | solution.py:275
  13.1 25.4 %collective-permute-start.2 = (bf16[3072,128]{1,0:T(8,128)(2,1)}, bf16[3072,128]{1,0:T(8,128)(2,1)S(1)}, u32[]{:S(2)}, u32[]{:S(2)}) collective-permute-start(bf16[3072,128]{1,0:T(8,128)(2,1)} %pad_maximum_fusion), channel_id=1, source_target_pairs={{0,2},{2,0},{4,6},{6,4},{8,10},{10,8},{12,14},{14,12},{16,18},{18,... | collective-permute-start | bytes 2359304 | tf_op jit(solution)/shard_map/ppermute | solution.py:275
  20.0 35.3 %collective-permute-start.6 = (bf16[4096,128]{1,0:T(8,128)(2,1)}, bf16[4096,128]{1,0:T(8,128)(2,1)S(1)}, u32[]{:S(2)}, u32[]{:S(2)}) collective-permute-start(bf16[4096,128]{1,0:T(8,128)(2,1)} %bitcast.2.refs_0_), channel_id=1, source_target_pairs={{0,1},{1,0},{2,3},{3,2},{4,5},{5,4},{6,7},{7,6},{8,9},{9,8},{10,11... | collective-permute-start | bytes 3145736 | tf_op jit(solution)/shard_map/ppermute | solution.py:278
  26.9 10.1 %collective-permute-start.7 = (bf16[1024,128]{1,0:T(8,128)(2,1)S(1)}, bf16[1024,128]{1,0:T(8,128)(2,1)S(1)}, u32[]{:S(2)}, u32[]{:S(2)}) collective-permute-start(bf16[1024,128]{1,0:T(8,128)(2,1)S(1)} %stitch.3), channel_id=1, source_target_pairs={{0,2},{2,0},{4,6},{6,4},{8,10},{10,8},{12,14},{14,12},{16,18},{18,... | collective-permute-start | bytes 786440 | tf_op jit(solution)/shard_map/ppermute | solution.py:275
  28.5 22.3 %collective-permute-start.5 = (bf16[2048,128]{1,0:T(8,128)(2,1)S(1)}, bf16[2048,128]{1,0:T(8,128)(2,1)S(1)}, u32[]{:S(2)}, u32[]{:S(2)}) collective-permute-start(bf16[2048,128]{1,0:T(8,128)(2,1)S(1)} %pad_maximum_fusion.2), channel_id=1, source_target_pairs={{0,8},{2,10},{4,12},{6,14},{8,0},{10,2},{12,4},{14,6},{16,24},{18,... | collective-permute-start | bytes 1572872 | tf_op jit(solution)/shard_map/ppermute | solution.py:275
  29.0 23.9 %collective-permute-start.8 = (bf16[2048,128]{1,0:T(8,128)(2,1)S(1)}, bf16[2048,128]{1,0:T(8,128)(2,1)S(1)}, u32[]{:S(2)}, u32[]{:S(2)}) collective-permute-start(bf16[2048,128]{1,0:T(8,128)(2,1)S(1)} %stitch.4), channel_id=1, source_target_pairs={{0,16},{2,18},{4,20},{6,22},{8,24},{10,26},{12,28},{14,30},{16,0},... | collective-permute-start | bytes 1572872 | tf_op jit(solution)/shard_map/ppermute | solution.py:275
  37.0 15.9 %collective-permute-start.9 = (bf16[2048,128]{1,0:T(8,128)(2,1)S(1)}, bf16[2048,128]{1,0:T(8,128)(2,1)S(1)}, u32[]{:S(2)}, u32[]{:S(2)}) collective-permute-start(bf16[2048,128]{1,0:T(8,128)(2,1)S(1)} %stitch.4), channel_id=1, source_target_pairs={{0,4},{2,6},{4,0},{6,2},{8,12},{10,14},{12,8},{14,10},{16,20},{18,... | collective-permute-start | bytes 1572872 | tf_op jit(solution)/shard_map/ppermute | solution.py:275
  38.6 15.6 %collective-permute-start.10 = (bf16[1024,128]{1,0:T(8,128)(2,1)S(1)}, bf16[1024,128]{1,0:T(8,128)(2,1)S(1)}, u32[]{:S(2)}, u32[]{:S(2)}) collective-permute-start(bf16[1024,128]{1,0:T(8,128)(2,1)S(1)} %collective-permute-done.4.refs_8_.refs_13_), channel_id=1, source_target_pairs={{0,4},{2,6},{4,0},{6,2},{8,12},{10,14},{12,8},{14,10},{16,20},{18,... | collective-permute-start | bytes 786440 | tf_op jit(solution)/shard_map/ppermute | solution.py:275
  54.2 2.2 %collective-permute-start.11 = (bf16[1024,128]{1,0:T(8,128)(2,1)S(1)}, bf16[1024,128]{1,0:T(8,128)(2,1)S(1)}, u32[]{:S(2)}, u32[]{:S(2)}) collective-permute-start(bf16[1024,128]{1,0:T(8,128)(2,1)S(1)} %collective-permute-done.refs_0_.refs_1_.refs_2_.refs_7_), channel_id=1, source_target_pairs={{0,1},{1,0},{2,3},{3,2},{4,5},{5,4},{6,7},{7,6},{8,9},{9,8},{10,11... | collective-permute-start | bytes 786440 | tf_op jit(solution)/shard_map/ppermute | solution.py:278
  54.2 7.5 %collective-permute-start.12 = (bf16[3072,128]{1,0:T(8,128)(2,1)S(1)}, bf16[3072,128]{1,0:T(8,128)(2,1)S(1)}, u32[]{:S(2)}, u32[]{:S(2)}) collective-permute-start(bf16[3072,128]{1,0:T(8,128)(2,1)S(1)} %collective-permute-done.2.refs_2_), channel_id=1, source_target_pairs={{0,1},{1,0},{2,3},{3,2},{4,5},{5,4},{6,7},{7,6},{8,9},{9,8},{10,11... | collective-permute-start | bytes 2359304 | tf_op jit(solution)/shard_map/ppermute | solution.py:278
  54.7 2.9 %collective-permute-start.13 = (bf16[2048,128]{1,0:T(8,128)(2,1)S(1)}, bf16[2048,128]{1,0:T(8,128)(2,1)S(1)}, u32[]{:S(2)}, u32[]{:S(2)}) collective-permute-start(bf16[2048,128]{1,0:T(8,128)(2,1)S(1)} %collective-permute-done.3.refs_0_.refs_1_.refs_3_.refs_8_), channel_id=1, source_target_pairs={{0,1},{1,0},{2,3},{3,2},{4,5},{5,4},{6,7},{7,6},{8,9},{9,8},{10,11... | collective-permute-start | bytes 1572872 | tf_op jit(solution)/shard_map/ppermute | solution.py:278
  54.7 5.5 %collective-permute-start.14 = (bf16[2048,128]{1,0:T(8,128)(2,1)S(1)}, bf16[2048,128]{1,0:T(8,128)(2,1)S(1)}, u32[]{:S(2)}, u32[]{:S(2)}) collective-permute-start(bf16[2048,128]{1,0:T(8,128)(2,1)S(1)} %collective-permute-done.5.refs_4_.refs_1_.refs_2_), channel_id=1, source_target_pairs={{0,1},{1,0},{2,3},{3,2},{4,5},{5,4},{6,7},{7,6},{8,9},{9,8},{10,11... | collective-permute-start | bytes 1572872 | tf_op jit(solution)/shard_map/ppermute | solution.py:278
  55.3 20.2 %collective-permute-start.19 = (bf16[3072,128]{1,0:T(8,128)(2,1)S(1)}, bf16[3072,128]{1,0:T(8,128)(2,1)S(1)}, u32[]{:S(2)}, u32[]{:S(2)}) collective-permute-start(bf16[3072,128]{1,0:T(8,128)(2,1)S(1)} %stitch.5), channel_id=1, source_target_pairs={{0,2},{2,0},{4,6},{6,4},{8,10},{10,8},{12,14},{14,12},{16,18},{18,... | collective-permute-start | bytes 2359304 | tf_op jit(solution)/shard_map/ppermute | solution.py:275
  56.4 19.2 %collective-permute-start.15 = (bf16[2048,128]{1,0:T(8,128)(2,1)S(1)}, bf16[2048,128]{1,0:T(8,128)(2,1)S(1)}, u32[]{:S(2)}, u32[]{:S(2)}) collective-permute-start(bf16[2048,128]{1,0:T(8,128)(2,1)S(1)} %collective-permute-done.8.refs_9_.refs_14_), channel_id=1, source_target_pairs={{0,4},{2,6},{4,0},{6,2},{8,12},{10,14},{12,8},{14,10},{16,20},{18,... | collective-permute-start | bytes 1572872 | tf_op jit(solution)/shard_map/ppermute | solution.py:275
  57.6 14.9 %collective-permute-start.16 = (bf16[1024,128]{1,0:T(8,128)(2,1)S(1)}, bf16[1024,128]{1,0:T(8,128)(2,1)S(1)}, u32[]{:S(2)}, u32[]{:S(2)}) collective-permute-start(bf16[1024,128]{1,0:T(8,128)(2,1)S(1)} %collective-permute-done.7.refs_4_.refs_0_.refs_9_), channel_id=1, source_target_pairs={{0,16},{2,18},{4,20},{6,22},{8,24},{10,26},{12,28},{14,30},{16,0},... | collective-permute-start | bytes 786440 | tf_op jit(solution)/shard_map/ppermute | solution.py:275
  60.2 15.4 %collective-permute-start.18 = (bf16[1024,128]{1,0:T(8,128)(2,1)S(1)}, bf16[1024,128]{1,0:T(8,128)(2,1)S(1)}, u32[]{:S(2)}, u32[]{:S(2)}) collective-permute-start(bf16[1024,128]{1,0:T(8,128)(2,1)S(1)} %collective-permute-done.7.refs_4_.refs_0_.refs_9_), channel_id=1, source_target_pairs={{0,4},{2,6},{4,0},{6,2},{8,12},{10,14},{12,8},{14,10},{16,20},{18,... | collective-permute-start | bytes 786440 | tf_op jit(solution)/shard_map/ppermute | solution.py:275
  75.6 4.5 %collective-permute-start.21 = (bf16[3072,128]{1,0:T(8,128)(2,1)S(1)}, bf16[3072,128]{1,0:T(8,128)(2,1)S(1)}, u32[]{:S(2)}, u32[]{:S(2)}) collective-permute-start(bf16[3072,128]{1,0:T(8,128)(2,1)S(1)} %collective-permute-done.19.refs_1_), channel_id=1, source_target_pairs={{0,1},{1,0},{2,3},{3,2},{4,5},{5,4},{6,7},{7,6},{8,9},{9,8},{10,11... | collective-permute-start | bytes 2359304 | tf_op jit(solution)/shard_map/ppermute | solution.py:278
  75.6 4.4 %collective-permute-start.20 = (bf16[1024,128]{1,0:T(8,128)(2,1)S(1)}, bf16[1024,128]{1,0:T(8,128)(2,1)S(1)}, u32[]{:S(2)}, u32[]{:S(2)}) collective-permute-start(bf16[1024,128]{1,0:T(8,128)(2,1)S(1)} %collective-permute-done.7.refs_4_.refs_0_.refs_9_), channel_id=1, source_target_pairs={{0,1},{1,0},{2,3},{3,2},{4,5},{5,4},{6,7},{7,6},{8,9},{9,8},{10,11... | collective-permute-start | bytes 786440 | tf_op jit(solution)/shard_map/ppermute | solution.py:278
  76.1 8.3 %collective-permute-start.17 = (bf16[1024,128]{1,0:T(8,128)(2,1)S(1)}, bf16[1024,128]{1,0:T(8,128)(2,1)S(1)}, u32[]{:S(2)}, u32[]{:S(2)}) collective-permute-start(bf16[1024,128]{1,0:T(8,128)(2,1)S(1)} %collective-permute-done.16.refs_10_.refs_15_), channel_id=1, source_target_pairs={{0,4},{2,6},{4,0},{6,2},{8,12},{10,14},{12,8},{14,10},{16,20},{18,... | collective-permute-start | bytes 786440 | tf_op jit(solution)/shard_map/ppermute | solution.py:275
  87.2 8.8 %copy-start.1 = (f32[3,1,64,128]{3,2,1,0:T(8,128)S(1)}, f32[3,1,64,128]{3,2,1,0:T(8,128)}, u32[]{:S(2)}) copy-start(f32[3,1,64,128]{3,2,1,0:T(8,128)} %param.11) | copy-start | bytes 294916
  87.2 1.8 %collective-permute-start.22 = (f32[12,64,128]{2,1,0:T(8,128)S(1)}, f32[12,64,128]{2,1,0:T(8,128)S(1)}, u32[]{:S(2)}, u32[]{:S(2)}) collective-permute-start(f32[12,64,128]{2,1,0:T(8,128)S(1)} %slice_bitcast_fusion), channel_id=1, source_target_pairs={{0,1},{1,0},{2,3},{3,2},{4,5},{5,4},{6,7},{7,6},{8,9},{9,8},{10,11... | collective-permute-start | bytes 1179656 | tf_op jit(solution)/shard_map/ppermute | solution.py:278
  89.1 5.2 %collective-permute-start.25 = (bf16[3,64,128]{2,1,0:T(8,128)(2,1)S(1)}, bf16[3,64,128]{2,1,0:T(8,128)(2,1)S(1)}, u32[]{:S(2)}, u32[]{:S(2)}) collective-permute-start(bf16[3,64,128]{2,1,0:T(8,128)(2,1)S(1)} %get-tuple-element.62), channel_id=1, source_target_pairs={{0,10},{2,8},{4,14},{6,12},{8,2},{10,0},{12,6},{14,4},{16,26},{18,... | collective-permute-start | bytes 147464 | tf_op jit(solution)/shard_map/ppermute | solution.py:275
  91.4 4.1 %collective-permute-start.24 = (bf16[3,64,128]{2,1,0:T(8,128)(2,1)S(1)}, bf16[3,64,128]{2,1,0:T(8,128)(2,1)S(1)}, u32[]{:S(2)}, u32[]{:S(2)}) collective-permute-start(bf16[3,64,128]{2,1,0:T(8,128)(2,1)S(1)} %get-tuple-element.63), channel_id=1, source_target_pairs={{0,8},{2,10},{4,12},{6,14},{8,0},{10,2},{12,4},{14,6},{16,24},{18,... | collective-permute-start | bytes 147464 | tf_op jit(solution)/shard_map/ppermute | solution.py:275
  91.9 4.1 %collective-permute-start.23 = (bf16[3,64,128]{2,1,0:T(8,128)(2,1)S(1)}, bf16[3,64,128]{2,1,0:T(8,128)(2,1)S(1)}, u32[]{:S(2)}, u32[]{:S(2)}) collective-permute-start(bf16[3,64,128]{2,1,0:T(8,128)(2,1)S(1)} %get-tuple-element.61), channel_id=1, source_target_pairs={{0,2},{2,0},{4,6},{6,4},{8,10},{10,8},{12,14},{14,12},{16,18},{18,... | collective-permute-start | bytes 147464 | tf_op jit(solution)/shard_map/ppermute | solution.py:275

commit v9 on v8

--- a/solution.py
+++ b/solution.py
@@ -14,22 +14,19 @@
 
 
 FIRST = ("c0", "c1", "s1.0")
-GATHER = ("p3", "r1", "r2")
-SECOND = GATHER + ("s2.1", "s1.1","s3.0")
+SECOND = ("p3", "r1", "r2", "s2.1", "s1.1","s3.0")
 WAITS = {
     **dict.fromkeys(FIRST, ()),
     "s2.0": (),
     "t1o": ("s2.0",),
     "r1": ("c0","s1.0"),
-    **dict.fromkeys(("p3", "r2", "s2.1", "s1.1"), FIRST+("i","s2.0")),
+    **dict.fromkeys(("p3", "r2", "s2.1", "s1.1"), FIRST+("i",)),
     **dict.fromkeys(("s3.0",), ("p3",)),
 
-    "r3": GATHER+("s1.1","s3.0"),
-    **dict.fromkeys(("s2.2","s3.1","s1.2"), SECOND),
-    **dict.fromkeys(("t1c0","t1c1","t1r1","t1r2","t1p3"), SECOND),
+    **dict.fromkeys(("s2.2","s3.1","s1.2","r3","u3"), SECOND),
+    **dict.fromkeys(("t1k1","t1k2"), SECOND),
     "q": (),
-
-    "t1r3": ("q","s2.2","s3.1","s1.2"),
+    "t1k3": ("q","s2.2","s3.1","s1.2"),
 }
 
 
@@ -299,6 +296,7 @@
         pieces = {0: [[0], list(range(1, group - 1)), [group - 1]], far: [[0], list(range(1, group - 1)), [group - 1]]}
         sizes = {}
         orders = {}
+        joins = {}
 
         slices = [
             lax.dynamic_slice_in_dim(own, (chunk ^ j) * rows, rows, 0) for j in range(group)
@@ -313,8 +311,9 @@
         def held(key, j):
             if key == 0:
                 return slices[j], 0, True
-            if j in orders[key]:
-                return get(f"r{key}"), orders[key].index(j), False
+            for name in (f"r{key}", f"u{key}"):
+                if j in orders.get(name, ()):
+                    return get(name), orders[name].index(j), False
             return (get(f"c{key.bit_length() - 1}"), j, False) if j else part(key)
 
         def joined(places, values):
@@ -353,25 +352,44 @@
         for key in sorted(range(1, group), key=lambda k: (bin(k).count("1"), k)):
             bit = key & -key
             before = key ^ bit
-            known = 1 if before else bit
-            send = [j for j in range(group) if j ^ bit >= known]
-            orders[key] = [j ^ bit for j in send]
-            plan[f"r{key}"] = (
-                lambda before=before, send=send: [held(before, j) for j in send],
-                functools.partial(swap, mask=spread(bit, inside)),
-            )
+            name = f"r{key}"
+            if before == 0:
+                send = [j for j in range(group) if j ^ bit >= bit]
+                joins[name] = jnp.concatenate([slices[j] for j in send], axis=0)
+                source = lambda name=name: [done["i"][name]]
+            elif before & (before - 1) == 0:
+                send = orders[f"r{before}"]
+                source = lambda before=before: [get(f"r{before}")]
+                other = [j ^ before for j in range(1, group) if j ^ bit not in send]
+                orders[f"u{key}"] = [j ^ before for j in other]
+                plan[f"u{key}"] = (
+                    lambda bit=bit, other=other: [held(bit, j) for j in other],
+                    functools.partial(swap, mask=spread(before, inside)),
+                )
+            else:
+                send = [j for j in range(group) if j != bit]
+                source = lambda before=before, send=send: [held(before, j) for j in send]
+            orders[name] = [j ^ bit for j in send]
+            plan[name] = (source, functools.partial(swap, mask=spread(bit, inside)))
+
         def rows_of(key):
             top = key.bit_length() - 1
-            if key == 1 << top:
-                return [(f"c{top}", list(range(key))), (f"r{key}", orders[key])]
-            return [(f"p{key}", [0]), (f"r{key}", orders[key])]
+            first = (f"c{top}", list(range(key))) if key == 1 << top else (f"p{key}", [0])
+            names = [name for name in (f"r{key}", f"u{key}") if name in plan]
+            return [first] + [(name, orders[name]) for name in names]
 
         for shift in range(1, halves):
             turn = functools.partial(rotate, shift=shift)
             plan[f"t{shift}o"] = (lambda: [own], turn)
             for key in range(1, group):
-                for name, _ in rows_of(key):
-                    plan[f"t{shift}{name}"] = (lambda name=name: [get(name)], turn)
+                plan[f"t{shift}k{key}"] = (
+                    lambda key=key: [
+                        (get(name), i, False)
+                        for name, order in rows_of(key)
+                        for i in range(len(order))
+                    ],
+                    turn,
+                )
 
         def projection(name, keys):
             values = []
@@ -383,8 +401,12 @@
                         values.append(in_vmem(get(away + "o")) if shift else in_hbm(own))
                         places.append((place, shift, [None] * group))
                         continue
+                    if shift:
+                        values.append(in_vmem(get(f"{away}k{key}")))
+                        places.append((place, shift, sum([js for _, js in rows_of(key)], [])))
+                        continue
                     for source, order in rows_of(key):
-                        values.append(in_vmem(get(away + source)))
+                        values.append(in_vmem(get(source)))
                         places.append((place, shift, order))
             return project(
                 name, pos, cols, counts, potential, values, places, inside, halves
@@ -394,9 +416,14 @@
             lambda: [projection("project", range(group - 1))],
             lambda value: value,
         )
-        tables = (block_cols.reshape(-1), block_counts.reshape(-1), partners.reshape(-1))
-        tables = lax.optimization_barrier((get("c0"), *tables))[1:]
-        cols, counts, pairing = done["i"] = tables
+        done["i"] = {
+            "cols": block_cols.reshape(-1),
+            "counts": block_counts.reshape(-1),
+            "pairing": partners.reshape(-1),
+            **joins,
+        }
+        done["i"] = lax.optimization_barrier((done["i"], get("c0")))[0]
+        cols, counts, pairing = (done["i"][name] for name in ("cols", "counts", "pairing"))
         for name in WAITS:
             if name in plan:
                 get(name)

time: 96.8 us -> 91.6 us (0.946)
  other arithmetic: 3.6 us -> 0.93 us
  starting transfers between devices: 27.6 us -> 25.6 us
    concatenate x3 -> x1, other arithmetic: 2.79 us -> 0.03 us  [joined(): return jnp.concatenate(values, axis=0)]
    ppermute x18 -> x19, starting transfers between devices: 26 us -> 24.8 us  [swap(): return lax.ppermute(value, 'ka', [(i, i ^ mask) for i in range(points)])]
    ppermute x18 -> x19, waiting for transfers between devices: 48.1 us -> 47.2 us  [swap(): return lax.ppermute(value, 'ka', [(i, i ^ mask) for i in range(points)])]
  transfers between devices with their start and end apart: 26 -> 24, of which waited for: 14 -> 13; matrix products, arithmetic and copies ran while one was open for 3% -> 1% of each run, Pallas kernels for 11% -> 12%
where the time goes in v9:
time: 91.6 us; the launch traced here: 91.3 us
  waiting for transfers between devices  48.9 us (53%)
  starting transfers between devices  25.6 us (28%)
  Pallas kernels  13.8 us (15%)
  local copies, waits for them, and re-layouts  1.76 us (2%)
  other arithmetic  0.93 us (1%)
    ppermute x19, waiting for transfers between devices, swap(): return lax.ppermute(value, 'ka', [(i, i ^ mask) for i in range(points)])  47.2 us
    ppermute x19, starting transfers between devices, swap(): return lax.ppermute(value, 'ka', [(i, i ^ mask) for i in range(points)])  24.8 us
    pallas_call x2, Pallas kernels, project(): pl.pallas_call(functools.partial(project_kernel, orders, inside, halves),...  7.88 us
    pallas_call x2, Pallas kernels, couple(): pl.pallas_call(functools.partial(couple_kernel, jobs, last, inside, outsi...  5.48 us
  transfers between devices with their start and end apart: 24, of which 13 were waited for; matrix products, arithmetic and copies ran while one was open for 1% of the time, Pallas kernels for 12%

profile of v9, /device:TPU:0, one launch (start us, length us, event | category | flops | bytes accessed | tf_op | source)
XLA Modules:
  0.0 91.3 jit_solution(13723296120621340192)
XLA Ops:
  0.1 1.3 %constant_dynamic-slice_fusion = (bf16[1024,128]{1,0:T(8,128)(2,1)S(1)}, bf16[1024,128]{1,0:T(8,128)(2,1)S(1)}, bf16[1024,128]{1,0:T(8,128)(2,1)S(1)}, bf16[1024,128]{1,0:T(8,128)(2,1)S(1)}) fusion(bf16[4096,128]{1,0:T(8,128)(2,1)} %bitcast.20, s32[]{:T(128)S(6)} %select_n.15, s32[]{:T(128)S(6)} %select_n.14, s32[]{:T(128)S(6)} %select_n.13, s32[]{:T(128)S(6)} %select_n.12), kind=kLoop, calls=%fused_computation.12 | loop fusion | bytes 2097168 | tf_op jit(solution)/shard_map/dynamic_slice | solution.py:302
  1.4 3.0 %collective-permute-start = (bf16[1024,128]{1,0:T(8,128)(2,1)S(1)}, bf16[1024,128]{1,0:T(8,128)(2,1)S(1)}, u32[]{:S(2)}, u32[]{:S(2)}) collective-permute-start(bf16[1024,128]{1,0:T(8,128)(2,1)S(1)} %get-tuple-element.67), channel_id=1, source_target_pairs={{0,2},{2,0},{4,6},{6,4},{8,10},{10,8},{12,14},{14,12},{16,18},{18,... | collective-permute-start | bytes 786440 | tf_op jit(solution)/shard_map/ppermute | solution.py:272
  4.4 1.5 %collective-permute-start.1 = (bf16[1024,128]{1,0:T(8,128)(2,1)S(1)}, bf16[1024,128]{1,0:T(8,128)(2,1)S(1)}, u32[]{:S(2)}, u32[]{:S(2)}) collective-permute-start(bf16[1024,128]{1,0:T(8,128)(2,1)S(1)} %get-tuple-element.70.refs_1_.refs_6_), channel_id=1, source_target_pairs={{0,4},{2,6},{4,0},{6,2},{8,12},{10,14},{12,8},{14,10},{16,20},{18,... | collective-permute-start | bytes 786440 | tf_op jit(solution)/shard_map/ppermute | solution.py:272
  5.9 1.6 %collective-permute-start.3 = (bf16[2048,128]{1,0:T(8,128)(2,1)S(1)}, bf16[2048,128]{1,0:T(8,128)(2,1)S(1)}, u32[]{:S(2)}, u32[]{:S(2)}) collective-permute-start(bf16[2048,128]{1,0:T(8,128)(2,1)S(1)} %pad_maximum_fusion.2), channel_id=1, source_target_pairs={{0,8},{2,10},{4,12},{6,14},{8,0},{10,2},{12,4},{14,6},{16,24},{18,... | collective-permute-start | bytes 1572872 | tf_op jit(solution)/shard_map/ppermute | solution.py:272
  8.1 2.5 %collective-permute-done.refs_0_.refs_1_.refs_2_.refs_7_ = bf16[1024,128]{1,0:T(8,128)(2,1)S(1)} collective-permute-done((bf16[1024,128]{1,0:T(8,128)(2,1)S(1)}, bf16[1024,128]{1,0:T(8,128)(2,1)S(1)}, u32[]{:S(2)}, u32[]{:S(2)}) %collective-permute-start) | collective-permute-done | bytes 262176 | tf_op jit(solution)/shard_map/ppermute | solution.py:272
  10.7 1.5 %collective-permute-done.1.refs_5_.refs_10_ = bf16[1024,128]{1,0:T(8,128)(2,1)S(1)} collective-permute-done((bf16[1024,128]{1,0:T(8,128)(2,1)S(1)}, bf16[1024,128]{1,0:T(8,128)(2,1)S(1)}, u32[]{:S(2)}, u32[]{:S(2)}) %collective-permute-start.1) | collective-permute-done | bytes 262176 | tf_op jit(solution)/shard_map/ppermute | solution.py:272
  12.5 2.8 %collective-permute-start.5 = (bf16[1024,128]{1,0:T(8,128)(2,1)S(1)}, bf16[1024,128]{1,0:T(8,128)(2,1)S(1)}, u32[]{:S(2)}, u32[]{:S(2)}) collective-permute-start(bf16[1024,128]{1,0:T(8,128)(2,1)S(1)} %get-tuple-element.70.refs_1_.refs_6_), channel_id=1, source_target_pairs={{0,16},{2,18},{4,20},{6,22},{8,24},{10,26},{12,28},{14,30},{16,0},... | collective-permute-start | bytes 786440 | tf_op jit(solution)/shard_map/ppermute | solution.py:272
  15.3 9.5 %collective-permute-done.3.refs_0_.refs_1_.refs_3_.refs_8_ = bf16[2048,128]{1,0:T(8,128)(2,1)S(1)} collective-permute-done((bf16[2048,128]{1,0:T(8,128)(2,1)S(1)}, bf16[2048,128]{1,0:T(8,128)(2,1)S(1)}, u32[]{:S(2)}, u32[]{:S(2)}) %collective-permute-start.3) | collective-permute-done | bytes 524320 | tf_op jit(solution)/shard_map/ppermute | solution.py:272
  24.8 0.6 collective-permute-start.7
  25.4 2.4 %collective-permute-start.8 = (bf16[2048,128]{1,0:T(8,128)(2,1)S(1)}, bf16[2048,128]{1,0:T(8,128)(2,1)S(1)}, u32[]{:S(2)}, u32[]{:S(2)}) collective-permute-start(bf16[2048,128]{1,0:T(8,128)(2,1)S(1)} %stitch.7), channel_id=1, source_target_pairs={{0,16},{2,18},{4,20},{6,22},{8,24},{10,26},{12,28},{14,30},{16,0},... | collective-permute-start | bytes 1572872 | tf_op jit(solution)/shard_map/ppermute | solution.py:272
  27.9 8.0 %collective-permute-done.7.refs_4_.refs_0_.refs_9_ = bf16[1024,128]{1,0:T(8,128)(2,1)S(1)} collective-permute-done((bf16[1024,128]{1,0:T(8,128)(2,1)S(1)}, bf16[1024,128]{1,0:T(8,128)(2,1)S(1)}, u32[]{:S(2)}, u32[]{:S(2)}) %collective-permute-start.7) | collective-permute-done | bytes 262176 | tf_op jit(solution)/shard_map/ppermute | solution.py:272
  35.9 1.5 %collective-permute-start.10 = (bf16[1024,128]{1,0:T(8,128)(2,1)S(1)}, bf16[1024,128]{1,0:T(8,128)(2,1)S(1)}, u32[]{:S(2)}, u32[]{:S(2)}) collective-permute-start(bf16[1024,128]{1,0:T(8,128)(2,1)S(1)} %collective-permute-done.5.refs_8_.refs_13_), channel_id=1, source_target_pairs={{0,4},{2,6},{4,0},{6,2},{8,12},{10,14},{12,8},{14,10},{16,20},{18,... | collective-permute-start | bytes 786440 | tf_op jit(solution)/shard_map/ppermute | solution.py:272
  37.4 10.4 %collective-permute-done.4.refs_2_.refs_3_.refs_4_ = bf16[2048,128]{1,0:T(8,128)(2,1)S(1)} collective-permute-done((bf16[2048,128]{1,0:T(8,128)(2,1)S(1)}, bf16[2048,128]{1,0:T(8,128)(2,1)S(1)}, u32[]{:S(2)}, u32[]{:S(2)}) %collective-permute-start.4) | collective-permute-done | bytes 524320 | tf_op jit(solution)/shard_map/ppermute | solution.py:272
  47.8 1.8 %collective-permute-done.8.refs_9_.refs_14_ = bf16[2048,128]{1,0:T(8,128)(2,1)S(1)} collective-permute-done((bf16[2048,128]{1,0:T(8,128)(2,1)S(1)}, bf16[2048,128]{1,0:T(8,128)(2,1)S(1)}, u32[]{:S(2)}, u32[]{:S(2)}) %collective-permute-start.8) | collective-permute-done | bytes 524320 | tf_op jit(solution)/shard_map/ppermute | solution.py:272
  50.5 0.9 %collective-permute-start.13 = (bf16[2048,128]{1,0:T(8,128)(2,1)S(1)}, bf16[2048,128]{1,0:T(8,128)(2,1)S(1)}, u32[]{:S(2)}, u32[]{:S(2)}) collective-permute-start(bf16[2048,128]{1,0:T(8,128)(2,1)S(1)} %collective-permute-done.8.refs_9_.refs_14_), channel_id=1, source_target_pairs={{0,4},{2,6},{4,0},{6,2},{8,12},{10,14},{12,8},{14,10},{16,20},{18,... | collective-permute-start | bytes 1572872 | tf_op jit(solution)/shard_map/ppermute | solution.py:272
  51.5 1.1 %collective-permute-start.17 = (bf16[2048,128]{1,0:T(8,128)(2,1)S(1)}, bf16[2048,128]{1,0:T(8,128)(2,1)S(1)}, u32[]{:S(2)}, u32[]{:S(2)}) collective-permute-start(bf16[2048,128]{1,0:T(8,128)(2,1)S(1)} %collective-permute-done.4.refs_2_.refs_3_.refs_4_), channel_id=1, source_target_pairs={{0,2},{2,0},{4,6},{6,4},{8,10},{10,8},{12,14},{14,12},{16,18},{18,... | collective-permute-start | bytes 1572872 | tf_op jit(solution)/shard_map/ppermute | solution.py:272
  52.8 1.5 %collective-permute-start.16 = (bf16[1024,128]{1,0:T(8,128)(2,1)S(1)}, bf16[1024,128]{1,0:T(8,128)(2,1)S(1)}, u32[]{:S(2)}, u32[]{:S(2)}) collective-permute-start(bf16[1024,128]{1,0:T(8,128)(2,1)S(1)} %collective-permute-done.7.refs_4_.refs_0_.refs_9_), channel_id=1, source_target_pairs={{0,4},{2,6},{4,0},{6,2},{8,12},{10,14},{12,8},{14,10},{16,20},{18,... | collective-permute-start | bytes 786440 | tf_op jit(solution)/shard_map/ppermute | solution.py:272
  54.2 2.8 %collective-permute-start.18 = (bf16[1024,128]{1,0:T(8,128)(2,1)S(1)}, bf16[1024,128]{1,0:T(8,128)(2,1)S(1)}, u32[]{:S(2)}, u32[]{:S(2)}) collective-permute-start(bf16[1024,128]{1,0:T(8,128)(2,1)S(1)} %stitch.10), channel_id=1, source_target_pairs={{0,8},{2,10},{4,12},{6,14},{8,0},{10,2},{12,4},{14,6},{16,24},{18,... | collective-permute-start | bytes 786440 | tf_op jit(solution)/shard_map/ppermute | solution.py:272
  57.0 4.6 %project.1.refs_0_ = bf16[9,128,1024]{2,1,0:T(8,128)(2,1)S(1)} custom-call(s32[2]{0:T(128)S(1)} %pad_add_fusion.pos, s32[288]{0:T(512)S(1)} %reshape.19.cols, s32[96]{0:T(128)S(1)} %reshape.20.counts, bf16[3,32,3,128,128]{4,3,2,1,0:T(8,128)(2,1)} %potential.3, bf16[4096,128]{1,0:T(8,128)(2,1)} %bitcast.21, ...), custom_call_target="tpu_custom_call" | custom-call | tf_op jit(solution)/shard_map/project/pallas_call | solution.py:157
  61.6 5.5 %collective-permute-done.14.refs_10_.refs_15_ = bf16[1024,128]{1,0:T(8,128)(2,1)S(1)} collective-permute-done((bf16[1024,128]{1,0:T(8,128)(2,1)S(1)}, bf16[1024,128]{1,0:T(8,128)(2,1)S(1)}, u32[]{:S(2)}, u32[]{:S(2)}) %collective-permute-start.14) | collective-permute-done | bytes 262176 | tf_op jit(solution)/shard_map/ppermute | solution.py:272
  67.1 3.0 %collective-permute-done.16.refs_7_.refs_12_ = bf16[1024,128]{1,0:T(8,128)(2,1)S(1)} collective-permute-done((bf16[1024,128]{1,0:T(8,128)(2,1)S(1)}, bf16[1024,128]{1,0:T(8,128)(2,1)S(1)}, u32[]{:S(2)}, u32[]{:S(2)}) %collective-permute-start.16) | collective-permute-done | bytes 262176 | tf_op jit(solution)/shard_map/ppermute | solution.py:272
  70.3 1.0 %collective-permute-start.15 = (bf16[1024,128]{1,0:T(8,128)(2,1)S(1)}, bf16[1024,128]{1,0:T(8,128)(2,1)S(1)}, u32[]{:S(2)}, u32[]{:S(2)}) collective-permute-start(bf16[1024,128]{1,0:T(8,128)(2,1)S(1)} %collective-permute-done.14.refs_10_.refs_15_), channel_id=1, source_target_pairs={{0,4},{2,6},{4,0},{6,2},{8,12},{10,14},{12,8},{14,10},{16,20},{18,... | collective-permute-start | bytes 786440 | tf_op jit(solution)/shard_map/ppermute | solution.py:272
  71.3 2.9 %couple.1.refs_4_ = f32[9,128,128]{2,1,0:T(8,128)S(1)} custom-call(s32[2]{0:T(128)S(1)} %pad_add_fusion.pos, s32[48]{0:T(128)S(1)} %reshape.21.partners, bf16[9,128,1024]{2,1,0:T(8,128)(2,1)S(1)} %project.1.refs_0_, bf16[1024,128]{1,0:T(8,128)(2,1)S(1)} %get-tuple-element.70.refs_1_.refs_6_, ...), custom_call_target="tpu_custom_call" | custom-call | tf_op jit(solution)/shard_map/couple/pallas_call | solution.py:244
  74.2 3.3 %project_last.1.refs_5_ = bf16[3,128,1024]{2,1,0:T(8,128)(2,1)S(1)} custom-call(s32[2]{0:T(128)S(1)} %pad_add_fusion.pos, s32[288]{0:T(512)S(1)} %reshape.19.cols, s32[96]{0:T(128)S(1)} %reshape.20.counts, bf16[3,32,3,128,128]{4,3,2,1,0:T(8,128)(2,1)} %potential.3, bf16[1024,128]{1,0:T(8,128)(2,1)S(1)} %collective-permute-done.7.refs_4_.refs_0_.refs_9_, ...), custom_call_target="tpu_custom_call" | custom-call | tf_op jit(solution)/shard_map/project_last/pallas_call | solution.py:157
  77.5 1.5 %collective-permute-done.15.refs_3_.refs_18_ = bf16[1024,128]{1,0:T(8,128)(2,1)S(1)} collective-permute-done((bf16[1024,128]{1,0:T(8,128)(2,1)S(1)}, bf16[1024,128]{1,0:T(8,128)(2,1)S(1)}, u32[]{:S(2)}, u32[]{:S(2)}) %collective-permute-start.15) | collective-permute-done | bytes 262176 | tf_op jit(solution)/shard_map/ppermute | solution.py:272
  79.0 2.6 %couple_last.1 = f32[2,12,64,128]{3,2,1,0:T(8,128)S(1)} custom-call(s32[2]{0:T(128)S(1)} %pad_add_fusion.pos, s32[48]{0:T(128)S(1)} %reshape.21.partners, bf16[9,128,1024]{2,1,0:T(8,128)(2,1)S(1)} %project.1.refs_0_, bf16[1024,128]{1,0:T(8,128)(2,1)S(1)} %collective-permute-done.10.refs_1_.refs_16_, ...), custom_call_target="tpu_custom_call" | custom-call | tf_op jit(solution)/shard_map/couple_last/pallas_call | solution.py:244
  81.7 1.7 %collective-permute-done.20 = f32[12,64,128]{2,1,0:T(8,128)S(1)} collective-permute-done((f32[12,64,128]{2,1,0:T(8,128)S(1)}, f32[12,64,128]{2,1,0:T(8,128)S(1)}, u32[]{:S(2)}, u32[]{:S(2)}) %collective-permute-start.20) | collective-permute-done | bytes 393248 | tf_op jit(solution)/shard_map/ppermute | solution.py:275
  83.8 2.7 %collective-permute-start.22 = (bf16[3,64,128]{2,1,0:T(8,128)(2,1)S(1)}, bf16[3,64,128]{2,1,0:T(8,128)(2,1)S(1)}, u32[]{:S(2)}, u32[]{:S(2)}) collective-permute-start(bf16[3,64,128]{2,1,0:T(8,128)(2,1)S(1)} %get-tuple-element.73), channel_id=1, source_target_pairs={{0,8},{2,10},{4,12},{6,14},{8,0},{10,2},{12,4},{14,6},{16,24},{18,... | collective-permute-start | bytes 147464 | tf_op jit(solution)/shard_map/ppermute | solution.py:272
  86.5 0.6 collective-permute-start.21
  87.1 1.7 %collective-permute-done.23 = bf16[3,64,128]{2,1,0:T(8,128)(2,1)S(1)} collective-permute-done((bf16[3,64,128]{2,1,0:T(8,128)(2,1)S(1)}, bf16[3,64,128]{2,1,0:T(8,128)(2,1)S(1)}, u32[]{:S(2)}, u32[]{:S(2)}) %collective-permute-start.23) | collective-permute-done | bytes 49184 | tf_op jit(solution)/shard_map/ppermute | solution.py:272
  89.3 1.3 %collective-permute-done.21 = bf16[3,64,128]{2,1,0:T(8,128)(2,1)S(1)} collective-permute-done((bf16[3,64,128]{2,1,0:T(8,128)(2,1)S(1)}, bf16[3,64,128]{2,1,0:T(8,128)(2,1)S(1)}, u32[]{:S(2)}, u32[]{:S(2)}) %collective-permute-start.21) | collective-permute-done | bytes 49184 | tf_op jit(solution)/shard_map/ppermute | solution.py:272
  90.6 0.7 fusion.5
  (49 shorter events, 3.2 us)
Async XLA Ops:
  1.3 6.3 %copy-start.2 = (s32[3,32,3]{1,2,0:T(4,128)S(1)}, s32[3,32,3]{1,2,0:T(4,128)}, u32[]{:S(2)}) copy-start(s32[3,32,3]{1,2,0:T(4,128)} %param.8) | copy-start | bytes 3460
  1.3 6.6 %copy-start.3 = (s32[3,32]{1,0:T(4,128)S(1)}, s32[3,32]{1,0:T(4,128)}, u32[]{:S(2)}) copy-start(s32[3,32]{1,0:T(4,128)} %param.9) | copy-start | bytes 1156
  1.4 6.6 %copy-start.4 = (s32[3,16]{1,0:T(4,128)S(1)}, s32[3,16]{1,0:T(4,128)}, u32[]{:S(2)}) copy-start(s32[3,16]{1,0:T(4,128)} %param.10) | copy-start | bytes 580
  1.4 9.3 %collective-permute-start = (bf16[1024,128]{1,0:T(8,128)(2,1)S(1)}, bf16[1024,128]{1,0:T(8,128)(2,1)S(1)}, u32[]{:S(2)}, u32[]{:S(2)}) collective-permute-start(bf16[1024,128]{1,0:T(8,128)(2,1)S(1)} %get-tuple-element.67), channel_id=1, source_target_pairs={{0,2},{2,0},{4,6},{6,4},{8,10},{10,8},{12,14},{14,12},{16,18},{18,... | collective-permute-start | bytes 786440 | tf_op jit(solution)/shard_map/ppermute | solution.py:272
  4.4 7.8 %collective-permute-start.1 = (bf16[1024,128]{1,0:T(8,128)(2,1)S(1)}, bf16[1024,128]{1,0:T(8,128)(2,1)S(1)}, u32[]{:S(2)}, u32[]{:S(2)}) collective-permute-start(bf16[1024,128]{1,0:T(8,128)(2,1)S(1)} %get-tuple-element.70.refs_1_.refs_6_), channel_id=1, source_target_pairs={{0,4},{2,6},{4,0},{6,2},{8,12},{10,14},{12,8},{14,10},{16,20},{18,... | collective-permute-start | bytes 786440 | tf_op jit(solution)/shard_map/ppermute | solution.py:272
  5.9 18.8 %collective-permute-start.3 = (bf16[2048,128]{1,0:T(8,128)(2,1)S(1)}, bf16[2048,128]{1,0:T(8,128)(2,1)S(1)}, u32[]{:S(2)}, u32[]{:S(2)}) collective-permute-start(bf16[2048,128]{1,0:T(8,128)(2,1)S(1)} %pad_maximum_fusion.2), channel_id=1, source_target_pairs={{0,8},{2,10},{4,12},{6,14},{8,0},{10,2},{12,4},{14,6},{16,24},{18,... | collective-permute-start | bytes 1572872 | tf_op jit(solution)/shard_map/ppermute | solution.py:272
  8.1 29.3 %copy-start = (bf16[1,4096,128]{2,1,0:T(8,128)(2,1)S(1)}, bf16[1,4096,128]{2,1,0:T(8,128)(2,1)}, u32[]{:S(2)}) copy-start(bf16[1,4096,128]{2,1,0:T(8,128)(2,1)} %param.6) | copy-start | bytes 3145732
  12.1 25.2 %collective-permute-start.2 = (bf16[3072,128]{1,0:T(8,128)(2,1)S(1)}, bf16[3072,128]{1,0:T(8,128)(2,1)S(1)}, u32[]{:S(2)}, u32[]{:S(2)}) collective-permute-start(bf16[3072,128]{1,0:T(8,128)(2,1)S(1)} %pad_maximum_fusion), channel_id=1, source_target_pairs={{0,2},{2,0},{4,6},{6,4},{8,10},{10,8},{12,14},{14,12},{16,18},{18,... | collective-permute-start | bytes 2359304 | tf_op jit(solution)/shard_map/ppermute | solution.py:272
  12.5 15.3 %collective-permute-start.5 = (bf16[1024,128]{1,0:T(8,128)(2,1)S(1)}, bf16[1024,128]{1,0:T(8,128)(2,1)S(1)}, u32[]{:S(2)}, u32[]{:S(2)}) collective-permute-start(bf16[1024,128]{1,0:T(8,128)(2,1)S(1)} %get-tuple-element.70.refs_1_.refs_6_), channel_id=1, source_target_pairs={{0,16},{2,18},{4,20},{6,22},{8,24},{10,26},{12,28},{14,30},{16,0},... | collective-permute-start | bytes 786440 | tf_op jit(solution)/shard_map/ppermute | solution.py:272
  24.7 23.1 %collective-permute-start.4 = (bf16[2048,128]{1,0:T(8,128)(2,1)S(1)}, bf16[2048,128]{1,0:T(8,128)(2,1)S(1)}, u32[]{:S(2)}, u32[]{:S(2)}) collective-permute-start(bf16[2048,128]{1,0:T(8,128)(2,1)S(1)} %pad_maximum_fusion.1), channel_id=1, source_target_pairs={{0,8},{2,10},{4,12},{6,14},{8,0},{10,2},{12,4},{14,6},{16,24},{18,... | collective-permute-start | bytes 1572872 | tf_op jit(solution)/shard_map/ppermute | solution.py:272
  24.8 11.1 %collective-permute-start.7 = (bf16[1024,128]{1,0:T(8,128)(2,1)S(1)}, bf16[1024,128]{1,0:T(8,128)(2,1)S(1)}, u32[]{:S(2)}, u32[]{:S(2)}) collective-permute-start(bf16[1024,128]{1,0:T(8,128)(2,1)S(1)} %stitch.6), channel_id=1, source_target_pairs={{0,2},{2,0},{4,6},{6,4},{8,10},{10,8},{12,14},{14,12},{16,18},{18,... | collective-permute-start | bytes 786440 | tf_op jit(solution)/shard_map/ppermute | solution.py:272
  25.4 24.2 %collective-permute-start.8 = (bf16[2048,128]{1,0:T(8,128)(2,1)S(1)}, bf16[2048,128]{1,0:T(8,128)(2,1)S(1)}, u32[]{:S(2)}, u32[]{:S(2)}) collective-permute-start(bf16[2048,128]{1,0:T(8,128)(2,1)S(1)} %stitch.7), channel_id=1, source_target_pairs={{0,16},{2,18},{4,20},{6,22},{8,24},{10,26},{12,28},{14,30},{16,0},... | collective-permute-start | bytes 1572872 | tf_op jit(solution)/shard_map/ppermute | solution.py:272
  27.8 21.8 %collective-permute-start.9 = (bf16[2048,128]{1,0:T(8,128)(2,1)S(1)}, bf16[2048,128]{1,0:T(8,128)(2,1)S(1)}, u32[]{:S(2)}, u32[]{:S(2)}) collective-permute-start(bf16[2048,128]{1,0:T(8,128)(2,1)S(1)} %stitch.7), channel_id=1, source_target_pairs={{0,4},{2,6},{4,0},{6,2},{8,12},{10,14},{12,8},{14,10},{16,20},{18,... | collective-permute-start | bytes 1572872 | tf_op jit(solution)/shard_map/ppermute | solution.py:272
  35.9 13.8 %collective-permute-start.10 = (bf16[1024,128]{1,0:T(8,128)(2,1)S(1)}, bf16[1024,128]{1,0:T(8,128)(2,1)S(1)}, u32[]{:S(2)}, u32[]{:S(2)}) collective-permute-start(bf16[1024,128]{1,0:T(8,128)(2,1)S(1)} %collective-permute-done.5.refs_8_.refs_13_), channel_id=1, source_target_pairs={{0,4},{2,6},{4,0},{6,2},{8,12},{10,14},{12,8},{14,10},{16,20},{18,... | collective-permute-start | bytes 786440 | tf_op jit(solution)/shard_map/ppermute | solution.py:272
  37.4 15.3 %collective-permute-start.6 = (bf16[4096,128]{1,0:T(8,128)(2,1)S(1)}, bf16[4096,128]{1,0:T(8,128)(2,1)S(1)}, u32[]{:S(2)}, u32[]{:S(2)}) collective-permute-start(bf16[4096,128]{1,0:T(8,128)(2,1)S(1)} %bitcast.22), channel_id=1, source_target_pairs={{0,1},{1,0},{2,3},{3,2},{4,5},{5,4},{6,7},{7,6},{8,9},{9,8},{10,11... | collective-permute-start | bytes 3145736 | tf_op jit(solution)/shard_map/ppermute | solution.py:275
  49.8 3.0 %collective-permute-start.11 = (bf16[4096,128]{1,0:T(8,128)(2,1)S(1)}, bf16[4096,128]{1,0:T(8,128)(2,1)S(1)}, u32[]{:S(2)}, u32[]{:S(2)}) collective-permute-start(bf16[4096,128]{1,0:T(8,128)(2,1)S(1)} %stitch.8), channel_id=1, source_target_pairs={{0,1},{1,0},{2,3},{3,2},{4,5},{5,4},{6,7},{7,6},{8,9},{9,8},{10,11... | collective-permute-start | bytes 3145736 | tf_op jit(solution)/shard_map/ppermute | solution.py:275
  50.0 4.2 %collective-permute-start.12 = (bf16[4096,128]{1,0:T(8,128)(2,1)S(1)}, bf16[4096,128]{1,0:T(8,128)(2,1)S(1)}, u32[]{:S(2)}, u32[]{:S(2)}) collective-permute-start(bf16[4096,128]{1,0:T(8,128)(2,1)S(1)} %stitch.9), channel_id=1, source_target_pairs={{0,1},{1,0},{2,3},{3,2},{4,5},{5,4},{6,7},{7,6},{8,9},{9,8},{10,11... | collective-permute-start | bytes 3145736 | tf_op jit(solution)/shard_map/ppermute | solution.py:275
  50.5 19.5 %collective-permute-start.13 = (bf16[2048,128]{1,0:T(8,128)(2,1)S(1)}, bf16[2048,128]{1,0:T(8,128)(2,1)S(1)}, u32[]{:S(2)}, u32[]{:S(2)}) collective-permute-start(bf16[2048,128]{1,0:T(8,128)(2,1)S(1)} %collective-permute-done.8.refs_9_.refs_14_), channel_id=1, source_target_pairs={{0,4},{2,6},{4,0},{6,2},{8,12},{10,14},{12,8},{14,10},{16,20},{18,... | collective-permute-start | bytes 1572872 | tf_op jit(solution)/shard_map/ppermute | solution.py:272
  51.5 18.6 %collective-permute-start.17 = (bf16[2048,128]{1,0:T(8,128)(2,1)S(1)}, bf16[2048,128]{1,0:T(8,128)(2,1)S(1)}, u32[]{:S(2)}, u32[]{:S(2)}) collective-permute-start(bf16[2048,128]{1,0:T(8,128)(2,1)S(1)} %collective-permute-done.4.refs_2_.refs_3_.refs_4_), channel_id=1, source_target_pairs={{0,2},{2,0},{4,6},{6,4},{8,10},{10,8},{12,14},{14,12},{16,18},{18,... | collective-permute-start | bytes 1572872 | tf_op jit(solution)/shard_map/ppermute | solution.py:272
  52.7 14.4 %collective-permute-start.14 = (bf16[1024,128]{1,0:T(8,128)(2,1)S(1)}, bf16[1024,128]{1,0:T(8,128)(2,1)S(1)}, u32[]{:S(2)}, u32[]{:S(2)}) collective-permute-start(bf16[1024,128]{1,0:T(8,128)(2,1)S(1)} %collective-permute-done.7.refs_4_.refs_0_.refs_9_), channel_id=1, source_target_pairs={{0,16},{2,18},{4,20},{6,22},{8,24},{10,26},{12,28},{14,30},{16,0},... | collective-permute-start | bytes 786440 | tf_op jit(solution)/shard_map/ppermute | solution.py:272
  52.8 17.3 %collective-permute-start.16 = (bf16[1024,128]{1,0:T(8,128)(2,1)S(1)}, bf16[1024,128]{1,0:T(8,128)(2,1)S(1)}, u32[]{:S(2)}, u32[]{:S(2)}) collective-permute-start(bf16[1024,128]{1,0:T(8,128)(2,1)S(1)} %collective-permute-done.7.refs_4_.refs_0_.refs_9_), channel_id=1, source_target_pairs={{0,4},{2,6},{4,0},{6,2},{8,12},{10,14},{12,8},{14,10},{16,20},{18,... | collective-permute-start | bytes 786440 | tf_op jit(solution)/shard_map/ppermute | solution.py:272
  54.2 15.8 %collective-permute-start.18 = (bf16[1024,128]{1,0:T(8,128)(2,1)S(1)}, bf16[1024,128]{1,0:T(8,128)(2,1)S(1)}, u32[]{:S(2)}, u32[]{:S(2)}) collective-permute-start(bf16[1024,128]{1,0:T(8,128)(2,1)S(1)} %stitch.10), channel_id=1, source_target_pairs={{0,8},{2,10},{4,12},{6,14},{8,0},{10,2},{12,4},{14,6},{16,24},{18,... | collective-permute-start | bytes 786440 | tf_op jit(solution)/shard_map/ppermute | solution.py:272
  70.2 4.0 %collective-permute-start.19 = (bf16[4096,128]{1,0:T(8,128)(2,1)S(1)}, bf16[4096,128]{1,0:T(8,128)(2,1)S(1)}, u32[]{:S(2)}, u32[]{:S(2)}) collective-permute-start(bf16[4096,128]{1,0:T(8,128)(2,1)S(1)} %stitch.11), channel_id=1, source_target_pairs={{0,1},{1,0},{2,3},{3,2},{4,5},{5,4},{6,7},{7,6},{8,9},{9,8},{10,11... | collective-permute-start | bytes 3145736 | tf_op jit(solution)/shard_map/ppermute | solution.py:275
  70.3 8.7 %collective-permute-start.15 = (bf16[1024,128]{1,0:T(8,128)(2,1)S(1)}, bf16[1024,128]{1,0:T(8,128)(2,1)S(1)}, u32[]{:S(2)}, u32[]{:S(2)}) collective-permute-start(bf16[1024,128]{1,0:T(8,128)(2,1)S(1)} %collective-permute-done.14.refs_10_.refs_15_), channel_id=1, source_target_pairs={{0,4},{2,6},{4,0},{6,2},{8,12},{10,14},{12,8},{14,10},{16,20},{18,... | collective-permute-start | bytes 786440 | tf_op jit(solution)/shard_map/ppermute | solution.py:272
  81.6 9.0 %copy-start.1 = (f32[3,1,64,128]{3,2,1,0:T(8,128)S(1)}, f32[3,1,64,128]{3,2,1,0:T(8,128)}, u32[]{:S(2)}) copy-start(f32[3,1,64,128]{3,2,1,0:T(8,128)} %param.11) | copy-start | bytes 294916
  81.7 1.8 %collective-permute-start.20 = (f32[12,64,128]{2,1,0:T(8,128)S(1)}, f32[12,64,128]{2,1,0:T(8,128)S(1)}, u32[]{:S(2)}, u32[]{:S(2)}) collective-permute-start(f32[12,64,128]{2,1,0:T(8,128)S(1)} %slice_bitcast_fusion), channel_id=1, source_target_pairs={{0,1},{1,0},{2,3},{3,2},{4,5},{5,4},{6,7},{7,6},{8,9},{9,8},{10,11... | collective-permute-start | bytes 1179656 | tf_op jit(solution)/shard_map/ppermute | solution.py:275
  83.5 5.3 %collective-permute-start.23 = (bf16[3,64,128]{2,1,0:T(8,128)(2,1)S(1)}, bf16[3,64,128]{2,1,0:T(8,128)(2,1)S(1)}, u32[]{:S(2)}, u32[]{:S(2)}) collective-permute-start(bf16[3,64,128]{2,1,0:T(8,128)(2,1)S(1)} %get-tuple-element.72), channel_id=1, source_target_pairs={{0,10},{2,8},{4,14},{6,12},{8,2},{10,0},{12,6},{14,4},{16,26},{18,... | collective-permute-start | bytes 147464 | tf_op jit(solution)/shard_map/ppermute | solution.py:272
  83.8 5.5 %collective-permute-start.22 = (bf16[3,64,128]{2,1,0:T(8,128)(2,1)S(1)}, bf16[3,64,128]{2,1,0:T(8,128)(2,1)S(1)}, u32[]{:S(2)}, u32[]{:S(2)}) collective-permute-start(bf16[3,64,128]{2,1,0:T(8,128)(2,1)S(1)} %get-tuple-element.73), channel_id=1, source_target_pairs={{0,8},{2,10},{4,12},{6,14},{8,0},{10,2},{12,4},{14,6},{16,24},{18,... | collective-permute-start | bytes 147464 | tf_op jit(solution)/shard_map/ppermute | solution.py:272
  86.5 4.1 %collective-permute-start.21 = (bf16[3,64,128]{2,1,0:T(8,128)(2,1)S(1)}, bf16[3,64,128]{2,1,0:T(8,128)(2,1)S(1)}, u32[]{:S(2)}, u32[]{:S(2)}) collective-permute-start(bf16[3,64,128]{2,1,0:T(8,128)(2,1)S(1)} %get-tuple-element.71), channel_id=1, source_target_pairs={{0,2},{2,0},{4,6},{6,4},{8,10},{10,8},{12,14},{14,12},{16,18},{18,... | collective-permute-start | bytes 147464 | tf_op jit(solution)/shard_map/ppermute | solution.py:272

commit v10 on v9

--- a/solution.py
+++ b/solution.py
@@ -14,19 +14,19 @@
 
 
 FIRST = ("c0", "c1", "s1.0")
-SECOND = ("p3", "r1", "r2", "s2.1", "s1.1","s3.0")
+SECOND = ("p3", "r1", "r2", "s2.1", "s1.1","s3.0","s1.2")
 WAITS = {
     **dict.fromkeys(FIRST, ()),
     "s2.0": (),
     "t1o": ("s2.0",),
     "r1": ("c0","s1.0"),
     **dict.fromkeys(("p3", "r2", "s2.1", "s1.1"), FIRST+("i",)),
-    **dict.fromkeys(("s3.0",), ("p3",)),
-
-    **dict.fromkeys(("s2.2","s3.1","s1.2","r3","u3"), SECOND),
+    **dict.fromkeys(("s3.0","s1.2"), ("p3",)),
+
+    **dict.fromkeys(("s2.2","s3.1","r3","u3"), SECOND),
     **dict.fromkeys(("t1k1","t1k2"), SECOND),
     "q": (),
-    "t1k3": ("q","s2.2","s3.1","s1.2"),
+    "t1k3": ("q","s2.2","s3.1"),
 }
 
 

time: 91.6 us -> 90.8 us (level)
  waiting for transfers between devices: 48.9 us -> 47.1 us
  other arithmetic: 0.93 us -> 2.56 us
    ppermute x19, waiting for transfers between devices: 47.2 us -> 45.4 us  [swap(): return lax.ppermute(value, 'ka', [(i, i ^ mask) for i in range(points)])]
  transfers between devices with their start and end apart: 24 -> 24, of which waited for: 13 -> 12; matrix products, arithmetic and copies ran while one was open for 1% -> 2% of each run, Pallas kernels for 12% -> 12%
where the time goes in v10:
time: 90.8 us; the launch traced here: 90.4 us
  waiting for transfers between devices  47.1 us (52%)
  starting transfers between devices  24.8 us (27%)
  Pallas kernels  13.9 us (15%)
  other arithmetic  2.56 us (3%)
  local copies, waits for them, and re-layouts  1.75 us (2%)
    ppermute x19, waiting for transfers between devices, swap(): return lax.ppermute(value, 'ka', [(i, i ^ mask) for i in range(points)])  45.4 us
    ppermute x19, starting transfers between devices, swap(): return lax.ppermute(value, 'ka', [(i, i ^ mask) for i in range(points)])  24 us
    pallas_call x2, Pallas kernels, project(): pl.pallas_call(functools.partial(project_kernel, orders, inside, halves),...  7.99 us
    pallas_call x2, Pallas kernels, couple(): pl.pallas_call(functools.partial(couple_kernel, jobs, last, inside, outsi...  5.45 us
  transfers between devices with their start and end apart: 24, of which 12 were waited for; matrix products, arithmetic and copies ran while one was open for 2% of the time, Pallas kernels for 12%

profile of v10, /device:TPU:0, one launch (start us, length us, event | category | flops | bytes accessed | tf_op | source)
XLA Modules:
  0.0 90.4 jit_solution(17424484796398446909)
XLA Ops:
  0.1 1.3 %constant_dynamic-slice_fusion = (bf16[1024,128]{1,0:T(8,128)(2,1)S(1)}, bf16[1024,128]{1,0:T(8,128)(2,1)S(1)}, bf16[1024,128]{1,0:T(8,128)(2,1)S(1)}, bf16[1024,128]{1,0:T(8,128)(2,1)S(1)}) fusion(bf16[4096,128]{1,0:T(8,128)(2,1)} %bitcast.20, s32[]{:T(128)S(6)} %select_n.15, s32[]{:T(128)S(6)} %select_n.14, s32[]{:T(128)S(6)} %select_n.13, s32[]{:T(128)S(6)} %select_n.12), kind=kLoop, calls=%fused_computation.12 | loop fusion | bytes 2097168 | tf_op jit(solution)/shard_map/dynamic_slice | solution.py:302
  1.3 3.0 %collective-permute-start = (bf16[1024,128]{1,0:T(8,128)(2,1)S(1)}, bf16[1024,128]{1,0:T(8,128)(2,1)S(1)}, u32[]{:S(2)}, u32[]{:S(2)}) collective-permute-start(bf16[1024,128]{1,0:T(8,128)(2,1)S(1)} %get-tuple-element.69), channel_id=1, source_target_pairs={{0,2},{2,0},{4,6},{6,4},{8,10},{10,8},{12,14},{14,12},{16,18},{18,... | collective-permute-start | bytes 786440 | tf_op jit(solution)/shard_map/ppermute | solution.py:272
  4.3 1.5 %collective-permute-start.1 = (bf16[1024,128]{1,0:T(8,128)(2,1)S(1)}, bf16[1024,128]{1,0:T(8,128)(2,1)S(1)}, u32[]{:S(2)}, u32[]{:S(2)}) collective-permute-start(bf16[1024,128]{1,0:T(8,128)(2,1)S(1)} %get-tuple-element.72.refs_1_.refs_6_), channel_id=1, source_target_pairs={{0,4},{2,6},{4,0},{6,2},{8,12},{10,14},{12,8},{14,10},{16,20},{18,... | collective-permute-start | bytes 786440 | tf_op jit(solution)/shard_map/ppermute | solution.py:272
  5.9 0.8 pad_maximum_fusion.2
  6.7 1.6 %collective-permute-start.3 = (bf16[2048,128]{1,0:T(8,128)(2,1)}, bf16[2048,128]{1,0:T(8,128)(2,1)S(1)}, u32[]{:S(2)}, u32[]{:S(2)}) collective-permute-start(bf16[2048,128]{1,0:T(8,128)(2,1)} %pad_maximum_fusion.2), channel_id=1, source_target_pairs={{0,8},{2,10},{4,12},{6,14},{8,0},{10,2},{12,4},{14,6},{16,24},{18,... | collective-permute-start | bytes 1572872 | tf_op jit(solution)/shard_map/ppermute | solution.py:272
  8.4 0.9 pad_maximum_fusion.1
  9.7 1.0 %collective-permute-done.refs_0_.refs_1_.refs_2_.refs_7_ = bf16[1024,128]{1,0:T(8,128)(2,1)S(1)} collective-permute-done((bf16[1024,128]{1,0:T(8,128)(2,1)S(1)}, bf16[1024,128]{1,0:T(8,128)(2,1)S(1)}, u32[]{:S(2)}, u32[]{:S(2)}) %collective-permute-start) | collective-permute-done | bytes 262176 | tf_op jit(solution)/shard_map/ppermute | solution.py:272
  10.6 1.5 %collective-permute-done.1.refs_5_.refs_10_ = bf16[1024,128]{1,0:T(8,128)(2,1)S(1)} collective-permute-done((bf16[1024,128]{1,0:T(8,128)(2,1)S(1)}, bf16[1024,128]{1,0:T(8,128)(2,1)S(1)}, u32[]{:S(2)}, u32[]{:S(2)}) %collective-permute-start.1) | collective-permute-done | bytes 262176 | tf_op jit(solution)/shard_map/ppermute | solution.py:272
  12.5 2.8 %collective-permute-start.5 = (bf16[1024,128]{1,0:T(8,128)(2,1)S(1)}, bf16[1024,128]{1,0:T(8,128)(2,1)S(1)}, u32[]{:S(2)}, u32[]{:S(2)}) collective-permute-start(bf16[1024,128]{1,0:T(8,128)(2,1)S(1)} %get-tuple-element.72.refs_1_.refs_6_), channel_id=1, source_target_pairs={{0,16},{2,18},{4,20},{6,22},{8,24},{10,26},{12,28},{14,30},{16,0},... | collective-permute-start | bytes 786440 | tf_op jit(solution)/shard_map/ppermute | solution.py:272
  15.2 10.4 %collective-permute-done.3.refs_0_.refs_1_.refs_3_.refs_8_ = bf16[2048,128]{1,0:T(8,128)(2,1)S(1)} collective-permute-done((bf16[2048,128]{1,0:T(8,128)(2,1)}, bf16[2048,128]{1,0:T(8,128)(2,1)S(1)}, u32[]{:S(2)}, u32[]{:S(2)}) %collective-permute-start.3) | collective-permute-done | bytes 524320 | tf_op jit(solution)/shard_map/ppermute | solution.py:272
  25.7 0.6 collective-permute-start.7
  26.3 3.4 %collective-permute-start.8 = (bf16[2048,128]{1,0:T(8,128)(2,1)S(1)}, bf16[2048,128]{1,0:T(8,128)(2,1)S(1)}, u32[]{:S(2)}, u32[]{:S(2)}) collective-permute-start(bf16[2048,128]{1,0:T(8,128)(2,1)S(1)} %stitch.7), channel_id=1, source_target_pairs={{0,16},{2,18},{4,20},{6,22},{8,24},{10,26},{12,28},{14,30},{16,0},... | collective-permute-start | bytes 1572872 | tf_op jit(solution)/shard_map/ppermute | solution.py:272
  29.7 6.1 %collective-permute-done.7.refs_4_.refs_0_.refs_9_ = bf16[1024,128]{1,0:T(8,128)(2,1)S(1)} collective-permute-done((bf16[1024,128]{1,0:T(8,128)(2,1)S(1)}, bf16[1024,128]{1,0:T(8,128)(2,1)S(1)}, u32[]{:S(2)}, u32[]{:S(2)}) %collective-permute-start.7) | collective-permute-done | bytes 262176 | tf_op jit(solution)/shard_map/ppermute | solution.py:272
  35.8 1.5 %collective-permute-start.10 = (bf16[1024,128]{1,0:T(8,128)(2,1)S(1)}, bf16[1024,128]{1,0:T(8,128)(2,1)S(1)}, u32[]{:S(2)}, u32[]{:S(2)}) collective-permute-start(bf16[1024,128]{1,0:T(8,128)(2,1)S(1)} %collective-permute-done.5.refs_8_.refs_13_), channel_id=1, source_target_pairs={{0,4},{2,6},{4,0},{6,2},{8,12},{10,14},{12,8},{14,10},{16,20},{18,... | collective-permute-start | bytes 786440 | tf_op jit(solution)/shard_map/ppermute | solution.py:272
  37.8 11.2 %collective-permute-done.4.refs_2_.refs_3_.refs_4_ = bf16[2048,128]{1,0:T(8,128)(2,1)S(1)} collective-permute-done((bf16[2048,128]{1,0:T(8,128)(2,1)}, bf16[2048,128]{1,0:T(8,128)(2,1)S(1)}, u32[]{:S(2)}, u32[]{:S(2)}) %collective-permute-start.4) | collective-permute-done | bytes 524320 | tf_op jit(solution)/shard_map/ppermute | solution.py:272
  49.0 2.2 %collective-permute-done.8.refs_9_.refs_14_ = bf16[2048,128]{1,0:T(8,128)(2,1)S(1)} collective-permute-done((bf16[2048,128]{1,0:T(8,128)(2,1)S(1)}, bf16[2048,128]{1,0:T(8,128)(2,1)S(1)}, u32[]{:S(2)}, u32[]{:S(2)}) %collective-permute-start.8) | collective-permute-done | bytes 524320 | tf_op jit(solution)/shard_map/ppermute | solution.py:272
  51.2 1.4 %collective-permute-done.11.refs_7_.refs_12_ = bf16[1024,128]{1,0:T(8,128)(2,1)S(1)} collective-permute-done((bf16[1024,128]{1,0:T(8,128)(2,1)S(1)}, bf16[1024,128]{1,0:T(8,128)(2,1)S(1)}, u32[]{:S(2)}, u32[]{:S(2)}) %collective-permute-start.11) | collective-permute-done | bytes 262176 | tf_op jit(solution)/shard_map/ppermute | solution.py:272
  53.8 1.7 %collective-permute-start.17 = (bf16[2048,128]{1,0:T(8,128)(2,1)S(1)}, bf16[2048,128]{1,0:T(8,128)(2,1)S(1)}, u32[]{:S(2)}, u32[]{:S(2)}) collective-permute-start(bf16[2048,128]{1,0:T(8,128)(2,1)S(1)} %collective-permute-done.4.refs_2_.refs_3_.refs_4_), channel_id=1, source_target_pairs={{0,2},{2,0},{4,6},{6,4},{8,10},{10,8},{12,14},{14,12},{16,18},{18,... | collective-permute-start | bytes 1572872 | tf_op jit(solution)/shard_map/ppermute | solution.py:272
  56.0 1.1 %collective-permute-start.18 = (bf16[1024,128]{1,0:T(8,128)(2,1)S(1)}, bf16[1024,128]{1,0:T(8,128)(2,1)S(1)}, u32[]{:S(2)}, u32[]{:S(2)}) collective-permute-start(bf16[1024,128]{1,0:T(8,128)(2,1)S(1)} %stitch.10), channel_id=1, source_target_pairs={{0,8},{2,10},{4,12},{6,14},{8,0},{10,2},{12,4},{14,6},{16,24},{18,... | collective-permute-start | bytes 786440 | tf_op jit(solution)/shard_map/ppermute | solution.py:272
  57.0 4.6 %project.1.refs_0_ = bf16[9,128,1024]{2,1,0:T(8,128)(2,1)S(1)} custom-call(s32[2]{0:T(128)S(1)} %pad_add_fusion.pos, s32[288]{0:T(512)S(1)} %reshape.19.cols, s32[96]{0:T(128)S(1)} %reshape.20.counts, bf16[3,32,3,128,128]{4,3,2,1,0:T(8,128)(2,1)} %potential.3, bf16[4096,128]{1,0:T(8,128)(2,1)} %bitcast.21, ...), custom_call_target="tpu_custom_call" | custom-call | tf_op jit(solution)/shard_map/project/pallas_call | solution.py:157
  61.7 8.0 %collective-permute-done.15.refs_10_.refs_15_ = bf16[1024,128]{1,0:T(8,128)(2,1)S(1)} collective-permute-done((bf16[1024,128]{1,0:T(8,128)(2,1)S(1)}, bf16[1024,128]{1,0:T(8,128)(2,1)S(1)}, u32[]{:S(2)}, u32[]{:S(2)}) %collective-permute-start.15) | collective-permute-done | bytes 262176 | tf_op jit(solution)/shard_map/ppermute | solution.py:272
  69.9 1.7 %collective-permute-start.16 = (bf16[1024,128]{1,0:T(8,128)(2,1)S(1)}, bf16[1024,128]{1,0:T(8,128)(2,1)S(1)}, u32[]{:S(2)}, u32[]{:S(2)}) collective-permute-start(bf16[1024,128]{1,0:T(8,128)(2,1)S(1)} %collective-permute-done.15.refs_10_.refs_15_), channel_id=1, source_target_pairs={{0,4},{2,6},{4,0},{6,2},{8,12},{10,14},{12,8},{14,10},{16,20},{18,... | collective-permute-start | bytes 786440 | tf_op jit(solution)/shard_map/ppermute | solution.py:272
  71.6 2.9 %couple.1.refs_4_ = f32[9,128,128]{2,1,0:T(8,128)S(1)} custom-call(s32[2]{0:T(128)S(1)} %pad_add_fusion.pos, s32[48]{0:T(128)S(1)} %reshape.21.partners, bf16[9,128,1024]{2,1,0:T(8,128)(2,1)S(1)} %project.1.refs_0_, bf16[1024,128]{1,0:T(8,128)(2,1)S(1)} %get-tuple-element.72.refs_1_.refs_6_, ...), custom_call_target="tpu_custom_call" | custom-call | tf_op jit(solution)/shard_map/couple/pallas_call | solution.py:244
  74.5 3.4 %project_last.1.refs_5_ = bf16[3,128,1024]{2,1,0:T(8,128)(2,1)S(1)} custom-call(s32[2]{0:T(128)S(1)} %pad_add_fusion.pos, s32[288]{0:T(512)S(1)} %reshape.19.cols, s32[96]{0:T(128)S(1)} %reshape.20.counts, bf16[3,32,3,128,128]{4,3,2,1,0:T(8,128)(2,1)} %potential.3, bf16[1024,128]{1,0:T(8,128)(2,1)S(1)} %collective-permute-done.7.refs_4_.refs_0_.refs_9_, ...), custom_call_target="tpu_custom_call" | custom-call | tf_op jit(solution)/shard_map/project_last/pallas_call | solution.py:157
  77.8 0.7 collective-permute-done.16.refs_3_.refs_18_
  78.6 2.6 %couple_last.1 = f32[2,12,64,128]{3,2,1,0:T(8,128)S(1)} custom-call(s32[2]{0:T(128)S(1)} %pad_add_fusion.pos, s32[48]{0:T(128)S(1)} %reshape.21.partners, bf16[9,128,1024]{2,1,0:T(8,128)(2,1)S(1)} %project.1.refs_0_, bf16[1024,128]{1,0:T(8,128)(2,1)S(1)} %collective-permute-done.10.refs_1_.refs_16_, ...), custom_call_target="tpu_custom_call" | custom-call | tf_op jit(solution)/shard_map/couple_last/pallas_call | solution.py:244
  81.3 1.7 %collective-permute-done.20 = f32[12,64,128]{2,1,0:T(8,128)S(1)} collective-permute-done((f32[12,64,128]{2,1,0:T(8,128)S(1)}, f32[12,64,128]{2,1,0:T(8,128)S(1)}, u32[]{:S(2)}, u32[]{:S(2)}) %collective-permute-start.20) | collective-permute-done | bytes 393248 | tf_op jit(solution)/shard_map/ppermute | solution.py:275
  83.5 2.1 %collective-permute-start.22 = (bf16[3,64,128]{2,1,0:T(8,128)(2,1)S(1)}, bf16[3,64,128]{2,1,0:T(8,128)(2,1)S(1)}, u32[]{:S(2)}, u32[]{:S(2)}) collective-permute-start(bf16[3,64,128]{2,1,0:T(8,128)(2,1)S(1)} %get-tuple-element.75), channel_id=1, source_target_pairs={{0,8},{2,10},{4,12},{6,14},{8,0},{10,2},{12,4},{14,6},{16,24},{18,... | collective-permute-start | bytes 147464 | tf_op jit(solution)/shard_map/ppermute | solution.py:272
  85.6 1.1 %collective-permute-start.21 = (bf16[3,64,128]{2,1,0:T(8,128)(2,1)S(1)}, bf16[3,64,128]{2,1,0:T(8,128)(2,1)S(1)}, u32[]{:S(2)}, u32[]{:S(2)}) collective-permute-start(bf16[3,64,128]{2,1,0:T(8,128)(2,1)S(1)} %get-tuple-element.73), channel_id=1, source_target_pairs={{0,2},{2,0},{4,6},{6,4},{8,10},{10,8},{12,14},{14,12},{16,18},{18,... | collective-permute-start | bytes 147464 | tf_op jit(solution)/shard_map/ppermute | solution.py:272
  86.7 1.8 %collective-permute-done.23 = bf16[3,64,128]{2,1,0:T(8,128)(2,1)S(1)} collective-permute-done((bf16[3,64,128]{2,1,0:T(8,128)(2,1)S(1)}, bf16[3,64,128]{2,1,0:T(8,128)(2,1)S(1)}, u32[]{:S(2)}, u32[]{:S(2)}) %collective-permute-start.23) | collective-permute-done | bytes 49184 | tf_op jit(solution)/shard_map/ppermute | solution.py:272
  88.5 1.2 %collective-permute-done.21 = bf16[3,64,128]{2,1,0:T(8,128)(2,1)S(1)} collective-permute-done((bf16[3,64,128]{2,1,0:T(8,128)(2,1)S(1)}, bf16[3,64,128]{2,1,0:T(8,128)(2,1)S(1)}, u32[]{:S(2)}, u32[]{:S(2)}) %collective-permute-start.21) | collective-permute-done | bytes 49184 | tf_op jit(solution)/shard_map/ppermute | solution.py:272
  89.7 0.7 fusion.5
  (49 shorter events, 4.0 us)
Async XLA Ops:
  1.3 9.3 %collective-permute-start = (bf16[1024,128]{1,0:T(8,128)(2,1)S(1)}, bf16[1024,128]{1,0:T(8,128)(2,1)S(1)}, u32[]{:S(2)}, u32[]{:S(2)}) collective-permute-start(bf16[1024,128]{1,0:T(8,128)(2,1)S(1)} %get-tuple-element.69), channel_id=1, source_target_pairs={{0,2},{2,0},{4,6},{6,4},{8,10},{10,8},{12,14},{14,12},{16,18},{18,... | collective-permute-start | bytes 786440 | tf_op jit(solution)/shard_map/ppermute | solution.py:272
  4.3 7.8 %collective-permute-start.1 = (bf16[1024,128]{1,0:T(8,128)(2,1)S(1)}, bf16[1024,128]{1,0:T(8,128)(2,1)S(1)}, u32[]{:S(2)}, u32[]{:S(2)}) collective-permute-start(bf16[1024,128]{1,0:T(8,128)(2,1)S(1)} %get-tuple-element.72.refs_1_.refs_6_), channel_id=1, source_target_pairs={{0,4},{2,6},{4,0},{6,2},{8,12},{10,14},{12,8},{14,10},{16,20},{18,... | collective-permute-start | bytes 786440 | tf_op jit(solution)/shard_map/ppermute | solution.py:272
  5.9 3.4 %copy-start.2 = (s32[3,32,3]{1,2,0:T(4,128)S(1)}, s32[3,32,3]{1,2,0:T(4,128)}, u32[]{:S(2)}) copy-start(s32[3,32,3]{1,2,0:T(4,128)} %param.8) | copy-start | bytes 3460
  6.7 2.8 %copy-start.3 = (s32[3,32]{1,0:T(4,128)S(1)}, s32[3,32]{1,0:T(4,128)}, u32[]{:S(2)}) copy-start(s32[3,32]{1,0:T(4,128)} %param.9) | copy-start | bytes 1156
  6.7 2.9 %copy-start.4 = (s32[3,16]{1,0:T(4,128)S(1)}, s32[3,16]{1,0:T(4,128)}, u32[]{:S(2)}) copy-start(s32[3,16]{1,0:T(4,128)} %param.10) | copy-start | bytes 580
  6.7 18.9 %collective-permute-start.3 = (bf16[2048,128]{1,0:T(8,128)(2,1)}, bf16[2048,128]{1,0:T(8,128)(2,1)S(1)}, u32[]{:S(2)}, u32[]{:S(2)}) collective-permute-start(bf16[2048,128]{1,0:T(8,128)(2,1)} %pad_maximum_fusion.2), channel_id=1, source_target_pairs={{0,8},{2,10},{4,12},{6,14},{8,0},{10,2},{12,4},{14,6},{16,24},{18,... | collective-permute-start | bytes 1572872 | tf_op jit(solution)/shard_map/ppermute | solution.py:272
  8.3 40.7 %copy-start = (bf16[1,4096,128]{2,1,0:T(8,128)(2,1)S(1)}, bf16[1,4096,128]{2,1,0:T(8,128)(2,1)}, u32[]{:S(2)}) copy-start(bf16[1,4096,128]{2,1,0:T(8,128)(2,1)} %param.6) | copy-start | bytes 3145732
  12.1 25.2 %collective-permute-start.2 = (bf16[3072,128]{1,0:T(8,128)(2,1)S(1)}, bf16[3072,128]{1,0:T(8,128)(2,1)S(1)}, u32[]{:S(2)}, u32[]{:S(2)}) collective-permute-start(bf16[3072,128]{1,0:T(8,128)(2,1)S(1)} %pad_maximum_fusion), channel_id=1, source_target_pairs={{0,2},{2,0},{4,6},{6,4},{8,10},{10,8},{12,14},{14,12},{16,18},{18,... | collective-permute-start | bytes 2359304 | tf_op jit(solution)/shard_map/ppermute | solution.py:272
  12.5 17.3 %collective-permute-start.5 = (bf16[1024,128]{1,0:T(8,128)(2,1)S(1)}, bf16[1024,128]{1,0:T(8,128)(2,1)S(1)}, u32[]{:S(2)}, u32[]{:S(2)}) collective-permute-start(bf16[1024,128]{1,0:T(8,128)(2,1)S(1)} %get-tuple-element.72.refs_1_.refs_6_), channel_id=1, source_target_pairs={{0,16},{2,18},{4,20},{6,22},{8,24},{10,26},{12,28},{14,30},{16,0},... | collective-permute-start | bytes 786440 | tf_op jit(solution)/shard_map/ppermute | solution.py:272
  25.6 23.4 %collective-permute-start.4 = (bf16[2048,128]{1,0:T(8,128)(2,1)}, bf16[2048,128]{1,0:T(8,128)(2,1)S(1)}, u32[]{:S(2)}, u32[]{:S(2)}) collective-permute-start(bf16[2048,128]{1,0:T(8,128)(2,1)} %pad_maximum_fusion.1), channel_id=1, source_target_pairs={{0,8},{2,10},{4,12},{6,14},{8,0},{10,2},{12,4},{14,6},{16,24},{18,... | collective-permute-start | bytes 1572872 | tf_op jit(solution)/shard_map/ppermute | solution.py:272
  25.7 10.1 %collective-permute-start.7 = (bf16[1024,128]{1,0:T(8,128)(2,1)S(1)}, bf16[1024,128]{1,0:T(8,128)(2,1)S(1)}, u32[]{:S(2)}, u32[]{:S(2)}) collective-permute-start(bf16[1024,128]{1,0:T(8,128)(2,1)S(1)} %stitch.6), channel_id=1, source_target_pairs={{0,2},{2,0},{4,6},{6,4},{8,10},{10,8},{12,14},{14,12},{16,18},{18,... | collective-permute-start | bytes 786440 | tf_op jit(solution)/shard_map/ppermute | solution.py:272
  26.3 24.8 %collective-permute-start.8 = (bf16[2048,128]{1,0:T(8,128)(2,1)S(1)}, bf16[2048,128]{1,0:T(8,128)(2,1)S(1)}, u32[]{:S(2)}, u32[]{:S(2)}) collective-permute-start(bf16[2048,128]{1,0:T(8,128)(2,1)S(1)} %stitch.7), channel_id=1, source_target_pairs={{0,16},{2,18},{4,20},{6,22},{8,24},{10,26},{12,28},{14,30},{16,0},... | collective-permute-start | bytes 1572872 | tf_op jit(solution)/shard_map/ppermute | solution.py:272
  29.7 21.4 %collective-permute-start.9 = (bf16[2048,128]{1,0:T(8,128)(2,1)S(1)}, bf16[2048,128]{1,0:T(8,128)(2,1)S(1)}, u32[]{:S(2)}, u32[]{:S(2)}) collective-permute-start(bf16[2048,128]{1,0:T(8,128)(2,1)S(1)} %stitch.7), channel_id=1, source_target_pairs={{0,4},{2,6},{4,0},{6,2},{8,12},{10,14},{12,8},{14,10},{16,20},{18,... | collective-permute-start | bytes 1572872 | tf_op jit(solution)/shard_map/ppermute | solution.py:272
  35.8 15.4 %collective-permute-start.10 = (bf16[1024,128]{1,0:T(8,128)(2,1)S(1)}, bf16[1024,128]{1,0:T(8,128)(2,1)S(1)}, u32[]{:S(2)}, u32[]{:S(2)}) collective-permute-start(bf16[1024,128]{1,0:T(8,128)(2,1)S(1)} %collective-permute-done.5.refs_8_.refs_13_), channel_id=1, source_target_pairs={{0,4},{2,6},{4,0},{6,2},{8,12},{10,14},{12,8},{14,10},{16,20},{18,... | collective-permute-start | bytes 786440 | tf_op jit(solution)/shard_map/ppermute | solution.py:272
  37.3 15.2 %collective-permute-start.11 = (bf16[1024,128]{1,0:T(8,128)(2,1)S(1)}, bf16[1024,128]{1,0:T(8,128)(2,1)S(1)}, u32[]{:S(2)}, u32[]{:S(2)}) collective-permute-start(bf16[1024,128]{1,0:T(8,128)(2,1)S(1)} %collective-permute-done.7.refs_4_.refs_0_.refs_9_), channel_id=1, source_target_pairs={{0,4},{2,6},{4,0},{6,2},{8,12},{10,14},{12,8},{14,10},{16,20},{18,... | collective-permute-start | bytes 786440 | tf_op jit(solution)/shard_map/ppermute | solution.py:272
  49.0 6.5 %collective-permute-start.6 = (bf16[4096,128]{1,0:T(8,128)(2,1)S(1)}, bf16[4096,128]{1,0:T(8,128)(2,1)S(1)}, u32[]{:S(2)}, u32[]{:S(2)}) collective-permute-start(bf16[4096,128]{1,0:T(8,128)(2,1)S(1)} %bitcast.22), channel_id=1, source_target_pairs={{0,1},{1,0},{2,3},{3,2},{4,5},{5,4},{6,7},{7,6},{8,9},{9,8},{10,11... | collective-permute-start | bytes 3145736 | tf_op jit(solution)/shard_map/ppermute | solution.py:275
  52.7 3.3 %collective-permute-start.12 = (bf16[4096,128]{1,0:T(8,128)(2,1)S(1)}, bf16[4096,128]{1,0:T(8,128)(2,1)S(1)}, u32[]{:S(2)}, u32[]{:S(2)}) collective-permute-start(bf16[4096,128]{1,0:T(8,128)(2,1)S(1)} %stitch.8), channel_id=1, source_target_pairs={{0,1},{1,0},{2,3},{3,2},{4,5},{5,4},{6,7},{7,6},{8,9},{9,8},{10,11... | collective-permute-start | bytes 3145736 | tf_op jit(solution)/shard_map/ppermute | solution.py:275
  52.9 4.1 %collective-permute-start.13 = (bf16[4096,128]{1,0:T(8,128)(2,1)S(1)}, bf16[4096,128]{1,0:T(8,128)(2,1)S(1)}, u32[]{:S(2)}, u32[]{:S(2)}) collective-permute-start(bf16[4096,128]{1,0:T(8,128)(2,1)S(1)} %stitch.9), channel_id=1, source_target_pairs={{0,1},{1,0},{2,3},{3,2},{4,5},{5,4},{6,7},{7,6},{8,9},{9,8},{10,11... | collective-permute-start | bytes 3145736 | tf_op jit(solution)/shard_map/ppermute | solution.py:275
  53.5 16.2 %collective-permute-start.14 = (bf16[2048,128]{1,0:T(8,128)(2,1)S(1)}, bf16[2048,128]{1,0:T(8,128)(2,1)S(1)}, u32[]{:S(2)}, u32[]{:S(2)}) collective-permute-start(bf16[2048,128]{1,0:T(8,128)(2,1)S(1)} %collective-permute-done.8.refs_9_.refs_14_), channel_id=1, source_target_pairs={{0,4},{2,6},{4,0},{6,2},{8,12},{10,14},{12,8},{14,10},{16,20},{18,... | collective-permute-start | bytes 1572872 | tf_op jit(solution)/shard_map/ppermute | solution.py:272
  53.8 15.9 %collective-permute-start.17 = (bf16[2048,128]{1,0:T(8,128)(2,1)S(1)}, bf16[2048,128]{1,0:T(8,128)(2,1)S(1)}, u32[]{:S(2)}, u32[]{:S(2)}) collective-permute-start(bf16[2048,128]{1,0:T(8,128)(2,1)S(1)} %collective-permute-done.4.refs_2_.refs_3_.refs_4_), channel_id=1, source_target_pairs={{0,2},{2,0},{4,6},{6,4},{8,10},{10,8},{12,14},{14,12},{16,18},{18,... | collective-permute-start | bytes 1572872 | tf_op jit(solution)/shard_map/ppermute | solution.py:272
  55.5 14.1 %collective-permute-start.15 = (bf16[1024,128]{1,0:T(8,128)(2,1)S(1)}, bf16[1024,128]{1,0:T(8,128)(2,1)S(1)}, u32[]{:S(2)}, u32[]{:S(2)}) collective-permute-start(bf16[1024,128]{1,0:T(8,128)(2,1)S(1)} %collective-permute-done.7.refs_4_.refs_0_.refs_9_), channel_id=1, source_target_pairs={{0,16},{2,18},{4,20},{6,22},{8,24},{10,26},{12,28},{14,30},{16,0},... | collective-permute-start | bytes 786440 | tf_op jit(solution)/shard_map/ppermute | solution.py:272
  56.0 13.7 %collective-permute-start.18 = (bf16[1024,128]{1,0:T(8,128)(2,1)S(1)}, bf16[1024,128]{1,0:T(8,128)(2,1)S(1)}, u32[]{:S(2)}, u32[]{:S(2)}) collective-permute-start(bf16[1024,128]{1,0:T(8,128)(2,1)S(1)} %stitch.10), channel_id=1, source_target_pairs={{0,8},{2,10},{4,12},{6,14},{8,0},{10,2},{12,4},{14,6},{16,24},{18,... | collective-permute-start | bytes 786440 | tf_op jit(solution)/shard_map/ppermute | solution.py:272
  69.8 4.7 %collective-permute-start.19 = (bf16[4096,128]{1,0:T(8,128)(2,1)S(1)}, bf16[4096,128]{1,0:T(8,128)(2,1)S(1)}, u32[]{:S(2)}, u32[]{:S(2)}) collective-permute-start(bf16[4096,128]{1,0:T(8,128)(2,1)S(1)} %stitch.11), channel_id=1, source_target_pairs={{0,1},{1,0},{2,3},{3,2},{4,5},{5,4},{6,7},{7,6},{8,9},{9,8},{10,11... | collective-permute-start | bytes 3145736 | tf_op jit(solution)/shard_map/ppermute | solution.py:275
  69.9 8.7 %collective-permute-start.16 = (bf16[1024,128]{1,0:T(8,128)(2,1)S(1)}, bf16[1024,128]{1,0:T(8,128)(2,1)S(1)}, u32[]{:S(2)}, u32[]{:S(2)}) collective-permute-start(bf16[1024,128]{1,0:T(8,128)(2,1)S(1)} %collective-permute-done.15.refs_10_.refs_15_), channel_id=1, source_target_pairs={{0,4},{2,6},{4,0},{6,2},{8,12},{10,14},{12,8},{14,10},{16,20},{18,... | collective-permute-start | bytes 786440 | tf_op jit(solution)/shard_map/ppermute | solution.py:272
  81.2 8.5 %copy-start.1 = (f32[3,1,64,128]{3,2,1,0:T(8,128)S(1)}, f32[3,1,64,128]{3,2,1,0:T(8,128)}, u32[]{:S(2)}) copy-start(f32[3,1,64,128]{3,2,1,0:T(8,128)} %param.11) | copy-start | bytes 294916
  81.2 1.8 %collective-permute-start.20 = (f32[12,64,128]{2,1,0:T(8,128)S(1)}, f32[12,64,128]{2,1,0:T(8,128)S(1)}, u32[]{:S(2)}, u32[]{:S(2)}) collective-permute-start(f32[12,64,128]{2,1,0:T(8,128)S(1)} %slice_bitcast_fusion), channel_id=1, source_target_pairs={{0,1},{1,0},{2,3},{3,2},{4,5},{5,4},{6,7},{7,6},{8,9},{9,8},{10,11... | collective-permute-start | bytes 1179656 | tf_op jit(solution)/shard_map/ppermute | solution.py:275
  83.1 5.4 %collective-permute-start.23 = (bf16[3,64,128]{2,1,0:T(8,128)(2,1)S(1)}, bf16[3,64,128]{2,1,0:T(8,128)(2,1)S(1)}, u32[]{:S(2)}, u32[]{:S(2)}) collective-permute-start(bf16[3,64,128]{2,1,0:T(8,128)(2,1)S(1)} %get-tuple-element.74), channel_id=1, source_target_pairs={{0,10},{2,8},{4,14},{6,12},{8,2},{10,0},{12,6},{14,4},{16,26},{18,... | collective-permute-start | bytes 147464 | tf_op jit(solution)/shard_map/ppermute | solution.py:272
  83.5 4.9 %collective-permute-start.22 = (bf16[3,64,128]{2,1,0:T(8,128)(2,1)S(1)}, bf16[3,64,128]{2,1,0:T(8,128)(2,1)S(1)}, u32[]{:S(2)}, u32[]{:S(2)}) collective-permute-start(bf16[3,64,128]{2,1,0:T(8,128)(2,1)S(1)} %get-tuple-element.75), channel_id=1, source_target_pairs={{0,8},{2,10},{4,12},{6,14},{8,0},{10,2},{12,4},{14,6},{16,24},{18,... | collective-permute-start | bytes 147464 | tf_op jit(solution)/shard_map/ppermute | solution.py:272
  85.6 4.1 %collective-permute-start.21 = (bf16[3,64,128]{2,1,0:T(8,128)(2,1)S(1)}, bf16[3,64,128]{2,1,0:T(8,128)(2,1)S(1)}, u32[]{:S(2)}, u32[]{:S(2)}) collective-permute-start(bf16[3,64,128]{2,1,0:T(8,128)(2,1)S(1)} %get-tuple-element.73), channel_id=1, source_target_pairs={{0,2},{2,0},{4,6},{6,4},{8,10},{10,8},{12,14},{14,12},{16,18},{18,... | collective-permute-start | bytes 147464 | tf_op jit(solution)/shard_map/ppermute | solution.py:272

commit v11 on v10

--- a/solution.py
+++ b/solution.py
@@ -14,19 +14,22 @@
 
 
 FIRST = ("c0", "c1", "s1.0")
-SECOND = ("p3", "r1", "r2", "s2.1", "s1.1","s3.0","s1.2")
+SECOND = ("p3","r1","r2","s1.1","s3.0","s2.2")
 WAITS = {
     **dict.fromkeys(FIRST, ()),
     "s2.0": (),
+    "s2.1": ("s2.0",),
     "t1o": ("s2.0",),
-    "r1": ("c0","s1.0"),
-    **dict.fromkeys(("p3", "r2", "s2.1", "s1.1"), FIRST+("i",)),
-    **dict.fromkeys(("s3.0","s1.2"), ("p3",)),
-
-    **dict.fromkeys(("s2.2","s3.1","r3","u3"), SECOND),
+    "r1": ("c0", "s1.0"),
+    **dict.fromkeys(("p3", "r2", "s1.1"), FIRST+("i","s2.0")),
+    "s2.2": ("s2.1",),
+    "s3.0": (),
+
+    "s3.1": SECOND,
+    **dict.fromkeys(("s2.3","r3","u3","s1.2"), SECOND),
     **dict.fromkeys(("t1k1","t1k2"), SECOND),
     "q": (),
-    "t1k3": ("q","s2.2","s3.1"),
+    "t1k3": ("q","s2.3","s3.1","s1.2"),
 }
 
 
@@ -293,7 +296,8 @@
             return done[name]
 
         far = 1 << (len(outside) - 1)
-        pieces = {0: [[0], list(range(1, group - 1)), [group - 1]], far: [[0], list(range(1, group - 1)), [group - 1]]}
+        pieces = [[0], list(range(1, group - 1)), [group - 1]]
+        finer = [[0], [1], list(range(2, group - 1)), [group - 1]]
         sizes = {}
         orders = {}
         joins = {}
@@ -339,9 +343,16 @@
         for key in range(1, 2 * far):
             bit = key & -key
             before = key ^ bit
-            sizes[key] = pieces[far if key >= far else 0]
+            sizes[key] = finer if key == far else pieces
             for i, js in enumerate(sizes[key]):
-                if before:
+                if before == far:
+                    source = lambda js=js: [
+                        (get(f"s{far}.{k}"), at, False)
+                        for k, parts in enumerate(finer)
+                        for at, j in enumerate(parts)
+                        if j in js
+                    ]
+                elif before:
                     source = lambda before=before, i=i: [get(f"s{before}.{i}")]
                 else:
                     source = lambda js=js: [part(j) for j in js]

time: 90.8 us -> 90.9 us (level)
    ppermute x19 -> x20, starting transfers between devices: 24 us -> 23.7 us  [swap(): return lax.ppermute(value, 'ka', [(i, i ^ mask) for i in range(points)])]
    ppermute x19 -> x20, waiting for transfers between devices: 45.4 us -> 45.6 us  [swap(): return lax.ppermute(value, 'ka', [(i, i ^ mask) for i in range(points)])]
  transfers between devices with their start and end apart: 24 -> 25, of which waited for: 12 -> 13; matrix products, arithmetic and copies ran while one was open for 2% -> 3% of each run, Pallas kernels for 12% -> 12%
where the time goes in v11:
time: 90.9 us; the launch traced here: 90.4 us
  waiting for transfers between devices  47.3 us (52%)
  starting transfers between devices  24.4 us (27%)
  Pallas kernels  14.1 us (16%)
  other arithmetic  2.65 us (3%)
  local copies, waits for them, and re-layouts  1.75 us (2%)
    ppermute x20, waiting for transfers between devices, swap(): return lax.ppermute(value, 'ka', [(i, i ^ mask) for i in range(points)])  45.6 us
    ppermute x20, starting transfers between devices, swap(): return lax.ppermute(value, 'ka', [(i, i ^ mask) for i in range(points)])  23.7 us
    pallas_call x2, Pallas kernels, project(): pl.pallas_call(functools.partial(project_kernel, orders, inside, halves),...  7.99 us
    pallas_call x2, Pallas kernels, couple(): pl.pallas_call(functools.partial(couple_kernel, jobs, last, inside, outsi...  5.54 us
  transfers between devices with their start and end apart: 25, of which 13 were waited for; matrix products, arithmetic and copies ran while one was open for 3% of the time, Pallas kernels for 12%

profile of v11, /device:TPU:0, one launch (start us, length us, event | category | flops | bytes accessed | tf_op | source)
XLA Modules:
  0.0 90.4 jit_solution(11853172128848030658)
XLA Ops:
  0.1 1.3 %constant_dynamic-slice_fusion = (bf16[1024,128]{1,0:T(8,128)(2,1)S(1)}, bf16[1024,128]{1,0:T(8,128)(2,1)S(1)}, bf16[1024,128]{1,0:T(8,128)(2,1)S(1)}, bf16[1024,128]{1,0:T(8,128)(2,1)S(1)}) fusion(bf16[4096,128]{1,0:T(8,128)(2,1)} %bitcast.20, s32[]{:T(128)S(6)} %select_n.15, s32[]{:T(128)S(6)} %select_n.14, s32[]{:T(128)S(6)} %select_n.13, s32[]{:T(128)S(6)} %select_n.12), kind=kLoop, calls=%fused_computation.12 | loop fusion | bytes 2097168 | tf_op jit(solution)/shard_map/dynamic_slice | solution.py:306
  1.3 3.0 %collective-permute-start.1 = (bf16[1024,128]{1,0:T(8,128)(2,1)S(1)}, bf16[1024,128]{1,0:T(8,128)(2,1)S(1)}, u32[]{:S(2)}, u32[]{:S(2)}) collective-permute-start(bf16[1024,128]{1,0:T(8,128)(2,1)S(1)} %get-tuple-element.74.refs_1_.refs_6_), channel_id=1, source_target_pairs={{0,4},{2,6},{4,0},{6,2},{8,12},{10,14},{12,8},{14,10},{16,20},{18,... | collective-permute-start | bytes 786440 | tf_op jit(solution)/shard_map/ppermute | solution.py:275
  4.4 2.6 %collective-permute-start.4 = (bf16[1024,128]{1,0:T(8,128)(2,1)S(1)}, bf16[1024,128]{1,0:T(8,128)(2,1)S(1)}, u32[]{:S(2)}, u32[]{:S(2)}) collective-permute-start(bf16[1024,128]{1,0:T(8,128)(2,1)S(1)} %get-tuple-element.74.refs_1_.refs_6_), channel_id=1, source_target_pairs={{0,16},{2,18},{4,20},{6,22},{8,24},{10,26},{12,28},{14,30},{16,0},... | collective-permute-start | bytes 786440 | tf_op jit(solution)/shard_map/ppermute | solution.py:275
  7.0 1.5 %collective-permute-start = (bf16[1024,128]{1,0:T(8,128)(2,1)S(1)}, bf16[1024,128]{1,0:T(8,128)(2,1)S(1)}, u32[]{:S(2)}, u32[]{:S(2)}) collective-permute-start(bf16[1024,128]{1,0:T(8,128)(2,1)S(1)} %get-tuple-element.71), channel_id=1, source_target_pairs={{0,2},{2,0},{4,6},{6,4},{8,10},{10,8},{12,14},{14,12},{16,18},{18,... | collective-permute-start | bytes 786440 | tf_op jit(solution)/shard_map/ppermute | solution.py:275
  8.4 0.9 pad_maximum_fusion.2
  9.3 1.6 %collective-permute-start.3 = (bf16[2048,128]{1,0:T(8,128)(2,1)}, bf16[2048,128]{1,0:T(8,128)(2,1)S(1)}, u32[]{:S(2)}, u32[]{:S(2)}) collective-permute-start(bf16[2048,128]{1,0:T(8,128)(2,1)} %pad_maximum_fusion.2), channel_id=1, source_target_pairs={{0,8},{2,10},{4,12},{6,14},{8,0},{10,2},{12,4},{14,6},{16,24},{18,... | collective-permute-start | bytes 1572872 | tf_op jit(solution)/shard_map/ppermute | solution.py:275
  10.9 0.9 %pad_maximum_fusion = bf16[3072,128]{1,0:T(8,128)(2,1)} fusion(bf16[1024,128]{1,0:T(8,128)(2,1)S(1)} %get-tuple-element.72, bf16[1024,128]{1,0:T(8,128)(2,1)S(1)} %get-tuple-element.73, bf16[1024,128]{1,0:T(8,128)(2,1)S(1)} %get-tuple-element.74.refs_1_.refs_6_), kind=kLoop, calls=%fused_computation | loop fusion | flops 2359296 | bytes 1572864 | tf_op jit(solution)/shard_map/concatenate | solution.py:369
  12.3 2.1 %collective-permute-done.refs_0_.refs_1_.refs_2_.refs_7_ = bf16[1024,128]{1,0:T(8,128)(2,1)S(1)} collective-permute-done((bf16[1024,128]{1,0:T(8,128)(2,1)S(1)}, bf16[1024,128]{1,0:T(8,128)(2,1)S(1)}, u32[]{:S(2)}, u32[]{:S(2)}) %collective-permute-start) | collective-permute-done | bytes 262176 | tf_op jit(solution)/shard_map/ppermute | solution.py:275
  14.4 1.5 %collective-permute-start.2 = (bf16[3072,128]{1,0:T(8,128)(2,1)}, bf16[3072,128]{1,0:T(8,128)(2,1)S(1)}, u32[]{:S(2)}, u32[]{:S(2)}) collective-permute-start(bf16[3072,128]{1,0:T(8,128)(2,1)} %pad_maximum_fusion), channel_id=1, source_target_pairs={{0,2},{2,0},{4,6},{6,4},{8,10},{10,8},{12,14},{14,12},{16,18},{18,... | collective-permute-start | bytes 2359304 | tf_op jit(solution)/shard_map/ppermute | solution.py:275
  15.9 2.8 %collective-permute-done.4.refs_8_.refs_13_ = bf16[1024,128]{1,0:T(8,128)(2,1)S(1)} collective-permute-done((bf16[1024,128]{1,0:T(8,128)(2,1)S(1)}, bf16[1024,128]{1,0:T(8,128)(2,1)S(1)}, u32[]{:S(2)}, u32[]{:S(2)}) %collective-permute-start.4) | collective-permute-done | bytes 262176 | tf_op jit(solution)/shard_map/ppermute | solution.py:275
  19.2 12.5 %collective-permute-done.3.refs_0_.refs_1_.refs_3_.refs_8_ = bf16[2048,128]{1,0:T(8,128)(2,1)S(1)} collective-permute-done((bf16[2048,128]{1,0:T(8,128)(2,1)}, bf16[2048,128]{1,0:T(8,128)(2,1)S(1)}, u32[]{:S(2)}, u32[]{:S(2)}) %collective-permute-start.3) | collective-permute-done | bytes 524320 | tf_op jit(solution)/shard_map/ppermute | solution.py:275
  32.5 1.4 %collective-permute-start.7 = (bf16[1024,128]{1,0:T(8,128)(2,1)S(1)}, bf16[1024,128]{1,0:T(8,128)(2,1)S(1)}, u32[]{:S(2)}, u32[]{:S(2)}) collective-permute-start(bf16[1024,128]{1,0:T(8,128)(2,1)S(1)} %stitch.8), channel_id=1, source_target_pairs={{0,2},{2,0},{4,6},{6,4},{8,10},{10,8},{12,14},{14,12},{16,18},{18,... | collective-permute-start | bytes 786440 | tf_op jit(solution)/shard_map/ppermute | solution.py:275
  34.0 0.7 collective-permute-start.11
  34.7 4.2 %collective-permute-done.7.refs_4_.refs_0_.refs_9_ = bf16[1024,128]{1,0:T(8,128)(2,1)S(1)} collective-permute-done((bf16[1024,128]{1,0:T(8,128)(2,1)S(1)}, bf16[1024,128]{1,0:T(8,128)(2,1)S(1)}, u32[]{:S(2)}, u32[]{:S(2)}) %collective-permute-start.7) | collective-permute-done | bytes 262176 | tf_op jit(solution)/shard_map/ppermute | solution.py:275
  38.9 7.7 %collective-permute-done.11.refs_1_.refs_10_.refs_15_ = bf16[1024,128]{1,0:T(8,128)(2,1)S(1)} collective-permute-done((bf16[1024,128]{1,0:T(8,128)(2,1)S(1)}, bf16[1024,128]{1,0:T(8,128)(2,1)S(1)}, u32[]{:S(2)}, u32[]{:S(2)}) %collective-permute-start.11) | collective-permute-done | bytes 262176 | tf_op jit(solution)/shard_map/ppermute | solution.py:275
  46.6 2.7 %collective-permute-done.5.refs_2_.refs_3_.refs_4_ = bf16[2048,128]{1,0:T(8,128)(2,1)S(1)} collective-permute-done((bf16[2048,128]{1,0:T(8,128)(2,1)S(1)}, bf16[2048,128]{1,0:T(8,128)(2,1)S(1)}, u32[]{:S(2)}, u32[]{:S(2)}) %collective-permute-start.5) | collective-permute-done | bytes 524320 | tf_op jit(solution)/shard_map/ppermute | solution.py:275
  50.8 0.7 collective-permute-start.18
  51.5 1.1 %collective-permute-start.15 = (bf16[1024,128]{1,0:T(8,128)(2,1)S(1)}, bf16[1024,128]{1,0:T(8,128)(2,1)S(1)}, u32[]{:S(2)}, u32[]{:S(2)}) collective-permute-start(bf16[1024,128]{1,0:T(8,128)(2,1)S(1)} %collective-permute-done.7.refs_4_.refs_0_.refs_9_), channel_id=1, source_target_pairs={{0,16},{2,18},{4,20},{6,22},{8,24},{10,26},{12,28},{14,30},{16,0},... | collective-permute-start | bytes 786440 | tf_op jit(solution)/shard_map/ppermute | solution.py:275
  52.7 1.5 %collective-permute-start.17 = (bf16[1024,128]{1,0:T(8,128)(2,1)S(1)}, bf16[1024,128]{1,0:T(8,128)(2,1)S(1)}, u32[]{:S(2)}, u32[]{:S(2)}) collective-permute-start(bf16[1024,128]{1,0:T(8,128)(2,1)S(1)} %collective-permute-done.7.refs_4_.refs_0_.refs_9_), channel_id=1, source_target_pairs={{0,4},{2,6},{4,0},{6,2},{8,12},{10,14},{12,8},{14,10},{16,20},{18,... | collective-permute-start | bytes 786440 | tf_op jit(solution)/shard_map/ppermute | solution.py:275
  54.2 2.5 %collective-permute-start.19 = (bf16[1024,128]{1,0:T(8,128)(2,1)S(1)}, bf16[1024,128]{1,0:T(8,128)(2,1)S(1)}, u32[]{:S(2)}, u32[]{:S(2)}) collective-permute-start(bf16[1024,128]{1,0:T(8,128)(2,1)S(1)} %stitch.14), channel_id=1, source_target_pairs={{0,8},{2,10},{4,12},{6,14},{8,0},{10,2},{12,4},{14,6},{16,24},{18,... | collective-permute-start | bytes 786440 | tf_op jit(solution)/shard_map/ppermute | solution.py:275
  56.6 4.6 %project.1.refs_0_ = bf16[9,128,1024]{2,1,0:T(8,128)(2,1)S(1)} custom-call(s32[2]{0:T(128)S(1)} %pad_add_fusion.pos, s32[288]{0:T(512)S(1)} %reshape.19.cols, s32[96]{0:T(128)S(1)} %reshape.20.counts, bf16[3,32,3,128,128]{4,3,2,1,0:T(8,128)(2,1)} %potential.3, bf16[4096,128]{1,0:T(8,128)(2,1)} %bitcast.21, ...), custom_call_target="tpu_custom_call" | custom-call | tf_op jit(solution)/shard_map/project/pallas_call | solution.py:160
  61.3 4.6 %collective-permute-done.15.refs_11_.refs_16_ = bf16[1024,128]{1,0:T(8,128)(2,1)S(1)} collective-permute-done((bf16[1024,128]{1,0:T(8,128)(2,1)S(1)}, bf16[1024,128]{1,0:T(8,128)(2,1)S(1)}, u32[]{:S(2)}, u32[]{:S(2)}) %collective-permute-start.15) | collective-permute-done | bytes 262176 | tf_op jit(solution)/shard_map/ppermute | solution.py:275
  65.9 3.9 %collective-permute-done.17.refs_7_.refs_12_ = bf16[1024,128]{1,0:T(8,128)(2,1)S(1)} collective-permute-done((bf16[1024,128]{1,0:T(8,128)(2,1)S(1)}, bf16[1024,128]{1,0:T(8,128)(2,1)S(1)}, u32[]{:S(2)}, u32[]{:S(2)}) %collective-permute-start.17) | collective-permute-done | bytes 262176 | tf_op jit(solution)/shard_map/ppermute | solution.py:275
  70.5 2.7 %couple.1.refs_4_ = f32[9,128,128]{2,1,0:T(8,128)S(1)} custom-call(s32[2]{0:T(128)S(1)} %pad_add_fusion.pos, s32[48]{0:T(128)S(1)} %reshape.21.partners, bf16[9,128,1024]{2,1,0:T(8,128)(2,1)S(1)} %project.1.refs_0_, bf16[1024,128]{1,0:T(8,128)(2,1)S(1)} %get-tuple-element.74.refs_1_.refs_6_, ...), custom_call_target="tpu_custom_call" | custom-call | tf_op jit(solution)/shard_map/couple/pallas_call | solution.py:247
  73.3 3.4 %project_last.1.refs_5_ = bf16[3,128,1024]{2,1,0:T(8,128)(2,1)S(1)} custom-call(s32[2]{0:T(128)S(1)} %pad_add_fusion.pos, s32[288]{0:T(512)S(1)} %reshape.19.cols, s32[96]{0:T(128)S(1)} %reshape.20.counts, bf16[3,32,3,128,128]{4,3,2,1,0:T(8,128)(2,1)} %potential.3, bf16[1024,128]{1,0:T(8,128)(2,1)S(1)} %collective-permute-done.7.refs_4_.refs_0_.refs_9_, ...), custom_call_target="tpu_custom_call" | custom-call | tf_op jit(solution)/shard_map/project_last/pallas_call | solution.py:160
  76.6 2.1 %collective-permute-done.16.refs_3_.refs_19_ = bf16[1024,128]{1,0:T(8,128)(2,1)S(1)} collective-permute-done((bf16[1024,128]{1,0:T(8,128)(2,1)S(1)}, bf16[1024,128]{1,0:T(8,128)(2,1)S(1)}, u32[]{:S(2)}, u32[]{:S(2)}) %collective-permute-start.16) | collective-permute-done | bytes 262176 | tf_op jit(solution)/shard_map/ppermute | solution.py:275
  78.7 2.8 %couple_last.1 = f32[2,12,64,128]{3,2,1,0:T(8,128)S(1)} custom-call(s32[2]{0:T(128)S(1)} %pad_add_fusion.pos, s32[48]{0:T(128)S(1)} %reshape.21.partners, bf16[9,128,1024]{2,1,0:T(8,128)(2,1)S(1)} %project.1.refs_0_, bf16[1024,128]{1,0:T(8,128)(2,1)S(1)} %collective-permute-done.9.refs_1_.refs_17_, ...), custom_call_target="tpu_custom_call" | custom-call | tf_op jit(solution)/shard_map/couple_last/pallas_call | solution.py:247
  81.7 1.7 %collective-permute-done.21 = f32[12,64,128]{2,1,0:T(8,128)S(1)} collective-permute-done((f32[12,64,128]{2,1,0:T(8,128)S(1)}, f32[12,64,128]{2,1,0:T(8,128)S(1)}, u32[]{:S(2)}, u32[]{:S(2)}) %collective-permute-start.21) | collective-permute-done | bytes 393248 | tf_op jit(solution)/shard_map/ppermute | solution.py:278
  83.8 1.9 %collective-permute-start.23 = (bf16[3,64,128]{2,1,0:T(8,128)(2,1)S(1)}, bf16[3,64,128]{2,1,0:T(8,128)(2,1)S(1)}, u32[]{:S(2)}, u32[]{:S(2)}) collective-permute-start(bf16[3,64,128]{2,1,0:T(8,128)(2,1)S(1)} %get-tuple-element.77), channel_id=1, source_target_pairs={{0,8},{2,10},{4,12},{6,14},{8,0},{10,2},{12,4},{14,6},{16,24},{18,... | collective-permute-start | bytes 147464 | tf_op jit(solution)/shard_map/ppermute | solution.py:275
  85.7 1.4 %collective-permute-start.22 = (bf16[3,64,128]{2,1,0:T(8,128)(2,1)S(1)}, bf16[3,64,128]{2,1,0:T(8,128)(2,1)S(1)}, u32[]{:S(2)}, u32[]{:S(2)}) collective-permute-start(bf16[3,64,128]{2,1,0:T(8,128)(2,1)S(1)} %get-tuple-element.75), channel_id=1, source_target_pairs={{0,2},{2,0},{4,6},{6,4},{8,10},{10,8},{12,14},{14,12},{16,18},{18,... | collective-permute-start | bytes 147464 | tf_op jit(solution)/shard_map/ppermute | solution.py:275
  87.1 1.7 %collective-permute-done.24 = bf16[3,64,128]{2,1,0:T(8,128)(2,1)S(1)} collective-permute-done((bf16[3,64,128]{2,1,0:T(8,128)(2,1)S(1)}, bf16[3,64,128]{2,1,0:T(8,128)(2,1)S(1)}, u32[]{:S(2)}, u32[]{:S(2)}) %collective-permute-start.24) | collective-permute-done | bytes 49184 | tf_op jit(solution)/shard_map/ppermute | solution.py:275
  88.8 0.9 %collective-permute-done.22 = bf16[3,64,128]{2,1,0:T(8,128)(2,1)S(1)} collective-permute-done((bf16[3,64,128]{2,1,0:T(8,128)(2,1)S(1)}, bf16[3,64,128]{2,1,0:T(8,128)(2,1)S(1)}, u32[]{:S(2)}, u32[]{:S(2)}) %collective-permute-start.22) | collective-permute-done | bytes 49184 | tf_op jit(solution)/shard_map/ppermute | solution.py:275
  (53 shorter events, 5.1 us)
Async XLA Ops:
  1.3 13.1 %collective-permute-start.1 = (bf16[1024,128]{1,0:T(8,128)(2,1)S(1)}, bf16[1024,128]{1,0:T(8,128)(2,1)S(1)}, u32[]{:S(2)}, u32[]{:S(2)}) collective-permute-start(bf16[1024,128]{1,0:T(8,128)(2,1)S(1)} %get-tuple-element.74.refs_1_.refs_6_), channel_id=1, source_target_pairs={{0,4},{2,6},{4,0},{6,2},{8,12},{10,14},{12,8},{14,10},{16,20},{18,... | collective-permute-start | bytes 786440 | tf_op jit(solution)/shard_map/ppermute | solution.py:275
  4.4 14.4 %collective-permute-start.4 = (bf16[1024,128]{1,0:T(8,128)(2,1)S(1)}, bf16[1024,128]{1,0:T(8,128)(2,1)S(1)}, u32[]{:S(2)}, u32[]{:S(2)}) collective-permute-start(bf16[1024,128]{1,0:T(8,128)(2,1)S(1)} %get-tuple-element.74.refs_1_.refs_6_), channel_id=1, source_target_pairs={{0,16},{2,18},{4,20},{6,22},{8,24},{10,26},{12,28},{14,30},{16,0},... | collective-permute-start | bytes 786440 | tf_op jit(solution)/shard_map/ppermute | solution.py:275
  7.0 7.5 %collective-permute-start = (bf16[1024,128]{1,0:T(8,128)(2,1)S(1)}, bf16[1024,128]{1,0:T(8,128)(2,1)S(1)}, u32[]{:S(2)}, u32[]{:S(2)}) collective-permute-start(bf16[1024,128]{1,0:T(8,128)(2,1)S(1)} %get-tuple-element.71), channel_id=1, source_target_pairs={{0,2},{2,0},{4,6},{6,4},{8,10},{10,8},{12,14},{14,12},{16,18},{18,... | collective-permute-start | bytes 786440 | tf_op jit(solution)/shard_map/ppermute | solution.py:275
  8.4 3.4 %copy-start.2 = (s32[3,32,3]{1,2,0:T(4,128)S(1)}, s32[3,32,3]{1,2,0:T(4,128)}, u32[]{:S(2)}) copy-start(s32[3,32,3]{1,2,0:T(4,128)} %param.8) | copy-start | bytes 3460
  9.3 2.9 %copy-start.3 = (s32[3,32]{1,0:T(4,128)S(1)}, s32[3,32]{1,0:T(4,128)}, u32[]{:S(2)}) copy-start(s32[3,32]{1,0:T(4,128)} %param.9) | copy-start | bytes 1156
  9.3 3.0 %copy-start.4 = (s32[3,16]{1,0:T(4,128)S(1)}, s32[3,16]{1,0:T(4,128)}, u32[]{:S(2)}) copy-start(s32[3,16]{1,0:T(4,128)} %param.10) | copy-start | bytes 580
  9.3 22.4 %collective-permute-start.3 = (bf16[2048,128]{1,0:T(8,128)(2,1)}, bf16[2048,128]{1,0:T(8,128)(2,1)S(1)}, u32[]{:S(2)}, u32[]{:S(2)}) collective-permute-start(bf16[2048,128]{1,0:T(8,128)(2,1)} %pad_maximum_fusion.2), channel_id=1, source_target_pairs={{0,8},{2,10},{4,12},{6,14},{8,0},{10,2},{12,4},{14,6},{16,24},{18,... | collective-permute-start | bytes 1572872 | tf_op jit(solution)/shard_map/ppermute | solution.py:275
  11.9 27.0 %copy-start = (bf16[1,4096,128]{2,1,0:T(8,128)(2,1)S(1)}, bf16[1,4096,128]{2,1,0:T(8,128)(2,1)}, u32[]{:S(2)}) copy-start(bf16[1,4096,128]{2,1,0:T(8,128)(2,1)} %param.6) | copy-start | bytes 3145732
  14.4 32.1 %collective-permute-start.2 = (bf16[3072,128]{1,0:T(8,128)(2,1)}, bf16[3072,128]{1,0:T(8,128)(2,1)S(1)}, u32[]{:S(2)}, u32[]{:S(2)}) collective-permute-start(bf16[3072,128]{1,0:T(8,128)(2,1)} %pad_maximum_fusion), channel_id=1, source_target_pairs={{0,2},{2,0},{4,6},{6,4},{8,10},{10,8},{12,14},{14,12},{16,18},{18,... | collective-permute-start | bytes 2359304 | tf_op jit(solution)/shard_map/ppermute | solution.py:275
  18.8 13.8 %collective-permute-start.10 = (bf16[1024,128]{1,0:T(8,128)(2,1)S(1)}, bf16[1024,128]{1,0:T(8,128)(2,1)S(1)}, u32[]{:S(2)}, u32[]{:S(2)}) collective-permute-start(bf16[1024,128]{1,0:T(8,128)(2,1)S(1)} %collective-permute-done.refs_0_.refs_1_.refs_2_.refs_7_), channel_id=1, source_target_pairs={{0,16},{2,18},{4,20},{6,22},{8,24},{10,26},{12,28},{14,30},{16,0},... | collective-permute-start | bytes 786440 | tf_op jit(solution)/shard_map/ppermute | solution.py:275
  18.8 15.2 %collective-permute-start.9 = (bf16[1024,128]{1,0:T(8,128)(2,1)S(1)}, bf16[1024,128]{1,0:T(8,128)(2,1)S(1)}, u32[]{:S(2)}, u32[]{:S(2)}) collective-permute-start(bf16[1024,128]{1,0:T(8,128)(2,1)S(1)} %collective-permute-done.4.refs_8_.refs_13_), channel_id=1, source_target_pairs={{0,4},{2,6},{4,0},{6,2},{8,12},{10,14},{12,8},{14,10},{16,20},{18,... | collective-permute-start | bytes 786440 | tf_op jit(solution)/shard_map/ppermute | solution.py:275
  31.7 17.6 %collective-permute-start.5 = (bf16[2048,128]{1,0:T(8,128)(2,1)S(1)}, bf16[2048,128]{1,0:T(8,128)(2,1)S(1)}, u32[]{:S(2)}, u32[]{:S(2)}) collective-permute-start(bf16[2048,128]{1,0:T(8,128)(2,1)S(1)} %pad_maximum_fusion.1), channel_id=1, source_target_pairs={{0,8},{2,10},{4,12},{6,14},{8,0},{10,2},{12,4},{14,6},{16,24},{18,... | collective-permute-start | bytes 1572872 | tf_op jit(solution)/shard_map/ppermute | solution.py:275
  31.8 17.5 %collective-permute-start.8 = (bf16[2048,128]{1,0:T(8,128)(2,1)S(1)}, bf16[2048,128]{1,0:T(8,128)(2,1)S(1)}, u32[]{:S(2)}, u32[]{:S(2)}) collective-permute-start(bf16[2048,128]{1,0:T(8,128)(2,1)S(1)} %stitch.9), channel_id=1, source_target_pairs={{0,4},{2,6},{4,0},{6,2},{8,12},{10,14},{12,8},{14,10},{16,20},{18,... | collective-permute-start | bytes 1572872 | tf_op jit(solution)/shard_map/ppermute | solution.py:275
  32.5 6.4 %collective-permute-start.7 = (bf16[1024,128]{1,0:T(8,128)(2,1)S(1)}, bf16[1024,128]{1,0:T(8,128)(2,1)S(1)}, u32[]{:S(2)}, u32[]{:S(2)}) collective-permute-start(bf16[1024,128]{1,0:T(8,128)(2,1)S(1)} %stitch.8), channel_id=1, source_target_pairs={{0,2},{2,0},{4,6},{6,4},{8,10},{10,8},{12,14},{14,12},{16,18},{18,... | collective-permute-start | bytes 786440 | tf_op jit(solution)/shard_map/ppermute | solution.py:275
  34.0 12.6 %collective-permute-start.11 = (bf16[1024,128]{1,0:T(8,128)(2,1)S(1)}, bf16[1024,128]{1,0:T(8,128)(2,1)S(1)}, u32[]{:S(2)}, u32[]{:S(2)}) collective-permute-start(bf16[1024,128]{1,0:T(8,128)(2,1)S(1)} %stitch.10), channel_id=1, source_target_pairs={{0,16},{2,18},{4,20},{6,22},{8,24},{10,26},{12,28},{14,30},{16,0},... | collective-permute-start | bytes 786440 | tf_op jit(solution)/shard_map/ppermute | solution.py:275
  38.9 12.6 %collective-permute-start.6 = (bf16[4096,128]{1,0:T(8,128)(2,1)S(1)}, bf16[4096,128]{1,0:T(8,128)(2,1)S(1)}, u32[]{:S(2)}, u32[]{:S(2)}) collective-permute-start(bf16[4096,128]{1,0:T(8,128)(2,1)S(1)} %bitcast.22), channel_id=1, source_target_pairs={{0,1},{1,0},{2,3},{3,2},{4,5},{5,4},{6,7},{7,6},{8,9},{9,8},{10,11... | collective-permute-start | bytes 3145736 | tf_op jit(solution)/shard_map/ppermute | solution.py:278
  49.4 3.2 %collective-permute-start.12 = (bf16[4096,128]{1,0:T(8,128)(2,1)S(1)}, bf16[4096,128]{1,0:T(8,128)(2,1)S(1)}, u32[]{:S(2)}, u32[]{:S(2)}) collective-permute-start(bf16[4096,128]{1,0:T(8,128)(2,1)S(1)} %stitch.11), channel_id=1, source_target_pairs={{0,1},{1,0},{2,3},{3,2},{4,5},{5,4},{6,7},{7,6},{8,9},{9,8},{10,11... | collective-permute-start | bytes 3145736 | tf_op jit(solution)/shard_map/ppermute | solution.py:278
  49.7 4.5 %collective-permute-start.13 = (bf16[4096,128]{1,0:T(8,128)(2,1)S(1)}, bf16[4096,128]{1,0:T(8,128)(2,1)S(1)}, u32[]{:S(2)}, u32[]{:S(2)}) collective-permute-start(bf16[4096,128]{1,0:T(8,128)(2,1)S(1)} %stitch.12), channel_id=1, source_target_pairs={{0,1},{1,0},{2,3},{3,2},{4,5},{5,4},{6,7},{7,6},{8,9},{9,8},{10,11... | collective-permute-start | bytes 3145736 | tf_op jit(solution)/shard_map/ppermute | solution.py:278
  50.3 19.5 %collective-permute-start.14 = (bf16[2048,128]{1,0:T(8,128)(2,1)S(1)}, bf16[2048,128]{1,0:T(8,128)(2,1)S(1)}, u32[]{:S(2)}, u32[]{:S(2)}) collective-permute-start(bf16[2048,128]{1,0:T(8,128)(2,1)S(1)} %stitch.13), channel_id=1, source_target_pairs={{0,4},{2,6},{4,0},{6,2},{8,12},{10,14},{12,8},{14,10},{16,20},{18,... | collective-permute-start | bytes 1572872 | tf_op jit(solution)/shard_map/ppermute | solution.py:275
  50.8 19.0 %collective-permute-start.18 = (bf16[2048,128]{1,0:T(8,128)(2,1)S(1)}, bf16[2048,128]{1,0:T(8,128)(2,1)S(1)}, u32[]{:S(2)}, u32[]{:S(2)}) collective-permute-start(bf16[2048,128]{1,0:T(8,128)(2,1)S(1)} %collective-permute-done.5.refs_2_.refs_3_.refs_4_), channel_id=1, source_target_pairs={{0,2},{2,0},{4,6},{6,4},{8,10},{10,8},{12,14},{14,12},{16,18},{18,... | collective-permute-start | bytes 1572872 | tf_op jit(solution)/shard_map/ppermute | solution.py:275
  51.5 14.4 %collective-permute-start.15 = (bf16[1024,128]{1,0:T(8,128)(2,1)S(1)}, bf16[1024,128]{1,0:T(8,128)(2,1)S(1)}, u32[]{:S(2)}, u32[]{:S(2)}) collective-permute-start(bf16[1024,128]{1,0:T(8,128)(2,1)S(1)} %collective-permute-done.7.refs_4_.refs_0_.refs_9_), channel_id=1, source_target_pairs={{0,16},{2,18},{4,20},{6,22},{8,24},{10,26},{12,28},{14,30},{16,0},... | collective-permute-start | bytes 786440 | tf_op jit(solution)/shard_map/ppermute | solution.py:275
  52.7 17.1 %collective-permute-start.17 = (bf16[1024,128]{1,0:T(8,128)(2,1)S(1)}, bf16[1024,128]{1,0:T(8,128)(2,1)S(1)}, u32[]{:S(2)}, u32[]{:S(2)}) collective-permute-start(bf16[1024,128]{1,0:T(8,128)(2,1)S(1)} %collective-permute-done.7.refs_4_.refs_0_.refs_9_), channel_id=1, source_target_pairs={{0,4},{2,6},{4,0},{6,2},{8,12},{10,14},{12,8},{14,10},{16,20},{18,... | collective-permute-start | bytes 786440 | tf_op jit(solution)/shard_map/ppermute | solution.py:275
  54.2 15.6 %collective-permute-start.19 = (bf16[1024,128]{1,0:T(8,128)(2,1)S(1)}, bf16[1024,128]{1,0:T(8,128)(2,1)S(1)}, u32[]{:S(2)}, u32[]{:S(2)}) collective-permute-start(bf16[1024,128]{1,0:T(8,128)(2,1)S(1)} %stitch.14), channel_id=1, source_target_pairs={{0,8},{2,10},{4,12},{6,14},{8,0},{10,2},{12,4},{14,6},{16,24},{18,... | collective-permute-start | bytes 786440 | tf_op jit(solution)/shard_map/ppermute | solution.py:275
  69.9 3.3 %collective-permute-start.20 = (bf16[4096,128]{1,0:T(8,128)(2,1)S(1)}, bf16[4096,128]{1,0:T(8,128)(2,1)S(1)}, u32[]{:S(2)}, u32[]{:S(2)}) collective-permute-start(bf16[4096,128]{1,0:T(8,128)(2,1)S(1)} %stitch.15), channel_id=1, source_target_pairs={{0,1},{1,0},{2,3},{3,2},{4,5},{5,4},{6,7},{7,6},{8,9},{9,8},{10,11... | collective-permute-start | bytes 3145736 | tf_op jit(solution)/shard_map/ppermute | solution.py:278
  70.0 8.7 %collective-permute-start.16 = (bf16[1024,128]{1,0:T(8,128)(2,1)S(1)}, bf16[1024,128]{1,0:T(8,128)(2,1)S(1)}, u32[]{:S(2)}, u32[]{:S(2)}) collective-permute-start(bf16[1024,128]{1,0:T(8,128)(2,1)S(1)} %collective-permute-done.15.refs_11_.refs_16_), channel_id=1, source_target_pairs={{0,4},{2,6},{4,0},{6,2},{8,12},{10,14},{12,8},{14,10},{16,20},{18,... | collective-permute-start | bytes 786440 | tf_op jit(solution)/shard_map/ppermute | solution.py:275
  81.6 8.2 %copy-start.1 = (f32[3,1,64,128]{3,2,1,0:T(8,128)S(1)}, f32[3,1,64,128]{3,2,1,0:T(8,128)}, u32[]{:S(2)}) copy-start(f32[3,1,64,128]{3,2,1,0:T(8,128)} %param.11) | copy-start | bytes 294916
  81.6 1.8 %collective-permute-start.21 = (f32[12,64,128]{2,1,0:T(8,128)S(1)}, f32[12,64,128]{2,1,0:T(8,128)S(1)}, u32[]{:S(2)}, u32[]{:S(2)}) collective-permute-start(f32[12,64,128]{2,1,0:T(8,128)S(1)} %slice_bitcast_fusion), channel_id=1, source_target_pairs={{0,1},{1,0},{2,3},{3,2},{4,5},{5,4},{6,7},{7,6},{8,9},{9,8},{10,11... | collective-permute-start | bytes 1179656 | tf_op jit(solution)/shard_map/ppermute | solution.py:278
  83.5 5.3 %collective-permute-start.24 = (bf16[3,64,128]{2,1,0:T(8,128)(2,1)S(1)}, bf16[3,64,128]{2,1,0:T(8,128)(2,1)S(1)}, u32[]{:S(2)}, u32[]{:S(2)}) collective-permute-start(bf16[3,64,128]{2,1,0:T(8,128)(2,1)S(1)} %get-tuple-element.76), channel_id=1, source_target_pairs={{0,10},{2,8},{4,14},{6,12},{8,2},{10,0},{12,6},{14,4},{16,26},{18,... | collective-permute-start | bytes 147464 | tf_op jit(solution)/shard_map/ppermute | solution.py:275
  83.8 5.0 %collective-permute-start.23 = (bf16[3,64,128]{2,1,0:T(8,128)(2,1)S(1)}, bf16[3,64,128]{2,1,0:T(8,128)(2,1)S(1)}, u32[]{:S(2)}, u32[]{:S(2)}) collective-permute-start(bf16[3,64,128]{2,1,0:T(8,128)(2,1)S(1)} %get-tuple-element.77), channel_id=1, source_target_pairs={{0,8},{2,10},{4,12},{6,14},{8,0},{10,2},{12,4},{14,6},{16,24},{18,... | collective-permute-start | bytes 147464 | tf_op jit(solution)/shard_map/ppermute | solution.py:275
  85.7 4.1 %collective-permute-start.22 = (bf16[3,64,128]{2,1,0:T(8,128)(2,1)S(1)}, bf16[3,64,128]{2,1,0:T(8,128)(2,1)S(1)}, u32[]{:S(2)}, u32[]{:S(2)}) collective-permute-start(bf16[3,64,128]{2,1,0:T(8,128)(2,1)S(1)} %get-tuple-element.75), channel_id=1, source_target_pairs={{0,2},{2,0},{4,6},{6,4},{8,10},{10,8},{12,14},{14,12},{16,18},{18,... | collective-permute-start | bytes 147464 | tf_op jit(solution)/shard_map/ppermute | solution.py:275

commit v12 on v11

--- a/solution.py
+++ b/solution.py
@@ -14,7 +14,7 @@
 
 
 FIRST = ("c0", "c1", "s1.0")
-SECOND = ("p3","r1","r2","s1.1","s3.0","s2.2")
+SECOND = ("p3","r1","r2","s1.1","s3.0","s2.2","s1.2")
 WAITS = {
     **dict.fromkeys(FIRST, ()),
     "s2.0": (),
@@ -24,12 +24,12 @@
     **dict.fromkeys(("p3", "r2", "s1.1"), FIRST+("i","s2.0")),
     "s2.2": ("s2.1",),
     "s3.0": (),
-
+    "s1.2": ("p3","s3.0"),
     "s3.1": SECOND,
-    **dict.fromkeys(("s2.3","r3","u3","s1.2"), SECOND),
+    **dict.fromkeys(("s2.3","r3","u3"), SECOND),
     **dict.fromkeys(("t1k1","t1k2"), SECOND),
     "q": (),
-    "t1k3": ("q","s2.3","s3.1","s1.2"),
+    "t1k3": ("q","s2.3","s3.1"),
 }
 
 

time: 90.9 us -> 88.9 us (0.978)
  the two profiles are of different devices: /device:TPU:0 before, /device:TPU:24 now
where the time goes in v12:
time: 88.9 us; the launch traced here: 88.3 us
  waiting for transfers between devices  55 us (62%)
  starting transfers between devices  16.3 us (18%)
  Pallas kernels  14 us (16%)
  local copies, waits for them, and re-layouts  1.76 us (2%)
  other arithmetic  0.93 us (1%)
    ppermute x20, waiting for transfers between devices, swap(): return lax.ppermute(value, 'ka', [(i, i ^ mask) for i in range(points)])  52.1 us
    ppermute x20, starting transfers between devices, swap(): return lax.ppermute(value, 'ka', [(i, i ^ mask) for i in range(points)])  15.6 us
    pallas_call x2, Pallas kernels, project(): pl.pallas_call(functools.partial(project_kernel, orders, inside, halves),...  7.89 us
    pallas_call x2, Pallas kernels, couple(): pl.pallas_call(functools.partial(couple_kernel, jobs, last, inside, outsi...  5.55 us
    ppermute x5, waiting for transfers between devices, rotate(): lax.ppermute(value, 'orb', [(i, (i + shift) % halves) for i in range(halv...  2.84 us
  transfers between devices with their start and end apart: 25, of which 16 were waited for; matrix products, arithmetic and copies ran while one was open for 1% of the time, Pallas kernels for 13%

profile of v12, /device:TPU:24, one launch (start us, length us, event | category | flops | bytes accessed | tf_op | source)
XLA Modules:
  0.0 88.3 jit_solution(6524029287146087812)
XLA Ops:
  0.1 1.3 %constant_dynamic-slice_fusion = (bf16[1024,128]{1,0:T(8,128)(2,1)S(1)}, bf16[1024,128]{1,0:T(8,128)(2,1)S(1)}, bf16[1024,128]{1,0:T(8,128)(2,1)S(1)}, bf16[1024,128]{1,0:T(8,128)(2,1)S(1)}) fusion(bf16[4096,128]{1,0:T(8,128)(2,1)} %bitcast.20, s32[]{:T(128)S(6)} %select_n.15, s32[]{:T(128)S(6)} %select_n.14, s32[]{:T(128)S(6)} %select_n.13, s32[]{:T(128)S(6)} %select_n.12), kind=kLoop, calls=%fused_computation.12 | loop fusion | bytes 2097168 | tf_op jit(solution)/shard_map/dynamic_slice | solution.py:306
  1.4 1.6 %collective-permute-start.1 = (bf16[1024,128]{1,0:T(8,128)(2,1)S(1)}, bf16[1024,128]{1,0:T(8,128)(2,1)S(1)}, u32[]{:S(2)}, u32[]{:S(2)}) collective-permute-start(bf16[1024,128]{1,0:T(8,128)(2,1)S(1)} %get-tuple-element.76.refs_1_.refs_6_), channel_id=1, source_target_pairs={{0,4},{2,6},{4,0},{6,2},{8,12},{10,14},{12,8},{14,10},{16,20},{18,... | collective-permute-start | bytes 786440 | tf_op jit(solution)/shard_map/ppermute | solution.py:275
  3.3 1.5 %collective-permute-start = (bf16[1024,128]{1,0:T(8,128)(2,1)S(1)}, bf16[1024,128]{1,0:T(8,128)(2,1)S(1)}, u32[]{:S(2)}, u32[]{:S(2)}) collective-permute-start(bf16[1024,128]{1,0:T(8,128)(2,1)S(1)} %get-tuple-element.73), channel_id=1, source_target_pairs={{0,2},{2,0},{4,6},{6,4},{8,10},{10,8},{12,14},{14,12},{16,18},{18,... | collective-permute-start | bytes 786440 | tf_op jit(solution)/shard_map/ppermute | solution.py:275
  4.8 0.5 collective-permute-start.3
  5.9 4.9 %collective-permute-done.refs_0_.refs_1_.refs_2_.refs_7_ = bf16[1024,128]{1,0:T(8,128)(2,1)S(1)} collective-permute-done((bf16[1024,128]{1,0:T(8,128)(2,1)S(1)}, bf16[1024,128]{1,0:T(8,128)(2,1)S(1)}, u32[]{:S(2)}, u32[]{:S(2)}) %collective-permute-start) | collective-permute-done | bytes 262176 | tf_op jit(solution)/shard_map/ppermute | solution.py:275
  10.8 1.5 %collective-permute-start.2 = (bf16[3072,128]{1,0:T(8,128)(2,1)S(1)}, bf16[3072,128]{1,0:T(8,128)(2,1)S(1)}, u32[]{:S(2)}, u32[]{:S(2)}) collective-permute-start(bf16[3072,128]{1,0:T(8,128)(2,1)S(1)} %pad_maximum_fusion), channel_id=1, source_target_pairs={{0,2},{2,0},{4,6},{6,4},{8,10},{10,8},{12,14},{14,12},{16,18},{18,... | collective-permute-start | bytes 2359304 | tf_op jit(solution)/shard_map/ppermute | solution.py:275
  12.3 5.0 %collective-permute-done.4.refs_8_.refs_13_ = bf16[1024,128]{1,0:T(8,128)(2,1)S(1)} collective-permute-done((bf16[1024,128]{1,0:T(8,128)(2,1)S(1)}, bf16[1024,128]{1,0:T(8,128)(2,1)S(1)}, u32[]{:S(2)}, u32[]{:S(2)}) %collective-permute-start.4) | collective-permute-done | bytes 262176 | tf_op jit(solution)/shard_map/ppermute | solution.py:275
  17.7 7.9 %collective-permute-done.3.refs_0_.refs_1_.refs_3_.refs_8_ = bf16[2048,128]{1,0:T(8,128)(2,1)S(1)} collective-permute-done((bf16[2048,128]{1,0:T(8,128)(2,1)S(1)}, bf16[2048,128]{1,0:T(8,128)(2,1)S(1)}, u32[]{:S(2)}, u32[]{:S(2)}) %collective-permute-start.3) | collective-permute-done | bytes 524320 | tf_op jit(solution)/shard_map/ppermute | solution.py:275
  25.7 1.2 %collective-permute-start.7 = (bf16[1024,128]{1,0:T(8,128)(2,1)S(1)}, bf16[1024,128]{1,0:T(8,128)(2,1)S(1)}, u32[]{:S(2)}, u32[]{:S(2)}) collective-permute-start(bf16[1024,128]{1,0:T(8,128)(2,1)S(1)} %stitch.8), channel_id=1, source_target_pairs={{0,2},{2,0},{4,6},{6,4},{8,10},{10,8},{12,14},{14,12},{16,18},{18,... | collective-permute-start | bytes 786440 | tf_op jit(solution)/shard_map/ppermute | solution.py:275
  27.0 5.1 %collective-permute-done.10.refs_0_.refs_9_.refs_14_ = bf16[1024,128]{1,0:T(8,128)(2,1)S(1)} collective-permute-done((bf16[1024,128]{1,0:T(8,128)(2,1)S(1)}, bf16[1024,128]{1,0:T(8,128)(2,1)S(1)}, u32[]{:S(2)}, u32[]{:S(2)}) %collective-permute-start.10) | collective-permute-done | bytes 262176 | tf_op jit(solution)/shard_map/ppermute | solution.py:275
  32.7 1.5 %collective-permute-done.7.refs_4_.refs_0_.refs_9_ = bf16[1024,128]{1,0:T(8,128)(2,1)S(1)} collective-permute-done((bf16[1024,128]{1,0:T(8,128)(2,1)S(1)}, bf16[1024,128]{1,0:T(8,128)(2,1)S(1)}, u32[]{:S(2)}, u32[]{:S(2)}) %collective-permute-start.7) | collective-permute-done | bytes 262176 | tf_op jit(solution)/shard_map/ppermute | solution.py:275
  34.2 0.8 collective-permute-start.12
  35.0 11.3 %collective-permute-done.11.refs_1_.refs_10_.refs_15_ = bf16[1024,128]{1,0:T(8,128)(2,1)S(1)} collective-permute-done((bf16[1024,128]{1,0:T(8,128)(2,1)S(1)}, bf16[1024,128]{1,0:T(8,128)(2,1)S(1)}, u32[]{:S(2)}, u32[]{:S(2)}) %collective-permute-start.11) | collective-permute-done | bytes 262176 | tf_op jit(solution)/shard_map/ppermute | solution.py:275
  46.9 3.8 %collective-permute-done.12.refs_7_.refs_12_ = bf16[1024,128]{1,0:T(8,128)(2,1)S(1)} collective-permute-done((bf16[1024,128]{1,0:T(8,128)(2,1)S(1)}, bf16[1024,128]{1,0:T(8,128)(2,1)S(1)}, u32[]{:S(2)}, u32[]{:S(2)}) %collective-permute-start.12) | collective-permute-done | bytes 262176 | tf_op jit(solution)/shard_map/ppermute | solution.py:275
  51.0 0.6 collective-permute-start.14
  51.6 0.6 collective-permute-start.15
  52.2 1.5 %collective-permute-start.18 = (bf16[2048,128]{1,0:T(8,128)(2,1)S(1)}, bf16[2048,128]{1,0:T(8,128)(2,1)S(1)}, u32[]{:S(2)}, u32[]{:S(2)}) collective-permute-start(bf16[2048,128]{1,0:T(8,128)(2,1)S(1)} %collective-permute-done.5.refs_2_.refs_3_.refs_4_), channel_id=1, source_target_pairs={{0,2},{2,0},{4,6},{6,4},{8,10},{10,8},{12,14},{14,12},{16,18},{18,... | collective-permute-start | bytes 1572872 | tf_op jit(solution)/shard_map/ppermute | solution.py:275
  53.9 1.1 %collective-permute-done.14.refs_7_ = bf16[4096,128]{1,0:T(8,128)(2,1)S(1)} collective-permute-done((bf16[4096,128]{1,0:T(8,128)(2,1)S(1)}, bf16[4096,128]{1,0:T(8,128)(2,1)S(1)}, u32[]{:S(2)}, u32[]{:S(2)}) %collective-permute-start.14) | collective-permute-done | bytes 1048608 | tf_op jit(solution)/shard_map/ppermute | solution.py:278
  55.0 4.6 %project.1.refs_0_ = bf16[9,128,1024]{2,1,0:T(8,128)(2,1)S(1)} custom-call(s32[2]{0:T(128)S(1)} %pad_add_fusion.pos, s32[288]{0:T(512)S(1)} %reshape.19.cols, s32[96]{0:T(128)S(1)} %reshape.20.counts, bf16[3,32,3,128,128]{4,3,2,1,0:T(8,128)(2,1)} %potential.3, bf16[4096,128]{1,0:T(8,128)(2,1)} %bitcast.21, ...), custom_call_target="tpu_custom_call" | custom-call | tf_op jit(solution)/shard_map/project/pallas_call | solution.py:160
  59.6 4.3 %collective-permute-done.16.refs_11_.refs_16_ = bf16[1024,128]{1,0:T(8,128)(2,1)S(1)} collective-permute-done((bf16[1024,128]{1,0:T(8,128)(2,1)S(1)}, bf16[1024,128]{1,0:T(8,128)(2,1)S(1)}, u32[]{:S(2)}, u32[]{:S(2)}) %collective-permute-start.16) | collective-permute-done | bytes 262176 | tf_op jit(solution)/shard_map/ppermute | solution.py:275
  64.0 3.6 %collective-permute-done.19.refs_3_.refs_2_ = bf16[1024,128]{1,0:T(8,128)(2,1)S(1)} collective-permute-done((bf16[1024,128]{1,0:T(8,128)(2,1)S(1)}, bf16[1024,128]{1,0:T(8,128)(2,1)S(1)}, u32[]{:S(2)}, u32[]{:S(2)}) %collective-permute-start.19) | collective-permute-done | bytes 262176 | tf_op jit(solution)/shard_map/ppermute | solution.py:275
  67.7 1.3 %collective-permute-start.17 = (bf16[1024,128]{1,0:T(8,128)(2,1)S(1)}, bf16[1024,128]{1,0:T(8,128)(2,1)S(1)}, u32[]{:S(2)}, u32[]{:S(2)}) collective-permute-start(bf16[1024,128]{1,0:T(8,128)(2,1)S(1)} %collective-permute-done.16.refs_11_.refs_16_), channel_id=1, source_target_pairs={{0,4},{2,6},{4,0},{6,2},{8,12},{10,14},{12,8},{14,10},{16,20},{18,... | collective-permute-start | bytes 786440 | tf_op jit(solution)/shard_map/ppermute | solution.py:275
  69.0 3.2 %couple.1.refs_4_ = f32[9,128,128]{2,1,0:T(8,128)S(1)} custom-call(s32[2]{0:T(128)S(1)} %pad_add_fusion.pos, s32[48]{0:T(128)S(1)} %reshape.21.partners, bf16[9,128,1024]{2,1,0:T(8,128)(2,1)S(1)} %project.1.refs_0_, bf16[1024,128]{1,0:T(8,128)(2,1)S(1)} %get-tuple-element.76.refs_1_.refs_6_, ...), custom_call_target="tpu_custom_call" | custom-call | tf_op jit(solution)/shard_map/couple/pallas_call | solution.py:247
  72.2 3.3 %project_last.1.refs_5_ = bf16[3,128,1024]{2,1,0:T(8,128)(2,1)S(1)} custom-call(s32[2]{0:T(128)S(1)} %pad_add_fusion.pos, s32[288]{0:T(512)S(1)} %reshape.19.cols, s32[96]{0:T(128)S(1)} %reshape.20.counts, bf16[3,32,3,128,128]{4,3,2,1,0:T(8,128)(2,1)} %potential.3, bf16[1024,128]{1,0:T(8,128)(2,1)S(1)} %collective-permute-done.7.refs_4_.refs_0_.refs_9_, ...), custom_call_target="tpu_custom_call" | custom-call | tf_op jit(solution)/shard_map/project_last/pallas_call | solution.py:160
  75.5 1.0 %collective-permute-done.17.refs_3_.refs_19_ = bf16[1024,128]{1,0:T(8,128)(2,1)S(1)} collective-permute-done((bf16[1024,128]{1,0:T(8,128)(2,1)S(1)}, bf16[1024,128]{1,0:T(8,128)(2,1)S(1)}, u32[]{:S(2)}, u32[]{:S(2)}) %collective-permute-start.17) | collective-permute-done | bytes 262176 | tf_op jit(solution)/shard_map/ppermute | solution.py:275
  76.4 2.4 %couple_last.1 = f32[2,12,64,128]{3,2,1,0:T(8,128)S(1)} custom-call(s32[2]{0:T(128)S(1)} %pad_add_fusion.pos, s32[48]{0:T(128)S(1)} %reshape.21.partners, bf16[9,128,1024]{2,1,0:T(8,128)(2,1)S(1)} %project.1.refs_0_, bf16[1024,128]{1,0:T(8,128)(2,1)S(1)} %collective-permute-done.9.refs_1_.refs_17_, ...), custom_call_target="tpu_custom_call" | custom-call | tf_op jit(solution)/shard_map/couple_last/pallas_call | solution.py:247
  79.0 1.7 %collective-permute-done.21 = f32[12,64,128]{2,1,0:T(8,128)S(1)} collective-permute-done((f32[12,64,128]{2,1,0:T(8,128)S(1)}, f32[12,64,128]{2,1,0:T(8,128)S(1)}, u32[]{:S(2)}, u32[]{:S(2)}) %collective-permute-start.21) | collective-permute-done | bytes 393248 | tf_op jit(solution)/shard_map/ppermute | solution.py:278
  81.3 2.3 %collective-permute-start.23 = (bf16[3,64,128]{2,1,0:T(8,128)(2,1)S(1)}, bf16[3,64,128]{2,1,0:T(8,128)(2,1)S(1)}, u32[]{:S(2)}, u32[]{:S(2)}) collective-permute-start(bf16[3,64,128]{2,1,0:T(8,128)(2,1)S(1)} %get-tuple-element.79), channel_id=1, source_target_pairs={{0,8},{2,10},{4,12},{6,14},{8,0},{10,2},{12,4},{14,6},{16,24},{18,... | collective-permute-start | bytes 147464 | tf_op jit(solution)/shard_map/ppermute | solution.py:275
  83.5 0.8 collective-permute-start.22
  84.3 1.8 %collective-permute-done.24 = bf16[3,64,128]{2,1,0:T(8,128)(2,1)S(1)} collective-permute-done((bf16[3,64,128]{2,1,0:T(8,128)(2,1)S(1)}, bf16[3,64,128]{2,1,0:T(8,128)(2,1)S(1)}, u32[]{:S(2)}, u32[]{:S(2)}) %collective-permute-start.24) | collective-permute-done | bytes 49184 | tf_op jit(solution)/shard_map/ppermute | solution.py:275
  86.3 1.3 %collective-permute-done.22 = bf16[3,64,128]{2,1,0:T(8,128)(2,1)S(1)} collective-permute-done((bf16[3,64,128]{2,1,0:T(8,128)(2,1)S(1)}, bf16[3,64,128]{2,1,0:T(8,128)(2,1)S(1)}, u32[]{:S(2)}, u32[]{:S(2)}) %collective-permute-start.22) | collective-permute-done | bytes 49184 | tf_op jit(solution)/shard_map/ppermute | solution.py:275
  87.6 0.7 fusion.5
  (53 shorter events, 4.3 us)
Async XLA Ops:
  1.3 4.1 %copy-start.2 = (s32[3,32,3]{1,2,0:T(4,128)S(1)}, s32[3,32,3]{1,2,0:T(4,128)}, u32[]{:S(2)}) copy-start(s32[3,32,3]{1,2,0:T(4,128)} %param.8) | copy-start | bytes 3460
  1.3 4.3 %copy-start.3 = (s32[3,32]{1,0:T(4,128)S(1)}, s32[3,32]{1,0:T(4,128)}, u32[]{:S(2)}) copy-start(s32[3,32]{1,0:T(4,128)} %param.9) | copy-start | bytes 1156
  1.4 4.4 %copy-start.4 = (s32[3,16]{1,0:T(4,128)S(1)}, s32[3,16]{1,0:T(4,128)}, u32[]{:S(2)}) copy-start(s32[3,16]{1,0:T(4,128)} %param.10) | copy-start | bytes 580
  1.4 9.4 %collective-permute-start.1 = (bf16[1024,128]{1,0:T(8,128)(2,1)S(1)}, bf16[1024,128]{1,0:T(8,128)(2,1)S(1)}, u32[]{:S(2)}, u32[]{:S(2)}) collective-permute-start(bf16[1024,128]{1,0:T(8,128)(2,1)S(1)} %get-tuple-element.76.refs_1_.refs_6_), channel_id=1, source_target_pairs={{0,4},{2,6},{4,0},{6,2},{8,12},{10,14},{12,8},{14,10},{16,20},{18,... | collective-permute-start | bytes 786440 | tf_op jit(solution)/shard_map/ppermute | solution.py:275
  3.0 14.3 %collective-permute-start.4 = (bf16[1024,128]{1,0:T(8,128)(2,1)S(1)}, bf16[1024,128]{1,0:T(8,128)(2,1)S(1)}, u32[]{:S(2)}, u32[]{:S(2)}) collective-permute-start(bf16[1024,128]{1,0:T(8,128)(2,1)S(1)} %get-tuple-element.76.refs_1_.refs_6_), channel_id=1, source_target_pairs={{0,16},{2,18},{4,20},{6,22},{8,24},{10,26},{12,28},{14,30},{16,0},... | collective-permute-start | bytes 786440 | tf_op jit(solution)/shard_map/ppermute | solution.py:275
  3.3 7.5 %collective-permute-start = (bf16[1024,128]{1,0:T(8,128)(2,1)S(1)}, bf16[1024,128]{1,0:T(8,128)(2,1)S(1)}, u32[]{:S(2)}, u32[]{:S(2)}) collective-permute-start(bf16[1024,128]{1,0:T(8,128)(2,1)S(1)} %get-tuple-element.73), channel_id=1, source_target_pairs={{0,2},{2,0},{4,6},{6,4},{8,10},{10,8},{12,14},{14,12},{16,18},{18,... | collective-permute-start | bytes 786440 | tf_op jit(solution)/shard_map/ppermute | solution.py:275
  4.8 20.8 %collective-permute-start.3 = (bf16[2048,128]{1,0:T(8,128)(2,1)S(1)}, bf16[2048,128]{1,0:T(8,128)(2,1)S(1)}, u32[]{:S(2)}, u32[]{:S(2)}) collective-permute-start(bf16[2048,128]{1,0:T(8,128)(2,1)S(1)} %pad_maximum_fusion.2), channel_id=1, source_target_pairs={{0,8},{2,10},{4,12},{6,14},{8,0},{10,2},{12,4},{14,6},{16,24},{18,... | collective-permute-start | bytes 1572872 | tf_op jit(solution)/shard_map/ppermute | solution.py:275
  5.9 40.5 %copy-start = (bf16[1,4096,128]{2,1,0:T(8,128)(2,1)S(1)}, bf16[1,4096,128]{2,1,0:T(8,128)(2,1)}, u32[]{:S(2)}) copy-start(bf16[1,4096,128]{2,1,0:T(8,128)(2,1)} %param.6) | copy-start | bytes 3145732
  10.8 35.6 %collective-permute-start.2 = (bf16[3072,128]{1,0:T(8,128)(2,1)S(1)}, bf16[3072,128]{1,0:T(8,128)(2,1)S(1)}, u32[]{:S(2)}, u32[]{:S(2)}) collective-permute-start(bf16[3072,128]{1,0:T(8,128)(2,1)S(1)} %pad_maximum_fusion), channel_id=1, source_target_pairs={{0,2},{2,0},{4,6},{6,4},{8,10},{10,8},{12,14},{14,12},{16,18},{18,... | collective-permute-start | bytes 2359304 | tf_op jit(solution)/shard_map/ppermute | solution.py:275
  17.2 14.8 %collective-permute-start.10 = (bf16[1024,128]{1,0:T(8,128)(2,1)S(1)}, bf16[1024,128]{1,0:T(8,128)(2,1)S(1)}, u32[]{:S(2)}, u32[]{:S(2)}) collective-permute-start(bf16[1024,128]{1,0:T(8,128)(2,1)S(1)} %collective-permute-done.refs_0_.refs_1_.refs_2_.refs_7_), channel_id=1, source_target_pairs={{0,16},{2,18},{4,20},{6,22},{8,24},{10,26},{12,28},{14,30},{16,0},... | collective-permute-start | bytes 786440 | tf_op jit(solution)/shard_map/ppermute | solution.py:275
  17.2 15.3 %collective-permute-start.9 = (bf16[1024,128]{1,0:T(8,128)(2,1)S(1)}, bf16[1024,128]{1,0:T(8,128)(2,1)S(1)}, u32[]{:S(2)}, u32[]{:S(2)}) collective-permute-start(bf16[1024,128]{1,0:T(8,128)(2,1)S(1)} %collective-permute-done.4.refs_8_.refs_13_), channel_id=1, source_target_pairs={{0,4},{2,6},{4,0},{6,2},{8,12},{10,14},{12,8},{14,10},{16,20},{18,... | collective-permute-start | bytes 786440 | tf_op jit(solution)/shard_map/ppermute | solution.py:275
  25.7 20.7 %collective-permute-start.5 = (bf16[2048,128]{1,0:T(8,128)(2,1)S(1)}, bf16[2048,128]{1,0:T(8,128)(2,1)S(1)}, u32[]{:S(2)}, u32[]{:S(2)}) collective-permute-start(bf16[2048,128]{1,0:T(8,128)(2,1)S(1)} %pad_maximum_fusion.1), channel_id=1, source_target_pairs={{0,8},{2,10},{4,12},{6,14},{8,0},{10,2},{12,4},{14,6},{16,24},{18,... | collective-permute-start | bytes 1572872 | tf_op jit(solution)/shard_map/ppermute | solution.py:275
  25.7 8.5 %collective-permute-start.7 = (bf16[1024,128]{1,0:T(8,128)(2,1)S(1)}, bf16[1024,128]{1,0:T(8,128)(2,1)S(1)}, u32[]{:S(2)}, u32[]{:S(2)}) collective-permute-start(bf16[1024,128]{1,0:T(8,128)(2,1)S(1)} %stitch.8), channel_id=1, source_target_pairs={{0,2},{2,0},{4,6},{6,4},{8,10},{10,8},{12,14},{14,12},{16,18},{18,... | collective-permute-start | bytes 786440 | tf_op jit(solution)/shard_map/ppermute | solution.py:275
  32.0 14.9 %collective-permute-start.8 = (bf16[2048,128]{1,0:T(8,128)(2,1)S(1)}, bf16[2048,128]{1,0:T(8,128)(2,1)S(1)}, u32[]{:S(2)}, u32[]{:S(2)}) collective-permute-start(bf16[2048,128]{1,0:T(8,128)(2,1)S(1)} %stitch.9), channel_id=1, source_target_pairs={{0,4},{2,6},{4,0},{6,2},{8,12},{10,14},{12,8},{14,10},{16,20},{18,... | collective-permute-start | bytes 1572872 | tf_op jit(solution)/shard_map/ppermute | solution.py:275
  32.6 13.8 %collective-permute-start.11 = (bf16[1024,128]{1,0:T(8,128)(2,1)S(1)}, bf16[1024,128]{1,0:T(8,128)(2,1)S(1)}, u32[]{:S(2)}, u32[]{:S(2)}) collective-permute-start(bf16[1024,128]{1,0:T(8,128)(2,1)S(1)} %stitch.10), channel_id=1, source_target_pairs={{0,16},{2,18},{4,20},{6,22},{8,24},{10,26},{12,28},{14,30},{16,0},... | collective-permute-start | bytes 786440 | tf_op jit(solution)/shard_map/ppermute | solution.py:275
  34.2 16.5 %collective-permute-start.12 = (bf16[1024,128]{1,0:T(8,128)(2,1)S(1)}, bf16[1024,128]{1,0:T(8,128)(2,1)S(1)}, u32[]{:S(2)}, u32[]{:S(2)}) collective-permute-start(bf16[1024,128]{1,0:T(8,128)(2,1)S(1)} %collective-permute-done.7.refs_4_.refs_0_.refs_9_), channel_id=1, source_target_pairs={{0,4},{2,6},{4,0},{6,2},{8,12},{10,14},{12,8},{14,10},{16,20},{18,... | collective-permute-start | bytes 786440 | tf_op jit(solution)/shard_map/ppermute | solution.py:275
  46.4 7.4 %collective-permute-start.6 = (bf16[4096,128]{1,0:T(8,128)(2,1)S(1)}, bf16[4096,128]{1,0:T(8,128)(2,1)S(1)}, u32[]{:S(2)}, u32[]{:S(2)}) collective-permute-start(bf16[4096,128]{1,0:T(8,128)(2,1)S(1)} %bitcast.22), channel_id=1, source_target_pairs={{0,1},{1,0},{2,3},{3,2},{4,5},{5,4},{6,7},{7,6},{8,9},{9,8},{10,11... | collective-permute-start | bytes 3145736 | tf_op jit(solution)/shard_map/ppermute | solution.py:278
  50.8 3.0 %collective-permute-start.13 = (bf16[4096,128]{1,0:T(8,128)(2,1)S(1)}, bf16[4096,128]{1,0:T(8,128)(2,1)S(1)}, u32[]{:S(2)}, u32[]{:S(2)}) collective-permute-start(bf16[4096,128]{1,0:T(8,128)(2,1)S(1)} %stitch.11), channel_id=1, source_target_pairs={{0,1},{1,0},{2,3},{3,2},{4,5},{5,4},{6,7},{7,6},{8,9},{9,8},{10,11... | collective-permute-start | bytes 3145736 | tf_op jit(solution)/shard_map/ppermute | solution.py:278
  51.0 4.0 %collective-permute-start.14 = (bf16[4096,128]{1,0:T(8,128)(2,1)S(1)}, bf16[4096,128]{1,0:T(8,128)(2,1)S(1)}, u32[]{:S(2)}, u32[]{:S(2)}) collective-permute-start(bf16[4096,128]{1,0:T(8,128)(2,1)S(1)} %stitch.12), channel_id=1, source_target_pairs={{0,1},{1,0},{2,3},{3,2},{4,5},{5,4},{6,7},{7,6},{8,9},{9,8},{10,11... | collective-permute-start | bytes 3145736 | tf_op jit(solution)/shard_map/ppermute | solution.py:278
  51.6 15.9 %collective-permute-start.15 = (bf16[2048,128]{1,0:T(8,128)(2,1)S(1)}, bf16[2048,128]{1,0:T(8,128)(2,1)S(1)}, u32[]{:S(2)}, u32[]{:S(2)}) collective-permute-start(bf16[2048,128]{1,0:T(8,128)(2,1)S(1)} %stitch.13), channel_id=1, source_target_pairs={{0,4},{2,6},{4,0},{6,2},{8,12},{10,14},{12,8},{14,10},{16,20},{18,... | collective-permute-start | bytes 1572872 | tf_op jit(solution)/shard_map/ppermute | solution.py:275
  52.2 15.3 %collective-permute-start.18 = (bf16[2048,128]{1,0:T(8,128)(2,1)S(1)}, bf16[2048,128]{1,0:T(8,128)(2,1)S(1)}, u32[]{:S(2)}, u32[]{:S(2)}) collective-permute-start(bf16[2048,128]{1,0:T(8,128)(2,1)S(1)} %collective-permute-done.5.refs_2_.refs_3_.refs_4_), channel_id=1, source_target_pairs={{0,2},{2,0},{4,6},{6,4},{8,10},{10,8},{12,14},{14,12},{16,18},{18,... | collective-permute-start | bytes 1572872 | tf_op jit(solution)/shard_map/ppermute | solution.py:275
  53.8 10.2 %collective-permute-start.16 = (bf16[1024,128]{1,0:T(8,128)(2,1)S(1)}, bf16[1024,128]{1,0:T(8,128)(2,1)S(1)}, u32[]{:S(2)}, u32[]{:S(2)}) collective-permute-start(bf16[1024,128]{1,0:T(8,128)(2,1)S(1)} %collective-permute-done.7.refs_4_.refs_0_.refs_9_), channel_id=1, source_target_pairs={{0,16},{2,18},{4,20},{6,22},{8,24},{10,26},{12,28},{14,30},{16,0},... | collective-permute-start | bytes 786440 | tf_op jit(solution)/shard_map/ppermute | solution.py:275
  53.8 13.7 %collective-permute-start.19 = (bf16[1024,128]{1,0:T(8,128)(2,1)S(1)}, bf16[1024,128]{1,0:T(8,128)(2,1)S(1)}, u32[]{:S(2)}, u32[]{:S(2)}) collective-permute-start(bf16[1024,128]{1,0:T(8,128)(2,1)S(1)} %stitch.14), channel_id=1, source_target_pairs={{0,8},{2,10},{4,12},{6,14},{8,0},{10,2},{12,4},{14,6},{16,24},{18,... | collective-permute-start | bytes 786440 | tf_op jit(solution)/shard_map/ppermute | solution.py:275
  67.6 4.5 %collective-permute-start.20 = (bf16[4096,128]{1,0:T(8,128)(2,1)S(1)}, bf16[4096,128]{1,0:T(8,128)(2,1)S(1)}, u32[]{:S(2)}, u32[]{:S(2)}) collective-permute-start(bf16[4096,128]{1,0:T(8,128)(2,1)S(1)} %stitch.15), channel_id=1, source_target_pairs={{0,1},{1,0},{2,3},{3,2},{4,5},{5,4},{6,7},{7,6},{8,9},{9,8},{10,11... | collective-permute-start | bytes 3145736 | tf_op jit(solution)/shard_map/ppermute | solution.py:278
  67.7 8.7 %collective-permute-start.17 = (bf16[1024,128]{1,0:T(8,128)(2,1)S(1)}, bf16[1024,128]{1,0:T(8,128)(2,1)S(1)}, u32[]{:S(2)}, u32[]{:S(2)}) collective-permute-start(bf16[1024,128]{1,0:T(8,128)(2,1)S(1)} %collective-permute-done.16.refs_11_.refs_16_), channel_id=1, source_target_pairs={{0,4},{2,6},{4,0},{6,2},{8,12},{10,14},{12,8},{14,10},{16,20},{18,... | collective-permute-start | bytes 786440 | tf_op jit(solution)/shard_map/ppermute | solution.py:275
  78.9 8.8 %copy-start.1 = (f32[3,1,64,128]{3,2,1,0:T(8,128)S(1)}, f32[3,1,64,128]{3,2,1,0:T(8,128)}, u32[]{:S(2)}) copy-start(f32[3,1,64,128]{3,2,1,0:T(8,128)} %param.11) | copy-start | bytes 294916
  78.9 1.8 %collective-permute-start.21 = (f32[12,64,128]{2,1,0:T(8,128)S(1)}, f32[12,64,128]{2,1,0:T(8,128)S(1)}, u32[]{:S(2)}, u32[]{:S(2)}) collective-permute-start(f32[12,64,128]{2,1,0:T(8,128)S(1)} %slice_bitcast_fusion), channel_id=1, source_target_pairs={{0,1},{1,0},{2,3},{3,2},{4,5},{5,4},{6,7},{7,6},{8,9},{9,8},{10,11... | collective-permute-start | bytes 1179656 | tf_op jit(solution)/shard_map/ppermute | solution.py:278
  80.8 5.4 %collective-permute-start.24 = (bf16[3,64,128]{2,1,0:T(8,128)(2,1)S(1)}, bf16[3,64,128]{2,1,0:T(8,128)(2,1)S(1)}, u32[]{:S(2)}, u32[]{:S(2)}) collective-permute-start(bf16[3,64,128]{2,1,0:T(8,128)(2,1)S(1)} %get-tuple-element.78), channel_id=1, source_target_pairs={{0,10},{2,8},{4,14},{6,12},{8,2},{10,0},{12,6},{14,4},{16,26},{18,... | collective-permute-start | bytes 147464 | tf_op jit(solution)/shard_map/ppermute | solution.py:275
  81.3 5.1 %collective-permute-start.23 = (bf16[3,64,128]{2,1,0:T(8,128)(2,1)S(1)}, bf16[3,64,128]{2,1,0:T(8,128)(2,1)S(1)}, u32[]{:S(2)}, u32[]{:S(2)}) collective-permute-start(bf16[3,64,128]{2,1,0:T(8,128)(2,1)S(1)} %get-tuple-element.79), channel_id=1, source_target_pairs={{0,8},{2,10},{4,12},{6,14},{8,0},{10,2},{12,4},{14,6},{16,24},{18,... | collective-permute-start | bytes 147464 | tf_op jit(solution)/shard_map/ppermute | solution.py:275
  83.5 4.1 %collective-permute-start.22 = (bf16[3,64,128]{2,1,0:T(8,128)(2,1)S(1)}, bf16[3,64,128]{2,1,0:T(8,128)(2,1)S(1)}, u32[]{:S(2)}, u32[]{:S(2)}) collective-permute-start(bf16[3,64,128]{2,1,0:T(8,128)(2,1)S(1)} %get-tuple-element.77), channel_id=1, source_target_pairs={{0,2},{2,0},{4,6},{6,4},{8,10},{10,8},{12,14},{14,12},{16,18},{18,... | collective-permute-start | bytes 147464 | tf_op jit(solution)/shard_map/ppermute | solution.py:275

commit v13 on v12

--- a/solution.py
+++ b/solution.py
@@ -471,10 +471,11 @@
         for shift in range(1, halves):
             summed = summed + rotate(total[shift], shift)
         summed = summed.reshape((group, modes) + summed.shape[1:])
+        for i in reversed(range(len(inside))):
+            kept = 1 << i
+            away = swap(summed[kept:].astype(jnp.bfloat16), 1 << inside[i])
+            summed = summed[:kept] + away.astype(jnp.float32)
         result = summed[0]
-        sent = summed.astype(jnp.bfloat16)
-        for point in range(1, group):
-            result = result + swap(sent[point], spread(point, inside)).astype(jnp.float32)
         return result[:, None] / gaps
 
     return jax.shard_map(

time: 88.9 us -> 90.9 us (1.022)
  the two profiles are of different devices: /device:TPU:24 before, /device:TPU:0 now
where the time goes in v13:
time: 90.9 us; the launch traced here: 89.5 us
  waiting for transfers between devices  43.6 us (48%)
  starting transfers between devices  28.9 us (32%)
  Pallas kernels  14 us (15%)
  local copies, waits for them, and re-layouts  1.79 us (2%)
  other arithmetic  0.94 us (1%)
    ppermute x19, waiting for transfers between devices, swap(): return lax.ppermute(value, 'ka', [(i, i ^ mask) for i in range(points)])  41.9 us
    ppermute x19, starting transfers between devices, swap(): return lax.ppermute(value, 'ka', [(i, i ^ mask) for i in range(points)])  28.2 us
    pallas_call x2, Pallas kernels, project(): pl.pallas_call(functools.partial(project_kernel, orders, inside, halves),...  7.89 us
    pallas_call x2, Pallas kernels, couple(): pl.pallas_call(functools.partial(couple_kernel, jobs, last, inside, outsi...  5.57 us
  transfers between devices with their start and end apart: 24, of which 13 were waited for; matrix products, arithmetic and copies ran while one was open for 1% of the time, Pallas kernels for 13%

profile of v13, /device:TPU:0, one launch (start us, length us, event | category | flops | bytes accessed | tf_op | source)
XLA Modules:
  0.0 89.5 jit_solution(8991801732181871663)
XLA Ops:
  0.1 1.3 %constant_dynamic-slice_fusion = (bf16[1024,128]{1,0:T(8,128)(2,1)S(1)}, bf16[1024,128]{1,0:T(8,128)(2,1)S(1)}, bf16[1024,128]{1,0:T(8,128)(2,1)S(1)}, bf16[1024,128]{1,0:T(8,128)(2,1)S(1)}) fusion(bf16[4096,128]{1,0:T(8,128)(2,1)} %bitcast.15, s32[]{:T(128)S(6)} %select_n.15, s32[]{:T(128)S(6)} %select_n.14, s32[]{:T(128)S(6)} %select_n.13, s32[]{:T(128)S(6)} %select_n.12), kind=kLoop, calls=%fused_computation.12 | loop fusion | bytes 2097168 | tf_op jit(solution)/shard_map/dynamic_slice | solution.py:306
  1.4 3.0 %collective-permute-start.1 = (bf16[1024,128]{1,0:T(8,128)(2,1)S(1)}, bf16[1024,128]{1,0:T(8,128)(2,1)S(1)}, u32[]{:S(2)}, u32[]{:S(2)}) collective-permute-start(bf16[1024,128]{1,0:T(8,128)(2,1)S(1)} %get-tuple-element.74.refs_1_.refs_6_), channel_id=1, source_target_pairs={{0,4},{2,6},{4,0},{6,2},{8,12},{10,14},{12,8},{14,10},{16,20},{18,... | collective-permute-start | bytes 786440 | tf_op jit(solution)/shard_map/ppermute | solution.py:275
  4.4 2.6 %collective-permute-start.4 = (bf16[1024,128]{1,0:T(8,128)(2,1)S(1)}, bf16[1024,128]{1,0:T(8,128)(2,1)S(1)}, u32[]{:S(2)}, u32[]{:S(2)}) collective-permute-start(bf16[1024,128]{1,0:T(8,128)(2,1)S(1)} %get-tuple-element.74.refs_1_.refs_6_), channel_id=1, source_target_pairs={{0,16},{2,18},{4,20},{6,22},{8,24},{10,26},{12,28},{14,30},{16,0},... | collective-permute-start | bytes 786440 | tf_op jit(solution)/shard_map/ppermute | solution.py:275
  7.0 1.5 %collective-permute-start = (bf16[1024,128]{1,0:T(8,128)(2,1)S(1)}, bf16[1024,128]{1,0:T(8,128)(2,1)S(1)}, u32[]{:S(2)}, u32[]{:S(2)}) collective-permute-start(bf16[1024,128]{1,0:T(8,128)(2,1)S(1)} %get-tuple-element.71), channel_id=1, source_target_pairs={{0,2},{2,0},{4,6},{6,4},{8,10},{10,8},{12,14},{14,12},{16,18},{18,... | collective-permute-start | bytes 786440 | tf_op jit(solution)/shard_map/ppermute | solution.py:275
  8.5 1.6 %collective-permute-start.3 = (bf16[2048,128]{1,0:T(8,128)(2,1)S(1)}, bf16[2048,128]{1,0:T(8,128)(2,1)S(1)}, u32[]{:S(2)}, u32[]{:S(2)}) collective-permute-start(bf16[2048,128]{1,0:T(8,128)(2,1)S(1)} %pad_maximum_fusion.2), channel_id=1, source_target_pairs={{0,8},{2,10},{4,12},{6,14},{8,0},{10,2},{12,4},{14,6},{16,24},{18,... | collective-permute-start | bytes 1572872 | tf_op jit(solution)/shard_map/ppermute | solution.py:275
  10.7 3.7 %collective-permute-done.refs_0_.refs_1_.refs_2_.refs_7_ = bf16[1024,128]{1,0:T(8,128)(2,1)S(1)} collective-permute-done((bf16[1024,128]{1,0:T(8,128)(2,1)S(1)}, bf16[1024,128]{1,0:T(8,128)(2,1)S(1)}, u32[]{:S(2)}, u32[]{:S(2)}) %collective-permute-start) | collective-permute-done | bytes 262176 | tf_op jit(solution)/shard_map/ppermute | solution.py:275
  14.5 1.5 %collective-permute-start.2 = (bf16[3072,128]{1,0:T(8,128)(2,1)S(1)}, bf16[3072,128]{1,0:T(8,128)(2,1)S(1)}, u32[]{:S(2)}, u32[]{:S(2)}) collective-permute-start(bf16[3072,128]{1,0:T(8,128)(2,1)S(1)} %pad_maximum_fusion), channel_id=1, source_target_pairs={{0,2},{2,0},{4,6},{6,4},{8,10},{10,8},{12,14},{14,12},{16,18},{18,... | collective-permute-start | bytes 2359304 | tf_op jit(solution)/shard_map/ppermute | solution.py:275
  16.0 2.8 %collective-permute-done.4.refs_8_.refs_13_ = bf16[1024,128]{1,0:T(8,128)(2,1)S(1)} collective-permute-done((bf16[1024,128]{1,0:T(8,128)(2,1)S(1)}, bf16[1024,128]{1,0:T(8,128)(2,1)S(1)}, u32[]{:S(2)}, u32[]{:S(2)}) %collective-permute-start.4) | collective-permute-done | bytes 262176 | tf_op jit(solution)/shard_map/ppermute | solution.py:275
  19.3 11.4 %collective-permute-done.3.refs_0_.refs_1_.refs_3_.refs_8_ = bf16[2048,128]{1,0:T(8,128)(2,1)S(1)} collective-permute-done((bf16[2048,128]{1,0:T(8,128)(2,1)S(1)}, bf16[2048,128]{1,0:T(8,128)(2,1)S(1)}, u32[]{:S(2)}, u32[]{:S(2)}) %collective-permute-start.3) | collective-permute-done | bytes 524320 | tf_op jit(solution)/shard_map/ppermute | solution.py:275
  30.9 1.6 %collective-permute-done.10.refs_0_.refs_9_.refs_14_ = bf16[1024,128]{1,0:T(8,128)(2,1)S(1)} collective-permute-done((bf16[1024,128]{1,0:T(8,128)(2,1)S(1)}, bf16[1024,128]{1,0:T(8,128)(2,1)S(1)}, u32[]{:S(2)}, u32[]{:S(2)}) %collective-permute-start.10) | collective-permute-done | bytes 262176 | tf_op jit(solution)/shard_map/ppermute | solution.py:275
  33.0 0.8 collective-permute-start.11
  33.8 4.1 %collective-permute-done.7.refs_4_.refs_0_.refs_9_ = bf16[1024,128]{1,0:T(8,128)(2,1)S(1)} collective-permute-done((bf16[1024,128]{1,0:T(8,128)(2,1)S(1)}, bf16[1024,128]{1,0:T(8,128)(2,1)S(1)}, u32[]{:S(2)}, u32[]{:S(2)}) %collective-permute-start.7) | collective-permute-done | bytes 262176 | tf_op jit(solution)/shard_map/ppermute | solution.py:275
  38.4 7.7 %collective-permute-done.11.refs_1_.refs_10_.refs_15_ = bf16[1024,128]{1,0:T(8,128)(2,1)S(1)} collective-permute-done((bf16[1024,128]{1,0:T(8,128)(2,1)S(1)}, bf16[1024,128]{1,0:T(8,128)(2,1)S(1)}, u32[]{:S(2)}, u32[]{:S(2)}) %collective-permute-start.11) | collective-permute-done | bytes 262176 | tf_op jit(solution)/shard_map/ppermute | solution.py:275
  46.1 2.4 %collective-permute-done.5.refs_2_.refs_3_.refs_4_ = bf16[2048,128]{1,0:T(8,128)(2,1)S(1)} collective-permute-done((bf16[2048,128]{1,0:T(8,128)(2,1)S(1)}, bf16[2048,128]{1,0:T(8,128)(2,1)S(1)}, u32[]{:S(2)}, u32[]{:S(2)}) %collective-permute-start.5) | collective-permute-done | bytes 524320 | tf_op jit(solution)/shard_map/ppermute | solution.py:275
  48.8 0.6 collective-permute-start.14
  50.0 1.2 %collective-permute-start.18 = (bf16[2048,128]{1,0:T(8,128)(2,1)S(1)}, bf16[2048,128]{1,0:T(8,128)(2,1)S(1)}, u32[]{:S(2)}, u32[]{:S(2)}) collective-permute-start(bf16[2048,128]{1,0:T(8,128)(2,1)S(1)} %collective-permute-done.5.refs_2_.refs_3_.refs_4_), channel_id=1, source_target_pairs={{0,2},{2,0},{4,6},{6,4},{8,10},{10,8},{12,14},{14,12},{16,18},{18,... | collective-permute-start | bytes 1572872 | tf_op jit(solution)/shard_map/ppermute | solution.py:275
  51.2 2.6 %collective-permute-start.16 = (bf16[1024,128]{1,0:T(8,128)(2,1)S(1)}, bf16[1024,128]{1,0:T(8,128)(2,1)S(1)}, u32[]{:S(2)}, u32[]{:S(2)}) collective-permute-start(bf16[1024,128]{1,0:T(8,128)(2,1)S(1)} %collective-permute-done.7.refs_4_.refs_0_.refs_9_), channel_id=1, source_target_pairs={{0,16},{2,18},{4,20},{6,22},{8,24},{10,26},{12,28},{14,30},{16,0},... | collective-permute-start | bytes 786440 | tf_op jit(solution)/shard_map/ppermute | solution.py:275
  53.8 5.6 %collective-permute-start.19 = (bf16[1024,128]{1,0:T(8,128)(2,1)S(1)}, bf16[1024,128]{1,0:T(8,128)(2,1)S(1)}, u32[]{:S(2)}, u32[]{:S(2)}) collective-permute-start(bf16[1024,128]{1,0:T(8,128)(2,1)S(1)} %stitch.14), channel_id=1, source_target_pairs={{0,8},{2,10},{4,12},{6,14},{8,0},{10,2},{12,4},{14,6},{16,24},{18,... | collective-permute-start | bytes 786440 | tf_op jit(solution)/shard_map/ppermute | solution.py:275
  59.4 4.6 %project.1.refs_0_ = bf16[9,128,1024]{2,1,0:T(8,128)(2,1)S(1)} custom-call(s32[2]{0:T(128)S(1)} %pad_add_fusion.pos, s32[288]{0:T(512)S(1)} %reshape.13.cols, s32[96]{0:T(128)S(1)} %reshape.14.counts, bf16[3,32,3,128,128]{4,3,2,1,0:T(8,128)(2,1)} %potential.3, bf16[4096,128]{1,0:T(8,128)(2,1)} %bitcast.16, ...), custom_call_target="tpu_custom_call" | custom-call | tf_op jit(solution)/shard_map/project/pallas_call | solution.py:160
  64.0 0.8 collective-permute-done.16.refs_11_.refs_16_
  64.9 0.8 collective-permute-done.19.refs_3_.refs_2_
  65.9 1.6 %collective-permute-start.17 = (bf16[1024,128]{1,0:T(8,128)(2,1)S(1)}, bf16[1024,128]{1,0:T(8,128)(2,1)S(1)}, u32[]{:S(2)}, u32[]{:S(2)}) collective-permute-start(bf16[1024,128]{1,0:T(8,128)(2,1)S(1)} %collective-permute-done.16.refs_11_.refs_16_), channel_id=1, source_target_pairs={{0,4},{2,6},{4,0},{6,2},{8,12},{10,14},{12,8},{14,10},{16,20},{18,... | collective-permute-start | bytes 786440 | tf_op jit(solution)/shard_map/ppermute | solution.py:275
  67.5 3.0 %couple.1.refs_4_ = f32[9,128,128]{2,1,0:T(8,128)S(1)} custom-call(s32[2]{0:T(128)S(1)} %pad_add_fusion.pos, s32[48]{0:T(128)S(1)} %reshape.15.partners, bf16[9,128,1024]{2,1,0:T(8,128)(2,1)S(1)} %project.1.refs_0_, bf16[1024,128]{1,0:T(8,128)(2,1)S(1)} %get-tuple-element.74.refs_1_.refs_6_, ...), custom_call_target="tpu_custom_call" | custom-call | tf_op jit(solution)/shard_map/couple/pallas_call | solution.py:247
  70.4 3.3 %project_last.1.refs_5_ = bf16[3,128,1024]{2,1,0:T(8,128)(2,1)S(1)} custom-call(s32[2]{0:T(128)S(1)} %pad_add_fusion.pos, s32[288]{0:T(512)S(1)} %reshape.13.cols, s32[96]{0:T(128)S(1)} %reshape.14.counts, bf16[3,32,3,128,128]{4,3,2,1,0:T(8,128)(2,1)} %potential.3, bf16[1024,128]{1,0:T(8,128)(2,1)S(1)} %collective-permute-done.7.refs_4_.refs_0_.refs_9_, ...), custom_call_target="tpu_custom_call" | custom-call | tf_op jit(solution)/shard_map/project_last/pallas_call | solution.py:160
  73.8 0.8 collective-permute-done.17.refs_3_.refs_19_
  74.6 2.6 %couple_last.1 = f32[2,12,64,128]{3,2,1,0:T(8,128)S(1)} custom-call(s32[2]{0:T(128)S(1)} %pad_add_fusion.pos, s32[48]{0:T(128)S(1)} %reshape.15.partners, bf16[9,128,1024]{2,1,0:T(8,128)(2,1)S(1)} %project.1.refs_0_, bf16[1024,128]{1,0:T(8,128)(2,1)S(1)} %collective-permute-done.9.refs_1_.refs_17_, ...), custom_call_target="tpu_custom_call" | custom-call | tf_op jit(solution)/shard_map/couple_last/pallas_call | solution.py:247
  77.3 1.7 %collective-permute-done.21 = f32[12,64,128]{2,1,0:T(8,128)S(1)} collective-permute-done((f32[12,64,128]{2,1,0:T(8,128)S(1)}, f32[12,64,128]{2,1,0:T(8,128)S(1)}, u32[]{:S(2)}, u32[]{:S(2)}) %collective-permute-start.21) | collective-permute-done | bytes 393248 | tf_op jit(solution)/shard_map/ppermute | solution.py:278
  79.1 2.4 %collective-permute-start.22 = (bf16[2,3,64,128]{3,2,1,0:T(8,128)(2,1)S(1)}, bf16[2,3,64,128]{3,2,1,0:T(8,128)(2,1)S(1)}, u32[]{:S(2)}, u32[]{:S(2)}) collective-permute-start(bf16[2,3,64,128]{3,2,1,0:T(8,128)(2,1)S(1)} %bitcast.19), channel_id=1, source_target_pairs={{0,8},{2,10},{4,12},{6,14},{8,0},{10,2},{12,4},{14,6},{16,24},{18,... | collective-permute-start | bytes 294920 | tf_op jit(solution)/shard_map/ppermute | solution.py:275
  81.6 3.1 %collective-permute-done.22 = bf16[2,3,64,128]{3,2,1,0:T(8,128)(2,1)S(1)} collective-permute-done((bf16[2,3,64,128]{3,2,1,0:T(8,128)(2,1)S(1)}, bf16[2,3,64,128]{3,2,1,0:T(8,128)(2,1)S(1)}, u32[]{:S(2)}, u32[]{:S(2)}) %collective-permute-start.22) | collective-permute-done | bytes 98336 | tf_op jit(solution)/shard_map/ppermute | solution.py:275
  84.7 1.6 %collective-permute-start.23 = (bf16[1,3,64,128]{3,2,1,0:T(8,128)(2,1)S(1)}, bf16[1,3,64,128]{3,2,1,0:T(8,128)(2,1)S(1)}, u32[]{:S(2)}, u32[]{:S(2)}) collective-permute-start(bf16[1,3,64,128]{3,2,1,0:T(8,128)(2,1)S(1)} %slice.49), channel_id=1, source_target_pairs={{0,2},{2,0},{4,6},{6,4},{8,10},{10,8},{12,14},{14,12},{16,18},{18,... | collective-permute-start | bytes 147464 | tf_op jit(solution)/shard_map/ppermute | solution.py:275
  86.2 2.6 %collective-permute-done.23 = bf16[1,3,64,128]{3,2,1,0:T(8,128)(2,1)S(1)} collective-permute-done((bf16[1,3,64,128]{3,2,1,0:T(8,128)(2,1)S(1)}, bf16[1,3,64,128]{3,2,1,0:T(8,128)(2,1)S(1)}, u32[]{:S(2)}, u32[]{:S(2)}) %collective-permute-start.23) | collective-permute-done | bytes 49184 | tf_op jit(solution)/shard_map/ppermute | solution.py:275
  88.9 0.7 fusion.2
  (54 shorter events, 3.7 us)
Async XLA Ops:
  1.3 8.9 %copy-start.2 = (s32[3,32,3]{1,2,0:T(4,128)S(1)}, s32[3,32,3]{1,2,0:T(4,128)}, u32[]{:S(2)}) copy-start(s32[3,32,3]{1,2,0:T(4,128)} %param.8) | copy-start | bytes 3460
  1.3 9.2 %copy-start.3 = (s32[3,32]{1,0:T(4,128)S(1)}, s32[3,32]{1,0:T(4,128)}, u32[]{:S(2)}) copy-start(s32[3,32]{1,0:T(4,128)} %param.9) | copy-start | bytes 1156
  1.4 9.2 %copy-start.4 = (s32[3,16]{1,0:T(4,128)S(1)}, s32[3,16]{1,0:T(4,128)}, u32[]{:S(2)}) copy-start(s32[3,16]{1,0:T(4,128)} %param.10) | copy-start | bytes 580
  1.4 13.1 %collective-permute-start.1 = (bf16[1024,128]{1,0:T(8,128)(2,1)S(1)}, bf16[1024,128]{1,0:T(8,128)(2,1)S(1)}, u32[]{:S(2)}, u32[]{:S(2)}) collective-permute-start(bf16[1024,128]{1,0:T(8,128)(2,1)S(1)} %get-tuple-element.74.refs_1_.refs_6_), channel_id=1, source_target_pairs={{0,4},{2,6},{4,0},{6,2},{8,12},{10,14},{12,8},{14,10},{16,20},{18,... | collective-permute-start | bytes 786440 | tf_op jit(solution)/shard_map/ppermute | solution.py:275
  4.4 14.4 %collective-permute-start.4 = (bf16[1024,128]{1,0:T(8,128)(2,1)S(1)}, bf16[1024,128]{1,0:T(8,128)(2,1)S(1)}, u32[]{:S(2)}, u32[]{:S(2)}) collective-permute-start(bf16[1024,128]{1,0:T(8,128)(2,1)S(1)} %get-tuple-element.74.refs_1_.refs_6_), channel_id=1, source_target_pairs={{0,16},{2,18},{4,20},{6,22},{8,24},{10,26},{12,28},{14,30},{16,0},... | collective-permute-start | bytes 786440 | tf_op jit(solution)/shard_map/ppermute | solution.py:275
  7.0 7.5 %collective-permute-start = (bf16[1024,128]{1,0:T(8,128)(2,1)S(1)}, bf16[1024,128]{1,0:T(8,128)(2,1)S(1)}, u32[]{:S(2)}, u32[]{:S(2)}) collective-permute-start(bf16[1024,128]{1,0:T(8,128)(2,1)S(1)} %get-tuple-element.71), channel_id=1, source_target_pairs={{0,2},{2,0},{4,6},{6,4},{8,10},{10,8},{12,14},{14,12},{16,18},{18,... | collective-permute-start | bytes 786440 | tf_op jit(solution)/shard_map/ppermute | solution.py:275
  8.5 22.1 %collective-permute-start.3 = (bf16[2048,128]{1,0:T(8,128)(2,1)S(1)}, bf16[2048,128]{1,0:T(8,128)(2,1)S(1)}, u32[]{:S(2)}, u32[]{:S(2)}) collective-permute-start(bf16[2048,128]{1,0:T(8,128)(2,1)S(1)} %pad_maximum_fusion.2), channel_id=1, source_target_pairs={{0,8},{2,10},{4,12},{6,14},{8,0},{10,2},{12,4},{14,6},{16,24},{18,... | collective-permute-start | bytes 1572872 | tf_op jit(solution)/shard_map/ppermute | solution.py:275
  10.7 35.4 %copy-start = (bf16[1,4096,128]{2,1,0:T(8,128)(2,1)S(1)}, bf16[1,4096,128]{2,1,0:T(8,128)(2,1)}, u32[]{:S(2)}) copy-start(bf16[1,4096,128]{2,1,0:T(8,128)(2,1)} %param.6) | copy-start | bytes 3145732
  14.5 31.6 %collective-permute-start.2 = (bf16[3072,128]{1,0:T(8,128)(2,1)S(1)}, bf16[3072,128]{1,0:T(8,128)(2,1)S(1)}, u32[]{:S(2)}, u32[]{:S(2)}) collective-permute-start(bf16[3072,128]{1,0:T(8,128)(2,1)S(1)} %pad_maximum_fusion), channel_id=1, source_target_pairs={{0,2},{2,0},{4,6},{6,4},{8,10},{10,8},{12,14},{14,12},{16,18},{18,... | collective-permute-start | bytes 2359304 | tf_op jit(solution)/shard_map/ppermute | solution.py:275
  18.8 13.7 %collective-permute-start.10 = (bf16[1024,128]{1,0:T(8,128)(2,1)S(1)}, bf16[1024,128]{1,0:T(8,128)(2,1)S(1)}, u32[]{:S(2)}, u32[]{:S(2)}) collective-permute-start(bf16[1024,128]{1,0:T(8,128)(2,1)S(1)} %collective-permute-done.refs_0_.refs_1_.refs_2_.refs_7_), channel_id=1, source_target_pairs={{0,16},{2,18},{4,20},{6,22},{8,24},{10,26},{12,28},{14,30},{16,0},... | collective-permute-start | bytes 786440 | tf_op jit(solution)/shard_map/ppermute | solution.py:275
  18.8 14.1 %collective-permute-start.9 = (bf16[1024,128]{1,0:T(8,128)(2,1)S(1)}, bf16[1024,128]{1,0:T(8,128)(2,1)S(1)}, u32[]{:S(2)}, u32[]{:S(2)}) collective-permute-start(bf16[1024,128]{1,0:T(8,128)(2,1)S(1)} %collective-permute-done.4.refs_8_.refs_13_), channel_id=1, source_target_pairs={{0,4},{2,6},{4,0},{6,2},{8,12},{10,14},{12,8},{14,10},{16,20},{18,... | collective-permute-start | bytes 786440 | tf_op jit(solution)/shard_map/ppermute | solution.py:275
  30.6 17.9 %collective-permute-start.5 = (bf16[2048,128]{1,0:T(8,128)(2,1)S(1)}, bf16[2048,128]{1,0:T(8,128)(2,1)S(1)}, u32[]{:S(2)}, u32[]{:S(2)}) collective-permute-start(bf16[2048,128]{1,0:T(8,128)(2,1)S(1)} %pad_maximum_fusion.1), channel_id=1, source_target_pairs={{0,8},{2,10},{4,12},{6,14},{8,0},{10,2},{12,4},{14,6},{16,24},{18,... | collective-permute-start | bytes 1572872 | tf_op jit(solution)/shard_map/ppermute | solution.py:275
  30.6 7.2 %collective-permute-start.7 = (bf16[1024,128]{1,0:T(8,128)(2,1)S(1)}, bf16[1024,128]{1,0:T(8,128)(2,1)S(1)}, u32[]{:S(2)}, u32[]{:S(2)}) collective-permute-start(bf16[1024,128]{1,0:T(8,128)(2,1)S(1)} %stitch.8), channel_id=1, source_target_pairs={{0,2},{2,0},{4,6},{6,4},{8,10},{10,8},{12,14},{14,12},{16,18},{18,... | collective-permute-start | bytes 786440 | tf_op jit(solution)/shard_map/ppermute | solution.py:275
  32.5 16.0 %collective-permute-start.8 = (bf16[2048,128]{1,0:T(8,128)(2,1)S(1)}, bf16[2048,128]{1,0:T(8,128)(2,1)S(1)}, u32[]{:S(2)}, u32[]{:S(2)}) collective-permute-start(bf16[2048,128]{1,0:T(8,128)(2,1)S(1)} %stitch.9), channel_id=1, source_target_pairs={{0,4},{2,6},{4,0},{6,2},{8,12},{10,14},{12,8},{14,10},{16,20},{18,... | collective-permute-start | bytes 1572872 | tf_op jit(solution)/shard_map/ppermute | solution.py:275
  33.0 13.2 %collective-permute-start.11 = (bf16[1024,128]{1,0:T(8,128)(2,1)S(1)}, bf16[1024,128]{1,0:T(8,128)(2,1)S(1)}, u32[]{:S(2)}, u32[]{:S(2)}) collective-permute-start(bf16[1024,128]{1,0:T(8,128)(2,1)S(1)} %stitch.10), channel_id=1, source_target_pairs={{0,16},{2,18},{4,20},{6,22},{8,24},{10,26},{12,28},{14,30},{16,0},... | collective-permute-start | bytes 786440 | tf_op jit(solution)/shard_map/ppermute | solution.py:275
  37.9 10.6 %collective-permute-start.12 = (bf16[1024,128]{1,0:T(8,128)(2,1)S(1)}, bf16[1024,128]{1,0:T(8,128)(2,1)S(1)}, u32[]{:S(2)}, u32[]{:S(2)}) collective-permute-start(bf16[1024,128]{1,0:T(8,128)(2,1)S(1)} %collective-permute-done.7.refs_4_.refs_0_.refs_9_), channel_id=1, source_target_pairs={{0,4},{2,6},{4,0},{6,2},{8,12},{10,14},{12,8},{14,10},{16,20},{18,... | collective-permute-start | bytes 786440 | tf_op jit(solution)/shard_map/ppermute | solution.py:275
  46.1 5.1 %collective-permute-start.6 = (bf16[4096,128]{1,0:T(8,128)(2,1)S(1)}, bf16[4096,128]{1,0:T(8,128)(2,1)S(1)}, u32[]{:S(2)}, u32[]{:S(2)}) collective-permute-start(bf16[4096,128]{1,0:T(8,128)(2,1)S(1)} %bitcast.17), channel_id=1, source_target_pairs={{0,1},{1,0},{2,3},{3,2},{4,5},{5,4},{6,7},{7,6},{8,9},{9,8},{10,11... | collective-permute-start | bytes 3145736 | tf_op jit(solution)/shard_map/ppermute | solution.py:278
  48.6 5.2 %collective-permute-start.13 = (bf16[4096,128]{1,0:T(8,128)(2,1)S(1)}, bf16[4096,128]{1,0:T(8,128)(2,1)S(1)}, u32[]{:S(2)}, u32[]{:S(2)}) collective-permute-start(bf16[4096,128]{1,0:T(8,128)(2,1)S(1)} %stitch.11), channel_id=1, source_target_pairs={{0,1},{1,0},{2,3},{3,2},{4,5},{5,4},{6,7},{7,6},{8,9},{9,8},{10,11... | collective-permute-start | bytes 3145736 | tf_op jit(solution)/shard_map/ppermute | solution.py:278
  48.8 10.6 %collective-permute-start.14 = (bf16[4096,128]{1,0:T(8,128)(2,1)S(1)}, bf16[4096,128]{1,0:T(8,128)(2,1)S(1)}, u32[]{:S(2)}, u32[]{:S(2)}) collective-permute-start(bf16[4096,128]{1,0:T(8,128)(2,1)S(1)} %stitch.12), channel_id=1, source_target_pairs={{0,1},{1,0},{2,3},{3,2},{4,5},{5,4},{6,7},{7,6},{8,9},{9,8},{10,11... | collective-permute-start | bytes 3145736 | tf_op jit(solution)/shard_map/ppermute | solution.py:278
  49.5 16.2 %collective-permute-start.15 = (bf16[2048,128]{1,0:T(8,128)(2,1)S(1)}, bf16[2048,128]{1,0:T(8,128)(2,1)S(1)}, u32[]{:S(2)}, u32[]{:S(2)}) collective-permute-start(bf16[2048,128]{1,0:T(8,128)(2,1)S(1)} %stitch.13), channel_id=1, source_target_pairs={{0,4},{2,6},{4,0},{6,2},{8,12},{10,14},{12,8},{14,10},{16,20},{18,... | collective-permute-start | bytes 1572872 | tf_op jit(solution)/shard_map/ppermute | solution.py:275
  50.0 15.7 %collective-permute-start.18 = (bf16[2048,128]{1,0:T(8,128)(2,1)S(1)}, bf16[2048,128]{1,0:T(8,128)(2,1)S(1)}, u32[]{:S(2)}, u32[]{:S(2)}) collective-permute-start(bf16[2048,128]{1,0:T(8,128)(2,1)S(1)} %collective-permute-done.5.refs_2_.refs_3_.refs_4_), channel_id=1, source_target_pairs={{0,2},{2,0},{4,6},{6,4},{8,10},{10,8},{12,14},{14,12},{16,18},{18,... | collective-permute-start | bytes 1572872 | tf_op jit(solution)/shard_map/ppermute | solution.py:275
  51.2 13.7 %collective-permute-start.16 = (bf16[1024,128]{1,0:T(8,128)(2,1)S(1)}, bf16[1024,128]{1,0:T(8,128)(2,1)S(1)}, u32[]{:S(2)}, u32[]{:S(2)}) collective-permute-start(bf16[1024,128]{1,0:T(8,128)(2,1)S(1)} %collective-permute-done.7.refs_4_.refs_0_.refs_9_), channel_id=1, source_target_pairs={{0,16},{2,18},{4,20},{6,22},{8,24},{10,26},{12,28},{14,30},{16,0},... | collective-permute-start | bytes 786440 | tf_op jit(solution)/shard_map/ppermute | solution.py:275
  53.8 11.8 %collective-permute-start.19 = (bf16[1024,128]{1,0:T(8,128)(2,1)S(1)}, bf16[1024,128]{1,0:T(8,128)(2,1)S(1)}, u32[]{:S(2)}, u32[]{:S(2)}) collective-permute-start(bf16[1024,128]{1,0:T(8,128)(2,1)S(1)} %stitch.14), channel_id=1, source_target_pairs={{0,8},{2,10},{4,12},{6,14},{8,0},{10,2},{12,4},{14,6},{16,24},{18,... | collective-permute-start | bytes 786440 | tf_op jit(solution)/shard_map/ppermute | solution.py:275
  65.8 4.7 %collective-permute-start.20 = (bf16[4096,128]{1,0:T(8,128)(2,1)S(1)}, bf16[4096,128]{1,0:T(8,128)(2,1)S(1)}, u32[]{:S(2)}, u32[]{:S(2)}) collective-permute-start(bf16[4096,128]{1,0:T(8,128)(2,1)S(1)} %stitch.15), channel_id=1, source_target_pairs={{0,1},{1,0},{2,3},{3,2},{4,5},{5,4},{6,7},{7,6},{8,9},{9,8},{10,11... | collective-permute-start | bytes 3145736 | tf_op jit(solution)/shard_map/ppermute | solution.py:278
  65.9 8.7 %collective-permute-start.17 = (bf16[1024,128]{1,0:T(8,128)(2,1)S(1)}, bf16[1024,128]{1,0:T(8,128)(2,1)S(1)}, u32[]{:S(2)}, u32[]{:S(2)}) collective-permute-start(bf16[1024,128]{1,0:T(8,128)(2,1)S(1)} %collective-permute-done.16.refs_11_.refs_16_), channel_id=1, source_target_pairs={{0,4},{2,6},{4,0},{6,2},{8,12},{10,14},{12,8},{14,10},{16,20},{18,... | collective-permute-start | bytes 786440 | tf_op jit(solution)/shard_map/ppermute | solution.py:275
  77.2 11.6 %copy-start.1 = (f32[3,1,64,128]{3,2,1,0:T(8,128)S(1)}, f32[3,1,64,128]{3,2,1,0:T(8,128)}, u32[]{:S(2)}) copy-start(f32[3,1,64,128]{3,2,1,0:T(8,128)} %param.11) | copy-start | bytes 294916
  77.3 1.8 %collective-permute-start.21 = (f32[12,64,128]{2,1,0:T(8,128)S(1)}, f32[12,64,128]{2,1,0:T(8,128)S(1)}, u32[]{:S(2)}, u32[]{:S(2)}) collective-permute-start(f32[12,64,128]{2,1,0:T(8,128)S(1)} %slice_bitcast_fusion), channel_id=1, source_target_pairs={{0,1},{1,0},{2,3},{3,2},{4,5},{5,4},{6,7},{7,6},{8,9},{9,8},{10,11... | collective-permute-start | bytes 1179656 | tf_op jit(solution)/shard_map/ppermute | solution.py:278
  79.1 5.5 %collective-permute-start.22 = (bf16[2,3,64,128]{3,2,1,0:T(8,128)(2,1)S(1)}, bf16[2,3,64,128]{3,2,1,0:T(8,128)(2,1)S(1)}, u32[]{:S(2)}, u32[]{:S(2)}) collective-permute-start(bf16[2,3,64,128]{3,2,1,0:T(8,128)(2,1)S(1)} %bitcast.19), channel_id=1, source_target_pairs={{0,8},{2,10},{4,12},{6,14},{8,0},{10,2},{12,4},{14,6},{16,24},{18,... | collective-permute-start | bytes 294920 | tf_op jit(solution)/shard_map/ppermute | solution.py:275
  84.7 4.2 %collective-permute-start.23 = (bf16[1,3,64,128]{3,2,1,0:T(8,128)(2,1)S(1)}, bf16[1,3,64,128]{3,2,1,0:T(8,128)(2,1)S(1)}, u32[]{:S(2)}, u32[]{:S(2)}) collective-permute-start(bf16[1,3,64,128]{3,2,1,0:T(8,128)(2,1)S(1)} %slice.49), channel_id=1, source_target_pairs={{0,2},{2,0},{4,6},{6,4},{8,10},{10,8},{12,14},{14,12},{16,18},{18,... | collective-permute-start | bytes 147464 | tf_op jit(solution)/shard_map/ppermute | solution.py:275
